TPU v7x, 32 devices: a whole 2x2x4 slice. The times are simulated.
32 devices in a mesh: exp: 8 (over z, y), tp: 4 (over x, core).
Axes of the slice: x: 2, y: 2, z: 4, core: 2. Of those that a mesh axis runs over, the one named last changes fastest.
Arguments:
- tokens: bfloat16 [3072, 768], P('exp', 'tp'), may hold values from -6 to 6
- w_query: bfloat16 [768, 768], P(None, 'tp'), may hold values from -0.02734375 to 0.02734375
- w_key: bfloat16 [768, 768], P(None, 'tp'), may hold values from -0.21875 to 0.21875
- w_value: bfloat16 [768, 768], P(None, 'tp'), may hold values from -0.21875 to 0.21875
- w_output: bfloat16 [768, 768], P('tp'), may hold values from -1.75 to 1.75
- bias_table: bfloat16 [32, 12], P(None, 'tp'), may hold values from -4 to 4
- w_router: bfloat16 [768, 8], P('tp'), may hold values from -0.15625 to 0.15625
- w_in: bfloat16 [8, 768, 3072], P('exp', None, 'tp'), may hold values from -0.21875 to 0.21875
- w_out: bfloat16 [8, 3072, 768], P('exp', 'tp'), may hold values from -3.5 to 3.5
- gain_attn: bfloat16 [768], P('tp'), may hold values from 0.5 to 1.5
- gain_ffn: bfloat16 [768], P('tp'), may hold values from 0.5 to 1.5
- routes: int32 [3072, 1], P('exp'), may hold values from 0 to 7; in each aligned block of 384 rows (0 to 383, 384 to 767, ...) at most 54 rows name the same one
- segments: int32 [8, 384], P('exp'), may hold values from 0 to 3, never falling along the last dimension, each value on 1 to 192 neighbouring positions
- buckets: int32 [767], replicated, may hold values from 0 to 31
- cotangent: bfloat16 [3072, 768], P('exp', 'tp'), may hold values from -6 to 6
Outputs:
- layer_out: bfloat16 [3072, 768], P('exp', 'tp')
- grad_tokens: bfloat16 [3072, 768], P('exp', 'tp')
- grad_query: bfloat16 [768, 768], P(None, 'tp')
- grad_key: bfloat16 [768, 768], P(None, 'tp')
- grad_value: bfloat16 [768, 768], P(None, 'tp')
- grad_output: bfloat16 [768, 768], P('tp')
- grad_table: bfloat16 [32, 12], P(None, 'tp')
- grad_router: bfloat16 [768, 8], P('tp')
- grad_in: bfloat16 [8, 768, 3072], P('exp', None, 'tp')
- grad_out: bfloat16 [8, 3072, 768], P('exp', 'tp')
- grad_gain_attn: bfloat16 [768], P('tp')
- grad_gain_ffn: bfloat16 [768], P('tp')
Inputs may be any that keep to these rules, and one draw needn't show every extreme that they name: `routes`: in the 384 tokens of one sequence no expert is named more than 54 times, a bound that some block reaches. `segments`: within a sequence the numbers never fall; each document has 1 to 192 tokens.
All inputs are finite; a program needn't handle non-finite values.
Results may differ from a plain program's by a relative error of at most 0.025.
Values may be sent and summed in bfloat16 or wider, within the bound.
No kernel may reach another device: no remote copies, remote signals or barrier semaphores. Data moves between devices by JAX's collectives and lax.ppermute only.
A program may use at most 128 MiB of HBM per device.

v0:
```python
import math

import jax
import jax.numpy as jnp
from jax import lax
from jax.experimental import pallas as pl
from jax.experimental.pallas import tpu as pltpu
from jax.sharding import PartitionSpec as P

HD = 64
EPSILON = 1e-06
NEG_FILL = -1e30
HIGHEST = lax.Precision.HIGHEST
f32 = jnp.float32
bf16 = jnp.bfloat16
PART_ORDER = (0, 2, 1, 3)
VMEM = pl.BlockSpec(memory_space=pltpu.VMEM)
SMEM = pl.BlockSpec(memory_space=pltpu.SMEM)


def run(body, outs, args, name, flops=0):
    specs = [SMEM if a.ndim == 1 else VMEM for a in args]
    moved = sum(a.size * a.dtype.itemsize for a in args)
    moved += sum(math.prod(s) * jnp.dtype(d).itemsize for s, d in outs)
    return pl.pallas_call(
        body,
        out_shape=[jax.ShapeDtypeStruct(s, d) for s, d in outs],
        in_specs=specs,
        out_specs=[VMEM] * len(outs),
        compiler_params=pltpu.CompilerParams(vmem_limit_bytes=48 * 2**20),
        cost_estimate=pl.CostEstimate(flops=flops, bytes_accessed=moved, transcendentals=0),
        name=name,
    )(*args)


def swap(value, axis, mask):
    size = lax.axis_size(axis)
    return lax.ppermute(value, axis, [(i, i ^ mask) for i in range(size)])


def mm(left, right):
    return jnp.dot(left, right, preferred_element_type=f32)


def mm_tn(left, right):
    return lax.dot_general(left, right, (((0,), (0,)), ((), ())), preferred_element_type=f32)


def mm_nt(left, right):
    return lax.dot_general(left, right, (((1,), (1,)), ((), ())), preferred_element_type=f32)


def iota(shape, dim):
    return lax.broadcasted_iota(jnp.int32, shape, dim)


def absolute(pieces, me, place):
    picked = pieces[place]
    for rel in range(1, len(pieces)):
        picked = jnp.where((me ^ rel) == place, pieces[rel], picked)
    return jnp.where(me == place, pieces[0], picked)


def join_lanes(pieces):
    return jnp.concatenate(pieces, axis=1)


def gather_pieces(value):
    across = swap(value, "tp", 2)
    beside = swap(value, "tp", 1)
    return value, beside, across, swap(across, "tp", 1)


def scatter_sum(parts):
    half = parts[:2] + swap(parts[2:], "tp", 1)
    return half[0], swap(half[1], "tp", 2)


def reduce_all(total, order):
    place = lax.axis_index("exp")
    for mask in order:
        half = total.shape[0] // 2
        bit = (place // mask) % 2
        keep = lax.dynamic_slice_in_dim(total, bit * half, half, 0)
        send = lax.dynamic_slice_in_dim(total, (1 - bit) * half, half, 0)
        total = keep + swap(send, "exp", mask)
    for mask in order[::-1]:
        bit = (place // mask) % 2
        other = swap(total, "exp", mask)
        total = jnp.where(
            bit == 0,
            jnp.concatenate([total, other], 0),
            jnp.concatenate([other, total], 0),
        )
    return total


def local(
    tokens,
    w_query,
    w_key,
    w_value,
    w_output,
    bias_table,
    w_router,
    w_in,
    w_out,
    gain_attn,
    gain_ffn,
    routes,
    segments,
    buckets,
    cotangent,
):
    length, quarter = tokens.shape
    ways = lax.axis_size("tp")
    owners = lax.axis_size("exp")
    width = quarter * ways
    here = w_query.shape[1]
    heads = here // HD
    experts = w_router.shape[1]
    bins = bias_table.shape[0]
    hidden_here = w_in.shape[2]
    capacity = max(2, length // owners * 9 // 8)
    per = -(-capacity // ways)
    while experts * per % 128:
        per += 1
    rows = experts * per
    span = 2 * length
    extra = -(-(experts + 2) // 16) * 16
    me_tp = lax.axis_index("tp").astype(jnp.int32)
    me = me_tp[None]
    lanes = 128

    def slot_body(me_ref, route_ref, cot_ref, dest_row_ref, dest_col_ref, cots_ref):
        mine = me_ref[0]
        col = route_ref[...]
        above = iota((length, length), 0)
        along = iota((length, length), 1)
        eye = above == along
        row = jnp.sum(jnp.where(eye, col, 0), axis=0, keepdims=True)
        same = col == row

        def dest(slot, expert):
            chunk = jnp.zeros_like(slot)
            for t in range(1, ways):
                chunk = chunk + (slot >= t * per).astype(jnp.int32)
            return (chunk ^ mine) * rows + expert * per + slot - chunk * per

        slot_row = jnp.sum(jnp.where(same & (above < along), 1, 0), axis=0, keepdims=True)
        slot_col = jnp.sum(jnp.where(same & (along < above), 1, 0), axis=1, keepdims=True)
        dest_row = dest(slot_row, row)
        dest_row_ref[...] = dest_row
        dest_col_ref[...] = dest(slot_col, col)
        cot = cot_ref[...]
        for rel in range(ways):
            hot = (iota((rows, length), 0) + rel * rows == dest_row).astype(bf16)
            cots_ref[rel] = mm(hot, cot).astype(bf16)

    dest_row, dest_col, cots = run(
        slot_body,
        [((1, length), jnp.int32), ((length, 1), jnp.int32), ((ways, rows, quarter), bf16)],
        (me, routes, cotangent),
        "slots",
    )

    shards = jnp.concatenate(
        [
            tokens,
            w_router.T,
            gain_attn[None],
            gain_ffn[None],
            jnp.zeros((extra - experts - 2, quarter), bf16),
        ],
        axis=0,
    )
    shards = gather_pieces(shards)
    cot_pieces = [cots[0]] + [swap(cots[rel], "tp", rel) for rel in range(1, ways)]

    bucket_row = jnp.pad(buckets, (0, span - buckets.shape[0]), constant_values=-1)[None]

    def attend_body(
        me_ref,
        s0,
        s1,
        s2,
        s3,
        wq_ref,
        wk_ref,
        wv_ref,
        wo_ref,
        table_ref,
        bucket_ref,
        seg_ref,
        dest_ref,
        x_ref,
        small_ref,
        r1_ref,
        n1_ref,
        q_ref,
        k_ref,
        v_ref,
        p_ref,
        attn_ref,
        part_ref,
        xrow_ref,
    ):
        mine = me_ref[0]
        pieces = [s0[...], s1[...], s2[...], s3[...]]
        full = join_lanes([absolute(pieces, mine, t) for t in range(ways)])
        x_low = full[:length]
        small = full[length:]
        x_ref[...] = x_low
        small_ref[...] = small
        x = x_low.astype(f32)
        gain = small[experts : experts + 1].astype(f32)
        r1 = lax.rsqrt(jnp.mean(x * x, axis=-1, keepdims=True) + EPSILON)
        r1_ref[...] = r1
        n1 = (x * r1 * gain).astype(bf16)
        n1_ref[...] = n1
        q = mm(n1, wq_ref[...]).astype(bf16)
        k = mm(n1, wk_ref[...]).astype(bf16)
        v = mm(n1, wv_ref[...]).astype(bf16)
        q_ref[...] = q
        k_ref[...] = k
        v_ref[...] = v
        hot = (iota((bins, span), 0) == bucket_ref[...]).astype(bf16)
        offsets = mm_tn(table_ref[...], hot)
        above = iota((length, length), 0)
        along = iota((length, length), 1)
        seg_row = seg_ref[...]
        seg_col = jnp.sum(jnp.where(above == along, seg_row, 0), axis=1, keepdims=True)
        same = seg_col == seg_row
        head_of = iota((1, here), 1) // HD
        attn = jnp.zeros((length, here), f32)
        for h in range(heads):
            mask = (head_of == h).astype(bf16)
            spread = jnp.broadcast_to(offsets[h : h + 1], (length, span))
            bias = pltpu.roll(spread, length + 1, 1, stride=1, stride_axis=0)[:, :length]
            s = jnp.where(same, mm_nt(k * mask, q) + bias, NEG_FILL)
            e = jnp.exp(s - jnp.max(s, axis=0, keepdims=True))
            p = (e / jnp.sum(e, axis=0, keepdims=True)).astype(bf16)
            p_ref[h] = p
            attn = attn + mm_tn(p, v * mask)
        attn = attn.astype(bf16)
        attn_ref[...] = attn
        dest = dest_ref[...]
        for at, rel in enumerate(PART_ORDER):
            hot = (iota((rows, length), 0) + rel * rows == dest).astype(bf16)
            part_ref[at] = mm(mm(hot, attn).astype(bf16), wo_ref[...]).astype(bf16)
            if rel == 0:
                xrow_ref[...] = mm(hot, x_low).astype(bf16)

    x_full, small, r1, n1, q, k, v, probs, attn, o_parts, x_rows = run(
        attend_body,
        [
            ((length, width), bf16),
            ((extra, width), bf16),
            ((length, 1), f32),
            ((length, width), bf16),
            ((length, here), bf16),
            ((length, here), bf16),
            ((length, here), bf16),
            ((heads, length, length), bf16),
            ((length, here), bf16),
            ((ways, rows, width), bf16),
            ((rows, width), bf16),
        ],
        (
            me,
            *shards,
            w_query,
            w_key,
            w_value,
            w_output,
            bias_table,
            bucket_row,
            segments,
            dest_row,
        ),
        "attend",
    )
    o_kept, o_came = scatter_sum(o_parts)

    def route_body(
        me_ref,
        kept_ref,
        came_ref,
        xrow_ref,
        small_ref,
        c0,
        c1,
        c2,
        c3,
        h_ref,
        aux_ref,
        dout_ref,
        send_ref,
    ):
        mine = me_ref[0]
        h = xrow_ref[...].astype(f32) + (kept_ref[...].astype(f32) + came_ref[...].astype(f32))
        h_ref[...] = h
        r2 = lax.rsqrt(jnp.mean(h * h, axis=-1, keepdims=True) + EPSILON)
        gain = small_ref[experts + 1 : experts + 2].astype(f32)
        n2 = h * r2 * gain
        router = small_ref[0:experts].astype(f32)
        logits = lax.dot_general(
            n2, router, (((1,), (1,)), ((), ())), precision=HIGHEST, preferred_element_type=f32
        )
        e = jnp.exp(logits - jnp.max(logits, axis=-1, keepdims=True))
        p = e / jnp.sum(e, axis=-1, keepdims=True)
        owner = iota((rows, experts), 0) - iota((rows, experts), 1) * per
        own = (owner >= 0) & (owner < per)
        g = jnp.sum(jnp.where(own, p, 0.0), axis=-1, keepdims=True)
        pieces = [c0[...], c1[...], c2[...], c3[...]]
        dout = join_lanes([absolute(pieces, mine, t) for t in range(ways)])
        dout_ref[...] = dout
        aux_ref[...] = jnp.zeros_like(aux_ref)
        aux_ref[:, 0:experts] = p
        aux_ref[:, lanes - 2 : lanes - 1] = r2
        aux_ref[:, lanes - 1 : lanes] = g
        send_ref[:, 0:width] = n2.astype(bf16)
        send_ref[:, width : 2 * width] = (g * dout.astype(f32)).astype(bf16)

    h_rows, aux, dout_rows, send = run(
        route_body,
        [
            ((rows, width), f32),
            ((rows, lanes), f32),
            ((rows, width), bf16),
            ((rows, 2 * width), bf16),
        ],
        (me, o_kept, o_came, x_rows, small, *cot_pieces),
        "route",
    )

    def over_experts(value):
        blocks = value.reshape(experts, per, value.shape[1])
        moved = lax.all_to_all(blocks, "exp", split_axis=0, concat_axis=0, tiled=True)
        return moved.reshape(rows, value.shape[1])

    arrived = gather_pieces(over_experts(send))

    def expert_body(a0, a1, a2, a3, win_ref, wout_ref, act_ref, dz_ref, du_ref):
        pieces = [a0, a1, a2, a3]
        u = jnp.concatenate([a[:, 0:width] for a in pieces], axis=0)
        dy = jnp.concatenate([a[:, width : 2 * width] for a in pieces], axis=0)
        z = mm(u, win_ref[0])
        c = math.sqrt(2.0 / math.pi)
        t = jnp.tanh(c * (z + 0.044715 * z * z * z))
        act = (0.5 * z * (1.0 + t)).astype(bf16)
        act_ref[...] = act
        slope = 0.5 * (1.0 + t) + 0.5 * z * (1.0 - t * t) * (c * (1.0 + 3 * 0.044715 * z * z))
        dact = mm_nt(dy, wout_ref[0])
        dot = jnp.sum(dact * act.astype(f32), axis=-1, keepdims=True)
        dz = (dact * slope).astype(bf16)
        dz_ref[...] = dz
        du = mm_nt(dz, win_ref[0]).astype(bf16)
        high = dot.astype(bf16)
        low = (dot - high.astype(f32)).astype(bf16)
        lane = iota((ways * rows, lanes), 1)
        tail = jnp.where(lane == 0, high.astype(f32), jnp.where(lane == 1, low.astype(f32), 0.0))
        tail = tail.astype(bf16)
        for at, rel in enumerate(PART_ORDER):
            du_ref[at, :, 0:width] = du[rel * rows : (rel + 1) * rows]
            du_ref[at, :, width : width + lanes] = tail[rel * rows : (rel + 1) * rows]

    act, dz, du_parts = run(
        expert_body,
        [
            ((ways * rows, hidden_here), bf16),
            ((ways * rows, hidden_here), bf16),
            ((ways, rows, width + lanes), bf16),
        ],
        (*arrived, w_in, w_out),
        "expert",
    )
    du_kept, du_came = scatter_sum(du_parts)
    du_rows = over_experts(du_kept + du_came)

    def value_body(act_ref, wout_ref, y_ref):
        y = mm(act_ref[...], wout_ref[0]).astype(bf16)
        for at, rel in enumerate(PART_ORDER):
            y_ref[at] = y[rel * rows : (rel + 1) * rows]

    (y_parts,) = run(value_body, [((ways, rows, width), bf16)], (act, w_out), "value")
    y_kept, y_came = scatter_sum(y_parts)
    y_rows = over_experts(y_kept + y_came)

    def weights_body(a0, a1, a2, a3, act_ref, dz_ref, gin_ref, gout_ref):
        pieces = [a0, a1, a2, a3]
        u = jnp.concatenate([a[:, 0:width] for a in pieces], axis=0)
        dy = jnp.concatenate([a[:, width : 2 * width] for a in pieces], axis=0)
        gin_ref[0] = mm_tn(u, dz_ref[...]).astype(bf16)
        gout_ref[0] = mm_tn(act_ref[...], dy).astype(bf16)

    grad_in, grad_out = run(
        weights_body,
        [((1, width, hidden_here), bf16), ((1, hidden_here, width), bf16)],
        (*arrived, act, dz),
        "expert_weights",
    )

    def back_body(du_ref, h_ref, aux_ref, dout_ref, small_ref, do_ref, parts_ref):
        du = du_ref[:, 0:width].astype(f32)
        gg = du_ref[:, width : width + 1].astype(f32) + du_ref[
            :, width + 1 : width + 2
        ].astype(f32)
        h = h_ref[...]
        p = aux_ref[:, 0:experts]
        r2 = aux_ref[:, lanes - 2 : lanes - 1]
        gain = small_ref[experts + 1 : experts + 2].astype(f32)
        router = small_ref[0:experts].astype(f32)
        owner = iota((rows, experts), 0) - iota((rows, experts), 1) * per
        own = ((owner >= 0) & (owner < per)).astype(f32)
        dlogits = gg * (own - p)
        dn2 = du + lax.dot_general(
            dlogits, router, (((1,), (0,)), ((), ())), precision=HIGHEST, preferred_element_type=f32
        )
        hr = h * r2
        n2 = hr * gain
        inner = jnp.sum(dn2 * gain * h, axis=-1, keepdims=True)
        dh = dout_ref[...].astype(f32) + r2 * gain * dn2 - hr * (r2 * r2 / width) * inner
        do_ref[...] = dh.astype(bf16)
        parts_ref[...] = jnp.zeros_like(parts_ref)
        parts_ref[0:experts] = lax.dot_general(
            dlogits, n2, (((0,), (0,)), ((), ())), precision=HIGHEST, preferred_element_type=f32
        )
        parts_ref[experts : experts + 1] = jnp.sum(dn2 * hr, axis=0, keepdims=True)

    do_rows, small_parts = run(
        back_body,
        [((rows, width), bf16), ((extra, width), f32)],
        (du_rows, h_rows, aux, dout_rows, small),
        "residual_back",
    )
    do_pieces = gather_pieces(do_rows)

    def outer_body(me_ref, d0, d1, d2, d3, dest_ref, wo_ref, attn_ref, da_ref, own_ref, gwo_ref):
        mine = me_ref[0]
        dest = dest_ref[...]
        total = jnp.zeros((length, width), f32)
        for rel, piece in enumerate((d0, d1, d2, d3)):
            hot = (iota((length, rows), 1) + rel * rows == dest).astype(bf16)
            total = total + mm(hot, piece[...])
        do = total.astype(bf16)
        gwo_ref[...] = mm_tn(attn_ref[...], do).astype(bf16)
        da_ref[...] = mm_nt(do, wo_ref[...]).astype(bf16)
        own = do[:, 0:quarter]
        for t in range(1, ways):
            own = jnp.where(mine == t, do[:, t * quarter : (t + 1) * quarter], own)
        own_ref[...] = own

    da, dh_own, grad_output = run(
        outer_body,
        [((length, here), bf16), ((length, quarter), bf16), ((here, width), bf16)],
        (me, *do_pieces, dest_col, w_output, attn),
        "output_back",
    )

    def softmax_back_body(
        me_ref,
        q_ref,
        k_ref,
        v_ref,
        p_ref,
        da_ref,
        n1_ref,
        bucket_ref,
        dq_ref,
        dk_ref,
        dv_ref,
        grads_ref,
        table_ref,
    ):
        mine = me_ref[0]
        q, k, v, da = q_ref[...], k_ref[...], v_ref[...], da_ref[...]
        head_of = iota((1, here), 1) // HD
        hot = (iota((bins, span), 0) == bucket_ref[...]).astype(f32)
        flip = (iota((length, length), 0) + iota((length, length), 1) == length - 1).astype(bf16)
        dq = jnp.zeros((length, here), f32)
        dk = jnp.zeros((length, here), f32)
        dv = jnp.zeros((length, here), f32)
        tables = []
        for h in range(heads):
            mask = (head_of == h).astype(bf16)
            p_low = p_ref[h]
            p = p_low.astype(f32)
            da_h = da * mask
            dp = mm_nt(v, da_h)
            dv = dv + mm(p_low, da_h)
            inner = jnp.sum(p * dp, axis=0, keepdims=True)
            ds = (p * (dp - inner)).astype(bf16)
            dq = dq + mm_tn(ds, k * mask)
            dk = dk + mm(ds, q * mask)
            flipped = mm(flip, ds)
            flipped = jnp.concatenate([flipped, jnp.zeros_like(flipped)], axis=1)
            offsets = jnp.sum(
                pltpu.roll(flipped, 0, 1, stride=1, stride_axis=0), axis=0, keepdims=True
            )
            tables.append(
                lax.dot_general(
                    offsets,
                    hot,
                    (((1,), (1,)), ((), ())),
                    precision=HIGHEST,
                    preferred_element_type=f32,
                )
            )
        dq, dk, dv = dq.astype(bf16), dk.astype(bf16), dv.astype(bf16)
        dq_ref[...] = dq
        dk_ref[...] = dk
        dv_ref[...] = dv
        n1 = n1_ref[...]
        grads_ref[0:width, 0:here] = mm_tn(n1, dq).astype(bf16)
        grads_ref[0:width, here : 2 * here] = mm_tn(n1, dk).astype(bf16)
        gv = mm_tn(n1, dv).astype(bf16)
        grads_ref[width : width + width // 2, 0:here] = gv[0 : width // 2]
        grads_ref[width : width + width // 2, here : 2 * here] = gv[width // 2 :]
        table_ref[...] = jnp.zeros_like(table_ref)
        for t in range(ways):
            keep = (mine == t).astype(f32)
            for h in range(heads):
                table_ref[h : h + 1, t * bins : (t + 1) * bins] = tables[h] * keep

    dq, dk, dv, grads, table_part = run(
        softmax_back_body,
        [
            ((length, here), bf16),
            ((length, here), bf16),
            ((length, here), bf16),
            ((width + width // 2, 2 * here), bf16),
            ((8, width), f32),
        ],
        (me, q, k, v, probs, da, n1, bucket_row),
        "softmax_back",
    )

    def norm_back_body(me_ref, dq_ref, dk_ref, dv_ref, wq, wk, wv, x_ref, r1_ref, small_ref, *outs):
        part_ref, gain_ref = outs
        mine = me_ref[0]
        dn1 = mm_nt(dq_ref[...], wq[...])
        dn1 = dn1 + mm_nt(dk_ref[...], wk[...])
        dn1 = dn1 + mm_nt(dv_ref[...], wv[...])
        x = x_ref[...].astype(f32)
        gain = small_ref[experts : experts + 1].astype(f32)
        prod = dn1 * x
        gain_ref[...] = jnp.zeros_like(gain_ref)
        gain_ref[0:1] = jnp.sum(prod * r1_ref[...], axis=0, keepdims=True)
        dot = jnp.sum(prod * gain, axis=-1, keepdims=True)
        high = dot.astype(bf16).astype(f32)
        lane = iota((length, lanes), 1)
        tail = jnp.where(lane == 0, high, jnp.where(lane == 1, dot - high, 0.0)).astype(bf16)
        low = dn1.astype(bf16)
        wide = part_ref.shape[2]
        for at, rel in enumerate(PART_ORDER):
            piece = low[:, 0:quarter]
            for t in range(1, ways):
                piece = jnp.where((mine ^ rel) == t, low[:, t * quarter : (t + 1) * quarter], piece)
            part_ref[at, :, 0:quarter] = piece
            part_ref[at, :, quarter:wide] = tail[:, 0 : wide - quarter]

    wide = -(-(quarter + 2) // 128) * 128
    dn1_parts, gain_part = run(
        norm_back_body,
        [((ways, length, wide), bf16), ((8, width), f32)],
        (me, dq, dk, dv, w_query, w_key, w_value, x_full, r1, small),
        "norm_back",
    )
    dn1_kept, dn1_came = scatter_sum(dn1_parts)

    def tokens_body(kept_ref, came_ref, dh_ref, tok_ref, r1_ref, gain_ref, out_ref):
        total = kept_ref[...].astype(f32) + came_ref[...].astype(f32)
        dn1 = total[:, 0:quarter]
        dot = total[:, quarter : quarter + 1] + total[:, quarter + 1 : quarter + 2]
        one = r1_ref[...]
        x = tok_ref[...].astype(f32)
        out_ref[...] = (
            dh_ref[...].astype(f32)
            + one * gain_ref[...].astype(f32) * dn1
            - x * (one * one * one / width) * dot
        ).astype(bf16)

    (grad_tokens,) = run(
        tokens_body,
        [((length, quarter), bf16)],
        (dn1_kept, dn1_came, dh_own, tokens, r1, gain_attn[None]),
        "tokens_back",
    )

    def out_rows_body(me_ref, h_ref, aux_ref, y_ref, out_ref):
        mine = me_ref[0]
        out = (h_ref[...] + aux_ref[:, lanes - 1 : lanes] * y_ref[...].astype(f32)).astype(bf16)
        for rel in range(ways):
            piece = out[:, 0:quarter]
            for t in range(1, ways):
                piece = jnp.where((mine ^ rel) == t, out[:, t * quarter : (t + 1) * quarter], piece)
            out_ref[rel] = piece

    (lo,) = run(
        out_rows_body,
        [((ways, rows, quarter), bf16)],
        (me, h_rows, aux, y_rows),
        "layer_rows",
    )
    lo_pieces = [lo[0]] + [swap(lo[rel], "tp", rel) for rel in range(1, ways)]

    def out_body(dest_ref, l0, l1, l2, l3, out_ref):
        dest = dest_ref[...]
        total = jnp.zeros((length, quarter), f32)
        for rel, piece in enumerate((l0, l1, l2, l3)):
            hot = (iota((length, rows), 1) + rel * rows == dest).astype(bf16)
            total = total + mm(hot, piece[...])
        out_ref[...] = total.astype(bf16)

    (layer_out,) = run(
        out_body, [((length, quarter), bf16)], (dest_col, *lo_pieces), "layer_out"
    )

    bits = [1 << b for b in range(owners.bit_length() - 1)]
    turned = bits[1:] + bits[:1]
    grad_output = reduce_all(grad_output, bits)
    half = grads.shape[0] // 2
    first = reduce_all(grads[:half], bits)
    second = reduce_all(grads[half:], turned)
    few = jnp.concatenate([small_parts, gain_part, table_part], axis=0)
    for mask in (1, 2):
        few = few + swap(few, "tp", mask)
    for mask in bits:
        few = few + swap(few, "exp", mask)
    both = jnp.concatenate([first, second], axis=0)
    grad_query = both[:width, :here]
    grad_key = both[:width, here:]
    grad_value = jnp.concatenate([both[width:, :here], both[width:, here:]], axis=0)
    mine = lax.dynamic_slice_in_dim(few, me_tp * quarter, quarter, 1)
    tables = lax.dynamic_slice_in_dim(few[extra + 8 :], me_tp * bins, bins, 1)
    return (
        layer_out,
        grad_tokens,
        grad_query,
        grad_key,
        grad_value,
        grad_output,
        tables[:heads].T.astype(bf16),
        mine[:experts].T.astype(bf16),
        grad_in,
        grad_out,
        mine[extra].astype(bf16),
        mine[experts].astype(bf16),
    )


def solution(mesh):
    placed = (
        P("exp", "tp"),
        P(None, "tp"),
        P(None, "tp"),
        P(None, "tp"),
        P("tp", None),
        P(None, "tp"),
        P("tp", None),
        P("exp", None, "tp"),
        P("exp", "tp", None),
        P("tp"),
        P("tp"),
        P("exp", None),
        P("exp", None),
        P(),
        P("exp", "tp"),
    )
    return jax.shard_map(
        local,
        mesh=mesh,
        in_specs=placed,
        out_specs=(
            P("exp", "tp"),
            P("exp", "tp"),
            P(None, "tp"),
            P(None, "tp"),
            P(None, "tp"),
            P("tp", None),
            P(None, "tp"),
            P("tp", None),
            P("exp", None, "tp"),
            P("exp", "tp", None),
            P("tp"),
            P("tp"),
        ),
        check_vma=False,
    )
```

profile of v0, /device:TPU:0, one launch (start us, length us, event | category | flops | bytes accessed | tf_op | source)
XLA Modules:
  0.0 188.4 jit_solution(1065584428361329618)
XLA Ops:
  3.9 3.0 %collective-permute-start.1 = (bf16[400,192]{1,0:T(8,128)(2,1)S(1)}, bf16[400,192]{1,0:T(8,128)(2,1)S(1)}, u32[]{:S(2)}, u32[]{:S(2)}) collective-permute-start(bf16[400,192]{1,0:T(8,128)(2,1)S(1)} %concatenate.66.s0), channel_id=1, source_target_pairs={{0,2},{1,3},{2,0},{3,1},{4,6},{5,7},{6,4},{7,5},{8,10},{9,11},{10,... | collective-permute-start | bytes 460808 | tf_op jit(solution)/shard_map/ppermute | solution.py:38
  6.9 5.1 %collective-permute-done.1.s2 = bf16[400,192]{1,0:T(8,128)(2,1)S(1)} collective-permute-done((bf16[400,192]{1,0:T(8,128)(2,1)S(1)}, bf16[400,192]{1,0:T(8,128)(2,1)S(1)}, u32[]{:S(2)}, u32[]{:S(2)}) %collective-permute-start.1) | collective-permute-done | bytes 153632 | tf_op jit(solution)/shard_map/ppermute | solution.py:38
  15.8 4.4 %attend.1 = (bf16[384,768]{1,0:T(8,128)(2,1)S(1)}, bf16[16,768]{1,0:T(8,128)(2,1)S(1)}, f32[384,1]{1,0:T(8,128)S(1)}, bf16[384,768]{1,0:T(8,128)(2,1)S(1)}, bf16...) custom-call(s32[1]{0:T(128)} %bitcast.me_ref, ...), custom_call_target="tpu_custom_call" | custom-call | bytes 5463748 | tf_op jit(solution)/shard_map/attend/pallas_call | solution.py:25
  20.9 1.3 collective-permute-done.3
  22.4 1.8 collective-permute-start.4
  24.7 1.5 collective-permute-start.7
  26.2 5.4 %collective-permute-done.6.c2 = bf16[128,192]{1,0:T(8,128)(2,1)S(1)} collective-permute-done((bf16[128,192]{1,0:T(8,128)(2,1)S(1)}, bf16[128,192]{1,0:T(8,128)(2,1)S(1)}, u32[]{:S(2)}, u32[]{:S(2)}) %collective-permute-start.6) | collective-permute-done | bytes 49184 | tf_op jit(solution)/shard_map/ppermute | solution.py:38
  32.8 18.5 %all_to_all.15 = bf16[8,16,1536]{2,1,0:T(8,128)(2,1)S(1)} all-to-all(bf16[8,16,1536]{2,1,0:T(8,128)(2,1)S(1)} %bitcast.53), channel_id=1, replica_groups=mesh['exp'=8,'tp'=4] {'exp'}, dimensions={0} | all-to-all | bytes 786432 | tf_op jit(solution)/shard_map/all_to_all | solution.py:339
  51.2 1.5 collective-permute-start.9
  52.7 8.4 %collective-permute-done.9.a2 = bf16[128,1536]{1,0:T(8,128)(2,1)S(1)} collective-permute-done((bf16[128,1536]{1,0:T(8,128)(2,1)S(1)}, bf16[128,1536]{1,0:T(8,128)(2,1)S(1)}, u32[]{:S(2)}, u32[]{:S(2)}) %collective-permute-start.9) | collective-permute-done | bytes 393248 | tf_op jit(solution)/shard_map/ppermute | solution.py:38
  61.2 1.7 collective-permute-done.10.a3
  62.9 3.8 %expert.1 = (bf16[512,768]{1,0:T(8,128)(2,1)S(1)}, bf16[512,768]{1,0:T(8,128)(2,1)S(1)}, bf16[4,128,896]{2,1,0:T(8,128)(2,1)S(1)}) custom-call(bf16[128,1536]{1,0:T(8,128)(2,1)S(1)} %bitcast.50, bf16[128,1536]{1,0:T(8,128)(2,1)S(1)} %collective-permute-done.8.a1, bf16[128,1536]{1,0:T(8,128)(2,1)S(1)} %collective-permute-done.9.a2, ...), custom_call_target="tpu_custom_call" | custom-call | bytes 6422528 | tf_op jit(solution)/shard_map/expert/pallas_call | solution.py:25
  70.1 1.6 collective-permute-start.17
  72.3 6.3 %collective-permute-done.17 = bf16[128,896]{1,0:T(8,128)(2,1)S(1)} collective-permute-done((bf16[128,896]{1,0:T(8,128)(2,1)S(1)}, bf16[128,896]{1,0:T(8,128)(2,1)S(1)}, u32[]{:S(2)}, u32[]{:S(2)}) %collective-permute-start.17) | collective-permute-done | bytes 229408 | tf_op jit(solution)/shard_map/ppermute | solution.py:38
  79.4 4.1 %all-to-all-start.2 = ((bf16[8,16,896]{2,1,0:T(8,128)(2,1)}), bf16[8,16,896]{2,1,0:T(8,128)(2,1)}, u32[]{:S(2)}, u32[]{:S(2)}) async-start(bf16[8,16,896]{2,1,0:T(8,128)(2,1)} %bitcast.54), calls=%async_computation.2 | async-start | bytes 458752 | tf_op jit(solution)/shard_map/all_to_all | solution.py:339
  83.4 1.7 fusion.1
  85.1 6.4 %all-to-all-done.2 = bf16[8,16,896]{2,1,0:T(8,128)(2,1)} async-done(((bf16[8,16,896]{2,1,0:T(8,128)(2,1)}), bf16[8,16,896]{2,1,0:T(8,128)(2,1)}, u32[]{:S(2)}, u32[]{:S(2)}) %all-to-all-start.2) | async-done | bytes 229408 | tf_op jit(solution)/shard_map/all_to_all | solution.py:339
  91.5 3.6 %all-to-all-start.1 = ((bf16[8,16,768]{2,1,0:T(8,128)(2,1)}), bf16[8,16,768]{2,1,0:T(8,128)(2,1)S(1)}, u32[]{:S(2)}, u32[]{:S(2)}) async-start(bf16[8,16,768]{2,1,0:T(8,128)(2,1)} %bitcast.55), calls=%async_computation.1 | async-start | bytes 393216 | tf_op jit(solution)/shard_map/all_to_all | solution.py:339
  97.6 2.4 %residual_back.1 = (bf16[128,768]{1,0:T(8,128)(2,1)}, f32[16,768]{1,0:T(8,128)S(1)}) custom-call(bf16[128,896]{1,0:T(8,128)(2,1)} %bitcast.21.du_ref, f32[128,768]{1,0:T(8,128)S(1)} %get-tuple-element.53.h_ref, f32[128,128]{1,0:T(8,128)S(1)} %copy-done.21, bf16[128,768]{1,0:T(8,128)(2,1)S(1)} %copy-done.27, bf16[16,768]{1,0:T(8,128)(2,1)S(1)} %copy-done.24), custom_call_target="tpu_custom_call" | custom-call | bytes 1155072 | tf_op jit(solution)/shard_map/residual_back/pallas_call | solution.py:25
  100.6 1.5 collective-permute-start.19
  104.0 2.6 %collective-permute-done.19.d2 = bf16[128,768]{1,0:T(8,128)(2,1)} collective-permute-done((bf16[128,768]{1,0:T(8,128)(2,1)}, bf16[128,768]{1,0:T(8,128)(2,1)}, u32[]{:S(2)}, u32[]{:S(2)}) %collective-permute-start.19) | collective-permute-done | bytes 196640 | tf_op jit(solution)/shard_map/ppermute | solution.py:38
  107.2 1.5 collective-permute-start.14
  111.8 2.4 %expert_weights.1 = (bf16[1,768,768]{2,1,0:T(8,128)(2,1)}, bf16[1,768,768]{2,1,0:T(8,128)(2,1)}) custom-call(bf16[128,1536]{1,0:T(8,128)(2,1)S(1)} %bitcast.51, bf16[128,1536]{1,0:T(8,128)(2,1)S(1)} %copy-done.2, bf16[128,1536]{1,0:T(8,128)(2,1)S(1)} %collective-permute-done.9.a2, bf16[128,1536]{1,0:T(8,128)(2,1)S(1)} %copy-done.4, ...), custom_call_target="tpu_custom_call" | custom-call | bytes 5505024 | tf_op jit(solution)/shard_map/expert_weights/pallas_call | solution.py:25
  115.8 1.4 layer_out.1
  118.0 2.9 %output_back.1 = (bf16[384,192]{1,0:T(8,128)(2,1)S(1)}, bf16[384,192]{1,0:T(8,128)(2,1)S(1)}, bf16[192,768]{1,0:T(8,128)(2,1)S(1)}) custom-call(s32[1]{0:T(128)} %bitcast.me_ref, bf16[128,768]{1,0:T(8,128)(2,1)} %get-tuple-element.63.d0, bf16[128,768]{1,0:T(8,128)(2,1)} %collective-permute-done.18.d1, bf16[128,768]{1,0:T(8,128)(2,1)} %collective-permute-done.19.d2, ...), custom_call_target="tpu_custom_call" | custom-call | bytes 1820164 | tf_op jit(solution)/shard_map/output_back/pallas_call | solution.py:25
  124.9 3.8 %softmax_back.1 = (bf16[384,192]{1,0:T(8,128)(2,1)S(1)}, bf16[384,192]{1,0:T(8,128)(2,1)S(1)}, bf16[384,192]{1,0:T(8,128)(2,1)S(1)}, bf16[1152,384]{1,0:T(8,128)(2,1)S(1)}, f32[8,768]{1,0:T(8,128)S(1)}) custom-call(s32[1]{0:T(128)} %bitcast.me_ref, bf16[384,192]{1,0:T(8,128)(2,1)S(1)} %copy-done.31, bf16[384,192]{1,0:T(8,128)(2,1)S(1)} %copy-done.33, ...), custom_call_target="tpu_custom_call" | custom-call | bytes 3419140 | tf_op jit(solution)/shard_map/softmax_back/pallas_call | solution.py:25
  128.7 1.9 norm_back.1
  131.4 1.8 collective-permute-start.35
  133.3 1.5 collective-permute-start.29
  134.9 1.6 collective-permute-start.42
  137.3 1.8 collective-permute-start.36
  139.2 1.5 collective-permute-start.23
  141.4 1.4 collective-permute-done.36
  142.8 2.5 %collective-permute-start.37 = (bf16[24,768]{1,0:T(8,128)(2,1)S(1)}, bf16[24,768]{1,0:T(8,128)(2,1)S(1)}, u32[]{:S(2)}, u32[]{:S(2)}) collective-permute-start(bf16[24,768]{1,0:T(8,128)(2,1)S(1)} %constant_dynamic-slice_fusion.1), channel_id=1, source_target_pairs={{0,16},{4,20},{8,24},{12,28},{16,0},{20,4},{24,8},{28,12},{1,17},{... | collective-permute-start | bytes 110600 | tf_op jit(solution)/shard_map/ppermute | solution.py:38
  146.6 1.2 collective-permute-done.37
  147.8 2.8 %collective-permute-start.38 = (bf16[24,768]{1,0:T(8,128)(2,1)S(1)}, bf16[24,768]{1,0:T(8,128)(2,1)S(1)}, u32[]{:S(2)}, u32[]{:S(2)}) collective-permute-start(bf16[24,768]{1,0:T(8,128)(2,1)S(1)} %dynamic-slice_add_fusion.8), channel_id=1, source_target_pairs={{0,16},{4,20},{8,24},{12,28},{16,0},{20,4},{24,8},{28,12},{1,17},{... | collective-permute-start | bytes 110600 | tf_op jit(solution)/shard_map/ppermute | solution.py:38
  150.6 3.9 %collective-permute-start.24 = (bf16[144,384]{1,0:T(8,128)(2,1)S(1)}, bf16[144,384]{1,0:T(8,128)(2,1)S(1)}, u32[]{:S(2)}, u32[]{:S(2)}) collective-permute-start(bf16[144,384]{1,0:T(8,128)(2,1)S(1)} %constant_dynamic-slice_fusion.8), channel_id=1, source_target_pairs={{0,8},{4,12},{8,0},{12,4},{16,24},{20,28},{24,16},{28,20},{1,9},{5... | collective-permute-start | bytes 331784 | tf_op jit(solution)/shard_map/ppermute | solution.py:38
  154.6 2.3 %collective-permute-start.39 = (bf16[48,768]{1,0:T(8,128)(2,1)S(1)}, bf16[48,768]{1,0:T(8,128)(2,1)S(1)}, u32[]{:S(2)}, u32[]{:S(2)}) collective-permute-start(bf16[48,768]{1,0:T(8,128)(2,1)S(1)} %maximum_select_fusion.8), channel_id=1, source_target_pairs={{0,8},{4,12},{8,0},{12,4},{16,24},{20,28},{24,16},{28,20},{1,9},{5... | collective-permute-start | bytes 221192 | tf_op jit(solution)/shard_map/ppermute | solution.py:38
  158.4 1.9 %collective-permute-start.25 = (bf16[72,384]{1,0:T(8,128)(2,1)S(1)}, bf16[72,384]{1,0:T(8,128)(2,1)S(1)}, u32[]{:S(2)}, u32[]{:S(2)}) collective-permute-start(bf16[72,384]{1,0:T(8,128)(2,1)S(1)} %constant_dynamic-slice_fusion.7), channel_id=1, source_target_pairs={{0,16},{4,20},{8,24},{12,28},{16,0},{20,4},{24,8},{28,12},{1,17},{... | collective-permute-start | bytes 165896 | tf_op jit(solution)/shard_map/ppermute | solution.py:38
  160.5 1.5 collective-permute-start.40
  163.5 1.9 %collective-permute-start.26 = (bf16[72,384]{1,0:T(8,128)(2,1)S(1)}, bf16[72,384]{1,0:T(8,128)(2,1)S(1)}, u32[]{:S(2)}, u32[]{:S(2)}) collective-permute-start(bf16[72,384]{1,0:T(8,128)(2,1)S(1)} %dynamic-slice_add_fusion.7), channel_id=1, source_target_pairs={{0,16},{4,20},{8,24},{12,28},{16,0},{20,4},{24,8},{28,12},{1,17},{... | collective-permute-start | bytes 165896 | tf_op jit(solution)/shard_map/ppermute | solution.py:38
  165.5 1.6 collective-permute-start.22
  167.1 1.1 collective-permute-start.45
  168.3 1.9 %collective-permute-start.33 = (bf16[144,384]{1,0:T(8,128)(2,1)S(1)}, bf16[144,384]{1,0:T(8,128)(2,1)S(1)}, u32[]{:S(2)}, u32[]{:S(2)}) collective-permute-start(bf16[144,384]{1,0:T(8,128)(2,1)S(1)} %maximum_select_fusion.7), channel_id=1, source_target_pairs={{0,16},{4,20},{8,24},{12,28},{16,0},{20,4},{24,8},{28,12},{1,17},{... | collective-permute-start | bytes 331784 | tf_op jit(solution)/shard_map/ppermute | solution.py:38
  170.2 1.8 collective-permute-done.26
  172.3 4.1 %collective-permute-done.45 = f32[32,768]{1,0:T(8,128)S(1)} collective-permute-done((f32[32,768]{1,0:T(8,128)S(1)}, f32[32,768]{1,0:T(8,128)S(1)}, u32[]{:S(2)}, u32[]{:S(2)}) %collective-permute-start.45) | collective-permute-done | bytes 98336 | tf_op jit(solution)/shard_map/ppermute | solution.py:38
  179.3 1.3 collective-permute-start.28
  181.7 2.8 %collective-permute-done.34 = bf16[288,384]{1,0:T(8,128)(2,1)S(1)} collective-permute-done((bf16[288,384]{1,0:T(8,128)(2,1)S(1)}, bf16[288,384]{1,0:T(8,128)(2,1)S(1)}, u32[]{:S(2)}, u32[]{:S(2)}) %collective-permute-start.34) | collective-permute-done | bytes 221216 | tf_op jit(solution)/shard_map/ppermute | solution.py:38
  (243 shorter events, 44.3 us)
Async XLA Ops:
  3.9 8.1 %collective-permute-start.1 = (bf16[400,192]{1,0:T(8,128)(2,1)S(1)}, bf16[400,192]{1,0:T(8,128)(2,1)S(1)}, u32[]{:S(2)}, u32[]{:S(2)}) collective-permute-start(bf16[400,192]{1,0:T(8,128)(2,1)S(1)} %concatenate.66.s0), channel_id=1, source_target_pairs={{0,2},{1,3},{2,0},{3,1},{4,6},{5,7},{6,4},{7,5},{8,10},{9,11},{10,... | collective-permute-start | bytes 460808 | tf_op jit(solution)/shard_map/ppermute | solution.py:38
  6.9 8.9 %collective-permute-start = (bf16[400,192]{1,0:T(8,128)(2,1)S(1)}, bf16[400,192]{1,0:T(8,128)(2,1)S(1)}, u32[]{:S(2)}, u32[]{:S(2)}) collective-permute-start(bf16[400,192]{1,0:T(8,128)(2,1)S(1)} %concatenate.66.s0), channel_id=1, source_target_pairs={{0,1},{1,0},{2,3},{3,2},{4,5},{5,4},{6,7},{7,6},{8,9},{9,8},{10,11... | collective-permute-start | bytes 460808 | tf_op jit(solution)/shard_map/ppermute | solution.py:38
  12.0 3.8 %collective-permute-start.2 = (bf16[400,192]{1,0:T(8,128)(2,1)S(1)}, bf16[400,192]{1,0:T(8,128)(2,1)S(1)}, u32[]{:S(2)}, u32[]{:S(2)}) collective-permute-start(bf16[400,192]{1,0:T(8,128)(2,1)S(1)} %collective-permute-done.1.s2), channel_id=1, source_target_pairs={{0,1},{1,0},{2,3},{3,2},{4,5},{5,4},{6,7},{7,6},{8,9},{9,8},{10,11... | collective-permute-start | bytes 460808 | tf_op jit(solution)/shard_map/ppermute | solution.py:38
  20.3 1.9 %collective-permute-start.3 = (bf16[2,128,768]{2,1,0:T(8,128)(2,1)S(1)}, bf16[2,128,768]{2,1,0:T(8,128)(2,1)S(1)}, u32[]{:S(2)}, u32[]{:S(2)}) collective-permute-start(bf16[2,128,768]{2,1,0:T(8,128)(2,1)S(1)} %slice.110), channel_id=1, source_target_pairs={{0,1},{1,0},{2,3},{3,2},{4,5},{5,4},{6,7},{7,6},{8,9},{9,8},{10,11... | collective-permute-start | bytes 1179656 | tf_op jit(solution)/shard_map/ppermute | solution.py:38
  22.4 9.5 %collective-permute-start.4 = (bf16[128,768]{1,0:T(8,128)(2,1)S(1)}, bf16[128,768]{1,0:T(8,128)(2,1)S(1)}, u32[]{:S(2)}, u32[]{:S(2)}) collective-permute-start(bf16[128,768]{1,0:T(8,128)(2,1)S(1)} %get-tuple-element.104), channel_id=1, source_target_pairs={{0,2},{1,3},{2,0},{3,1},{4,6},{5,7},{6,4},{7,5},{8,10},{9,11},{10,... | collective-permute-start | bytes 589832 | tf_op jit(solution)/shard_map/ppermute | solution.py:38
  24.2 1.9 %collective-permute-start.5 = (bf16[128,192]{1,0:T(8,128)(2,1)S(1)}, bf16[128,192]{1,0:T(8,128)(2,1)S(1)}, u32[]{:S(2)}, u32[]{:S(2)}) collective-permute-start(bf16[128,192]{1,0:T(8,128)(2,1)S(1)} %get-tuple-element.112), channel_id=1, source_target_pairs={{0,1},{1,0},{2,3},{3,2},{4,5},{5,4},{6,7},{7,6},{8,9},{9,8},{10,11... | collective-permute-start | bytes 147464 | tf_op jit(solution)/shard_map/ppermute | solution.py:38
  24.4 7.2 %collective-permute-start.6 = (bf16[128,192]{1,0:T(8,128)(2,1)S(1)}, bf16[128,192]{1,0:T(8,128)(2,1)S(1)}, u32[]{:S(2)}, u32[]{:S(2)}) collective-permute-start(bf16[128,192]{1,0:T(8,128)(2,1)S(1)} %get-tuple-element.111), channel_id=1, source_target_pairs={{0,2},{1,3},{2,0},{3,1},{4,6},{5,7},{6,4},{7,5},{8,10},{9,11},{10,... | collective-permute-start | bytes 147464 | tf_op jit(solution)/shard_map/ppermute | solution.py:38
  24.7 7.2 %collective-permute-start.7 = (bf16[128,192]{1,0:T(8,128)(2,1)S(1)}, bf16[128,192]{1,0:T(8,128)(2,1)S(1)}, u32[]{:S(2)}, u32[]{:S(2)}) collective-permute-start(bf16[128,192]{1,0:T(8,128)(2,1)S(1)} %get-tuple-element.110), channel_id=1, source_target_pairs={{0,3},{1,2},{2,1},{3,0},{4,7},{5,6},{6,5},{7,4},{8,11},{9,10},{10,... | collective-permute-start | bytes 147464 | tf_op jit(solution)/shard_map/ppermute | solution.py:38
  51.2 9.9 %collective-permute-start.9 = (bf16[128,1536]{1,0:T(8,128)(2,1)S(1)}, bf16[128,1536]{1,0:T(8,128)(2,1)S(1)}, u32[]{:S(2)}, u32[]{:S(2)}) collective-permute-start(bf16[128,1536]{1,0:T(8,128)(2,1)S(1)} %bitcast.48), channel_id=1, source_target_pairs={{0,2},{1,3},{2,0},{3,1},{4,6},{5,7},{6,4},{7,5},{8,10},{9,11},{10,... | collective-permute-start | bytes 1179656 | tf_op jit(solution)/shard_map/ppermute | solution.py:38
  52.7 8.4 %collective-permute-start.8 = (bf16[128,1536]{1,0:T(8,128)(2,1)S(1)}, bf16[128,1536]{1,0:T(8,128)(2,1)S(1)}, u32[]{:S(2)}, u32[]{:S(2)}) collective-permute-start(bf16[128,1536]{1,0:T(8,128)(2,1)S(1)} %bitcast.49), channel_id=1, source_target_pairs={{0,1},{1,0},{2,3},{3,2},{4,5},{5,4},{6,7},{7,6},{8,9},{9,8},{10,11... | collective-permute-start | bytes 1179656 | tf_op jit(solution)/shard_map/ppermute | solution.py:38
  61.1 1.7 collective-permute-start.10
  67.6 1.8 collective-permute-start.11
  67.8 2.2 %collective-permute-start.16 = (bf16[2,128,896]{2,1,0:T(8,128)(2,1)S(1)}, bf16[2,128,896]{2,1,0:T(8,128)(2,1)S(1)}, u32[]{:S(2)}, u32[]{:S(2)}) collective-permute-start(bf16[2,128,896]{2,1,0:T(8,128)(2,1)S(1)} %slice.126), channel_id=1, source_target_pairs={{0,1},{1,0},{2,3},{3,2},{4,5},{5,4},{6,7},{7,6},{8,9},{9,8},{10,11... | collective-permute-start | bytes 1376264 | tf_op jit(solution)/shard_map/ppermute | solution.py:38
  70.1 8.5 %collective-permute-start.17 = (bf16[128,896]{1,0:T(8,128)(2,1)S(1)}, bf16[128,896]{1,0:T(8,128)(2,1)S(1)}, u32[]{:S(2)}, u32[]{:S(2)}) collective-permute-start(bf16[128,896]{1,0:T(8,128)(2,1)S(1)} %slice_bitcast_fusion), channel_id=1, source_target_pairs={{0,2},{1,3},{2,0},{3,1},{4,6},{5,7},{6,4},{7,5},{8,10},{9,11},{10,... | collective-permute-start | bytes 688136 | tf_op jit(solution)/shard_map/ppermute | solution.py:38
  71.7 11.7 %collective-permute-start.12 = (bf16[128,768]{1,0:T(8,128)(2,1)S(1)}, bf16[128,768]{1,0:T(8,128)(2,1)}, u32[]{:S(2)}, u32[]{:S(2)}) collective-permute-start(bf16[128,768]{1,0:T(8,128)(2,1)S(1)} %slice_bitcast_fusion.4), channel_id=1, source_target_pairs={{0,2},{1,3},{2,0},{3,1},{4,6},{5,7},{6,4},{7,5},{8,10},{9,11},{10,... | collective-permute-start | bytes 589832 | tf_op jit(solution)/shard_map/ppermute | solution.py:38
  79.4 12.2 %all-to-all-start.2 = ((bf16[8,16,896]{2,1,0:T(8,128)(2,1)}), bf16[8,16,896]{2,1,0:T(8,128)(2,1)}, u32[]{:S(2)}, u32[]{:S(2)}) async-start(bf16[8,16,896]{2,1,0:T(8,128)(2,1)} %bitcast.54), calls=%async_computation.2 | async-start | bytes 458752 | tf_op jit(solution)/shard_map/all_to_all | solution.py:339
  91.5 11.1 %all-to-all-start.1 = ((bf16[8,16,768]{2,1,0:T(8,128)(2,1)}), bf16[8,16,768]{2,1,0:T(8,128)(2,1)S(1)}, u32[]{:S(2)}, u32[]{:S(2)}) async-start(bf16[8,16,768]{2,1,0:T(8,128)(2,1)} %bitcast.55), calls=%async_computation.1 | async-start | bytes 393216 | tf_op jit(solution)/shard_map/all_to_all | solution.py:339
  100.6 6.0 %collective-permute-start.19 = (bf16[128,768]{1,0:T(8,128)(2,1)}, bf16[128,768]{1,0:T(8,128)(2,1)}, u32[]{:S(2)}, u32[]{:S(2)}) collective-permute-start(bf16[128,768]{1,0:T(8,128)(2,1)} %get-tuple-element.63.d0), channel_id=1, source_target_pairs={{0,2},{1,3},{2,0},{3,1},{4,6},{5,7},{6,4},{7,5},{8,10},{9,11},{10,... | collective-permute-start | bytes 589832 | tf_op jit(solution)/shard_map/ppermute | solution.py:38
  103.9 14.0 %collective-permute-start.18 = (bf16[128,768]{1,0:T(8,128)(2,1)}, bf16[128,768]{1,0:T(8,128)(2,1)}, u32[]{:S(2)}, u32[]{:S(2)}) collective-permute-start(bf16[128,768]{1,0:T(8,128)(2,1)} %get-tuple-element.63.d0), channel_id=1, source_target_pairs={{0,1},{1,0},{2,3},{3,2},{4,5},{5,4},{6,7},{7,6},{8,9},{9,8},{10,11... | collective-permute-start | bytes 589832 | tf_op jit(solution)/shard_map/ppermute | solution.py:38
  106.6 11.3 %collective-permute-start.20 = (bf16[128,768]{1,0:T(8,128)(2,1)}, bf16[128,768]{1,0:T(8,128)(2,1)}, u32[]{:S(2)}, u32[]{:S(2)}) collective-permute-start(bf16[128,768]{1,0:T(8,128)(2,1)} %collective-permute-done.19.d2), channel_id=1, source_target_pairs={{0,1},{1,0},{2,3},{3,2},{4,5},{5,4},{6,7},{7,6},{8,9},{9,8},{10,11... | collective-permute-start | bytes 589832 | tf_op jit(solution)/shard_map/ppermute | solution.py:38
  106.6 7.6 %collective-permute-start.13 = (bf16[128,192]{1,0:T(8,128)(2,1)S(1)}, bf16[128,192]{1,0:T(8,128)(2,1)S(1)}, u32[]{:S(2)}, u32[]{:S(2)}) collective-permute-start(bf16[128,192]{1,0:T(8,128)(2,1)S(1)} %get-tuple-element.108), channel_id=1, source_target_pairs={{0,1},{1,0},{2,3},{3,2},{4,5},{5,4},{6,7},{7,6},{8,9},{9,8},{10,11... | collective-permute-start | bytes 147464 | tf_op jit(solution)/shard_map/ppermute | solution.py:38
  107.2 7.7 %collective-permute-start.14 = (bf16[128,192]{1,0:T(8,128)(2,1)S(1)}, bf16[128,192]{1,0:T(8,128)(2,1)}, u32[]{:S(2)}, u32[]{:S(2)}) collective-permute-start(bf16[128,192]{1,0:T(8,128)(2,1)S(1)} %get-tuple-element.107), channel_id=1, source_target_pairs={{0,2},{1,3},{2,0},{3,1},{4,6},{5,7},{6,4},{7,5},{8,10},{9,11},{10,... | collective-permute-start | bytes 147464 | tf_op jit(solution)/shard_map/ppermute | solution.py:38
  108.7 6.2 %collective-permute-start.15 = (bf16[128,192]{1,0:T(8,128)(2,1)S(1)}, bf16[128,192]{1,0:T(8,128)(2,1)}, u32[]{:S(2)}, u32[]{:S(2)}) collective-permute-start(bf16[128,192]{1,0:T(8,128)(2,1)S(1)} %get-tuple-element.106), channel_id=1, source_target_pairs={{0,3},{1,2},{2,1},{3,0},{4,7},{5,6},{6,5},{7,4},{8,11},{9,10},{10,... | collective-permute-start | bytes 147464 | tf_op jit(solution)/shard_map/ppermute | solution.py:38
  130.6 34.8 %collective-permute-start.21 = (bf16[2,384,256]{2,1,0:T(8,128)(2,1)S(1)}, bf16[2,384,256]{2,1,0:T(8,128)(2,1)S(1)}, u32[]{:S(2)}, u32[]{:S(2)}) collective-permute-start(bf16[2,384,256]{2,1,0:T(8,128)(2,1)S(1)} %slice.130), channel_id=1, source_target_pairs={{0,1},{1,0},{2,3},{3,2},{4,5},{5,4},{6,7},{7,6},{8,9},{9,8},{10,11... | collective-permute-start | bytes 1179656 | tf_op jit(solution)/shard_map/ppermute | solution.py:38
  131.4 5.8 %collective-permute-start.35 = (bf16[96,768]{1,0:T(8,128)(2,1)S(1)}, bf16[96,768]{1,0:T(8,128)(2,1)S(1)}, u32[]{:S(2)}, u32[]{:S(2)}) collective-permute-start(bf16[96,768]{1,0:T(8,128)(2,1)S(1)} %constant_dynamic-slice_fusion.3), channel_id=1, source_target_pairs={{0,4},{4,0},{8,12},{12,8},{16,20},{20,16},{24,28},{28,24},{1,5},{5... | collective-permute-start | bytes 442376 | tf_op jit(solution)/shard_map/ppermute | solution.py:38
  133.2 1.6 collective-permute-start.41
  133.3 12.0 %collective-permute-start.29 = (bf16[288,384]{1,0:T(8,128)(2,1)S(1)}, bf16[288,384]{1,0:T(8,128)(2,1)S(1)}, u32[]{:S(2)}, u32[]{:S(2)}) collective-permute-start(bf16[288,384]{1,0:T(8,128)(2,1)S(1)} %constant_dynamic-slice_fusion.6), channel_id=1, source_target_pairs={{0,8},{4,12},{8,0},{12,4},{16,24},{20,28},{24,16},{28,20},{1,9},{5... | collective-permute-start | bytes 663560 | tf_op jit(solution)/shard_map/ppermute | solution.py:38
  134.9 5.9 %collective-permute-start.42 = (f32[32,768]{1,0:T(8,128)S(1)}, f32[32,768]{1,0:T(8,128)S(1)}, u32[]{:S(2)}, u32[]{:S(2)}) collective-permute-start(f32[32,768]{1,0:T(8,128)S(1)} %add.186), channel_id=1, source_target_pairs={{0,2},{1,3},{2,0},{3,1},{4,6},{5,7},{6,4},{7,5},{8,10},{9,11},{10,... | collective-permute-start | bytes 294920 | tf_op jit(solution)/shard_map/ppermute | solution.py:38
  137.3 5.4 %collective-permute-start.36 = (bf16[48,768]{1,0:T(8,128)(2,1)S(1)}, bf16[48,768]{1,0:T(8,128)(2,1)S(1)}, u32[]{:S(2)}, u32[]{:S(2)}) collective-permute-start(bf16[48,768]{1,0:T(8,128)(2,1)S(1)} %constant_dynamic-slice_fusion.2), channel_id=1, source_target_pairs={{0,8},{4,12},{8,0},{12,4},{16,24},{20,28},{24,16},{28,20},{1,9},{5... | collective-permute-start | bytes 221192 | tf_op jit(solution)/shard_map/ppermute | solution.py:38
  139.2 7.3 %collective-permute-start.23 = (bf16[288,384]{1,0:T(8,128)(2,1)S(1)}, bf16[288,384]{1,0:T(8,128)(2,1)S(1)}, u32[]{:S(2)}, u32[]{:S(2)}) collective-permute-start(bf16[288,384]{1,0:T(8,128)(2,1)S(1)} %constant_dynamic-slice_fusion.9), channel_id=1, source_target_pairs={{0,4},{4,0},{8,12},{12,8},{16,20},{20,16},{24,28},{28,24},{1,5},{5... | collective-permute-start | bytes 663560 | tf_op jit(solution)/shard_map/ppermute | solution.py:38
  140.7 16.1 %collective-permute-start.43 = (f32[32,768]{1,0:T(8,128)S(1)}, f32[32,768]{1,0:T(8,128)S(1)}, u32[]{:S(2)}, u32[]{:S(2)}) collective-permute-start(f32[32,768]{1,0:T(8,128)S(1)} %add.187), channel_id=1, source_target_pairs={{0,4},{4,0},{8,12},{12,8},{16,20},{20,16},{24,28},{28,24},{1,5},{5... | collective-permute-start | bytes 294920 | tf_op jit(solution)/shard_map/ppermute | solution.py:38
  142.8 5.0 %collective-permute-start.37 = (bf16[24,768]{1,0:T(8,128)(2,1)S(1)}, bf16[24,768]{1,0:T(8,128)(2,1)S(1)}, u32[]{:S(2)}, u32[]{:S(2)}) collective-permute-start(bf16[24,768]{1,0:T(8,128)(2,1)S(1)} %constant_dynamic-slice_fusion.1), channel_id=1, source_target_pairs={{0,16},{4,20},{8,24},{12,28},{16,0},{20,4},{24,8},{28,12},{1,17},{... | collective-permute-start | bytes 110600 | tf_op jit(solution)/shard_map/ppermute | solution.py:38
  145.4 11.6 %collective-permute-start.30 = (bf16[144,384]{1,0:T(8,128)(2,1)S(1)}, bf16[144,384]{1,0:T(8,128)(2,1)S(1)}, u32[]{:S(2)}, u32[]{:S(2)}) collective-permute-start(bf16[144,384]{1,0:T(8,128)(2,1)S(1)} %constant_dynamic-slice_fusion.5), channel_id=1, source_target_pairs={{0,16},{4,20},{8,24},{12,28},{16,0},{20,4},{24,8},{28,12},{1,17},{... | collective-permute-start | bytes 331784 | tf_op jit(solution)/shard_map/ppermute | solution.py:38
  147.8 6.7 %collective-permute-start.38 = (bf16[24,768]{1,0:T(8,128)(2,1)S(1)}, bf16[24,768]{1,0:T(8,128)(2,1)S(1)}, u32[]{:S(2)}, u32[]{:S(2)}) collective-permute-start(bf16[24,768]{1,0:T(8,128)(2,1)S(1)} %dynamic-slice_add_fusion.8), channel_id=1, source_target_pairs={{0,16},{4,20},{8,24},{12,28},{16,0},{20,4},{24,8},{28,12},{1,17},{... | collective-permute-start | bytes 110600 | tf_op jit(solution)/shard_map/ppermute | solution.py:38
  150.6 7.7 %collective-permute-start.24 = (bf16[144,384]{1,0:T(8,128)(2,1)S(1)}, bf16[144,384]{1,0:T(8,128)(2,1)S(1)}, u32[]{:S(2)}, u32[]{:S(2)}) collective-permute-start(bf16[144,384]{1,0:T(8,128)(2,1)S(1)} %constant_dynamic-slice_fusion.8), channel_id=1, source_target_pairs={{0,8},{4,12},{8,0},{12,4},{16,24},{20,28},{24,16},{28,20},{1,9},{5... | collective-permute-start | bytes 331784 | tf_op jit(solution)/shard_map/ppermute | solution.py:38
  154.6 5.9 %collective-permute-start.39 = (bf16[48,768]{1,0:T(8,128)(2,1)S(1)}, bf16[48,768]{1,0:T(8,128)(2,1)S(1)}, u32[]{:S(2)}, u32[]{:S(2)}) collective-permute-start(bf16[48,768]{1,0:T(8,128)(2,1)S(1)} %maximum_select_fusion.8), channel_id=1, source_target_pairs={{0,8},{4,12},{8,0},{12,4},{16,24},{20,28},{24,16},{28,20},{1,9},{5... | collective-permute-start | bytes 221192 | tf_op jit(solution)/shard_map/ppermute | solution.py:38
  156.9 10.2 %collective-permute-start.44 = (f32[32,768]{1,0:T(8,128)S(1)}, f32[32,768]{1,0:T(8,128)S(1)}, u32[]{:S(2)}, u32[]{:S(2)}) collective-permute-start(f32[32,768]{1,0:T(8,128)S(1)} %add.188), channel_id=1, source_target_pairs={{0,8},{4,12},{8,0},{12,4},{16,24},{20,28},{24,16},{28,20},{1,9},{5... | collective-permute-start | bytes 294920 | tf_op jit(solution)/shard_map/ppermute | solution.py:38
  157.1 4.9 %collective-permute-start.31 = (bf16[72,384]{1,0:T(8,128)(2,1)S(1)}, bf16[72,384]{1,0:T(8,128)(2,1)S(1)}, u32[]{:S(2)}, u32[]{:S(2)}) collective-permute-start(bf16[72,384]{1,0:T(8,128)(2,1)S(1)} %constant_dynamic-slice_fusion.4), channel_id=1, source_target_pairs={{0,4},{4,0},{8,12},{12,8},{16,20},{20,16},{24,28},{28,24},{1,5},{5... | collective-permute-start | bytes 165896 | tf_op jit(solution)/shard_map/ppermute | solution.py:38
  158.4 5.1 %collective-permute-start.25 = (bf16[72,384]{1,0:T(8,128)(2,1)S(1)}, bf16[72,384]{1,0:T(8,128)(2,1)S(1)}, u32[]{:S(2)}, u32[]{:S(2)}) collective-permute-start(bf16[72,384]{1,0:T(8,128)(2,1)S(1)} %constant_dynamic-slice_fusion.7), channel_id=1, source_target_pairs={{0,16},{4,20},{8,24},{12,28},{16,0},{20,4},{24,8},{28,12},{1,17},{... | collective-permute-start | bytes 165896 | tf_op jit(solution)/shard_map/ppermute | solution.py:38
  160.5 17.9 %collective-permute-start.40 = (bf16[96,768]{1,0:T(8,128)(2,1)S(1)}, bf16[96,768]{1,0:T(8,128)(2,1)S(1)}, u32[]{:S(2)}, u32[]{:S(2)}) collective-permute-start(bf16[96,768]{1,0:T(8,128)(2,1)S(1)} %maximum_select_fusion.5), channel_id=1, source_target_pairs={{0,4},{4,0},{8,12},{12,8},{16,20},{20,16},{24,28},{28,24},{1,5},{5... | collective-permute-start | bytes 442376 | tf_op jit(solution)/shard_map/ppermute | solution.py:38
  162.0 6.2 %collective-permute-start.32 = (bf16[72,384]{1,0:T(8,128)(2,1)S(1)}, bf16[72,384]{1,0:T(8,128)(2,1)S(1)}, u32[]{:S(2)}, u32[]{:S(2)}) collective-permute-start(bf16[72,384]{1,0:T(8,128)(2,1)S(1)} %dynamic-slice_add_fusion.6), channel_id=1, source_target_pairs={{0,4},{4,0},{8,12},{12,8},{16,20},{20,16},{24,28},{28,24},{1,5},{5... | collective-permute-start | bytes 165896 | tf_op jit(solution)/shard_map/ppermute | solution.py:38
  163.5 8.5 %collective-permute-start.26 = (bf16[72,384]{1,0:T(8,128)(2,1)S(1)}, bf16[72,384]{1,0:T(8,128)(2,1)S(1)}, u32[]{:S(2)}, u32[]{:S(2)}) collective-permute-start(bf16[72,384]{1,0:T(8,128)(2,1)S(1)} %dynamic-slice_add_fusion.7), channel_id=1, source_target_pairs={{0,16},{4,20},{8,24},{12,28},{16,0},{20,4},{24,8},{28,12},{1,17},{... | collective-permute-start | bytes 165896 | tf_op jit(solution)/shard_map/ppermute | solution.py:38
  165.5 15.1 %collective-permute-start.22 = (bf16[384,256]{1,0:T(8,128)(2,1)S(1)}, bf16[384,256]{1,0:T(8,128)(2,1)S(1)}, u32[]{:S(2)}, u32[]{:S(2)}) collective-permute-start(bf16[384,256]{1,0:T(8,128)(2,1)S(1)} %get-tuple-element.102), channel_id=1, source_target_pairs={{0,2},{1,3},{2,0},{3,1},{4,6},{5,7},{6,4},{7,5},{8,10},{9,11},{10,... | collective-permute-start | bytes 589832 | tf_op jit(solution)/shard_map/ppermute | solution.py:38
  167.1 9.3 %collective-permute-start.45 = (f32[32,768]{1,0:T(8,128)S(1)}, f32[32,768]{1,0:T(8,128)S(1)}, u32[]{:S(2)}, u32[]{:S(2)}) collective-permute-start(f32[32,768]{1,0:T(8,128)S(1)} %add.189), channel_id=1, source_target_pairs={{0,16},{4,20},{8,24},{12,28},{16,0},{20,4},{24,8},{28,12},{1,17},{... | collective-permute-start | bytes 294920 | tf_op jit(solution)/shard_map/ppermute | solution.py:38
  168.3 10.0 %collective-permute-start.33 = (bf16[144,384]{1,0:T(8,128)(2,1)S(1)}, bf16[144,384]{1,0:T(8,128)(2,1)S(1)}, u32[]{:S(2)}, u32[]{:S(2)}) collective-permute-start(bf16[144,384]{1,0:T(8,128)(2,1)S(1)} %maximum_select_fusion.7), channel_id=1, source_target_pairs={{0,16},{4,20},{8,24},{12,28},{16,0},{20,4},{24,8},{28,12},{1,17},{... | collective-permute-start | bytes 331784 | tf_op jit(solution)/shard_map/ppermute | solution.py:38
  172.0 7.2 %collective-permute-start.27 = (bf16[144,384]{1,0:T(8,128)(2,1)S(1)}, bf16[144,384]{1,0:T(8,128)(2,1)S(1)}, u32[]{:S(2)}, u32[]{:S(2)}) collective-permute-start(bf16[144,384]{1,0:T(8,128)(2,1)S(1)} %maximum_select_fusion.6), channel_id=1, source_target_pairs={{0,8},{4,12},{8,0},{12,4},{16,24},{20,28},{24,16},{28,20},{1,9},{5... | collective-permute-start | bytes 331784 | tf_op jit(solution)/shard_map/ppermute | solution.py:38
  178.3 6.2 %collective-permute-start.34 = (bf16[288,384]{1,0:T(8,128)(2,1)S(1)}, bf16[288,384]{1,0:T(8,128)(2,1)S(1)}, u32[]{:S(2)}, u32[]{:S(2)}) collective-permute-start(bf16[288,384]{1,0:T(8,128)(2,1)S(1)} %maximum_select_fusion.4), channel_id=1, source_target_pairs={{0,8},{4,12},{8,0},{12,4},{16,24},{20,28},{24,16},{28,20},{1,9},{5... | collective-permute-start | bytes 663560 | tf_op jit(solution)/shard_map/ppermute | solution.py:38
  179.3 6.2 %collective-permute-start.28 = (bf16[288,384]{1,0:T(8,128)(2,1)S(1)}, bf16[288,384]{1,0:T(8,128)(2,1)S(1)}, u32[]{:S(2)}, u32[]{:S(2)}) collective-permute-start(bf16[288,384]{1,0:T(8,128)(2,1)S(1)} %maximum_select_fusion.3), channel_id=1, source_target_pairs={{0,4},{4,0},{8,12},{12,8},{16,20},{20,16},{24,28},{28,24},{1,5},{5... | collective-permute-start | bytes 663560 | tf_op jit(solution)/shard_map/ppermute | solution.py:38
  (51 other events, 303.0 us)
where the time goes:
time: 189 us; the launch traced here: 188 us
  starting transfers between devices  57.2 us (30%)
  waiting for transfers between devices  55.2 us (29%)
  local copies, waits for them, and re-layouts  25.8 us (14%)
  Pallas kernels  25.7 us (14%)
  blocking collectives  18.5 us (10%)
  other arithmetic  4.51 us (2%)
    ppermute x46, starting transfers between devices, swap(): return lax.ppermute(value, axis, [(i, i ^ mask) for i in range(size)])  49.6 us
    ppermute x46, waiting for transfers between devices, swap(): return lax.ppermute(value, axis, [(i, i ^ mask) for i in range(size)])  48.3 us
    pallas_call x13, Pallas kernels, run(): pl.pallas_call(body, out_shape=[jax.ShapeDtypeStruct(s, d) for s, d in ou...  25.7 us
    unnamed x116, local copies, waits for them, and re-layouts  21.1 us
    all_to_all x1, blocking collectives, over_experts(): lax.all_to_all(blocks, 'exp', split_axis=0, concat_axis=0, tiled=True)  18.5 us
    all_to_all x2, starting transfers between devices, over_experts(): lax.all_to_all(blocks, 'exp', split_axis=0, concat_axis=0, tiled=True)  7.63 us
    all_to_all x2, waiting for transfers between devices, over_experts(): lax.all_to_all(blocks, 'exp', split_axis=0, concat_axis=0, tiled=True)  6.91 us
  transfers between devices with their start and end apart: 48, of which 23 were waited for; matrix products, arithmetic and copies ran while one was open for 6% of the time, Pallas kernels for 4%

commit v1 on v0

v1 whole, which is shorter than its diff:
```python
import math

import jax
import jax.numpy as jnp
from jax import lax
from jax.experimental import pallas as pl
from jax.experimental.pallas import tpu as pltpu
from jax.sharding import PartitionSpec as P

HD = 64
EPSILON = 1e-06
NEG_FILL = -1e30
HIGHEST = lax.Precision.HIGHEST
LANES = 128
f32 = jnp.float32
bf16 = jnp.bfloat16
VMEM = pl.BlockSpec(memory_space=pltpu.VMEM)
SMEM = pl.BlockSpec(memory_space=pltpu.SMEM)


def run(body, outs, args, name, us=1.0, scratch=(), limit=16):
    specs = [SMEM if a.shape == (1,) else VMEM for a in args]
    moved = sum(a.size * a.dtype.itemsize for a in args)
    moved += sum(math.prod(s) * jnp.dtype(d).itemsize for s, d in outs)
    return pl.pallas_call(
        body,
        out_shape=[jax.ShapeDtypeStruct(s, d) for s, d in outs],
        in_specs=specs,
        out_specs=[VMEM] * len(outs),
        scratch_shapes=list(scratch),
        compiler_params=pltpu.CompilerParams(vmem_limit_bytes=limit * 2**20),
        cost_estimate=pl.CostEstimate(
            flops=int(us * 1.1e9), bytes_accessed=moved, transcendentals=0
        ),
        name=name,
    )(*args)


def swap(value, axis, mask):
    size = lax.axis_size(axis)
    return lax.ppermute(value, axis, [(i, i ^ mask) for i in range(size)])


def after(value, *others):
    return lax.optimization_barrier((value, *others))[0]


def mm(left, right):
    return jnp.dot(left, right, preferred_element_type=f32)


def mm_tn(left, right):
    return lax.dot_general(left, right, (((0,), (0,)), ((), ())), preferred_element_type=f32)


def mm_nt(left, right, precision=None):
    return lax.dot_general(
        left, right, (((1,), (1,)), ((), ())), precision=precision, preferred_element_type=f32
    )


def iota(shape, dim):
    return lax.broadcasted_iota(jnp.int32, shape, dim)


def absolute(pieces, me, place):
    picked = pieces[0]
    for rel in range(1, len(pieces)):
        picked = jnp.where((me ^ rel) == place, pieces[rel], picked)
    return picked


def split_low(value):
    high = value.astype(bf16)
    return high.astype(f32), value - high.astype(f32)


def two_lanes(value, count):
    high, low = split_low(value)
    lane = iota((value.shape[0], count), 1)
    return jnp.where(lane == 0, high, jnp.where(lane == 1, low, 0.0)).astype(bf16)


def gather_pieces(value):
    across = swap(value, "tp", 2)
    beside = swap(value, "tp", 1)
    return value, beside, across, swap(across, "tp", 1)


def scatter_sum(kept, passed, sent):
    came = swap(sent, "tp", 1)
    return kept, came, swap(passed + came[1], "tp", 2)


def chain_sum(keep, send, masks, tail):
    body = keep.shape[0] - tail
    total = keep
    for at, mask in enumerate(masks):
        total = keep + swap(send, "exp", mask)
        if at + 1 < len(masks):
            half = body // 2
            keep = total[:half]
            if tail:
                keep = jnp.concatenate([keep, total[body:]], axis=0)
            send = total[half:]
            body = half
    mine, few = total[:body], total[body:]
    for mask in masks[:0:-1]:
        mine = jnp.concatenate([mine, swap(mine, "exp", mask)], axis=0)
    return mine, swap(mine, "exp", masks[0]), few


def rel_of(place, masks):
    top = len(masks) - 1
    return sum(mask for at, mask in enumerate(masks) if (place >> (top - at)) & 1)


def local(
    tokens,
    w_query,
    w_key,
    w_value,
    w_output,
    bias_table,
    w_router,
    w_in,
    w_out,
    gain_attn,
    gain_ffn,
    routes,
    segments,
    buckets,
    cotangent,
):
    length, quarter = tokens.shape
    ways = lax.axis_size("tp")
    owners = lax.axis_size("exp")
    width = quarter * ways
    here = w_query.shape[1]
    heads = here // HD
    experts = w_router.shape[1]
    bins = bias_table.shape[0]
    hidden_here = w_in.shape[2]
    capacity = max(2, length // owners * 9 // 8)
    per = -(-capacity // ways)
    while experts * per % LANES:
        per += 1
    rows = experts * per
    span = 2 * length
    extra = -(-(experts + 2) // 16) * 16
    few_rows = -(-(experts + 2 + heads) // 16) * 16
    me = lax.axis_index(("exp", "tp")).astype(jnp.int32)[None]
    bits = [1 << b for b in range(owners.bit_length() - 1)]
    order_a = bits
    order_b = bits[1:] + bits[:1]
    shift = ways.bit_length() - 1

    tok_t = tokens.T
    wq_t, wk_t, wv_t = w_query.T, w_key.T, w_value.T

    tok_pieces = gather_pieces(tok_t)

    def slot_body(
        me_ref, route_ref, cot_ref, router_ref, g1_ref, g2_ref, drow_ref, dcol_ref, cots_ref, d_ref
    ):
        mine = me_ref[0] & (ways - 1)
        row = route_ref[...]
        above = iota((length, length), 0)
        along = iota((length, length), 1)
        col = jnp.sum(jnp.where(above == along, row, 0), axis=1, keepdims=True)
        same = col == row

        def dest(slot, expert):
            chunk = jnp.zeros_like(slot)
            for t in range(1, ways):
                chunk = chunk + (slot >= t * per).astype(jnp.int32)
            return (chunk ^ mine) * rows + expert * per + slot - chunk * per

        slot_row = jnp.sum(jnp.where(same & (above < along), 1, 0), axis=0, keepdims=True)
        slot_col = jnp.sum(jnp.where(same & (along < above), 1, 0), axis=1, keepdims=True)
        dest_row = dest(slot_row, row)
        drow_ref[...] = dest_row
        dcol_ref[...] = dest(slot_col, col)
        cot = cot_ref[...]
        line = iota((extra - experts, quarter), 0)
        gains = jnp.where(
            line == 0,
            g1_ref[...].astype(f32),
            jnp.where(line == 1, g2_ref[...].astype(f32), 0.0),
        )
        few = jnp.concatenate([router_ref[...].astype(f32), gains], axis=0).astype(bf16)
        for rel in range(ways):
            hot = (iota((rows, length), 0) + rel * rows == dest_row).astype(bf16)
            piece = mm_nt(hot, cot).astype(bf16)
            cots_ref[rel, 0:rows] = piece
            cots_ref[rel, rows : rows + extra] = few
            d_ref[:, rel * quarter : (rel + 1) * quarter] = piece

    dest_row, dest_col, cots, d_send = run(
        slot_body,
        [
            ((1, length), jnp.int32),
            ((length, 1), jnp.int32),
            ((ways, rows + extra, quarter), bf16),
            ((rows, width), bf16),
        ],
        (me, routes.T, cotangent.T, w_router.T, gain_attn[None], gain_ffn[None]),
        "slots",
        us=0.7,
    )
    cot_pieces = [cots[0]] + [swap(cots[rel], "tp", rel) for rel in range(1, ways)]

    def over_experts(value):
        blocks = value.reshape(experts, per, value.shape[1])
        moved = lax.all_to_all(blocks, "exp", split_axis=0, concat_axis=0, tiled=True)
        return moved.reshape(rows, value.shape[1])

    bucket_row = jnp.pad(buckets, (0, span - buckets.shape[0]), constant_values=-1)[None]

    def spread_row(few, line, count):
        pick = (iota((few.shape[0], count), 0) == line).astype(bf16)
        return mm_tn(few, pick)

    def attend_body(
        me_ref,
        t0,
        t1,
        t2,
        t3,
        c0,
        c1,
        c2,
        c3,
        wq_ref,
        wk_ref,
        wv_ref,
        wo_ref,
        table_ref,
        bucket_ref,
        seg_ref,
        dest_ref,
        x_ref,
        small_ref,
        r1_ref,
        n1_ref,
        q_ref,
        k_ref,
        v_ref,
        p_ref,
        attn_ref,
        kept_ref,
        passed_ref,
        sent_ref,
        xrow_ref,
    ):
        mine = me_ref[0] & (ways - 1)
        for rel, piece in enumerate((t0, t1, t2, t3)):
            at = pl.multiple_of((mine ^ rel) * quarter, quarter)
            x_ref[pl.ds(at, quarter), :] = piece[...]
        pieces = [c[rows : rows + extra] for c in (c0, c1, c2, c3)]
        small = jnp.concatenate([absolute(pieces, mine, t) for t in range(ways)], axis=1)
        small_ref[...] = small
        x_low = x_ref[...]
        x = x_low.astype(f32)
        r1 = lax.rsqrt(jnp.mean(x * x, axis=0, keepdims=True) + EPSILON)
        r1_ref[...] = r1
        n1 = (x * r1 * spread_row(small, experts, length)).astype(bf16)
        n1_ref[...] = n1
        q = mm(wq_ref[...], n1).astype(bf16)
        k = mm(wk_ref[...], n1).astype(bf16)
        v = mm(wv_ref[...], n1).astype(bf16)
        q_ref[...] = q
        k_ref[...] = k
        v_ref[...] = v
        hot = (iota((bins, span), 0) == bucket_ref[...]).astype(bf16)
        offsets = mm(table_ref[...], hot)
        above = iota((length, length), 0)
        along = iota((length, length), 1)
        seg_row = seg_ref[...]
        seg_col = jnp.sum(jnp.where(above == along, seg_row, 0), axis=1, keepdims=True)
        same = seg_col == seg_row
        for h in range(heads):
            part = slice(h * HD, (h + 1) * HD)
            spread = jnp.broadcast_to(offsets[h : h + 1], (length, span))
            bias = pltpu.roll(spread, length + 1, 1, stride=1, stride_axis=0)[:, :length]
            s = jnp.where(same, mm_tn(k[part], q[part]) + bias, NEG_FILL)
            e = jnp.exp(s - jnp.max(s, axis=0, keepdims=True))
            p = (e / jnp.sum(e, axis=0, keepdims=True)).astype(bf16)
            p_ref[h] = p
            attn_ref[part] = mm(v[part], p).astype(bf16)
        attn = attn_ref[...]
        dest = dest_ref[...]
        wo = wo_ref[...]
        for rel, out in enumerate((kept_ref, sent_ref.at[0], passed_ref, sent_ref.at[1])):
            hot = (iota((rows, length), 0) + rel * rows == dest).astype(bf16)
            out[...] = mm(mm_nt(hot, attn).astype(bf16), wo).astype(bf16)
            if rel == 0:
                xrow_ref[...] = mm_nt(hot, x_low).astype(bf16)

    x_full, small, r1, n1, q, k, v, probs, attn, o_kept, o_passed, o_sent, x_rows = run(
        attend_body,
        [
            ((width, length), bf16),
            ((extra, width), bf16),
            ((1, length), f32),
            ((width, length), bf16),
            ((here, length), bf16),
            ((here, length), bf16),
            ((here, length), bf16),
            ((heads, length, length), bf16),
            ((here, length), bf16),
            ((rows, width), bf16),
            ((rows, width), bf16),
            ((2, rows, width), bf16),
            ((rows, width), bf16),
        ],
        (
            me,
            *tok_pieces,
            *cot_pieces,
            wq_t,
            wk_t,
            wv_t,
            w_output,
            bias_table.T,
            bucket_row,
            segments,
            dest_row,
        ),
        "attend",
        us=4.0,
        limit=24,
    )
    o_kept, o_beside, o_across = scatter_sum(o_kept, o_passed, o_sent)

    d_pieces = gather_pieces(over_experts(d_send))

    def route_body(
        me_ref,
        kept_ref,
        beside_ref,
        across_ref,
        xrow_ref,
        small_ref,
        c0,
        c1,
        c2,
        c3,
        h_ref,
        aux_ref,
        dout_ref,
        send_ref,
    ):
        mine = me_ref[0] & (ways - 1)
        o = kept_ref[...].astype(f32) + beside_ref[0].astype(f32) + across_ref[...].astype(f32)
        h = xrow_ref[...].astype(f32) + o
        h_ref[...] = h
        r2 = lax.rsqrt(jnp.mean(h * h, axis=-1, keepdims=True) + EPSILON)
        gain = small_ref[experts + 1 : experts + 2].astype(f32)
        n2 = h * r2 * gain
        logits = mm_nt(n2, small_ref[0:experts].astype(f32), HIGHEST)
        e = jnp.exp(logits - jnp.max(logits, axis=-1, keepdims=True))
        p = e / jnp.sum(e, axis=-1, keepdims=True)
        owner = iota((rows, experts), 0) - iota((rows, experts), 1) * per
        own = (owner >= 0) & (owner < per)
        g = jnp.sum(jnp.where(own, p, 0.0), axis=-1, keepdims=True)
        pieces = [c[0:rows] for c in (c0, c1, c2, c3)]
        dout_ref[...] = jnp.concatenate([absolute(pieces, mine, t) for t in range(ways)], axis=1)
        aux_ref[...] = jnp.zeros_like(aux_ref)
        aux_ref[:, 0:experts] = p
        aux_ref[:, LANES - 2 : LANES - 1] = r2
        aux_ref[:, LANES - 1 : LANES] = g
        send_ref[:, 0:width] = n2.astype(bf16)
        send_ref[:, width : width + LANES] = two_lanes(g, LANES)

    h_rows, aux, dout_rows, send = run(
        route_body,
        [
            ((rows, width), f32),
            ((rows, LANES), f32),
            ((rows, width), bf16),
            ((rows, width + LANES), bf16),
        ],
        (me, o_kept, o_beside, o_across, x_rows, small, *cot_pieces),
        "route",
        us=0.8,
    )
    arrived = gather_pieces(over_experts(send))

    def expert_body(me_ref, a0, a1, a2, a3, d0, d1, d2, d3, win_ref, wout_ref, *outs):
        u_ref, dy_ref, act_ref, dz_ref, kept_ref, passed_ref, sent_ref = outs
        mine = me_ref[0] & (ways - 1)
        douts = (d0, d1, d2, d3)
        for rel, a in enumerate((a0, a1, a2, a3)):
            part = slice(rel * rows, (rel + 1) * rows)
            u_ref[part] = a[:, 0:width]
            g = a[:, width : width + 1].astype(f32) + a[:, width + 1 : width + 2].astype(f32)
            pieces = []
            for src in range(ways):
                at = (rel ^ src) * quarter
                pieces.append(douts[src][:, at : at + quarter])
            dout = jnp.concatenate([absolute(pieces, mine, t) for t in range(ways)], axis=1)
            dy_ref[part] = (g * dout.astype(f32)).astype(bf16)
        u = u_ref[...]
        dy = dy_ref[...]
        z = mm(u, win_ref[0])
        c = math.sqrt(2.0 / math.pi)
        t = jnp.tanh(c * (z + 0.044715 * z * z * z))
        act = (0.5 * z * (1.0 + t)).astype(bf16)
        act_ref[...] = act
        slope = 0.5 * (1.0 + t) + 0.5 * z * (1.0 - t * t) * (c * (1.0 + 3 * 0.044715 * z * z))
        dact = mm_nt(dy, wout_ref[0])
        dot = jnp.sum(dact * act.astype(f32), axis=-1, keepdims=True)
        dz = (dact * slope).astype(bf16)
        dz_ref[...] = dz
        du = mm_nt(dz, win_ref[0]).astype(bf16)
        tail = two_lanes(dot, LANES)
        for rel, out in enumerate((kept_ref, sent_ref.at[0], passed_ref, sent_ref.at[1])):
            out[:, 0:width] = du[rel * rows : (rel + 1) * rows]
            out[:, width : width + LANES] = tail[rel * rows : (rel + 1) * rows]

    u_all, dy_all, act, dz, *du_parts = run(
        expert_body,
        [
            ((ways * rows, width), bf16),
            ((ways * rows, width), bf16),
            ((ways * rows, hidden_here), bf16),
            ((ways * rows, hidden_here), bf16),
            ((rows, width + LANES), bf16),
            ((rows, width + LANES), bf16),
            ((2, rows, width + LANES), bf16),
        ],
        (me, *arrived, *d_pieces, w_in, w_out),
        "expert",
        us=4.0,
        limit=24,
    )
    du_kept, du_beside, du_across = scatter_sum(*du_parts)
    du_sum = du_kept + du_beside[0] + du_across
    du_rows = over_experts(du_sum)

    def value_body(act_ref, wout_ref, kept_ref, passed_ref, sent_ref):
        y = mm(act_ref[...], wout_ref[0]).astype(bf16)
        for rel, out in enumerate((kept_ref, sent_ref.at[0], passed_ref, sent_ref.at[1])):
            out[...] = y[rel * rows : (rel + 1) * rows]

    act_late = after(act, du_sum)
    y_parts = run(
        value_body,
        [((rows, width), bf16), ((rows, width), bf16), ((2, rows, width), bf16)],
        (act_late, w_out),
        "value",
        us=0.8,
    )
    y_kept, y_beside, y_across = scatter_sum(*y_parts)
    y_sum = y_kept + y_beside[0] + y_across

    def weights_body(u_ref, dy_ref, act_ref, dz_ref, gin_ref, gout_ref):
        gin_ref[0] = mm_tn(u_ref[...], dz_ref[...]).astype(bf16)
        gout_ref[0] = mm_tn(act_ref[...], dy_ref[...]).astype(bf16)

    grad_in, grad_out = run(
        weights_body,
        [((1, width, hidden_here), bf16), ((1, hidden_here, width), bf16)],
        (u_all, dy_all, act_late, dz),
        "expert_weights",
        us=2.5,
    )
    du_rows, y_sum, grad_in, grad_out = lax.optimization_barrier(
        (du_rows, y_sum, grad_in, grad_out)
    )
    y_rows = over_experts(y_sum)

    def back_body(du_ref, h_ref, aux_ref, dout_ref, small_ref, do_ref, parts_ref):
        du = du_ref[:, 0:width].astype(f32)
        gg = du_ref[:, width : width + 1].astype(f32)
        gg = gg + du_ref[:, width + 1 : width + 2].astype(f32)
        h = h_ref[...]
        p = aux_ref[:, 0:experts]
        r2 = aux_ref[:, LANES - 2 : LANES - 1]
        gain = small_ref[experts + 1 : experts + 2].astype(f32)
        router = small_ref[0:experts].astype(f32)
        owner = iota((rows, experts), 0) - iota((rows, experts), 1) * per
        own = ((owner >= 0) & (owner < per)).astype(f32)
        dlogits = gg * (own - p)
        dn2 = du + lax.dot_general(
            dlogits, router, (((1,), (0,)), ((), ())), precision=HIGHEST, preferred_element_type=f32
        )
        hr = h * r2
        n2 = hr * gain
        inner = jnp.sum(dn2 * gain * h, axis=-1, keepdims=True)
        dh = dout_ref[...].astype(f32) + r2 * gain * dn2 - hr * (r2 * r2 / width) * inner
        do_ref[...] = dh.astype(bf16)
        parts_ref[...] = jnp.zeros_like(parts_ref)
        parts_ref[0:experts] = lax.dot_general(
            dlogits, n2, (((0,), (0,)), ((), ())), precision=HIGHEST, preferred_element_type=f32
        )
        parts_ref[experts : experts + 1] = jnp.sum(dn2 * hr, axis=0, keepdims=True)

    do_rows, few_parts = run(
        back_body,
        [((rows, width), bf16), ((few_rows, width), f32)],
        (du_rows, h_rows, aux, dout_rows, small),
        "residual_back",
        us=2.0,
    )
    do_pieces = gather_pieces(do_rows)

    chunk = 2 * here // owners

    def attend_back_body(
        me_ref,
        d0,
        d1,
        d2,
        d3,
        drow_ref,
        dcol_ref,
        wo_ref,
        attn_ref,
        q_ref,
        k_ref,
        v_ref,
        p_ref,
        n1_ref,
        wq_ref,
        wk_ref,
        wv_ref,
        small_ref,
        few_ref,
        bucket_ref,
        own_ref,
        dq_ref,
        dk_ref,
        dv_ref,
        akeep_ref,
        asend_ref,
        bkeep_ref,
        bsend_ref,
        a_ref,
        b_ref,
    ):
        mine = me_ref[0] & (ways - 1)
        place = me_ref[0] >> shift
        stack = jnp.concatenate([d[...] for d in (d0, d1, d2, d3)], axis=0)
        hot_t = (iota((length, ways * rows), 1) == dcol_ref[...]).astype(bf16)
        do = mm(hot_t, stack).astype(bf16)
        own = stack[:, 0:quarter]
        for t in range(1, ways):
            own = jnp.where(mine == t, stack[:, t * quarter : (t + 1) * quarter], own)
        hot = (iota((ways * rows, length), 0) == drow_ref[...]).astype(bf16)
        own_ref[...] = mm_tn(own, hot).astype(bf16)
        wo = wo_ref[...]
        da = mm_nt(wo, do).astype(bf16)
        hot = (iota((bins, span), 0) == bucket_ref[...]).astype(f32)
        flip = (iota((length, length), 0) + iota((length, length), 1) == length - 1).astype(bf16)
        tables = []
        for h in range(heads):
            part = slice(h * HD, (h + 1) * HD)
            p_low = p_ref[h]
            p = p_low.astype(f32)
            dp = mm_tn(v_ref[part], da[part])
            dv_ref[part] = mm_nt(da[part], p_low).astype(bf16)
            inner = jnp.sum(p * dp, axis=0, keepdims=True)
            ds = (p * (dp - inner)).astype(bf16)
            dq_ref[part] = mm(k_ref[part], ds).astype(bf16)
            dk_ref[part] = mm_nt(q_ref[part], ds).astype(bf16)
            flipped = mm(flip, ds)
            flipped = jnp.concatenate([flipped, jnp.zeros_like(flipped)], axis=1)
            offsets = pltpu.roll(flipped, 0, 1, stride=1, stride_axis=0)
            offsets = jnp.sum(offsets, axis=0, keepdims=True)
            tables.append(mm_nt(offsets, hot, HIGHEST))
        n1 = n1_ref[...]
        gq = mm_nt(dq_ref[...], n1)
        gk = mm_nt(dk_ref[...], n1)
        gv = mm_nt(dv_ref[...], n1)
        back = gq * wq_ref[...].astype(f32) + gk * wk_ref[...].astype(f32)
        back = jnp.sum(back + gv * wv_ref[...].astype(f32), axis=0, keepdims=True)
        gain = small_ref[experts : experts + 1].astype(f32)
        gwo = mm(attn_ref[...], do)
        for c in range(owners):
            for total, ref in (((gq, gk), a_ref), ((gv, gwo), b_ref)):
                low, high = c * chunk, (c + 1) * chunk
                picked = total[0][low:high] if high <= here else total[1][low - here : high - here]
                ref[c] = picked.astype(bf16)
        tail = (owners // 2) * chunk
        for order, ref, keep, send in (
            (order_a, a_ref, akeep_ref, asend_ref),
            (order_b, b_ref, bkeep_ref, bsend_ref),
        ):
            for at in range(owners):
                out, line = (keep, at) if at < owners // 2 else (send, at - owners // 2)
                out[line * chunk : (line + 1) * chunk] = ref[rel_of(at, order) ^ place]
        few = few_ref[...]
        line = iota((few_rows, 1), 0)
        few = few + jnp.where(line == experts + 1, back / gain, 0.0)
        wide = jnp.concatenate(
            [jnp.concatenate([tables[h] * (mine == t).astype(f32) for t in range(ways)], axis=1)
             for h in range(heads)],
            axis=0,
        )
        pad = jnp.zeros((heads, width - ways * bins), f32)
        wide = jnp.concatenate([wide, pad], axis=1)
        for h in range(heads):
            few = few + jnp.where(line == experts + 2 + h, wide[h : h + 1], 0.0)
        few = few.astype(bf16)
        akeep_ref[tail : tail + few_rows] = few
        asend_ref[tail : tail + few_rows] = few

    side = (owners // 2) * chunk
    dh_own, dq, dk, dv, a_keep, a_send, b_keep, b_send = run(
        attend_back_body,
        [
            ((quarter, length), bf16),
            ((here, length), bf16),
            ((here, length), bf16),
            ((here, length), bf16),
            ((side + few_rows, width), bf16),
            ((side + few_rows, width), bf16),
            ((side, width), bf16),
            ((side, width), bf16),
        ],
        (
            me,
            *do_pieces,
            dest_row,
            dest_col,
            w_output,
            attn,
            q,
            k,
            v,
            probs,
            n1,
            wq_t,
            wk_t,
            wv_t,
            small,
            few_parts,
            bucket_row,
        ),
        "attend_back",
        us=6.0,
        scratch=[
            pltpu.VMEM((owners, chunk, width), bf16),
            pltpu.VMEM((owners, chunk, width), bf16),
        ],
        limit=24,
    )

    a_mine, a_other, few = chain_sum(a_keep, a_send, order_a, few_rows)
    b_mine, b_other, none = chain_sum(b_keep, b_send, order_b, 0)

    def norm_back_body(
        me_ref, dq_ref, dk_ref, dv_ref, wq, wk, wv, x_ref, small_ref, *outs
    ):
        kept_ref, passed_ref, sent_ref, all_ref = outs
        mine = me_ref[0] & (ways - 1)
        dn1 = mm_tn(wq[...], dq_ref[...])
        dn1 = dn1 + mm_tn(wk[...], dk_ref[...])
        dn1 = dn1 + mm_tn(wv[...], dv_ref[...])
        all_ref[...] = dn1.astype(bf16)
        gain = spread_row(small_ref[...], experts, length)
        dot = jnp.sum(dn1 * gain * x_ref[...].astype(f32), axis=0, keepdims=True)
        high, low = split_low(dot)
        line = iota((16, length), 0)
        tail = jnp.where(line == 0, high, jnp.where(line == 1, low, 0.0)).astype(bf16)
        for rel, out in enumerate((kept_ref, sent_ref.at[0], passed_ref, sent_ref.at[1])):
            at = pl.multiple_of((mine ^ rel) * quarter, quarter)
            out[0:quarter] = all_ref[pl.ds(at, quarter), :]
            out[quarter : quarter + 16] = tail

    dn1_parts = run(
        norm_back_body,
        [
            ((quarter + 16, length), bf16),
            ((quarter + 16, length), bf16),
            ((2, quarter + 16, length), bf16),
        ],
        (me, dq, dk, dv, wq_t, wk_t, wv_t, x_full, small),
        "norm_back",
        us=1.5,
        scratch=[pltpu.VMEM((width, length), bf16)],
    )
    dn1_parts = scatter_sum(*dn1_parts)

    def tokens_body(kept_ref, beside_ref, across_ref, dh_ref, tok_ref, r1_ref, c_ref, out_ref):
        total = kept_ref[...].astype(f32) + beside_ref[0].astype(f32)
        total = total + across_ref[...].astype(f32)
        dn1 = total[0:quarter]
        dot = total[quarter : quarter + 1] + total[quarter + 1 : quarter + 2]
        one = r1_ref[...]
        gain = spread_row(c_ref[rows : rows + extra], experts, length)
        x = tok_ref[...].astype(f32)
        out_ref[...] = (
            dh_ref[...].astype(f32) + one * gain * dn1 - x * (one * one * one / width) * dot
        ).astype(bf16)

    (grad_tokens,) = run(
        tokens_body,
        [((quarter, length), bf16)],
        (*dn1_parts, dh_own, tok_t, r1, cot_pieces[0]),
        "tokens_back",
        us=0.5,
    )

    def out_rows_body(me_ref, h_ref, aux_ref, y_ref, o0, o1, o2, o3, all_ref):
        mine = me_ref[0] & (ways - 1)
        out = (h_ref[...] + aux_ref[:, LANES - 1 : LANES] * y_ref[...].astype(f32)).astype(bf16)
        eye = (iota((rows, rows), 0) == iota((rows, rows), 1)).astype(bf16)
        all_ref[...] = mm_tn(out, eye).astype(bf16)
        for rel, piece in enumerate((o0, o1, o2, o3)):
            at = pl.multiple_of((mine ^ rel) * quarter, quarter)
            piece[...] = all_ref[pl.ds(at, quarter), :]

    lo = run(
        out_rows_body,
        [((quarter, rows), bf16)] * ways,
        (me, h_rows, aux, y_rows),
        "layer_rows",
        us=0.5,
        scratch=[pltpu.VMEM((width, rows), bf16)],
    )
    lo = [lo[0]] + [swap(lo[rel], "tp", rel) for rel in range(1, ways)]

    def out_body(dest_ref, l0, l1, l2, l3, out_ref):
        dest = dest_ref[...]
        total = jnp.zeros((quarter, length), f32)
        for rel, piece in enumerate((l0, l1, l2, l3)):
            hot = (iota((rows, length), 0) + rel * rows == dest).astype(bf16)
            total = total + mm(piece[...], hot)
        out_ref[...] = total.astype(bf16)

    (layer_out,) = run(
        out_body, [((quarter, length), bf16)], (dest_row, *lo), "layer_out", us=0.5
    )

    few = few.astype(f32)
    few = few + swap(few, "tp", 1)
    few_other = swap(few, "tp", 2)

    def unpack_body(
        me_ref,
        am_ref,
        ao_ref,
        bm_ref,
        bo_ref,
        few_ref,
        other_ref,
        gq_ref,
        gk_ref,
        gv_ref,
        go_ref,
        router_ref,
        g1_ref,
        g2_ref,
        table_ref,
        a_ref,
        b_ref,
    ):
        mine = me_ref[0] & (ways - 1)
        place = me_ref[0] >> shift
        for order, ref, first, second in (
            (order_a, a_ref, am_ref, ao_ref),
            (order_b, b_ref, bm_ref, bo_ref),
        ):
            for at in range(owners):
                src, line = (first, at) if at < owners // 2 else (second, at - owners // 2)
                ref[rel_of(at, order) ^ place] = src[line * chunk : (line + 1) * chunk]
        for c in range(owners):
            low, high = c * chunk, (c + 1) * chunk
            for ref, outs in ((a_ref, (gq_ref, gk_ref)), (b_ref, (gv_ref, go_ref))):
                if high <= here:
                    outs[0][low:high] = ref[c]
                else:
                    outs[1][low - here : high - here] = ref[c]
        total = few_ref[...] + other_ref[...]
        own = total[:, 0:quarter]
        for t in range(1, ways):
            own = jnp.where(mine == t, total[:, t * quarter : (t + 1) * quarter], own)
        router_ref[...] = own[0:experts].astype(bf16)
        g2_ref[...] = own[experts : experts + 1].astype(bf16)
        g1_ref[...] = own[experts + 1 : experts + 2].astype(bf16)
        lines = total[experts + 2 : experts + 2 + heads]
        table = lines[:, 0:bins]
        for t in range(1, ways):
            table = jnp.where(mine == t, lines[:, t * bins : (t + 1) * bins], table)
        table_ref[...] = table.astype(bf16)

    gq, gk, gv, go, g_router, g_one, g_two, g_table = run(
        unpack_body,
        [
            ((here, width), bf16),
            ((here, width), bf16),
            ((here, width), bf16),
            ((here, width), bf16),
            ((experts, quarter), bf16),
            ((1, quarter), bf16),
            ((1, quarter), bf16),
            ((heads, bins), bf16),
        ],
        (me, a_mine, a_other, b_mine, b_other, few, few_other),
        "unpack",
        us=1.0,
        scratch=[
            pltpu.VMEM((owners, chunk, width), bf16),
            pltpu.VMEM((owners, chunk, width), bf16),
        ],
    )
    return (
        layer_out.T,
        grad_tokens.T,
        gq.T,
        gk.T,
        gv.T,
        go,
        g_table.T,
        g_router.T,
        grad_in,
        grad_out,
        g_one[0],
        g_two[0],
    )


def solution(mesh):
    placed = (
        P("exp", "tp"),
        P(None, "tp"),
        P(None, "tp"),
        P(None, "tp"),
        P("tp", None),
        P(None, "tp"),
        P("tp", None),
        P("exp", None, "tp"),
        P("exp", "tp", None),
        P("tp"),
        P("tp"),
        P("exp", None),
        P("exp", None),
        P(),
        P("exp", "tp"),
    )
    return jax.shard_map(
        local,
        mesh=mesh,
        in_specs=placed,
        out_specs=(
            P("exp", "tp"),
            P("exp", "tp"),
            P(None, "tp"),
            P(None, "tp"),
            P(None, "tp"),
            P("tp", None),
            P(None, "tp"),
            P("tp", None),
            P("exp", None, "tp"),
            P("exp", "tp", None),
            P("tp"),
            P("tp"),
        ),
        check_vma=False,
    )
```

time: 189 us -> 175 us (0.926)
  starting transfers between devices: 57.2 us -> 43.2 us
  waiting for transfers between devices: 55.2 us -> 69.1 us
  blocking collectives: 18.5 us -> 13.6 us
  local copies, waits for them, and re-layouts: 25.8 us -> 21.6 us
  Pallas kernels: 25.7 us -> 21.9 us
    ppermute x46 -> x40, starting transfers between devices: 49.6 us -> 30.7 us  [swap(): return lax.ppermute(value, axis, [(i, i ^ mask) for i in range(size)])]
    ppermute x46 -> x40, waiting for transfers between devices: 48.3 us -> 61.2 us  [swap(): return lax.ppermute(value, axis, [(i, i ^ mask) for i in range(size)])]
    all_to_all x1, blocking collectives: 18.5 us -> 13.6 us  [over_experts(): lax.all_to_all(blocks, 'exp', split_axis=0, concat_axis=0, tiled=True)]
    all_to_all x2 -> x3, starting transfers between devices: 7.63 us -> 12.4 us  [over_experts(): lax.all_to_all(blocks, 'exp', split_axis=0, concat_axis=0, tiled=True)]
    pallas_call x13, Pallas kernels: 25.7 us -> 21.9 us  [run(): pl.pallas_call(body, out_shape=[jax.ShapeDtypeStruct(s, d) for s, d in ou...]
    all_to_all x2 -> x3, waiting for transfers between devices: 6.91 us -> 7.92 us  [over_experts(): lax.all_to_all(blocks, 'exp', split_axis=0, concat_axis=0, tiled=True)]
    unnamed x116 -> x122, local copies, waits for them, and re-layouts: 21.1 us -> 20.2 us
  transfers between devices with their start and end apart: 48 -> 43, of which waited for: 23 -> 19; matrix products, arithmetic and copies ran while one was open for 6% -> 1% of each run, Pallas kernels for 4% -> 7%
where the time goes in v1:
time: 175 us; the launch traced here: 174 us
  waiting for transfers between devices  69.1 us (39%)
  starting transfers between devices  43.2 us (25%)
  Pallas kernels  21.9 us (13%)
  local copies, waits for them, and re-layouts  21.6 us (12%)
  blocking collectives  13.6 us (8%)
  other arithmetic  2.95 us (2%)
    ppermute x40, waiting for transfers between devices, swap(): return lax.ppermute(value, axis, [(i, i ^ mask) for i in range(size)])  61.2 us
    ppermute x40, starting transfers between devices, swap(): return lax.ppermute(value, axis, [(i, i ^ mask) for i in range(size)])  30.7 us
    pallas_call x13, Pallas kernels, run(): pl.pallas_call(body, out_shape=[jax.ShapeDtypeStruct(s, d) for s, d in ou...  21.9 us
    unnamed x122, local copies, waits for them, and re-layouts  20.2 us
    all_to_all x1, blocking collectives, over_experts(): lax.all_to_all(blocks, 'exp', split_axis=0, concat_axis=0, tiled=True)  13.6 us
    all_to_all x3, starting transfers between devices, over_experts(): lax.all_to_all(blocks, 'exp', split_axis=0, concat_axis=0, tiled=True)  12.4 us
    all_to_all x3, waiting for transfers between devices, over_experts(): lax.all_to_all(blocks, 'exp', split_axis=0, concat_axis=0, tiled=True)  7.92 us
  transfers between devices with their start and end apart: 43, of which 19 were waited for; matrix products, arithmetic and copies ran while one was open for 1% of the time, Pallas kernels for 7%

profile of v1, /device:TPU:0, one launch (start us, length us, event | category | flops | bytes accessed | tf_op | source)
XLA Modules:
  0.0 173.8 jit_solution(13699761247244396943)
XLA Ops:
  0.6 3.0 %collective-permute-start.1 = (bf16[192,384]{1,0:T(8,128)(2,1)}, bf16[192,384]{1,0:T(8,128)(2,1)S(1)}, u32[]{:S(2)}, u32[]{:S(2)}) collective-permute-start(bf16[192,384]{1,0:T(8,128)(2,1)} %bitcast.79), channel_id=1, source_target_pairs={{0,2},{1,3},{2,0},{3,1},{4,6},{5,7},{6,4},{7,5},{8,10},{9,11},{10,... | collective-permute-start | bytes 442376 | tf_op jit(solution)/shard_map/ppermute | solution.py:41
  7.3 1.4 slots.1
  9.6 1.3 collective-permute-start.4
  11.2 2.5 %collective-permute-done.5.c3 = bf16[144,192]{1,0:T(8,128)(2,1)S(1)} collective-permute-done((bf16[144,192]{1,0:T(8,128)(2,1)S(1)}, bf16[144,192]{1,0:T(8,128)(2,1)S(1)}, u32[]{:S(2)}, u32[]{:S(2)}) %collective-permute-start.5) | collective-permute-done | bytes 55328 | tf_op jit(solution)/shard_map/ppermute | solution.py:41
  13.7 1.8 %collective-permute-done.4.c2 = bf16[144,192]{1,0:T(8,128)(2,1)S(1)} collective-permute-done((bf16[144,192]{1,0:T(8,128)(2,1)S(1)}, bf16[144,192]{1,0:T(8,128)(2,1)S(1)}, u32[]{:S(2)}, u32[]{:S(2)}) %collective-permute-start.4) | collective-permute-done | bytes 55328 | tf_op jit(solution)/shard_map/ppermute | solution.py:41
  15.5 3.5 %attend.1 = (bf16[768,384]{1,0:T(8,128)(2,1)S(1)}, bf16[16,768]{1,0:T(8,128)(2,1)S(1)}, f32[1,384]{1,0:T(1,128)S(1)}, bf16[768,384]{1,0:T(8,128)(2,1)S(1)}, bf16...) custom-call(s32[1]{0:T(128)} %bitcast.me_ref, ...), custom_call_target="tpu_custom_call" | custom-call | flops 4400000000 | bytes 5660356 | tf_op jit(solution)/shard_map/attend/pallas_call | solution.py:25
  19.2 1.7 collective-permute-done.6.beside_ref
  21.2 6.7 %collective-permute-done.7.across_ref = bf16[128,768]{1,0:T(8,128)(2,1)S(1)} collective-permute-done((bf16[128,768]{1,0:T(8,128)(2,1)S(1)}, bf16[128,768]{1,0:T(8,128)(2,1)S(1)}, u32[]{:S(2)}, u32[]{:S(2)}) %collective-permute-start.7) | collective-permute-done | bytes 196640 | tf_op jit(solution)/shard_map/ppermute | solution.py:41
  29.6 13.6 %all_to_all.20 = bf16[8,16,896]{2,1,0:T(8,128)(2,1)S(1)} all-to-all(bf16[8,16,896]{2,1,0:T(8,128)(2,1)S(1)} %bitcast.64), channel_id=1, replica_groups=mesh['exp'=8,'tp'=4] {'exp'}, dimensions={0} | all-to-all | bytes 458752 | tf_op jit(solution)/shard_map/all_to_all | solution.py:215
  43.2 3.4 %all-to-all-start.1 = ((bf16[8,16,768]{2,1,0:T(8,128)(2,1)}), bf16[8,16,768]{2,1,0:T(8,128)(2,1)S(1)}, u32[]{:S(2)}, u32[]{:S(2)}) async-start(bf16[8,16,768]{2,1,0:T(8,128)(2,1)} %bitcast.16), calls=%async_computation.1 | async-start | bytes 393216 | tf_op jit(solution)/shard_map/all_to_all | solution.py:215
  47.2 7.1 %all-to-all-done.1 = bf16[8,16,768]{2,1,0:T(8,128)(2,1)S(1)} async-done(((bf16[8,16,768]{2,1,0:T(8,128)(2,1)}), bf16[8,16,768]{2,1,0:T(8,128)(2,1)S(1)}, u32[]{:S(2)}, u32[]{:S(2)}) %all-to-all-start.1) | async-done | bytes 196640 | tf_op jit(solution)/shard_map/all_to_all | solution.py:215
  55.4 4.6 %collective-permute-done.12.d2 = bf16[128,768]{1,0:T(8,128)(2,1)S(1)} collective-permute-done((bf16[128,768]{1,0:T(8,128)(2,1)S(1)}, bf16[128,768]{1,0:T(8,128)(2,1)S(1)}, u32[]{:S(2)}, u32[]{:S(2)}) %collective-permute-start.12) | collective-permute-done | bytes 196640 | tf_op jit(solution)/shard_map/ppermute | solution.py:41
  60.0 1.4 collective-permute-done.13.d3
  61.4 2.9 %expert.1 = (bf16[512,768]{1,0:T(8,128)(2,1)S(1)}, bf16[512,768]{1,0:T(8,128)(2,1)S(1)}, bf16[512,768]{1,0:T(8,128)(2,1)S(1)}, bf16[512,768]{1,0:T(8,128)(2,1)S(...) custom-call(s32[1]{0:T(128)} %bitcast.me_ref, ...), custom_call_target="tpu_custom_call" | custom-call | flops 4400000000 | bytes 8126468 | tf_op jit(solution)/shard_map/expert/pallas_call | solution.py:25
  64.6 1.7 collective-permute-done.14
  66.9 7.1 %collective-permute-done.15 = bf16[128,896]{1,0:T(8,128)(2,1)S(1)} collective-permute-done((bf16[128,896]{1,0:T(8,128)(2,1)S(1)}, bf16[128,896]{1,0:T(8,128)(2,1)S(1)}, u32[]{:S(2)}, u32[]{:S(2)}) %collective-permute-start.15) | collective-permute-done | bytes 229408 | tf_op jit(solution)/shard_map/ppermute | solution.py:41
  75.7 3.6 %all-to-all-start.2 = ((bf16[8,16,896]{2,1,0:T(8,128)(2,1)}), bf16[8,16,896]{2,1,0:T(8,128)(2,1)S(1)}, u32[]{:S(2)}, u32[]{:S(2)}) async-start(bf16[8,16,896]{2,1,0:T(8,128)(2,1)} %bitcast.20), calls=%async_computation.2 | async-start | bytes 458752 | tf_op jit(solution)/shard_map/all_to_all | solution.py:215
  79.9 1.1 copy-done.17
  81.1 1.1 copy-done.32
  82.2 1.1 copy-done.34
  83.3 1.1 copy-done.36
  84.5 2.4 %expert_weights.1 = (bf16[1,768,768]{2,1,0:T(8,128)(2,1)}, bf16[1,768,768]{2,1,0:T(8,128)(2,1)}) custom-call(bf16[512,768]{1,0:T(8,128)(2,1)S(1)} %copy-done.32, bf16[512,768]{1,0:T(8,128)(2,1)S(1)} %copy-done.34, bf16[512,768]{1,0:T(8,128)(2,1)S(1)} %copy-done.17, bf16[512,768]{1,0:T(8,128)(2,1)S(1)} %copy-done.36), custom_call_target="tpu_custom_call" | custom-call | flops 2750000128 | bytes 5505024 | tf_op jit(solution)/shard_map/expert_weights/pallas_call | solution.py:25
  90.6 5.5 %collective-permute-done.22.d2 = bf16[128,768]{1,0:T(8,128)(2,1)S(1)} collective-permute-done((bf16[128,768]{1,0:T(8,128)(2,1)S(1)}, bf16[128,768]{1,0:T(8,128)(2,1)S(1)}, u32[]{:S(2)}, u32[]{:S(2)}) %collective-permute-start.22) | collective-permute-done | bytes 196640 | tf_op jit(solution)/shard_map/ppermute | solution.py:41
  96.2 5.5 %all-to-all-start.3 = ((bf16[8,16,768]{2,1,0:T(8,128)(2,1)}), bf16[8,16,768]{2,1,0:T(8,128)(2,1)S(1)}, u32[]{:S(2)}, u32[]{:S(2)}) async-start(bf16[8,16,768]{2,1,0:T(8,128)(2,1)} %bitcast.24), calls=%async_computation.3 | async-start | bytes 393216 | tf_op jit(solution)/shard_map/all_to_all | solution.py:215
  103.3 1.2 copy-done.47
  104.5 1.1 copy-done.49
  110.0 4.6 %attend_back.1 = (bf16[192,384]{1,0:T(8,128)(2,1)S(1)}, bf16[192,384]{1,0:T(8,128)(2,1)S(1)}, bf16[192,384]{1,0:T(8,128)(2,1)S(1)}, bf16[192,384]{1,0:T(8,128)(2...) custom-call(s32[1]{0:T(128)} %bitcast.me_ref, ...), custom_call_target="tpu_custom_call" | custom-call | flops 6600000000 | bytes 5928964 | tf_op jit(solution)/shard_map/attend_back/pallas_call | solution.py:25
  117.2 2.0 %collective-permute-start.32 = (bf16[192,768]{1,0:T(8,128)(2,1)S(1)}, bf16[192,768]{1,0:T(8,128)(2,1)S(1)}, u32[]{:S(2)}, u32[]{:S(2)}) collective-permute-start(bf16[192,768]{1,0:T(8,128)(2,1)S(1)} %get-tuple-element.127), channel_id=1, source_target_pairs={{0,8},{4,12},{8,0},{12,4},{16,24},{20,28},{24,16},{28,20},{1,9},{5... | collective-permute-start | bytes 884744 | tf_op jit(solution)/shard_map/ppermute | solution.py:41
  119.2 1.5 collective-permute-start.26
  122.1 1.6 collective-permute-start.19
  124.0 2.4 %collective-permute-done.32 = bf16[192,768]{1,0:T(8,128)(2,1)S(1)} collective-permute-done((bf16[192,768]{1,0:T(8,128)(2,1)S(1)}, bf16[192,768]{1,0:T(8,128)(2,1)S(1)}, u32[]{:S(2)}, u32[]{:S(2)}) %collective-permute-start.32) | collective-permute-done | bytes 294944 | tf_op jit(solution)/shard_map/ppermute | solution.py:41
  126.5 2.7 %collective-permute-start.33 = (bf16[96,768]{1,0:T(8,128)(2,1)S(1)}, bf16[96,768]{1,0:T(8,128)(2,1)S(1)}, u32[]{:S(2)}, u32[]{:S(2)}) collective-permute-start(bf16[96,768]{1,0:T(8,128)(2,1)S(1)} %slice.102), channel_id=1, source_target_pairs={{0,16},{4,20},{8,24},{12,28},{16,0},{20,4},{24,8},{28,12},{1,17},{... | collective-permute-start | bytes 442376 | tf_op jit(solution)/shard_map/ppermute | solution.py:41
  129.2 1.1 norm_back.1
  131.5 1.5 collective-permute-start.27
  133.1 2.8 %collective-permute-done.33 = bf16[96,768]{1,0:T(8,128)(2,1)S(1)} collective-permute-done((bf16[96,768]{1,0:T(8,128)(2,1)S(1)}, bf16[96,768]{1,0:T(8,128)(2,1)S(1)}, u32[]{:S(2)}, u32[]{:S(2)}) %collective-permute-start.33) | collective-permute-done | bytes 147488 | tf_op jit(solution)/shard_map/ppermute | solution.py:41
  135.9 1.5 collective-permute-start.34
  137.4 2.1 %collective-permute-done.27 = bf16[112,768]{1,0:T(8,128)(2,1)S(1)} collective-permute-done((bf16[112,768]{1,0:T(8,128)(2,1)S(1)}, bf16[112,768]{1,0:T(8,128)(2,1)S(1)}, u32[]{:S(2)}, u32[]{:S(2)}) %collective-permute-start.27) | collective-permute-done | bytes 172064 | tf_op jit(solution)/shard_map/ppermute | solution.py:41
  139.5 1.4 collective-permute-start.28
  140.9 1.5 collective-permute-start.35
  142.4 4.9 %collective-permute-done.28 = bf16[64,768]{1,0:T(8,128)(2,1)S(1)} collective-permute-done((bf16[64,768]{1,0:T(8,128)(2,1)S(1)}, bf16[64,768]{1,0:T(8,128)(2,1)S(1)}, u32[]{:S(2)}, u32[]{:S(2)}) %collective-permute-start.28) | collective-permute-done | bytes 98336 | tf_op jit(solution)/shard_map/ppermute | solution.py:41
  147.5 3.0 %collective-permute-start.36 = (bf16[96,768]{1,0:T(8,128)(2,1)S(1)}, bf16[96,768]{1,0:T(8,128)(2,1)S(1)}, u32[]{:S(2)}, u32[]{:S(2)}) collective-permute-start(bf16[96,768]{1,0:T(8,128)(2,1)S(1)} %pad_maximum_fusion.3), channel_id=1, source_target_pairs={{0,16},{4,20},{8,24},{12,28},{16,0},{20,4},{24,8},{28,12},{1,17},{... | collective-permute-start | bytes 442376 | tf_op jit(solution)/shard_map/ppermute | solution.py:41
  150.5 6.5 %collective-permute-done.29 = bf16[48,768]{1,0:T(8,128)(2,1)S(1)} collective-permute-done((bf16[48,768]{1,0:T(8,128)(2,1)S(1)}, bf16[48,768]{1,0:T(8,128)(2,1)S(1)}, u32[]{:S(2)}, u32[]{:S(2)}) %collective-permute-start.29) | collective-permute-done | bytes 73760 | tf_op jit(solution)/shard_map/ppermute | solution.py:41
  157.2 2.8 %collective-permute-done.36 = bf16[96,768]{1,0:T(8,128)(2,1)S(1)} collective-permute-done((bf16[96,768]{1,0:T(8,128)(2,1)S(1)}, bf16[96,768]{1,0:T(8,128)(2,1)S(1)}, u32[]{:S(2)}, u32[]{:S(2)}) %collective-permute-start.36) | collective-permute-done | bytes 147488 | tf_op jit(solution)/shard_map/ppermute | solution.py:41
  160.1 3.5 %collective-permute-done.30 = bf16[96,768]{1,0:T(8,128)(2,1)S(1)} collective-permute-done((bf16[96,768]{1,0:T(8,128)(2,1)S(1)}, bf16[96,768]{1,0:T(8,128)(2,1)S(1)}, u32[]{:S(2)}, u32[]{:S(2)}) %collective-permute-start.30) | collective-permute-done | bytes 147488 | tf_op jit(solution)/shard_map/ppermute | solution.py:41
  163.6 1.5 collective-permute-start.31
  165.2 1.6 collective-permute-start.25
  167.4 3.2 %collective-permute-done.25.across_ref = bf16[208,384]{1,0:T(8,128)(2,1)S(1)} collective-permute-done((bf16[208,384]{1,0:T(8,128)(2,1)S(1)}, bf16[208,384]{1,0:T(8,128)(2,1)S(1)}, u32[]{:S(2)}, u32[]{:S(2)}) %collective-permute-start.25) | collective-permute-done | bytes 159776 | tf_op jit(solution)/shard_map/ppermute | solution.py:41
  171.5 1.3 unpack.1
  (208 shorter events, 30.1 us)
Async XLA Ops:
  0.6 8.0 %collective-permute-start.1 = (bf16[192,384]{1,0:T(8,128)(2,1)}, bf16[192,384]{1,0:T(8,128)(2,1)S(1)}, u32[]{:S(2)}, u32[]{:S(2)}) collective-permute-start(bf16[192,384]{1,0:T(8,128)(2,1)} %bitcast.79), channel_id=1, source_target_pairs={{0,2},{1,3},{2,0},{3,1},{4,6},{5,7},{6,4},{7,5},{8,10},{9,11},{10,... | collective-permute-start | bytes 442376 | tf_op jit(solution)/shard_map/ppermute | solution.py:41
  3.6 11.8 %collective-permute-start = (bf16[192,384]{1,0:T(8,128)(2,1)}, bf16[192,384]{1,0:T(8,128)(2,1)S(1)}, u32[]{:S(2)}, u32[]{:S(2)}) collective-permute-start(bf16[192,384]{1,0:T(8,128)(2,1)} %bitcast.80), channel_id=1, source_target_pairs={{0,1},{1,0},{2,3},{3,2},{4,5},{5,4},{6,7},{7,6},{8,9},{9,8},{10,11... | collective-permute-start | bytes 442376 | tf_op jit(solution)/shard_map/ppermute | solution.py:41
  8.7 6.8 %collective-permute-start.2 = (bf16[192,384]{1,0:T(8,128)(2,1)S(1)}, bf16[192,384]{1,0:T(8,128)(2,1)S(1)}, u32[]{:S(2)}, u32[]{:S(2)}) collective-permute-start(bf16[192,384]{1,0:T(8,128)(2,1)S(1)} %collective-permute-done.1.t2), channel_id=1, source_target_pairs={{0,1},{1,0},{2,3},{3,2},{4,5},{5,4},{6,7},{7,6},{8,9},{9,8},{10,11... | collective-permute-start | bytes 442376 | tf_op jit(solution)/shard_map/ppermute | solution.py:41
  9.2 4.5 %collective-permute-start.5 = (bf16[144,192]{1,0:T(8,128)(2,1)S(1)}, bf16[144,192]{1,0:T(8,128)(2,1)S(1)}, u32[]{:S(2)}, u32[]{:S(2)}) collective-permute-start(bf16[144,192]{1,0:T(8,128)(2,1)S(1)} %get-tuple-element.138), channel_id=1, source_target_pairs={{0,3},{1,2},{2,1},{3,0},{4,7},{5,6},{6,5},{7,4},{8,11},{9,10},{10,... | collective-permute-start | bytes 165896 | tf_op jit(solution)/shard_map/ppermute | solution.py:41
  9.6 5.8 %collective-permute-start.4 = (bf16[144,192]{1,0:T(8,128)(2,1)S(1)}, bf16[144,192]{1,0:T(8,128)(2,1)S(1)}, u32[]{:S(2)}, u32[]{:S(2)}) collective-permute-start(bf16[144,192]{1,0:T(8,128)(2,1)S(1)} %get-tuple-element.139), channel_id=1, source_target_pairs={{0,2},{1,3},{2,0},{3,1},{4,6},{5,7},{6,4},{7,5},{8,10},{9,11},{10,... | collective-permute-start | bytes 165896 | tf_op jit(solution)/shard_map/ppermute | solution.py:41
  10.9 4.5 %collective-permute-start.3 = (bf16[144,192]{1,0:T(8,128)(2,1)S(1)}, bf16[144,192]{1,0:T(8,128)(2,1)S(1)}, u32[]{:S(2)}, u32[]{:S(2)}) collective-permute-start(bf16[144,192]{1,0:T(8,128)(2,1)S(1)} %get-tuple-element.140), channel_id=1, source_target_pairs={{0,1},{1,0},{2,3},{3,2},{4,5},{5,4},{6,7},{7,6},{8,9},{9,8},{10,11... | collective-permute-start | bytes 165896 | tf_op jit(solution)/shard_map/ppermute | solution.py:41
  19.1 69.3 %copy-start.43 = (bf16[16,768]{1,0:T(8,128)(2,1)}, bf16[16,768]{1,0:T(8,128)(2,1)S(1)}, u32[]{:S(2)}) copy-start(bf16[16,768]{1,0:T(8,128)(2,1)S(1)} %get-tuple-element.81.small_ref) | copy-start | bytes 73732
  19.1 1.8 %collective-permute-start.6 = (bf16[2,128,768]{2,1,0:T(8,128)(2,1)S(1)}, bf16[2,128,768]{2,1,0:T(8,128)(2,1)S(1)}, u32[]{:S(2)}, u32[]{:S(2)}) collective-permute-start(bf16[2,128,768]{2,1,0:T(8,128)(2,1)S(1)} %get-tuple-element.78), channel_id=1, source_target_pairs={{0,1},{1,0},{2,3},{3,2},{4,5},{5,4},{6,7},{7,6},{8,9},{9,8},{10,11... | collective-permute-start | bytes 1179656 | tf_op jit(solution)/shard_map/ppermute | solution.py:41
  20.9 7.0 %collective-permute-start.7 = (bf16[128,768]{1,0:T(8,128)(2,1)S(1)}, bf16[128,768]{1,0:T(8,128)(2,1)S(1)}, u32[]{:S(2)}, u32[]{:S(2)}) collective-permute-start(bf16[128,768]{1,0:T(8,128)(2,1)S(1)} %fusion.6), channel_id=1, source_target_pairs={{0,2},{1,3},{2,0},{3,1},{4,6},{5,7},{6,4},{7,5},{8,10},{9,11},{10,... | collective-permute-start | bytes 589832 | tf_op jit(solution)/shard_map/ppermute | solution.py:41
  27.9 33.5 %copy-start = (bf16[1,768,768]{2,1,0:T(8,128)(2,1)S(1)}, bf16[1,768,768]{2,1,0:T(8,128)(2,1)}, u32[]{:S(2)}) copy-start(bf16[1,768,768]{2,1,0:T(8,128)(2,1)} %win_ref.1) | copy-start | bytes 3538948
  27.9 33.5 %copy-start.1 = (bf16[1,768,768]{2,1,0:T(8,128)(2,1)S(1)}, bf16[1,768,768]{2,1,0:T(8,128)(2,1)}, u32[]{:S(2)}) copy-start(bf16[1,768,768]{2,1,0:T(8,128)(2,1)} %wout_ref.3) | copy-start | bytes 3538948
  29.6 58.9 %copy-start.25 = (f32[128,128]{1,0:T(8,128)}, f32[128,128]{1,0:T(8,128)S(1)}, u32[]{:S(2)}) copy-start(f32[128,128]{1,0:T(8,128)S(1)} %get-tuple-element.83.aux_ref) | copy-start | bytes 196612
  43.2 11.1 %all-to-all-start.1 = ((bf16[8,16,768]{2,1,0:T(8,128)(2,1)}), bf16[8,16,768]{2,1,0:T(8,128)(2,1)S(1)}, u32[]{:S(2)}, u32[]{:S(2)}) async-start(bf16[8,16,768]{2,1,0:T(8,128)(2,1)} %bitcast.16), calls=%async_computation.1 | async-start | bytes 393216 | tf_op jit(solution)/shard_map/all_to_all | solution.py:215
  46.6 8.3 %collective-permute-start.9 = (bf16[128,896]{1,0:T(8,128)(2,1)S(1)}, bf16[128,896]{1,0:T(8,128)(2,1)S(1)}, u32[]{:S(2)}, u32[]{:S(2)}) collective-permute-start(bf16[128,896]{1,0:T(8,128)(2,1)S(1)} %bitcast.60), channel_id=1, source_target_pairs={{0,2},{1,3},{2,0},{3,1},{4,6},{5,7},{6,4},{7,5},{8,10},{9,11},{10,... | collective-permute-start | bytes 688136 | tf_op jit(solution)/shard_map/ppermute | solution.py:41
  54.3 5.7 %collective-permute-start.12 = (bf16[128,768]{1,0:T(8,128)(2,1)S(1)}, bf16[128,768]{1,0:T(8,128)(2,1)S(1)}, u32[]{:S(2)}, u32[]{:S(2)}) collective-permute-start(bf16[128,768]{1,0:T(8,128)(2,1)S(1)} %bitcast.65), channel_id=1, source_target_pairs={{0,2},{1,3},{2,0},{3,1},{4,6},{5,7},{6,4},{7,5},{8,10},{9,11},{10,... | collective-permute-start | bytes 589832 | tf_op jit(solution)/shard_map/ppermute | solution.py:41
  54.8 6.6 %collective-permute-start.8 = (bf16[128,896]{1,0:T(8,128)(2,1)S(1)}, bf16[128,896]{1,0:T(8,128)(2,1)S(1)}, u32[]{:S(2)}, u32[]{:S(2)}) collective-permute-start(bf16[128,896]{1,0:T(8,128)(2,1)S(1)} %bitcast.61), channel_id=1, source_target_pairs={{0,1},{1,0},{2,3},{3,2},{4,5},{5,4},{6,7},{7,6},{8,9},{9,8},{10,11... | collective-permute-start | bytes 688136 | tf_op jit(solution)/shard_map/ppermute | solution.py:41
  54.8 6.6 %collective-permute-start.10 = (bf16[128,896]{1,0:T(8,128)(2,1)S(1)}, bf16[128,896]{1,0:T(8,128)(2,1)S(1)}, u32[]{:S(2)}, u32[]{:S(2)}) collective-permute-start(bf16[128,896]{1,0:T(8,128)(2,1)S(1)} %collective-permute-done.9.a2), channel_id=1, source_target_pairs={{0,1},{1,0},{2,3},{3,2},{4,5},{5,4},{6,7},{7,6},{8,9},{9,8},{10,11... | collective-permute-start | bytes 688136 | tf_op jit(solution)/shard_map/ppermute | solution.py:41
  55.4 4.6 %collective-permute-start.11 = (bf16[128,768]{1,0:T(8,128)(2,1)S(1)}, bf16[128,768]{1,0:T(8,128)(2,1)S(1)}, u32[]{:S(2)}, u32[]{:S(2)}) collective-permute-start(bf16[128,768]{1,0:T(8,128)(2,1)S(1)} %bitcast.66), channel_id=1, source_target_pairs={{0,1},{1,0},{2,3},{3,2},{4,5},{5,4},{6,7},{7,6},{8,9},{9,8},{10,11... | collective-permute-start | bytes 589832 | tf_op jit(solution)/shard_map/ppermute | solution.py:41
  60.0 1.4 collective-permute-start.13
  64.4 1.9 %collective-permute-start.14 = (bf16[2,128,896]{2,1,0:T(8,128)(2,1)S(1)}, bf16[2,128,896]{2,1,0:T(8,128)(2,1)S(1)}, u32[]{:S(2)}, u32[]{:S(2)}) collective-permute-start(bf16[2,128,896]{2,1,0:T(8,128)(2,1)S(1)} %get-tuple-element.87), channel_id=1, source_target_pairs={{0,1},{1,0},{2,3},{3,2},{4,5},{5,4},{6,7},{7,6},{8,9},{9,8},{10,11... | collective-permute-start | bytes 1376264 | tf_op jit(solution)/shard_map/ppermute | solution.py:41
  66.3 7.7 %collective-permute-start.15 = (bf16[128,896]{1,0:T(8,128)(2,1)S(1)}, bf16[128,896]{1,0:T(8,128)(2,1)S(1)}, u32[]{:S(2)}, u32[]{:S(2)}) collective-permute-start(bf16[128,896]{1,0:T(8,128)(2,1)S(1)} %fusion), channel_id=1, source_target_pairs={{0,2},{1,3},{2,0},{3,1},{4,6},{5,7},{6,4},{7,5},{8,10},{9,11},{10,... | collective-permute-start | bytes 688136 | tf_op jit(solution)/shard_map/ppermute | solution.py:41
  75.6 3.7 %collective-permute-start.16 = (bf16[2,128,768]{2,1,0:T(8,128)(2,1)S(1)}, bf16[2,128,768]{2,1,0:T(8,128)(2,1)S(1)}, u32[]{:S(2)}, u32[]{:S(2)}) collective-permute-start(bf16[2,128,768]{2,1,0:T(8,128)(2,1)S(1)} %get-tuple-element.92), channel_id=1, source_target_pairs={{0,1},{1,0},{2,3},{3,2},{4,5},{5,4},{6,7},{7,6},{8,9},{9,8},{10,11... | collective-permute-start | bytes 1179656 | tf_op jit(solution)/shard_map/ppermute | solution.py:41
  75.7 12.7 %all-to-all-start.2 = ((bf16[8,16,896]{2,1,0:T(8,128)(2,1)}), bf16[8,16,896]{2,1,0:T(8,128)(2,1)S(1)}, u32[]{:S(2)}, u32[]{:S(2)}) async-start(bf16[8,16,896]{2,1,0:T(8,128)(2,1)} %bitcast.20), calls=%async_computation.2 | async-start | bytes 458752 | tf_op jit(solution)/shard_map/all_to_all | solution.py:215
  79.3 7.6 %collective-permute-start.17 = (bf16[128,768]{1,0:T(8,128)(2,1)S(1)}, bf16[128,768]{1,0:T(8,128)(2,1)S(1)}, u32[]{:S(2)}, u32[]{:S(2)}) collective-permute-start(bf16[128,768]{1,0:T(8,128)(2,1)S(1)} %fusion.3), channel_id=1, source_target_pairs={{0,2},{1,3},{2,0},{3,1},{4,6},{5,7},{6,4},{7,5},{8,10},{9,11},{10,... | collective-permute-start | bytes 589832 | tf_op jit(solution)/shard_map/ppermute | solution.py:41
  89.9 6.2 %collective-permute-start.22 = (bf16[128,768]{1,0:T(8,128)(2,1)S(1)}, bf16[128,768]{1,0:T(8,128)(2,1)S(1)}, u32[]{:S(2)}, u32[]{:S(2)}) collective-permute-start(bf16[128,768]{1,0:T(8,128)(2,1)S(1)} %get-tuple-element.106.d0), channel_id=1, source_target_pairs={{0,2},{1,3},{2,0},{3,1},{4,6},{5,7},{6,4},{7,5},{8,10},{9,11},{10,... | collective-permute-start | bytes 589832 | tf_op jit(solution)/shard_map/ppermute | solution.py:41
  90.6 11.0 %collective-permute-start.21 = (bf16[128,768]{1,0:T(8,128)(2,1)S(1)}, bf16[128,768]{1,0:T(8,128)(2,1)S(1)}, u32[]{:S(2)}, u32[]{:S(2)}) collective-permute-start(bf16[128,768]{1,0:T(8,128)(2,1)S(1)} %get-tuple-element.106.d0), channel_id=1, source_target_pairs={{0,1},{1,0},{2,3},{3,2},{4,5},{5,4},{6,7},{7,6},{8,9},{9,8},{10,11... | collective-permute-start | bytes 589832 | tf_op jit(solution)/shard_map/ppermute | solution.py:41
  96.2 5.5 %collective-permute-start.23 = (bf16[128,768]{1,0:T(8,128)(2,1)S(1)}, bf16[128,768]{1,0:T(8,128)(2,1)S(1)}, u32[]{:S(2)}, u32[]{:S(2)}) collective-permute-start(bf16[128,768]{1,0:T(8,128)(2,1)S(1)} %collective-permute-done.22.d2), channel_id=1, source_target_pairs={{0,1},{1,0},{2,3},{3,2},{4,5},{5,4},{6,7},{7,6},{8,9},{9,8},{10,11... | collective-permute-start | bytes 589832 | tf_op jit(solution)/shard_map/ppermute | solution.py:41
  96.2 24.5 %all-to-all-start.3 = ((bf16[8,16,768]{2,1,0:T(8,128)(2,1)}), bf16[8,16,768]{2,1,0:T(8,128)(2,1)S(1)}, u32[]{:S(2)}, u32[]{:S(2)}) async-start(bf16[8,16,768]{2,1,0:T(8,128)(2,1)} %bitcast.24), calls=%async_computation.3 | async-start | bytes 393216 | tf_op jit(solution)/shard_map/all_to_all | solution.py:215
  117.2 9.1 %collective-permute-start.32 = (bf16[192,768]{1,0:T(8,128)(2,1)S(1)}, bf16[192,768]{1,0:T(8,128)(2,1)S(1)}, u32[]{:S(2)}, u32[]{:S(2)}) collective-permute-start(bf16[192,768]{1,0:T(8,128)(2,1)S(1)} %get-tuple-element.127), channel_id=1, source_target_pairs={{0,8},{4,12},{8,0},{12,4},{16,24},{20,28},{24,16},{28,20},{1,9},{5... | collective-permute-start | bytes 884744 | tf_op jit(solution)/shard_map/ppermute | solution.py:41
  119.2 12.2 %collective-permute-start.26 = (bf16[208,768]{1,0:T(8,128)(2,1)S(1)}, bf16[208,768]{1,0:T(8,128)(2,1)S(1)}, u32[]{:S(2)}, u32[]{:S(2)}) collective-permute-start(bf16[208,768]{1,0:T(8,128)(2,1)S(1)} %get-tuple-element.125), channel_id=1, source_target_pairs={{0,4},{4,0},{8,12},{12,8},{16,20},{20,16},{24,28},{28,24},{1,5},{5... | collective-permute-start | bytes 958472 | tf_op jit(solution)/shard_map/ppermute | solution.py:41
  122.1 8.2 %collective-permute-start.18 = (bf16[192,128]{1,0:T(8,128)(2,1)S(1)}, bf16[192,128]{1,0:T(8,128)(2,1)S(1)}, u32[]{:S(2)}, u32[]{:S(2)}) collective-permute-start(bf16[192,128]{1,0:T(8,128)(2,1)S(1)} %get-tuple-element.101), channel_id=1, source_target_pairs={{0,1},{1,0},{2,3},{3,2},{4,5},{5,4},{6,7},{7,6},{8,9},{9,8},{10,11... | collective-permute-start | bytes 147464 | tf_op jit(solution)/shard_map/ppermute | solution.py:41
  122.1 8.3 %collective-permute-start.19 = (bf16[192,128]{1,0:T(8,128)(2,1)S(1)}, bf16[192,128]{1,0:T(8,128)(2,1)S(1)}, u32[]{:S(2)}, u32[]{:S(2)}) collective-permute-start(bf16[192,128]{1,0:T(8,128)(2,1)S(1)} %get-tuple-element.102), channel_id=1, source_target_pairs={{0,2},{1,3},{2,0},{3,1},{4,6},{5,7},{6,4},{7,5},{8,10},{9,11},{10,... | collective-permute-start | bytes 147464 | tf_op jit(solution)/shard_map/ppermute | solution.py:41
  123.7 6.7 %collective-permute-start.20 = (bf16[192,128]{1,0:T(8,128)(2,1)S(1)}, bf16[192,128]{1,0:T(8,128)(2,1)S(1)}, u32[]{:S(2)}, u32[]{:S(2)}) collective-permute-start(bf16[192,128]{1,0:T(8,128)(2,1)S(1)} %get-tuple-element.103), channel_id=1, source_target_pairs={{0,3},{1,2},{2,1},{3,0},{4,7},{5,6},{6,5},{7,4},{8,11},{9,10},{10,... | collective-permute-start | bytes 147464 | tf_op jit(solution)/shard_map/ppermute | solution.py:41
  126.5 9.4 %collective-permute-start.33 = (bf16[96,768]{1,0:T(8,128)(2,1)S(1)}, bf16[96,768]{1,0:T(8,128)(2,1)S(1)}, u32[]{:S(2)}, u32[]{:S(2)}) collective-permute-start(bf16[96,768]{1,0:T(8,128)(2,1)S(1)} %slice.102), channel_id=1, source_target_pairs={{0,16},{4,20},{8,24},{12,28},{16,0},{20,4},{24,8},{28,12},{1,17},{... | collective-permute-start | bytes 442376 | tf_op jit(solution)/shard_map/ppermute | solution.py:41
  130.3 34.8 %collective-permute-start.24 = (bf16[2,208,384]{2,1,0:T(8,128)(2,1)S(1)}, bf16[2,208,384]{2,1,0:T(8,128)(2,1)S(1)}, u32[]{:S(2)}, u32[]{:S(2)}) collective-permute-start(bf16[2,208,384]{2,1,0:T(8,128)(2,1)S(1)} %get-tuple-element.120), channel_id=1, source_target_pairs={{0,1},{1,0},{2,3},{3,2},{4,5},{5,4},{6,7},{7,6},{8,9},{9,8},{10,11... | collective-permute-start | bytes 958472 | tf_op jit(solution)/shard_map/ppermute | solution.py:41
  131.5 7.9 %collective-permute-start.27 = (bf16[112,768]{1,0:T(8,128)(2,1)S(1)}, bf16[112,768]{1,0:T(8,128)(2,1)S(1)}, u32[]{:S(2)}, u32[]{:S(2)}) collective-permute-start(bf16[112,768]{1,0:T(8,128)(2,1)S(1)} %slice.96), channel_id=1, source_target_pairs={{0,8},{4,12},{8,0},{12,4},{16,24},{20,28},{24,16},{28,20},{1,9},{5... | collective-permute-start | bytes 516104 | tf_op jit(solution)/shard_map/ppermute | solution.py:41
  135.9 5.0 %collective-permute-start.34 = (bf16[48,768]{1,0:T(8,128)(2,1)S(1)}, bf16[48,768]{1,0:T(8,128)(2,1)S(1)}, u32[]{:S(2)}, u32[]{:S(2)}) collective-permute-start(bf16[48,768]{1,0:T(8,128)(2,1)S(1)} %slice.104), channel_id=1, source_target_pairs={{0,4},{4,0},{8,12},{12,8},{16,20},{20,16},{24,28},{28,24},{1,5},{5... | collective-permute-start | bytes 221192 | tf_op jit(solution)/shard_map/ppermute | solution.py:41
  139.5 7.8 %collective-permute-start.28 = (bf16[64,768]{1,0:T(8,128)(2,1)S(1)}, bf16[64,768]{1,0:T(8,128)(2,1)S(1)}, u32[]{:S(2)}, u32[]{:S(2)}) collective-permute-start(bf16[64,768]{1,0:T(8,128)(2,1)S(1)} %slice.99), channel_id=1, source_target_pairs={{0,16},{4,20},{8,24},{12,28},{16,0},{20,4},{24,8},{28,12},{1,17},{... | collective-permute-start | bytes 294920 | tf_op jit(solution)/shard_map/ppermute | solution.py:41
  140.9 6.6 %collective-permute-start.35 = (bf16[48,768]{1,0:T(8,128)(2,1)S(1)}, bf16[48,768]{1,0:T(8,128)(2,1)S(1)}, u32[]{:S(2)}, u32[]{:S(2)}) collective-permute-start(bf16[48,768]{1,0:T(8,128)(2,1)S(1)} %slice_add_fusion.1), channel_id=1, source_target_pairs={{0,4},{4,0},{8,12},{12,8},{16,20},{20,16},{24,28},{28,24},{1,5},{5... | collective-permute-start | bytes 221192 | tf_op jit(solution)/shard_map/ppermute | solution.py:41
  147.4 23.1 %copy-start.11 = (bf16[384,192]{0,1:T(8,128)(2,1)S(1)}, bf16[384,192]{0,1:T(8,128)(2,1)}, u32[]{:S(2)}) copy-start(bf16[384,192]{0,1:T(8,128)(2,1)} %param.15) | copy-start | bytes 442372
  147.4 9.6 %collective-permute-start.29 = (bf16[48,768]{1,0:T(8,128)(2,1)S(1)}, bf16[48,768]{1,0:T(8,128)(2,1)S(1)}, u32[]{:S(2)}, u32[]{:S(2)}) collective-permute-start(bf16[48,768]{1,0:T(8,128)(2,1)S(1)} %slice.100), channel_id=1, source_target_pairs={{0,16},{4,20},{8,24},{12,28},{16,0},{20,4},{24,8},{28,12},{1,17},{... | collective-permute-start | bytes 221192 | tf_op jit(solution)/shard_map/ppermute | solution.py:41
  147.5 12.4 %collective-permute-start.36 = (bf16[96,768]{1,0:T(8,128)(2,1)S(1)}, bf16[96,768]{1,0:T(8,128)(2,1)S(1)}, u32[]{:S(2)}, u32[]{:S(2)}) collective-permute-start(bf16[96,768]{1,0:T(8,128)(2,1)S(1)} %pad_maximum_fusion.3), channel_id=1, source_target_pairs={{0,16},{4,20},{8,24},{12,28},{16,0},{20,4},{24,8},{28,12},{1,17},{... | collective-permute-start | bytes 442376 | tf_op jit(solution)/shard_map/ppermute | solution.py:41
  157.0 6.6 %collective-permute-start.30 = (bf16[96,768]{1,0:T(8,128)(2,1)S(1)}, bf16[96,768]{1,0:T(8,128)(2,1)S(1)}, u32[]{:S(2)}, u32[]{:S(2)}) collective-permute-start(bf16[96,768]{1,0:T(8,128)(2,1)S(1)} %pad_maximum_fusion.2), channel_id=1, source_target_pairs={{0,8},{4,12},{8,0},{12,4},{16,24},{20,28},{24,16},{28,20},{1,9},{5... | collective-permute-start | bytes 442376 | tf_op jit(solution)/shard_map/ppermute | solution.py:41
  157.1 9.6 %collective-permute-start.38 = (f32[16,768]{1,0:T(8,128)S(1)}, f32[16,768]{1,0:T(8,128)S(1)}, u32[]{:S(2)}, u32[]{:S(2)}) collective-permute-start(f32[16,768]{1,0:T(8,128)S(1)} %slice_convert_fusion), channel_id=1, source_target_pairs={{0,1},{1,0},{2,3},{3,2},{4,5},{5,4},{6,7},{7,6},{8,9},{9,8},{10,11... | collective-permute-start | bytes 147464 | tf_op jit(solution)/shard_map/ppermute | solution.py:41
  160.0 11.5 %collective-permute-start.37 = (bf16[192,768]{1,0:T(8,128)(2,1)S(1)}, bf16[192,768]{1,0:T(8,128)(2,1)S(1)}, u32[]{:S(2)}, u32[]{:S(2)}) collective-permute-start(bf16[192,768]{1,0:T(8,128)(2,1)S(1)} %pad_maximum_fusion.1.bm_ref), channel_id=1, source_target_pairs={{0,8},{4,12},{8,0},{12,4},{16,24},{20,28},{24,16},{28,20},{1,9},{5... | collective-permute-start | bytes 884744 | tf_op jit(solution)/shard_map/ppermute | solution.py:41
  163.6 7.8 %collective-permute-start.31 = (bf16[192,768]{1,0:T(8,128)(2,1)S(1)}, bf16[192,768]{1,0:T(8,128)(2,1)S(1)}, u32[]{:S(2)}, u32[]{:S(2)}) collective-permute-start(bf16[192,768]{1,0:T(8,128)(2,1)S(1)} %pad_maximum_fusion.am_ref), channel_id=1, source_target_pairs={{0,4},{4,0},{8,12},{12,8},{16,20},{20,16},{24,28},{28,24},{1,5},{5... | collective-permute-start | bytes 884744 | tf_op jit(solution)/shard_map/ppermute | solution.py:41
  165.2 5.3 %collective-permute-start.25 = (bf16[208,384]{1,0:T(8,128)(2,1)S(1)}, bf16[208,384]{1,0:T(8,128)(2,1)S(1)}, u32[]{:S(2)}, u32[]{:S(2)}) collective-permute-start(bf16[208,384]{1,0:T(8,128)(2,1)S(1)} %fusion.7), channel_id=1, source_target_pairs={{0,2},{1,3},{2,0},{3,1},{4,6},{5,7},{6,4},{7,5},{8,10},{9,11},{10,... | collective-permute-start | bytes 479240 | tf_op jit(solution)/shard_map/ppermute | solution.py:41
  166.8 4.7 %collective-permute-start.39 = (f32[16,768]{1,0:T(8,128)S(1)}, f32[16,768]{1,0:T(8,128)S(1)}, u32[]{:S(2)}, u32[]{:S(2)}) collective-permute-start(f32[16,768]{1,0:T(8,128)S(1)} %fusion.8.few_ref), channel_id=1, source_target_pairs={{0,2},{1,3},{2,0},{3,1},{4,6},{5,7},{6,4},{7,5},{8,10},{9,11},{10,... | collective-permute-start | bytes 147464 | tf_op jit(solution)/shard_map/ppermute | solution.py:41
  (56 other events, 333.8 us)

commit v2 on v1

--- a/solution.py
+++ b/solution.py
@@ -18,16 +18,90 @@
 SMEM = pl.BlockSpec(memory_space=pltpu.SMEM)
 
 
+class Far:
+    def __init__(self, value):
+        self.value = value
+
+
+class Loaded:
+    def __init__(self, copy, held):
+        self.copy, self.held = copy, held
+
+    def wait(self):
+        if self.copy is not None:
+            self.copy.wait()
+            self.copy = None
+
+    def __getitem__(self, index):
+        self.wait()
+        return self.held[index]
+
+
+class Stored:
+    def __init__(self, copy, held):
+        self.copy, self.held, self.started = copy, held, False
+
+    def __setitem__(self, index, value):
+        self.held[index] = value
+
+    def __getitem__(self, index):
+        return self.held[index]
+
+    def send(self):
+        if not self.started:
+            self.started = True
+            self.copy.start()
+
+
 def run(body, outs, args, name, us=1.0, scratch=(), limit=16):
-    specs = [SMEM if a.shape == (1,) else VMEM for a in args]
+    far_in = [isinstance(a, Far) for a in args]
+    args = [a.value if isinstance(a, Far) else a for a in args]
+    far_out = [len(o) == 3 for o in outs]
+    bufs = [pltpu.VMEM(a.shape, a.dtype) for a, far in zip(args, far_in) if far]
+    bufs += [pltpu.VMEM(o[0], o[1]) for o, far in zip(outs, far_out) if far]
+    n_in, n_out, n_own = len(args), len(outs), len(scratch)
+    hbm = pl.BlockSpec(memory_space=pltpu.HBM)
+    specs = [
+        SMEM if a.shape == (1,) and a.dtype == jnp.int32 else hbm if far else VMEM
+        for a, far in zip(args, far_in)
+    ]
     moved = sum(a.size * a.dtype.itemsize for a in args)
-    moved += sum(math.prod(s) * jnp.dtype(d).itemsize for s, d in outs)
+    moved += sum(math.prod(o[0]) * jnp.dtype(o[1]).itemsize for o in outs)
+
+    def wrapped(*refs):
+        ins, results = refs[:n_in], refs[n_in : n_in + n_out]
+        own = refs[n_in + n_out : n_in + n_out + n_own]
+        held = refs[n_in + n_out + n_own :]
+        given, at = [], 0
+        for ref, far in zip((*ins, *results), (*far_in, *far_out)):
+            if not far:
+                given.append(ref)
+                continue
+            if len(given) < n_in:
+                copy = pltpu.make_async_copy(ref, held[at], held[-1].at[at])
+                copy.start()
+                given.append(Loaded(copy, held[at]))
+            else:
+                copy = pltpu.make_async_copy(held[at], ref, held[-1].at[at])
+                given.append(Stored(copy, held[at]))
+            at += 1
+        body(*given, *own)
+        for g in given:
+            if isinstance(g, Stored):
+                g.send()
+        for g in given:
+            if isinstance(g, Stored):
+                g.copy.wait()
+            elif isinstance(g, Loaded):
+                g.wait()
+
+    sems = [pltpu.SemaphoreType.DMA((len(bufs),))] if bufs else []
     return pl.pallas_call(
-        body,
-        out_shape=[jax.ShapeDtypeStruct(s, d) for s, d in outs],
+        wrapped,
+        out_shape=[jax.ShapeDtypeStruct(o[0], o[1]) for o in outs],
         in_specs=specs,
-        out_specs=[VMEM] * len(outs),
-        scratch_shapes=list(scratch),
+        out_specs=[hbm if far else VMEM for far in far_out],
+        scratch_shapes=[*scratch, *bufs, *sems],
         compiler_params=pltpu.CompilerParams(vmem_limit_bytes=limit * 2**20),
         cost_estimate=pl.CostEstimate(
             flops=int(us * 1.1e9), bytes_accessed=moved, transcendentals=0
@@ -89,7 +163,8 @@
 
 def scatter_sum(kept, passed, sent):
     came = swap(sent, "tp", 1)
-    return kept, came, swap(passed + came[1], "tp", 2)
+    half = passed + came[1]
+    return kept, came, swap(half, "tp", 2), half
 
 
 def chain_sum(keep, send, masks, tail):
@@ -161,8 +236,9 @@
     tok_pieces = gather_pieces(tok_t)
 
     def slot_body(
-        me_ref, route_ref, cot_ref, router_ref, g1_ref, g2_ref, drow_ref, dcol_ref, cots_ref, d_ref
+        me_ref, route_ref, cot_ref, router_ref, g1_ref, g2_ref, *outs
     ):
+        drow_ref, drow_far, dcol_ref, cots_ref, d_ref = outs
         mine = me_ref[0] & (ways - 1)
         row = route_ref[...]
         above = iota((length, length), 0)
@@ -180,7 +256,10 @@
         slot_col = jnp.sum(jnp.where(same & (along < above), 1, 0), axis=1, keepdims=True)
         dest_row = dest(slot_row, row)
         drow_ref[...] = dest_row
+        drow_far[...] = dest_row
+        drow_far.send()
         dcol_ref[...] = dest(slot_col, col)
+        dcol_ref.send()
         cot = cot_ref[...]
         line = iota((extra - experts, quarter), 0)
         gains = jnp.where(
@@ -196,15 +275,23 @@
             cots_ref[rel, rows : rows + extra] = few
             d_ref[:, rel * quarter : (rel + 1) * quarter] = piece
 
-    dest_row, dest_col, cots, d_send = run(
+    dest_row, dest_far, dest_col, cots, d_send = run(
         slot_body,
         [
             ((1, length), jnp.int32),
-            ((length, 1), jnp.int32),
+            ((1, length), jnp.int32, True),
+            ((length, 1), jnp.int32, True),
             ((ways, rows + extra, quarter), bf16),
             ((rows, width), bf16),
         ],
-        (me, routes.T, cotangent.T, w_router.T, gain_attn[None], gain_ffn[None]),
+        (
+            me,
+            Far(routes.T),
+            Far(cotangent.T),
+            Far(w_router.T),
+            gain_attn[None],
+            gain_ffn[None],
+        ),
         "slots",
         us=0.7,
     )
@@ -241,6 +328,7 @@
         dest_ref,
         x_ref,
         small_ref,
+        small_far,
         r1_ref,
         n1_ref,
         q_ref,
@@ -260,18 +348,26 @@
         pieces = [c[rows : rows + extra] for c in (c0, c1, c2, c3)]
         small = jnp.concatenate([absolute(pieces, mine, t) for t in range(ways)], axis=1)
         small_ref[...] = small
+        small_far[...] = small
+        small_far.send()
         x_low = x_ref[...]
+        x_ref.send()
         x = x_low.astype(f32)
         r1 = lax.rsqrt(jnp.mean(x * x, axis=0, keepdims=True) + EPSILON)
         r1_ref[...] = r1
+        r1_ref.send()
         n1 = (x * r1 * spread_row(small, experts, length)).astype(bf16)
         n1_ref[...] = n1
+        n1_ref.send()
         q = mm(wq_ref[...], n1).astype(bf16)
         k = mm(wk_ref[...], n1).astype(bf16)
         v = mm(wv_ref[...], n1).astype(bf16)
         q_ref[...] = q
         k_ref[...] = k
         v_ref[...] = v
+        q_ref.send()
+        k_ref.send()
+        v_ref.send()
         hot = (iota((bins, span), 0) == bucket_ref[...]).astype(bf16)
         offsets = mm(table_ref[...], hot)
         above = iota((length, length), 0)
@@ -288,7 +384,9 @@
             p = (e / jnp.sum(e, axis=0, keepdims=True)).astype(bf16)
             p_ref[h] = p
             attn_ref[part] = mm(v[part], p).astype(bf16)
+        p_ref.send()
         attn = attn_ref[...]
+        attn_ref.send()
         dest = dest_ref[...]
         wo = wo_ref[...]
         for rel, out in enumerate((kept_ref, sent_ref.at[0], passed_ref, sent_ref.at[1])):
@@ -297,18 +395,19 @@
             if rel == 0:
                 xrow_ref[...] = mm_nt(hot, x_low).astype(bf16)
 
-    x_full, small, r1, n1, q, k, v, probs, attn, o_kept, o_passed, o_sent, x_rows = run(
+    x_full, small, small_far, r1, n1, q, k, v, probs, attn, *o_parts, x_rows = run(
         attend_body,
         [
-            ((width, length), bf16),
+            ((width, length), bf16, True),
             ((extra, width), bf16),
-            ((1, length), f32),
-            ((width, length), bf16),
-            ((here, length), bf16),
-            ((here, length), bf16),
-            ((here, length), bf16),
-            ((heads, length, length), bf16),
-            ((here, length), bf16),
+            ((extra, width), bf16, True),
+            ((1, length), f32, True),
+            ((width, length), bf16, True),
+            ((here, length), bf16, True),
+            ((here, length), bf16, True),
+            ((here, length), bf16, True),
+            ((heads, length, length), bf16, True),
+            ((here, length), bf16, True),
             ((rows, width), bf16),
             ((rows, width), bf16),
             ((2, rows, width), bf16),
@@ -331,9 +430,11 @@
         us=4.0,
         limit=24,
     )
-    o_kept, o_beside, o_across = scatter_sum(o_kept, o_passed, o_sent)
-
-    d_pieces = gather_pieces(over_experts(d_send))
+    o_kept, o_beside, o_across, none = scatter_sum(*o_parts)
+
+    d_arrived = over_experts(d_send)
+    o_across, d_arrived = lax.optimization_barrier((o_across, d_arrived))
+    d_pieces = gather_pieces(d_arrived)
 
     def route_body(
         me_ref,
@@ -366,26 +467,30 @@
         g = jnp.sum(jnp.where(own, p, 0.0), axis=-1, keepdims=True)
         pieces = [c[0:rows] for c in (c0, c1, c2, c3)]
         dout_ref[...] = jnp.concatenate([absolute(pieces, mine, t) for t in range(ways)], axis=1)
-        aux_ref[...] = jnp.zeros_like(aux_ref)
+        aux_ref[...] = jnp.zeros((rows, LANES), f32)
         aux_ref[:, 0:experts] = p
         aux_ref[:, LANES - 2 : LANES - 1] = r2
         aux_ref[:, LANES - 1 : LANES] = g
+        h_ref.send()
+        aux_ref.send()
+        dout_ref.send()
         send_ref[:, 0:width] = n2.astype(bf16)
         send_ref[:, width : width + LANES] = two_lanes(g, LANES)
 
     h_rows, aux, dout_rows, send = run(
         route_body,
         [
-            ((rows, width), f32),
-            ((rows, LANES), f32),
-            ((rows, width), bf16),
+            ((rows, width), f32, True),
+            ((rows, LANES), f32, True),
+            ((rows, width), bf16, True),
             ((rows, width + LANES), bf16),
         ],
         (me, o_kept, o_beside, o_across, x_rows, small, *cot_pieces),
         "route",
         us=0.8,
     )
-    arrived = gather_pieces(over_experts(send))
+    arrived, *d_pieces = lax.optimization_barrier((over_experts(send), *d_pieces))
+    arrived = gather_pieces(arrived)
 
     def expert_body(me_ref, a0, a1, a2, a3, d0, d1, d2, d3, win_ref, wout_ref, *outs):
         u_ref, dy_ref, act_ref, dz_ref, kept_ref, passed_ref, sent_ref = outs
@@ -401,6 +506,8 @@
                 pieces.append(douts[src][:, at : at + quarter])
             dout = jnp.concatenate([absolute(pieces, mine, t) for t in range(ways)], axis=1)
             dy_ref[part] = (g * dout.astype(f32)).astype(bf16)
+        u_ref.send()
+        dy_ref.send()
         u = u_ref[...]
         dy = dy_ref[...]
         z = mm(u, win_ref[0])
@@ -408,11 +515,13 @@
         t = jnp.tanh(c * (z + 0.044715 * z * z * z))
         act = (0.5 * z * (1.0 + t)).astype(bf16)
         act_ref[...] = act
+        act_ref.send()
         slope = 0.5 * (1.0 + t) + 0.5 * z * (1.0 - t * t) * (c * (1.0 + 3 * 0.044715 * z * z))
         dact = mm_nt(dy, wout_ref[0])
         dot = jnp.sum(dact * act.astype(f32), axis=-1, keepdims=True)
         dz = (dact * slope).astype(bf16)
         dz_ref[...] = dz
+        dz_ref.send()
         du = mm_nt(dz, win_ref[0]).astype(bf16)
         tail = two_lanes(dot, LANES)
         for rel, out in enumerate((kept_ref, sent_ref.at[0], passed_ref, sent_ref.at[1])):
@@ -422,10 +531,10 @@
     u_all, dy_all, act, dz, *du_parts = run(
         expert_body,
         [
-            ((ways * rows, width), bf16),
-            ((ways * rows, width), bf16),
-            ((ways * rows, hidden_here), bf16),
-            ((ways * rows, hidden_here), bf16),
+            ((ways * rows, width), bf16, True),
+            ((ways * rows, width), bf16, True),
+            ((ways * rows, hidden_here), bf16, True),
+            ((ways * rows, hidden_here), bf16, True),
             ((rows, width + LANES), bf16),
             ((rows, width + LANES), bf16),
             ((2, rows, width + LANES), bf16),
@@ -435,7 +544,7 @@
         us=4.0,
         limit=24,
     )
-    du_kept, du_beside, du_across = scatter_sum(*du_parts)
+    du_kept, du_beside, du_across, du_half = scatter_sum(*du_parts)
     du_sum = du_kept + du_beside[0] + du_across
     du_rows = over_experts(du_sum)
 
@@ -444,15 +553,16 @@
         for rel, out in enumerate((kept_ref, sent_ref.at[0], passed_ref, sent_ref.at[1])):
             out[...] = y[rel * rows : (rel + 1) * rows]
 
-    act_late = after(act, du_sum)
     y_parts = run(
         value_body,
         [((rows, width), bf16), ((rows, width), bf16), ((2, rows, width), bf16)],
-        (act_late, w_out),
+        (Far(after(act, du_half)), w_out),
         "value",
         us=0.8,
     )
-    y_kept, y_beside, y_across = scatter_sum(*y_parts)
+    y_kept, y_passed, y_sent = y_parts
+    y_beside = swap(y_sent, "tp", 1)
+    y_across = swap(after(y_passed + y_beside[1], du_sum), "tp", 2)
     y_sum = y_kept + y_beside[0] + y_across
 
     def weights_body(u_ref, dy_ref, act_ref, dz_ref, gin_ref, gout_ref):
@@ -462,14 +572,12 @@
     grad_in, grad_out = run(
         weights_body,
         [((1, width, hidden_here), bf16), ((1, hidden_here, width), bf16)],
-        (u_all, dy_all, act_late, dz),
+        (Far(u_all), Far(dy_all), Far(act), Far(after(dz, du_sum))),
         "expert_weights",
         us=2.5,
     )
-    du_rows, y_sum, grad_in, grad_out = lax.optimization_barrier(
-        (du_rows, y_sum, grad_in, grad_out)
-    )
     y_rows = over_experts(y_sum)
+    du_rows, grad_in, grad_out = lax.optimization_barrier((du_rows, grad_in, grad_out))
 
     def back_body(du_ref, h_ref, aux_ref, dout_ref, small_ref, do_ref, parts_ref):
         du = du_ref[:, 0:width].astype(f32)
@@ -491,7 +599,7 @@
         inner = jnp.sum(dn2 * gain * h, axis=-1, keepdims=True)
         dh = dout_ref[...].astype(f32) + r2 * gain * dn2 - hr * (r2 * r2 / width) * inner
         do_ref[...] = dh.astype(bf16)
-        parts_ref[...] = jnp.zeros_like(parts_ref)
+        parts_ref[...] = jnp.zeros((few_rows, width), f32)
         parts_ref[0:experts] = lax.dot_general(
             dlogits, n2, (((0,), (0,)), ((), ())), precision=HIGHEST, preferred_element_type=f32
         )
@@ -499,8 +607,8 @@
 
     do_rows, few_parts = run(
         back_body,
-        [((rows, width), bf16), ((few_rows, width), f32)],
-        (du_rows, h_rows, aux, dout_rows, small),
+        [((rows, width), bf16), ((few_rows, width), f32, True)],
+        (du_rows, h_rows, aux, dout_rows, small_far),
         "residual_back",
         us=2.0,
     )
@@ -526,19 +634,24 @@
         wq_ref,
         wk_ref,
         wv_ref,
+        x_ref,
         small_ref,
         few_ref,
         bucket_ref,
         own_ref,
-        dq_ref,
-        dk_ref,
-        dv_ref,
         akeep_ref,
         asend_ref,
         bkeep_ref,
         bsend_ref,
+        kept_ref,
+        passed_ref,
+        sent_ref,
         a_ref,
         b_ref,
+        dq_ref,
+        dk_ref,
+        dv_ref,
+        all_ref,
     ):
         mine = me_ref[0] & (ways - 1)
         place = me_ref[0] >> shift
@@ -550,6 +663,7 @@
             own = jnp.where(mine == t, stack[:, t * quarter : (t + 1) * quarter], own)
         hot = (iota((ways * rows, length), 0) == drow_ref[...]).astype(bf16)
         own_ref[...] = mm_tn(own, hot).astype(bf16)
+        own_ref.send()
         wo = wo_ref[...]
         da = mm_nt(wo, do).astype(bf16)
         hot = (iota((bins, span), 0) == bucket_ref[...]).astype(f32)
@@ -606,59 +720,9 @@
         few = few.astype(bf16)
         akeep_ref[tail : tail + few_rows] = few
         asend_ref[tail : tail + few_rows] = few
-
-    side = (owners // 2) * chunk
-    dh_own, dq, dk, dv, a_keep, a_send, b_keep, b_send = run(
-        attend_back_body,
-        [
-            ((quarter, length), bf16),
-            ((here, length), bf16),
-            ((here, length), bf16),
-            ((here, length), bf16),
-            ((side + few_rows, width), bf16),
-            ((side + few_rows, width), bf16),
-            ((side, width), bf16),
-            ((side, width), bf16),
-        ],
-        (
-            me,
-            *do_pieces,
-            dest_row,
-            dest_col,
-            w_output,
-            attn,
-            q,
-            k,
-            v,
-            probs,
-            n1,
-            wq_t,
-            wk_t,
-            wv_t,
-            small,
-            few_parts,
-            bucket_row,
-        ),
-        "attend_back",
-        us=6.0,
-        scratch=[
-            pltpu.VMEM((owners, chunk, width), bf16),
-            pltpu.VMEM((owners, chunk, width), bf16),
-        ],
-        limit=24,
-    )
-
-    a_mine, a_other, few = chain_sum(a_keep, a_send, order_a, few_rows)
-    b_mine, b_other, none = chain_sum(b_keep, b_send, order_b, 0)
-
-    def norm_back_body(
-        me_ref, dq_ref, dk_ref, dv_ref, wq, wk, wv, x_ref, small_ref, *outs
-    ):
-        kept_ref, passed_ref, sent_ref, all_ref = outs
-        mine = me_ref[0] & (ways - 1)
-        dn1 = mm_tn(wq[...], dq_ref[...])
-        dn1 = dn1 + mm_tn(wk[...], dk_ref[...])
-        dn1 = dn1 + mm_tn(wv[...], dv_ref[...])
+        dn1 = mm_tn(wq_ref[...], dq_ref[...])
+        dn1 = dn1 + mm_tn(wk_ref[...], dk_ref[...])
+        dn1 = dn1 + mm_tn(wv_ref[...], dv_ref[...])
         all_ref[...] = dn1.astype(bf16)
         gain = spread_row(small_ref[...], experts, length)
         dot = jnp.sum(dn1 * gain * x_ref[...].astype(f32), axis=0, keepdims=True)
@@ -670,27 +734,71 @@
             out[0:quarter] = all_ref[pl.ds(at, quarter), :]
             out[quarter : quarter + 16] = tail
 
-    dn1_parts = run(
-        norm_back_body,
+    side = (owners // 2) * chunk
+    dh_own, a_keep, a_send, b_keep, b_send, *dn1_parts = run(
+        attend_back_body,
         [
+            ((quarter, length), bf16, True),
+            ((side + few_rows, width), bf16),
+            ((side + few_rows, width), bf16),
+            ((side, width), bf16),
+            ((side, width), bf16),
             ((quarter + 16, length), bf16),
             ((quarter + 16, length), bf16),
             ((2, quarter + 16, length), bf16),
         ],
-        (me, dq, dk, dv, wq_t, wk_t, wv_t, x_full, small),
-        "norm_back",
-        us=1.5,
-        scratch=[pltpu.VMEM((width, length), bf16)],
-    )
-    dn1_parts = scatter_sum(*dn1_parts)
-
-    def tokens_body(kept_ref, beside_ref, across_ref, dh_ref, tok_ref, r1_ref, c_ref, out_ref):
+        (
+            me,
+            *do_pieces,
+            Far(dest_far),
+            Far(dest_col),
+            Far(w_output),
+            Far(attn),
+            Far(q),
+            Far(k),
+            Far(v),
+            Far(probs),
+            Far(n1),
+            Far(wq_t),
+            Far(wk_t),
+            Far(wv_t),
+            Far(x_full),
+            Far(small_far),
+            Far(few_parts),
+            Far(bucket_row),
+        ),
+        "attend_back",
+        us=6.0,
+        scratch=[
+            pltpu.VMEM((owners, chunk, width), bf16),
+            pltpu.VMEM((owners, chunk, width), bf16),
+            pltpu.VMEM((here, length), bf16),
+            pltpu.VMEM((here, length), bf16),
+            pltpu.VMEM((here, length), bf16),
+            pltpu.VMEM((width, length), bf16),
+        ],
+        limit=32,
+    )
+
+    a_mine, a_other, few = chain_sum(a_keep, a_send, order_a, few_rows)
+    b_mine, b_other, none = chain_sum(b_keep, b_send, order_b, 0)
+
+    *dn1_parts, none = scatter_sum(*dn1_parts)
+
+    def tokens_body(
+        me_ref, kept_ref, beside_ref, across_ref, dh_ref, tok_ref, r1_ref, small_ref, out_ref
+    ):
+        mine = me_ref[0] & (ways - 1)
         total = kept_ref[...].astype(f32) + beside_ref[0].astype(f32)
         total = total + across_ref[...].astype(f32)
         dn1 = total[0:quarter]
         dot = total[quarter : quarter + 1] + total[quarter + 1 : quarter + 2]
         one = r1_ref[...]
-        gain = spread_row(c_ref[rows : rows + extra], experts, length)
+        small = small_ref[...]
+        own = small[:, 0:quarter]
+        for t in range(1, ways):
+            own = jnp.where(mine == t, small[:, t * quarter : (t + 1) * quarter], own)
+        gain = spread_row(own, experts, length)
         x = tok_ref[...].astype(f32)
         out_ref[...] = (
             dh_ref[...].astype(f32) + one * gain * dn1 - x * (one * one * one / width) * dot
@@ -699,7 +807,7 @@
     (grad_tokens,) = run(
         tokens_body,
         [((quarter, length), bf16)],
-        (*dn1_parts, dh_own, tok_t, r1, cot_pieces[0]),
+        (me, *dn1_parts, Far(dh_own), Far(tok_t), Far(r1), Far(small_far)),
         "tokens_back",
         us=0.5,
     )
@@ -716,7 +824,7 @@
     lo = run(
         out_rows_body,
         [((quarter, rows), bf16)] * ways,
-        (me, h_rows, aux, y_rows),
+        (me, Far(h_rows), Far(aux), y_rows),
         "layer_rows",
         us=0.5,
         scratch=[pltpu.VMEM((width, rows), bf16)],
@@ -732,7 +840,7 @@
         out_ref[...] = total.astype(bf16)
 
     (layer_out,) = run(
-        out_body, [((quarter, length), bf16)], (dest_row, *lo), "layer_out", us=0.5
+        out_body, [((quarter, length), bf16)], (Far(dest_far), *lo), "layer_out", us=0.5
     )
 
     few = few.astype(f32)

time: 175 us -> 204 us (1.17)
  local copies, waits for them, and re-layouts: 21.6 us -> 36.5 us
  blocking collectives: 13.6 us -> 0 us
  Pallas kernels: 21.9 us -> 35.2 us
  starting transfers between devices: 43.2 us -> 53.3 us
  waiting for transfers between devices: 69.1 us -> 72.4 us
    unnamed x122 -> x154, local copies, waits for them, and re-layouts: 20.2 us -> 35.1 us
    all_to_all x1 -> x0, blocking collectives: 13.6 us -> none  [over_experts(): lax.all_to_all(blocks, 'exp', split_axis=0, concat_axis=0, tiled=True)]
    pallas_call x13 -> x12, Pallas kernels: 21.9 us -> 35.2 us  [run(): pl.pallas_call(wrapped, out_shape=[jax.ShapeDtypeStruct(o[0], o[1]) for o...]
    all_to_all x3 -> x4, starting transfers between devices: 12.4 us -> 22 us  [over_experts(): lax.all_to_all(blocks, 'exp', split_axis=0, concat_axis=0, tiled=True)]
    ppermute x40, waiting for transfers between devices: 61.2 us -> 63.4 us  [swap(): return lax.ppermute(value, axis, [(i, i ^ mask) for i in range(size)])]
    all_to_all x3 -> x4, waiting for transfers between devices: 7.92 us -> 9 us  [over_experts(): lax.all_to_all(blocks, 'exp', split_axis=0, concat_axis=0, tiled=True)]
  transfers between devices with their start and end apart: 43 -> 44, of which waited for: 19 -> 22; matrix products, arithmetic and copies ran while one was open for 1% -> 2% of each run, Pallas kernels for 7% -> 10%
where the time goes in v2:
time: 204 us; the launch traced here: 203 us
  waiting for transfers between devices  72.4 us (35%)
  starting transfers between devices  53.3 us (26%)
  local copies, waits for them, and re-layouts  36.5 us (18%)
  Pallas kernels  35.2 us (17%)
  other arithmetic  3.88 us (2%)
    ppermute x40, waiting for transfers between devices, swap(): return lax.ppermute(value, axis, [(i, i ^ mask) for i in range(size)])  63.4 us
    pallas_call x12, Pallas kernels, run(): pl.pallas_call(wrapped, out_shape=[jax.ShapeDtypeStruct(o[0], o[1]) for o...  35.2 us
    unnamed x154, local copies, waits for them, and re-layouts  35.1 us
    ppermute x40, starting transfers between devices, swap(): return lax.ppermute(value, axis, [(i, i ^ mask) for i in range(size)])  31.4 us
    all_to_all x4, starting transfers between devices, over_experts(): lax.all_to_all(blocks, 'exp', split_axis=0, concat_axis=0, tiled=True)  22 us
    all_to_all x4, waiting for transfers between devices, over_experts(): lax.all_to_all(blocks, 'exp', split_axis=0, concat_axis=0, tiled=True)  9 us
  transfers between devices with their start and end apart: 44, of which 22 were waited for; matrix products, arithmetic and copies ran while one was open for 2% of the time, Pallas kernels for 10%

profile of v2, /device:TPU:0, one launch (start us, length us, event | category | flops | bytes accessed | tf_op | source)
XLA Modules:
  0.0 202.8 jit_solution(2263840862818272373)
XLA Ops:
  0.6 3.0 %collective-permute-start.1 = (bf16[192,384]{1,0:T(8,128)(2,1)}, bf16[192,384]{1,0:T(8,128)(2,1)S(1)}, u32[]{:S(2)}, u32[]{:S(2)}) collective-permute-start(bf16[192,384]{1,0:T(8,128)(2,1)} %bitcast.75), channel_id=1, source_target_pairs={{0,2},{1,3},{2,0},{3,1},{4,6},{5,7},{6,4},{7,5},{8,10},{9,11},{10,... | collective-permute-start | bytes 442376 | tf_op jit(solution)/shard_map/ppermute | solution.py:115
  7.3 2.1 %slots.1 = (s32[1,384]{1,0:T(1,128)S(1)}, s32[1,384]{1,0:T(1,128)S(1)}, s32[384,1]{1,0:T(8,128)S(1)}, bf16[4,144,192]{2,1,0:T(8,128)(2,1)S(1)}, bf16[128,768]{1,0:T(8,128)(2,1)}) custom-call(s32[1]{0:T(128)} %bitcast.refs_0_, s32[1,384]{1,0:T(1,128)S(1)} %bitcast.80, bf16[192,384]{1,0:T(8,128)(2,1)S(1)} %bitcast.74, bf16[8,192]{1,0:T(8,128)(2,1)S(1)} %bitcast.79, ...), custom_call_target="tpu_custom_call" | custom-call | flops 770000000 | bytes 575236 | tf_op jit(solution)/shard_map/slots/pallas_call | solution.py:99
  10.3 1.7 collective-permute-start.5
  12.0 3.2 %collective-permute-done.4.refs_7_.refs_8_ = bf16[144,192]{1,0:T(8,128)(2,1)S(1)} collective-permute-done((bf16[144,192]{1,0:T(8,128)(2,1)S(1)}, bf16[144,192]{1,0:T(8,128)(2,1)S(1)}, u32[]{:S(2)}, u32[]{:S(2)}) %collective-permute-start.4) | collective-permute-done | bytes 55328 | tf_op jit(solution)/shard_map/ppermute | solution.py:115
  16.0 5.6 %attend.1 = (bf16[768,384]{1,0:T(8,128)(2,1)S(1)}, bf16[16,768]{1,0:T(8,128)(2,1)S(1)}, bf16[16,768]{1,0:T(8,128)(2,1)S(1)}, f32[1,384]{1,0:T(1,128)S(1)}, bf16[...) custom-call(s32[1]{0:T(128)} %bitcast.refs_0_, ...), custom_call_target="tpu_custom_call" | custom-call | flops 4400000000 | bytes 5684932 | tf_op jit(solution)/shard_map/attend/pallas_call | solution.py:99
  29.7 5.8 %all-to-all-start = ((bf16[8,16,768]{2,1,0:T(8,128)(2,1)}), bf16[8,16,768]{2,1,0:T(8,128)(2,1)S(1)}, u32[]{:S(2)}, u32[]{:S(2)}) async-start(bf16[8,16,768]{2,1,0:T(8,128)(2,1)} %bitcast.14), calls=%async_computation | async-start | bytes 393216 | tf_op jit(solution)/shard_map/all_to_all | solution.py:302
  36.3 7.6 %all-to-all-done = bf16[8,16,768]{2,1,0:T(8,128)(2,1)S(1)} async-done(((bf16[8,16,768]{2,1,0:T(8,128)(2,1)}), bf16[8,16,768]{2,1,0:T(8,128)(2,1)S(1)}, u32[]{:S(2)}, u32[]{:S(2)}) %all-to-all-start) | async-done | bytes 196640 | tf_op jit(solution)/shard_map/all_to_all | solution.py:302
  49.2 2.1 %route.1 = (f32[128,768]{1,0:T(8,128)S(1)}, f32[128,128]{1,0:T(8,128)S(1)}, bf16[128,768]{1,0:T(8,128)(2,1)S(1)}, bf16[128,896]{1,0:T(8,128)(2,1)}) custom-call(s32[1]{0:T(128)} %bitcast.refs_0_, bf16[128,768]{1,0:T(8,128)(2,1)S(1)} %copy-done.38, bf16[2,128,768]{2,1,0:T(8,128)(2,1)S(1)} %collective-permute-done.6.refs_2_, ...), custom_call_target="tpu_custom_call" | custom-call | flops 880000000 | bytes 2113540 | tf_op jit(solution)/shard_map/route/pallas_call | solution.py:99
  53.4 4.2 %all-to-all-start.1 = ((bf16[8,16,896]{2,1,0:T(8,128)(2,1)}), bf16[8,16,896]{2,1,0:T(8,128)(2,1)S(1)}, u32[]{:S(2)}, u32[]{:S(2)}) async-start(bf16[8,16,896]{2,1,0:T(8,128)(2,1)} %bitcast.16), calls=%async_computation.1 | async-start | bytes 458752 | tf_op jit(solution)/shard_map/all_to_all | solution.py:302
  58.4 4.8 %collective-permute-done.9.refs_7_ = bf16[128,768]{1,0:T(8,128)(2,1)S(1)} collective-permute-done((bf16[128,768]{1,0:T(8,128)(2,1)S(1)}, bf16[128,768]{1,0:T(8,128)(2,1)S(1)}, u32[]{:S(2)}, u32[]{:S(2)}) %collective-permute-start.9) | collective-permute-done | bytes 196640 | tf_op jit(solution)/shard_map/ppermute | solution.py:115
  66.4 6.9 %collective-permute-done.12.refs_3_ = bf16[128,896]{1,0:T(8,128)(2,1)S(1)} collective-permute-done((bf16[128,896]{1,0:T(8,128)(2,1)S(1)}, bf16[128,896]{1,0:T(8,128)(2,1)S(1)}, u32[]{:S(2)}, u32[]{:S(2)}) %collective-permute-start.12) | collective-permute-done | bytes 229408 | tf_op jit(solution)/shard_map/ppermute | solution.py:115
  73.3 1.5 collective-permute-done.13.refs_4_
  77.6 5.7 %expert.1 = (bf16[512,768]{1,0:T(8,128)(2,1)S(1)}, bf16[512,768]{1,0:T(8,128)(2,1)S(1)}, bf16[512,768]{1,0:T(8,128)(2,1)S(1)}, bf16[512,768]{1,0:T(8,128)(2,1)S(...) custom-call(s32[1]{0:T(128)} %bitcast.refs_0_, ...), custom_call_target="tpu_custom_call" | custom-call | flops 4400000000 | bytes 8126468 | tf_op jit(solution)/shard_map/expert/pallas_call | solution.py:99
  83.6 1.7 collective-permute-done.14
  87.2 5.8 %collective-permute-done.16 = bf16[128,896]{1,0:T(8,128)(2,1)S(1)} collective-permute-done((bf16[128,896]{1,0:T(8,128)(2,1)S(1)}, bf16[128,896]{1,0:T(8,128)(2,1)S(1)}, u32[]{:S(2)}, u32[]{:S(2)}) %collective-permute-start.16) | collective-permute-done | bytes 229408 | tf_op jit(solution)/shard_map/ppermute | solution.py:115
  93.7 6.2 %all-to-all-start.3 = ((bf16[8,16,896]{2,1,0:T(8,128)(2,1)}), bf16[8,16,896]{2,1,0:T(8,128)(2,1)S(1)}, u32[]{:S(2)}, u32[]{:S(2)}) async-start(bf16[8,16,896]{2,1,0:T(8,128)(2,1)} %bitcast.25), calls=%async_computation.3 | async-start | bytes 458752 | tf_op jit(solution)/shard_map/all_to_all | solution.py:302
  99.9 1.1 copy-done.50
  101.1 1.1 copy-done.52
  102.2 1.1 copy-done.54
  103.3 3.4 %expert_weights.1 = (bf16[1,768,768]{2,1,0:T(8,128)(2,1)}, bf16[1,768,768]{2,1,0:T(8,128)(2,1)}) custom-call(bf16[512,768]{1,0:T(8,128)(2,1)S(1)} %copy-done.50, bf16[512,768]{1,0:T(8,128)(2,1)S(1)} %copy-done.52, bf16[512,768]{1,0:T(8,128)(2,1)S(1)} %copy-done.29, bf16[512,768]{1,0:T(8,128)(2,1)S(1)} %copy-done.54), custom_call_target="tpu_custom_call" | custom-call | flops 2750000128 | bytes 5505024 | tf_op jit(solution)/shard_map/expert_weights/pallas_call | solution.py:99
  106.8 1.2 all-to-all-done.3
  109.8 1.2 collective-permute-start.17
  111.0 4.8 %collective-permute-done.22.refs_3_ = bf16[128,768]{1,0:T(8,128)(2,1)S(1)} collective-permute-done((bf16[128,768]{1,0:T(8,128)(2,1)S(1)}, bf16[128,768]{1,0:T(8,128)(2,1)S(1)}, u32[]{:S(2)}, u32[]{:S(2)}) %collective-permute-start.22) | collective-permute-done | bytes 196640 | tf_op jit(solution)/shard_map/ppermute | solution.py:115
  115.8 2.1 %collective-permute-done.17 = bf16[128,768]{1,0:T(8,128)(2,1)S(1)} collective-permute-done((bf16[128,768]{1,0:T(8,128)(2,1)S(1)}, bf16[128,768]{1,0:T(8,128)(2,1)S(1)}, u32[]{:S(2)}, u32[]{:S(2)}) %collective-permute-start.17) | collective-permute-done | bytes 196640 | tf_op jit(solution)/shard_map/ppermute | solution.py:115
  117.9 1.6 fusion.5
  119.5 5.7 %all-to-all-start.2 = ((bf16[8,16,768]{2,1,0:T(8,128)(2,1)}), bf16[8,16,768]{2,1,0:T(8,128)(2,1)S(1)}, u32[]{:S(2)}, u32[]{:S(2)}) async-start(bf16[8,16,768]{2,1,0:T(8,128)(2,1)} %bitcast.22), calls=%async_computation.2 | async-start | bytes 393216 | tf_op jit(solution)/shard_map/all_to_all | solution.py:302
  127.0 1.2 copy-done.58
  128.1 1.1 copy-done.60
  129.2 1.1 copy-done.62
  134.7 9.9 %attend_back.1 = (bf16[192,384]{1,0:T(8,128)(2,1)S(1)}, bf16[208,768]{1,0:T(8,128)(2,1)S(1)}, bf16[208,768]{1,0:T(8,128)(2,1)S(1)}, bf16[192,768]{1,0:T(8,128)(2...) custom-call(s32[1]{0:T(128)} %bitcast.refs_0_, ...), custom_call_target="tpu_custom_call" | custom-call | flops 6600000000 | bytes 6715396 | tf_op jit(solution)/shard_map/attend_back/pallas_call | solution.py:99
  144.7 2.1 %collective-permute-start.32 = (bf16[192,768]{1,0:T(8,128)(2,1)S(1)}, bf16[192,768]{1,0:T(8,128)(2,1)S(1)}, u32[]{:S(2)}, u32[]{:S(2)}) collective-permute-start(bf16[192,768]{1,0:T(8,128)(2,1)S(1)} %get-tuple-element.141), channel_id=1, source_target_pairs={{0,8},{4,12},{8,0},{12,4},{16,24},{20,28},{24,16},{28,20},{1,9},{5... | collective-permute-start | bytes 884744 | tf_op jit(solution)/shard_map/ppermute | solution.py:115
  146.8 1.5 collective-permute-start.26
  148.2 3.6 %collective-permute-done.32 = bf16[192,768]{1,0:T(8,128)(2,1)S(1)} collective-permute-done((bf16[192,768]{1,0:T(8,128)(2,1)S(1)}, bf16[192,768]{1,0:T(8,128)(2,1)S(1)}, u32[]{:S(2)}, u32[]{:S(2)}) %collective-permute-start.32) | collective-permute-done | bytes 294944 | tf_op jit(solution)/shard_map/ppermute | solution.py:115
  151.9 3.2 %collective-permute-start.33 = (bf16[96,768]{1,0:T(8,128)(2,1)S(1)}, bf16[96,768]{1,0:T(8,128)(2,1)S(1)}, u32[]{:S(2)}, u32[]{:S(2)}) collective-permute-start(bf16[96,768]{1,0:T(8,128)(2,1)S(1)} %slice.102), channel_id=1, source_target_pairs={{0,16},{4,20},{8,24},{12,28},{16,0},{20,4},{24,8},{28,12},{1,17},{... | collective-permute-start | bytes 442376 | tf_op jit(solution)/shard_map/ppermute | solution.py:115
  157.7 2.5 %collective-permute-done.19.refs_3_ = bf16[192,128]{1,0:T(8,128)(2,1)S(1)} collective-permute-done((bf16[192,128]{1,0:T(8,128)(2,1)S(1)}, bf16[192,128]{1,0:T(8,128)(2,1)S(1)}, u32[]{:S(2)}, u32[]{:S(2)}) %collective-permute-start.19) | collective-permute-done | bytes 49184 | tf_op jit(solution)/shard_map/ppermute | solution.py:115
  163.2 1.5 collective-permute-start.34
  164.7 4.2 %collective-permute-done.27 = bf16[112,768]{1,0:T(8,128)(2,1)S(1)} collective-permute-done((bf16[112,768]{1,0:T(8,128)(2,1)S(1)}, bf16[112,768]{1,0:T(8,128)(2,1)S(1)}, u32[]{:S(2)}, u32[]{:S(2)}) %collective-permute-start.27) | collective-permute-done | bytes 172064 | tf_op jit(solution)/shard_map/ppermute | solution.py:115
  169.1 1.5 collective-permute-start.35
  170.6 5.7 %collective-permute-done.28 = bf16[64,768]{1,0:T(8,128)(2,1)S(1)} collective-permute-done((bf16[64,768]{1,0:T(8,128)(2,1)S(1)}, bf16[64,768]{1,0:T(8,128)(2,1)S(1)}, u32[]{:S(2)}, u32[]{:S(2)}) %collective-permute-start.28) | collective-permute-done | bytes 98336 | tf_op jit(solution)/shard_map/ppermute | solution.py:115
  176.5 3.0 %collective-permute-start.36 = (bf16[96,768]{1,0:T(8,128)(2,1)S(1)}, bf16[96,768]{1,0:T(8,128)(2,1)S(1)}, u32[]{:S(2)}, u32[]{:S(2)}) collective-permute-start(bf16[96,768]{1,0:T(8,128)(2,1)S(1)} %pad_maximum_fusion.3), channel_id=1, source_target_pairs={{0,16},{4,20},{8,24},{12,28},{16,0},{20,4},{24,8},{28,12},{1,17},{... | collective-permute-start | bytes 442376 | tf_op jit(solution)/shard_map/ppermute | solution.py:115
  179.4 5.8 %collective-permute-done.29 = bf16[48,768]{1,0:T(8,128)(2,1)S(1)} collective-permute-done((bf16[48,768]{1,0:T(8,128)(2,1)S(1)}, bf16[48,768]{1,0:T(8,128)(2,1)S(1)}, u32[]{:S(2)}, u32[]{:S(2)}) %collective-permute-start.29) | collective-permute-done | bytes 73760 | tf_op jit(solution)/shard_map/ppermute | solution.py:115
  185.4 2.8 %collective-permute-done.36 = bf16[96,768]{1,0:T(8,128)(2,1)S(1)} collective-permute-done((bf16[96,768]{1,0:T(8,128)(2,1)S(1)}, bf16[96,768]{1,0:T(8,128)(2,1)S(1)}, u32[]{:S(2)}, u32[]{:S(2)}) %collective-permute-start.36) | collective-permute-done | bytes 147488 | tf_op jit(solution)/shard_map/ppermute | solution.py:115
  188.2 3.6 %collective-permute-done.30 = bf16[96,768]{1,0:T(8,128)(2,1)S(1)} collective-permute-done((bf16[96,768]{1,0:T(8,128)(2,1)S(1)}, bf16[96,768]{1,0:T(8,128)(2,1)S(1)}, u32[]{:S(2)}, u32[]{:S(2)}) %collective-permute-start.30) | collective-permute-done | bytes 147488 | tf_op jit(solution)/shard_map/ppermute | solution.py:115
  191.8 1.5 collective-permute-start.31
  194.2 1.3 collective-permute-start.39
  195.5 3.2 %collective-permute-done.25.refs_3_ = bf16[208,384]{1,0:T(8,128)(2,1)S(1)} collective-permute-done((bf16[208,384]{1,0:T(8,128)(2,1)S(1)}, bf16[208,384]{1,0:T(8,128)(2,1)S(1)}, u32[]{:S(2)}, u32[]{:S(2)}) %collective-permute-start.25) | collective-permute-done | bytes 159776 | tf_op jit(solution)/shard_map/ppermute | solution.py:115
  198.7 1.7 tokens_back.1
  200.5 1.3 unpack.1
  (240 shorter events, 46.9 us)
Async XLA Ops:
  0.6 8.8 %collective-permute-start.1 = (bf16[192,384]{1,0:T(8,128)(2,1)}, bf16[192,384]{1,0:T(8,128)(2,1)S(1)}, u32[]{:S(2)}, u32[]{:S(2)}) collective-permute-start(bf16[192,384]{1,0:T(8,128)(2,1)} %bitcast.75), channel_id=1, source_target_pairs={{0,2},{1,3},{2,0},{3,1},{4,6},{5,7},{6,4},{7,5},{8,10},{9,11},{10,... | collective-permute-start | bytes 442376 | tf_op jit(solution)/shard_map/ppermute | solution.py:115
  3.6 12.3 %collective-permute-start = (bf16[192,384]{1,0:T(8,128)(2,1)}, bf16[192,384]{1,0:T(8,128)(2,1)S(1)}, u32[]{:S(2)}, u32[]{:S(2)}) collective-permute-start(bf16[192,384]{1,0:T(8,128)(2,1)} %bitcast.76), channel_id=1, source_target_pairs={{0,1},{1,0},{2,3},{3,2},{4,5},{5,4},{6,7},{7,6},{8,9},{9,8},{10,11... | collective-permute-start | bytes 442376 | tf_op jit(solution)/shard_map/ppermute | solution.py:115
  9.5 6.5 %collective-permute-start.2 = (bf16[192,384]{1,0:T(8,128)(2,1)S(1)}, bf16[192,384]{1,0:T(8,128)(2,1)S(1)}, u32[]{:S(2)}, u32[]{:S(2)}) collective-permute-start(bf16[192,384]{1,0:T(8,128)(2,1)S(1)} %collective-permute-done.1.refs_3_), channel_id=1, source_target_pairs={{0,1},{1,0},{2,3},{3,2},{4,5},{5,4},{6,7},{7,6},{8,9},{9,8},{10,11... | collective-permute-start | bytes 442376 | tf_op jit(solution)/shard_map/ppermute | solution.py:115
  10.0 2.0 collective-permute-start.3
  10.1 5.1 %collective-permute-start.4 = (bf16[144,192]{1,0:T(8,128)(2,1)S(1)}, bf16[144,192]{1,0:T(8,128)(2,1)S(1)}, u32[]{:S(2)}, u32[]{:S(2)}) collective-permute-start(bf16[144,192]{1,0:T(8,128)(2,1)S(1)} %get-tuple-element.153), channel_id=1, source_target_pairs={{0,2},{1,3},{2,0},{3,1},{4,6},{5,7},{6,4},{7,5},{8,10},{9,11},{10,... | collective-permute-start | bytes 165896 | tf_op jit(solution)/shard_map/ppermute | solution.py:115
  10.3 5.7 %collective-permute-start.5 = (bf16[144,192]{1,0:T(8,128)(2,1)S(1)}, bf16[144,192]{1,0:T(8,128)(2,1)S(1)}, u32[]{:S(2)}, u32[]{:S(2)}) collective-permute-start(bf16[144,192]{1,0:T(8,128)(2,1)S(1)} %get-tuple-element.152), channel_id=1, source_target_pairs={{0,3},{1,2},{2,1},{3,0},{4,7},{5,6},{6,5},{7,4},{8,11},{9,10},{10,... | collective-permute-start | bytes 165896 | tf_op jit(solution)/shard_map/ppermute | solution.py:115
  29.4 6.1 %collective-permute-start.6 = (bf16[2,128,768]{2,1,0:T(8,128)(2,1)S(1)}, bf16[2,128,768]{2,1,0:T(8,128)(2,1)S(1)}, u32[]{:S(2)}, u32[]{:S(2)}) collective-permute-start(bf16[2,128,768]{2,1,0:T(8,128)(2,1)S(1)} %get-tuple-element.86), channel_id=1, source_target_pairs={{0,1},{1,0},{2,3},{3,2},{4,5},{5,4},{6,7},{7,6},{8,9},{9,8},{10,11... | collective-permute-start | bytes 1179656 | tf_op jit(solution)/shard_map/ppermute | solution.py:115
  29.7 14.2 %all-to-all-start = ((bf16[8,16,768]{2,1,0:T(8,128)(2,1)}), bf16[8,16,768]{2,1,0:T(8,128)(2,1)S(1)}, u32[]{:S(2)}, u32[]{:S(2)}) async-start(bf16[8,16,768]{2,1,0:T(8,128)(2,1)} %bitcast.14), calls=%async_computation | async-start | bytes 393216 | tf_op jit(solution)/shard_map/all_to_all | solution.py:302
  35.6 8.3 %collective-permute-start.7 = (bf16[128,768]{1,0:T(8,128)(2,1)S(1)}, bf16[128,768]{1,0:T(8,128)(2,1)S(1)}, u32[]{:S(2)}, u32[]{:S(2)}) collective-permute-start(bf16[128,768]{1,0:T(8,128)(2,1)S(1)} %fusion.6), channel_id=1, source_target_pairs={{0,2},{1,3},{2,0},{3,1},{4,6},{5,7},{6,4},{7,5},{8,10},{9,11},{10,... | collective-permute-start | bytes 589832 | tf_op jit(solution)/shard_map/ppermute | solution.py:115
  49.2 25.6 %copy-start = (bf16[1,768,768]{2,1,0:T(8,128)(2,1)S(1)}, bf16[1,768,768]{2,1,0:T(8,128)(2,1)}, u32[]{:S(2)}) copy-start(bf16[1,768,768]{2,1,0:T(8,128)(2,1)} %refs_9_.1) | copy-start | bytes 3538948
  49.2 25.6 %copy-start.1 = (bf16[1,768,768]{2,1,0:T(8,128)(2,1)S(1)}, bf16[1,768,768]{2,1,0:T(8,128)(2,1)}, u32[]{:S(2)}) copy-start(bf16[1,768,768]{2,1,0:T(8,128)(2,1)} %refs_1_.1) | copy-start | bytes 3538948
  53.4 12.2 %all-to-all-start.1 = ((bf16[8,16,896]{2,1,0:T(8,128)(2,1)}), bf16[8,16,896]{2,1,0:T(8,128)(2,1)S(1)}, u32[]{:S(2)}, u32[]{:S(2)}) async-start(bf16[8,16,896]{2,1,0:T(8,128)(2,1)} %bitcast.16), calls=%async_computation.1 | async-start | bytes 458752 | tf_op jit(solution)/shard_map/all_to_all | solution.py:302
  57.6 5.7 %collective-permute-start.9 = (bf16[128,768]{1,0:T(8,128)(2,1)S(1)}, bf16[128,768]{1,0:T(8,128)(2,1)S(1)}, u32[]{:S(2)}, u32[]{:S(2)}) collective-permute-start(bf16[128,768]{1,0:T(8,128)(2,1)S(1)} %bitcast.64), channel_id=1, source_target_pairs={{0,2},{1,3},{2,0},{3,1},{4,6},{5,7},{6,4},{7,5},{8,10},{9,11},{10,... | collective-permute-start | bytes 589832 | tf_op jit(solution)/shard_map/ppermute | solution.py:115
  58.4 5.5 %collective-permute-start.8 = (bf16[128,768]{1,0:T(8,128)(2,1)S(1)}, bf16[128,768]{1,0:T(8,128)(2,1)S(1)}, u32[]{:S(2)}, u32[]{:S(2)}) collective-permute-start(bf16[128,768]{1,0:T(8,128)(2,1)S(1)} %bitcast.65), channel_id=1, source_target_pairs={{0,1},{1,0},{2,3},{3,2},{4,5},{5,4},{6,7},{7,6},{8,9},{9,8},{10,11... | collective-permute-start | bytes 589832 | tf_op jit(solution)/shard_map/ppermute | solution.py:115
  63.3 1.4 collective-permute-start.10
  65.6 7.7 %collective-permute-start.12 = (bf16[128,896]{1,0:T(8,128)(2,1)S(1)}, bf16[128,896]{1,0:T(8,128)(2,1)S(1)}, u32[]{:S(2)}, u32[]{:S(2)}) collective-permute-start(bf16[128,896]{1,0:T(8,128)(2,1)S(1)} %bitcast.60), channel_id=1, source_target_pairs={{0,2},{1,3},{2,0},{3,1},{4,6},{5,7},{6,4},{7,5},{8,10},{9,11},{10,... | collective-permute-start | bytes 688136 | tf_op jit(solution)/shard_map/ppermute | solution.py:115
  66.4 6.9 %collective-permute-start.11 = (bf16[128,896]{1,0:T(8,128)(2,1)S(1)}, bf16[128,896]{1,0:T(8,128)(2,1)S(1)}, u32[]{:S(2)}, u32[]{:S(2)}) collective-permute-start(bf16[128,896]{1,0:T(8,128)(2,1)S(1)} %bitcast.61), channel_id=1, source_target_pairs={{0,1},{1,0},{2,3},{3,2},{4,5},{5,4},{6,7},{7,6},{8,9},{9,8},{10,11... | collective-permute-start | bytes 688136 | tf_op jit(solution)/shard_map/ppermute | solution.py:115
  73.3 1.5 collective-permute-start.13
  83.4 1.9 collective-permute-start.14
  85.3 7.7 %collective-permute-start.16 = (bf16[128,896]{1,0:T(8,128)(2,1)S(1)}, bf16[128,896]{1,0:T(8,128)(2,1)S(1)}, u32[]{:S(2)}, u32[]{:S(2)}) collective-permute-start(bf16[128,896]{1,0:T(8,128)(2,1)S(1)} %fusion.2), channel_id=1, source_target_pairs={{0,2},{1,3},{2,0},{3,1},{4,6},{5,7},{6,4},{7,5},{8,10},{9,11},{10,... | collective-permute-start | bytes 688136 | tf_op jit(solution)/shard_map/ppermute | solution.py:115
  87.1 19.6 %collective-permute-start.15 = (bf16[2,128,768]{2,1,0:T(8,128)(2,1)S(1)}, bf16[2,128,768]{2,1,0:T(8,128)(2,1)S(1)}, u32[]{:S(2)}, u32[]{:S(2)}) collective-permute-start(bf16[2,128,768]{2,1,0:T(8,128)(2,1)S(1)} %get-tuple-element.106), channel_id=1, source_target_pairs={{0,1},{1,0},{2,3},{3,2},{4,5},{5,4},{6,7},{7,6},{8,9},{9,8},{10,11... | collective-permute-start | bytes 1179656 | tf_op jit(solution)/shard_map/ppermute | solution.py:115
  93.7 14.2 %all-to-all-start.3 = ((bf16[8,16,896]{2,1,0:T(8,128)(2,1)}), bf16[8,16,896]{2,1,0:T(8,128)(2,1)S(1)}, u32[]{:S(2)}, u32[]{:S(2)}) async-start(bf16[8,16,896]{2,1,0:T(8,128)(2,1)} %bitcast.25), calls=%async_computation.3 | async-start | bytes 458752 | tf_op jit(solution)/shard_map/all_to_all | solution.py:302
  108.9 6.9 %collective-permute-start.22 = (bf16[128,768]{1,0:T(8,128)(2,1)S(1)}, bf16[128,768]{1,0:T(8,128)(2,1)S(1)}, u32[]{:S(2)}, u32[]{:S(2)}) collective-permute-start(bf16[128,768]{1,0:T(8,128)(2,1)S(1)} %get-tuple-element.123.refs_1_), channel_id=1, source_target_pairs={{0,2},{1,3},{2,0},{3,1},{4,6},{5,7},{6,4},{7,5},{8,10},{9,11},{10,... | collective-permute-start | bytes 589832 | tf_op jit(solution)/shard_map/ppermute | solution.py:115
  109.8 8.1 %collective-permute-start.17 = (bf16[128,768]{1,0:T(8,128)(2,1)S(1)}, bf16[128,768]{1,0:T(8,128)(2,1)S(1)}, u32[]{:S(2)}, u32[]{:S(2)}) collective-permute-start(bf16[128,768]{1,0:T(8,128)(2,1)S(1)} %fusion.3), channel_id=1, source_target_pairs={{0,2},{1,3},{2,0},{3,1},{4,6},{5,7},{6,4},{7,5},{8,10},{9,11},{10,... | collective-permute-start | bytes 589832 | tf_op jit(solution)/shard_map/ppermute | solution.py:115
  111.0 14.2 %collective-permute-start.21 = (bf16[128,768]{1,0:T(8,128)(2,1)S(1)}, bf16[128,768]{1,0:T(8,128)(2,1)S(1)}, u32[]{:S(2)}, u32[]{:S(2)}) collective-permute-start(bf16[128,768]{1,0:T(8,128)(2,1)S(1)} %get-tuple-element.123.refs_1_), channel_id=1, source_target_pairs={{0,1},{1,0},{2,3},{3,2},{4,5},{5,4},{6,7},{7,6},{8,9},{9,8},{10,11... | collective-permute-start | bytes 589832 | tf_op jit(solution)/shard_map/ppermute | solution.py:115
  115.8 9.5 %collective-permute-start.23 = (bf16[128,768]{1,0:T(8,128)(2,1)S(1)}, bf16[128,768]{1,0:T(8,128)(2,1)S(1)}, u32[]{:S(2)}, u32[]{:S(2)}) collective-permute-start(bf16[128,768]{1,0:T(8,128)(2,1)S(1)} %collective-permute-done.22.refs_3_), channel_id=1, source_target_pairs={{0,1},{1,0},{2,3},{3,2},{4,5},{5,4},{6,7},{7,6},{8,9},{9,8},{10,11... | collective-permute-start | bytes 589832 | tf_op jit(solution)/shard_map/ppermute | solution.py:115
  119.5 35.5 %all-to-all-start.2 = ((bf16[8,16,768]{2,1,0:T(8,128)(2,1)}), bf16[8,16,768]{2,1,0:T(8,128)(2,1)S(1)}, u32[]{:S(2)}, u32[]{:S(2)}) async-start(bf16[8,16,768]{2,1,0:T(8,128)(2,1)} %bitcast.22), calls=%async_computation.2 | async-start | bytes 393216 | tf_op jit(solution)/shard_map/all_to_all | solution.py:302
  144.7 7.1 %collective-permute-start.32 = (bf16[192,768]{1,0:T(8,128)(2,1)S(1)}, bf16[192,768]{1,0:T(8,128)(2,1)S(1)}, u32[]{:S(2)}, u32[]{:S(2)}) collective-permute-start(bf16[192,768]{1,0:T(8,128)(2,1)S(1)} %get-tuple-element.141), channel_id=1, source_target_pairs={{0,8},{4,12},{8,0},{12,4},{16,24},{20,28},{24,16},{28,20},{1,9},{5... | collective-permute-start | bytes 884744 | tf_op jit(solution)/shard_map/ppermute | solution.py:115
  146.8 15.2 %collective-permute-start.26 = (bf16[208,768]{1,0:T(8,128)(2,1)S(1)}, bf16[208,768]{1,0:T(8,128)(2,1)S(1)}, u32[]{:S(2)}, u32[]{:S(2)}) collective-permute-start(bf16[208,768]{1,0:T(8,128)(2,1)S(1)} %get-tuple-element.139), channel_id=1, source_target_pairs={{0,4},{4,0},{8,12},{12,8},{16,20},{20,16},{24,28},{28,24},{1,5},{5... | collective-permute-start | bytes 958472 | tf_op jit(solution)/shard_map/ppermute | solution.py:115
  151.9 11.2 %collective-permute-start.33 = (bf16[96,768]{1,0:T(8,128)(2,1)S(1)}, bf16[96,768]{1,0:T(8,128)(2,1)S(1)}, u32[]{:S(2)}, u32[]{:S(2)}) collective-permute-start(bf16[96,768]{1,0:T(8,128)(2,1)S(1)} %slice.102), channel_id=1, source_target_pairs={{0,16},{4,20},{8,24},{12,28},{16,0},{20,4},{24,8},{28,12},{1,17},{... | collective-permute-start | bytes 442376 | tf_op jit(solution)/shard_map/ppermute | solution.py:115
  155.7 1.9 collective-permute-start.18
  155.8 4.4 %collective-permute-start.19 = (bf16[192,128]{1,0:T(8,128)(2,1)S(1)}, bf16[192,128]{1,0:T(8,128)(2,1)S(1)}, u32[]{:S(2)}, u32[]{:S(2)}) collective-permute-start(bf16[192,128]{1,0:T(8,128)(2,1)S(1)} %get-tuple-element.112), channel_id=1, source_target_pairs={{0,2},{1,3},{2,0},{3,1},{4,6},{5,7},{6,4},{7,5},{8,10},{9,11},{10,... | collective-permute-start | bytes 147464 | tf_op jit(solution)/shard_map/ppermute | solution.py:115
  156.7 4.0 %collective-permute-start.20 = (bf16[192,128]{1,0:T(8,128)(2,1)S(1)}, bf16[192,128]{1,0:T(8,128)(2,1)S(1)}, u32[]{:S(2)}, u32[]{:S(2)}) collective-permute-start(bf16[192,128]{1,0:T(8,128)(2,1)S(1)} %get-tuple-element.113), channel_id=1, source_target_pairs={{0,3},{1,2},{2,1},{3,0},{4,7},{5,6},{6,5},{7,4},{8,11},{9,10},{10,... | collective-permute-start | bytes 147464 | tf_op jit(solution)/shard_map/ppermute | solution.py:115
  161.8 31.6 %collective-permute-start.24 = (bf16[2,208,384]{2,1,0:T(8,128)(2,1)S(1)}, bf16[2,208,384]{2,1,0:T(8,128)(2,1)S(1)}, u32[]{:S(2)}, u32[]{:S(2)}) collective-permute-start(bf16[2,208,384]{2,1,0:T(8,128)(2,1)S(1)} %get-tuple-element.134), channel_id=1, source_target_pairs={{0,1},{1,0},{2,3},{3,2},{4,5},{5,4},{6,7},{7,6},{8,9},{9,8},{10,11... | collective-permute-start | bytes 958472 | tf_op jit(solution)/shard_map/ppermute | solution.py:115
  162.1 6.7 %collective-permute-start.27 = (bf16[112,768]{1,0:T(8,128)(2,1)S(1)}, bf16[112,768]{1,0:T(8,128)(2,1)S(1)}, u32[]{:S(2)}, u32[]{:S(2)}) collective-permute-start(bf16[112,768]{1,0:T(8,128)(2,1)S(1)} %slice.96), channel_id=1, source_target_pairs={{0,8},{4,12},{8,0},{12,4},{16,24},{20,28},{24,16},{28,20},{1,9},{5... | collective-permute-start | bytes 516104 | tf_op jit(solution)/shard_map/ppermute | solution.py:115
  163.2 5.9 %collective-permute-start.34 = (bf16[48,768]{1,0:T(8,128)(2,1)S(1)}, bf16[48,768]{1,0:T(8,128)(2,1)S(1)}, u32[]{:S(2)}, u32[]{:S(2)}) collective-permute-start(bf16[48,768]{1,0:T(8,128)(2,1)S(1)} %slice.104), channel_id=1, source_target_pairs={{0,4},{4,0},{8,12},{12,8},{16,20},{20,16},{24,28},{28,24},{1,5},{5... | collective-permute-start | bytes 221192 | tf_op jit(solution)/shard_map/ppermute | solution.py:115
  168.9 7.3 %collective-permute-start.28 = (bf16[64,768]{1,0:T(8,128)(2,1)S(1)}, bf16[64,768]{1,0:T(8,128)(2,1)S(1)}, u32[]{:S(2)}, u32[]{:S(2)}) collective-permute-start(bf16[64,768]{1,0:T(8,128)(2,1)S(1)} %slice.99), channel_id=1, source_target_pairs={{0,16},{4,20},{8,24},{12,28},{16,0},{20,4},{24,8},{28,12},{1,17},{... | collective-permute-start | bytes 294920 | tf_op jit(solution)/shard_map/ppermute | solution.py:115
  169.1 7.4 %collective-permute-start.35 = (bf16[48,768]{1,0:T(8,128)(2,1)S(1)}, bf16[48,768]{1,0:T(8,128)(2,1)S(1)}, u32[]{:S(2)}, u32[]{:S(2)}) collective-permute-start(bf16[48,768]{1,0:T(8,128)(2,1)S(1)} %slice_add_fusion.1), channel_id=1, source_target_pairs={{0,4},{4,0},{8,12},{12,8},{16,20},{20,16},{24,28},{28,24},{1,5},{5... | collective-permute-start | bytes 221192 | tf_op jit(solution)/shard_map/ppermute | solution.py:115
  176.3 22.4 %copy-start.17 = (bf16[384,192]{0,1:T(8,128)(2,1)S(1)}, bf16[384,192]{0,1:T(8,128)(2,1)}, u32[]{:S(2)}) copy-start(bf16[384,192]{0,1:T(8,128)(2,1)} %param.15) | copy-start | bytes 442372
  176.3 22.4 %copy-start.34 = (bf16[192,384]{1,0:T(8,128)(2,1)S(1)}, bf16[192,384]{1,0:T(8,128)(2,1)}, u32[]{:S(2)}) copy-start(bf16[192,384]{1,0:T(8,128)(2,1)} %copy-done.33) | copy-start | bytes 442372
  176.3 8.8 %collective-permute-start.29 = (bf16[48,768]{1,0:T(8,128)(2,1)S(1)}, bf16[48,768]{1,0:T(8,128)(2,1)S(1)}, u32[]{:S(2)}, u32[]{:S(2)}) collective-permute-start(bf16[48,768]{1,0:T(8,128)(2,1)S(1)} %slice.100), channel_id=1, source_target_pairs={{0,16},{4,20},{8,24},{12,28},{16,0},{20,4},{24,8},{28,12},{1,17},{... | collective-permute-start | bytes 221192 | tf_op jit(solution)/shard_map/ppermute | solution.py:115
  176.5 11.7 %collective-permute-start.36 = (bf16[96,768]{1,0:T(8,128)(2,1)S(1)}, bf16[96,768]{1,0:T(8,128)(2,1)S(1)}, u32[]{:S(2)}, u32[]{:S(2)}) collective-permute-start(bf16[96,768]{1,0:T(8,128)(2,1)S(1)} %pad_maximum_fusion.3), channel_id=1, source_target_pairs={{0,16},{4,20},{8,24},{12,28},{16,0},{20,4},{24,8},{28,12},{1,17},{... | collective-permute-start | bytes 442376 | tf_op jit(solution)/shard_map/ppermute | solution.py:115
  185.2 6.6 %collective-permute-start.30 = (bf16[96,768]{1,0:T(8,128)(2,1)S(1)}, bf16[96,768]{1,0:T(8,128)(2,1)S(1)}, u32[]{:S(2)}, u32[]{:S(2)}) collective-permute-start(bf16[96,768]{1,0:T(8,128)(2,1)S(1)} %pad_maximum_fusion.2), channel_id=1, source_target_pairs={{0,8},{4,12},{8,0},{12,4},{16,24},{20,28},{24,16},{28,20},{1,9},{5... | collective-permute-start | bytes 442376 | tf_op jit(solution)/shard_map/ppermute | solution.py:115
  185.3 9.0 %collective-permute-start.38 = (f32[16,768]{1,0:T(8,128)S(1)}, f32[16,768]{1,0:T(8,128)S(1)}, u32[]{:S(2)}, u32[]{:S(2)}) collective-permute-start(f32[16,768]{1,0:T(8,128)S(1)} %slice_convert_fusion), channel_id=1, source_target_pairs={{0,1},{1,0},{2,3},{3,2},{4,5},{5,4},{6,7},{7,6},{8,9},{9,8},{10,11... | collective-permute-start | bytes 147464 | tf_op jit(solution)/shard_map/ppermute | solution.py:115
  188.1 12.3 %collective-permute-start.37 = (bf16[192,768]{1,0:T(8,128)(2,1)S(1)}, bf16[192,768]{1,0:T(8,128)(2,1)S(1)}, u32[]{:S(2)}, u32[]{:S(2)}) collective-permute-start(bf16[192,768]{1,0:T(8,128)(2,1)S(1)} %pad_maximum_fusion.1.refs_3_), channel_id=1, source_target_pairs={{0,8},{4,12},{8,0},{12,4},{16,24},{20,28},{24,16},{28,20},{1,9},{5... | collective-permute-start | bytes 884744 | tf_op jit(solution)/shard_map/ppermute | solution.py:115
  191.8 8.7 %collective-permute-start.31 = (bf16[192,768]{1,0:T(8,128)(2,1)S(1)}, bf16[192,768]{1,0:T(8,128)(2,1)S(1)}, u32[]{:S(2)}, u32[]{:S(2)}) collective-permute-start(bf16[192,768]{1,0:T(8,128)(2,1)S(1)} %pad_maximum_fusion.refs_1_), channel_id=1, source_target_pairs={{0,4},{4,0},{8,12},{12,8},{16,20},{20,16},{24,28},{28,24},{1,5},{5... | collective-permute-start | bytes 884744 | tf_op jit(solution)/shard_map/ppermute | solution.py:115
  193.4 5.3 %collective-permute-start.25 = (bf16[208,384]{1,0:T(8,128)(2,1)S(1)}, bf16[208,384]{1,0:T(8,128)(2,1)S(1)}, u32[]{:S(2)}, u32[]{:S(2)}) collective-permute-start(bf16[208,384]{1,0:T(8,128)(2,1)S(1)} %fusion.7), channel_id=1, source_target_pairs={{0,2},{1,3},{2,0},{3,1},{4,6},{5,7},{6,4},{7,5},{8,10},{9,11},{10,... | collective-permute-start | bytes 479240 | tf_op jit(solution)/shard_map/ppermute | solution.py:115
  194.2 6.2 %collective-permute-start.39 = (f32[16,768]{1,0:T(8,128)S(1)}, f32[16,768]{1,0:T(8,128)S(1)}, u32[]{:S(2)}, u32[]{:S(2)}) collective-permute-start(f32[16,768]{1,0:T(8,128)S(1)} %fusion.8.refs_5_), channel_id=1, source_target_pairs={{0,2},{1,3},{2,0},{3,1},{4,6},{5,7},{6,4},{7,5},{8,10},{9,11},{10,... | collective-permute-start | bytes 147464 | tf_op jit(solution)/shard_map/ppermute | solution.py:115
  (73 other events, 300.0 us)

commit v3 on v2

--- a/solution.py
+++ b/solution.py
@@ -20,7 +20,12 @@
 
 class Far:
     def __init__(self, value):
-        self.value = value
+        self.value = pltpu.with_memory_space_constraint(value, pltpu.HBM)
+
+
+class Pin:
+    def __init__(self, value):
+        self.value = pltpu.with_memory_space_constraint(value, pltpu.VMEM)
 
 
 class Loaded:
@@ -37,70 +42,45 @@
         return self.held[index]
 
 
-class Stored:
-    def __init__(self, copy, held):
-        self.copy, self.held, self.started = copy, held, False
-
-    def __setitem__(self, index, value):
-        self.held[index] = value
-
-    def __getitem__(self, index):
-        return self.held[index]
-
-    def send(self):
-        if not self.started:
-            self.started = True
-            self.copy.start()
-
-
 def run(body, outs, args, name, us=1.0, scratch=(), limit=16):
-    far_in = [isinstance(a, Far) for a in args]
-    args = [a.value if isinstance(a, Far) else a for a in args]
-    far_out = [len(o) == 3 for o in outs]
-    bufs = [pltpu.VMEM(a.shape, a.dtype) for a, far in zip(args, far_in) if far]
-    bufs += [pltpu.VMEM(o[0], o[1]) for o, far in zip(outs, far_out) if far]
+    far = [isinstance(a, Far) for a in args]
+    args = [a.value if isinstance(a, (Far, Pin)) else a for a in args]
+    bufs = [pltpu.VMEM(a.shape, a.dtype) for a, f in zip(args, far) if f]
     n_in, n_out, n_own = len(args), len(outs), len(scratch)
     hbm = pl.BlockSpec(memory_space=pltpu.HBM)
     specs = [
-        SMEM if a.shape == (1,) and a.dtype == jnp.int32 else hbm if far else VMEM
-        for a, far in zip(args, far_in)
+        SMEM if a.shape == (1,) and a.dtype == jnp.int32 else hbm if f else VMEM
+        for a, f in zip(args, far)
     ]
     moved = sum(a.size * a.dtype.itemsize for a in args)
     moved += sum(math.prod(o[0]) * jnp.dtype(o[1]).itemsize for o in outs)
 
     def wrapped(*refs):
-        ins, results = refs[:n_in], refs[n_in : n_in + n_out]
         own = refs[n_in + n_out : n_in + n_out + n_own]
         held = refs[n_in + n_out + n_own :]
         given, at = [], 0
-        for ref, far in zip((*ins, *results), (*far_in, *far_out)):
-            if not far:
-                given.append(ref)
-                continue
-            if len(given) < n_in:
+        for ref, f in zip(refs[:n_in], far):
+            if f:
                 copy = pltpu.make_async_copy(ref, held[at], held[-1].at[at])
                 copy.start()
                 given.append(Loaded(copy, held[at]))
+                at += 1
             else:
-                copy = pltpu.make_async_copy(held[at], ref, held[-1].at[at])
-                given.append(Stored(copy, held[at]))
-            at += 1
-        body(*given, *own)
+                given.append(ref)
+        body(*given, *refs[n_in : n_in + n_out], *own)
         for g in given:
-            if isinstance(g, Stored):
-                g.send()
-        for g in given:
-            if isinstance(g, Stored):
-                g.copy.wait()
-            elif isinstance(g, Loaded):
+            if isinstance(g, Loaded):
                 g.wait()
 
     sems = [pltpu.SemaphoreType.DMA((len(bufs),))] if bufs else []
     return pl.pallas_call(
         wrapped,
-        out_shape=[jax.ShapeDtypeStruct(o[0], o[1]) for o in outs],
+        out_shape=[
+            pltpu.VMEM(o[0], o[1]) if len(o) == 3 else jax.ShapeDtypeStruct(o[0], o[1])
+            for o in outs
+        ],
         in_specs=specs,
-        out_specs=[hbm if far else VMEM for far in far_out],
+        out_specs=[VMEM] * n_out,
         scratch_shapes=[*scratch, *bufs, *sems],
         compiler_params=pltpu.CompilerParams(vmem_limit_bytes=limit * 2**20),
         cost_estimate=pl.CostEstimate(
@@ -167,27 +147,61 @@
     return kept, came, swap(half, "tp", 2), half
 
 
-def chain_sum(keep, send, masks, tail):
-    body = keep.shape[0] - tail
-    total = keep
-    for at, mask in enumerate(masks):
-        total = keep + swap(send, "exp", mask)
-        if at + 1 < len(masks):
-            half = body // 2
-            keep = total[:half]
-            if tail:
-                keep = jnp.concatenate([keep, total[body:]], axis=0)
-            send = total[half:]
-            body = half
-    mine, few = total[:body], total[body:]
-    for mask in masks[:0:-1]:
-        mine = jnp.concatenate([mine, swap(mine, "exp", mask)], axis=0)
-    return mine, swap(mine, "exp", masks[0]), few
-
-
-def rel_of(place, masks):
-    top = len(masks) - 1
-    return sum(mask for at, mask in enumerate(masks) if (place >> (top - at)) & 1)
+def digits_of(count):
+    digits, shift = [(0, 2)], 1
+    while (1 << shift) < count:
+        radix = min(4, count >> shift)
+        digits.append((shift, radix))
+        shift += radix.bit_length() - 1
+    return digits
+
+
+def rel_of(place, order):
+    rel = 0
+    for shift, radix in reversed(order):
+        rel |= (place % radix) << shift
+        place //= radix
+    return rel
+
+
+def trade(blocks, digit):
+    shift, radix = digit
+    return [swap(blocks[k], "exp", k << shift) for k in range(1, radix)]
+
+
+def sum_blocks(kept, came):
+    total = kept.astype(f32)
+    for c in came:
+        total = total + c.astype(f32)
+    return total.astype(bf16)
+
+
+def two_chains(a_blocks, b_blocks, order_a, order_b, tail):
+    for at, (digit_a, digit_b) in enumerate(zip(order_a, order_b)):
+        b_came = trade(b_blocks, digit_b)
+        a_came = trade(a_blocks, digit_a)
+        got = lax.optimization_barrier((*a_came, *b_came))
+        a = sum_blocks(a_blocks[0], got[: len(a_came)])
+        b = sum_blocks(b_blocks[0], got[len(a_came) :])
+        few = b[b.shape[0] - tail :]
+        if at + 1 < len(order_a):
+            radix = order_a[at + 1][1]
+            part = a.shape[0] // radix
+            a_blocks = [a[k * part : (k + 1) * part] for k in range(radix)]
+            radix = order_b[at + 1][1]
+            part = (b.shape[0] - tail) // radix
+            b_blocks = [
+                jnp.concatenate([b[k * part : (k + 1) * part], few], axis=0) for k in range(radix)
+            ]
+    b = b[: b.shape[0] - tail]
+    for at, (digit_a, digit_b) in enumerate(zip(order_a[::-1], order_b[::-1])):
+        a_came = trade([a] * digit_a[1], digit_a)
+        b_came = trade([b] * digit_b[1], digit_b)
+        got = lax.optimization_barrier((*a_came, *b_came))
+        a_blocks, b_blocks = [a, *got[: len(a_came)]], [b, *got[len(a_came) :]]
+        if at + 1 < len(order_a):
+            a, b = jnp.concatenate(a_blocks, axis=0), jnp.concatenate(b_blocks, axis=0)
+    return a_blocks, b_blocks, few
 
 
 def local(
@@ -225,9 +239,9 @@
     extra = -(-(experts + 2) // 16) * 16
     few_rows = -(-(experts + 2 + heads) // 16) * 16
     me = lax.axis_index(("exp", "tp")).astype(jnp.int32)[None]
-    bits = [1 << b for b in range(owners.bit_length() - 1)]
-    order_a = bits
-    order_b = bits[1:] + bits[:1]
+    order_a = digits_of(owners)
+    order_b = order_a[1:] + order_a[:1]
+    first_a, first_b = order_a[0][1], order_b[0][1]
     shift = ways.bit_length() - 1
 
     tok_t = tokens.T
@@ -257,9 +271,7 @@
         dest_row = dest(slot_row, row)
         drow_ref[...] = dest_row
         drow_far[...] = dest_row
-        drow_far.send()
         dcol_ref[...] = dest(slot_col, col)
-        dcol_ref.send()
         cot = cot_ref[...]
         line = iota((extra - experts, quarter), 0)
         gains = jnp.where(
@@ -349,25 +361,18 @@
         small = jnp.concatenate([absolute(pieces, mine, t) for t in range(ways)], axis=1)
         small_ref[...] = small
         small_far[...] = small
-        small_far.send()
         x_low = x_ref[...]
-        x_ref.send()
         x = x_low.astype(f32)
         r1 = lax.rsqrt(jnp.mean(x * x, axis=0, keepdims=True) + EPSILON)
         r1_ref[...] = r1
-        r1_ref.send()
         n1 = (x * r1 * spread_row(small, experts, length)).astype(bf16)
         n1_ref[...] = n1
-        n1_ref.send()
         q = mm(wq_ref[...], n1).astype(bf16)
         k = mm(wk_ref[...], n1).astype(bf16)
         v = mm(wv_ref[...], n1).astype(bf16)
         q_ref[...] = q
         k_ref[...] = k
         v_ref[...] = v
-        q_ref.send()
-        k_ref.send()
-        v_ref.send()
         hot = (iota((bins, span), 0) == bucket_ref[...]).astype(bf16)
         offsets = mm(table_ref[...], hot)
         above = iota((length, length), 0)
@@ -384,9 +389,7 @@
             p = (e / jnp.sum(e, axis=0, keepdims=True)).astype(bf16)
             p_ref[h] = p
             attn_ref[part] = mm(v[part], p).astype(bf16)
-        p_ref.send()
         attn = attn_ref[...]
-        attn_ref.send()
         dest = dest_ref[...]
         wo = wo_ref[...]
         for rel, out in enumerate((kept_ref, sent_ref.at[0], passed_ref, sent_ref.at[1])):
@@ -430,11 +433,12 @@
         us=4.0,
         limit=24,
     )
-    o_kept, o_beside, o_across, none = scatter_sum(*o_parts)
+    o_kept, o_passed, o_sent = o_parts
+    o_beside = swap(o_sent, "tp", 1)
 
     d_arrived = over_experts(d_send)
-    o_across, d_arrived = lax.optimization_barrier((o_across, d_arrived))
-    d_pieces = gather_pieces(d_arrived)
+    o_half, d_arrived = lax.optimization_barrier((o_passed + o_beside[1], d_arrived))
+    o_across = swap(o_half, "tp", 2)
 
     def route_body(
         me_ref,
@@ -471,9 +475,6 @@
         aux_ref[:, 0:experts] = p
         aux_ref[:, LANES - 2 : LANES - 1] = r2
         aux_ref[:, LANES - 1 : LANES] = g
-        h_ref.send()
-        aux_ref.send()
-        dout_ref.send()
         send_ref[:, 0:width] = n2.astype(bf16)
         send_ref[:, width : width + LANES] = two_lanes(g, LANES)
 
@@ -489,6 +490,7 @@
         "route",
         us=0.8,
     )
+    d_pieces = gather_pieces(after(d_arrived, send))
     arrived, *d_pieces = lax.optimization_barrier((over_experts(send), *d_pieces))
     arrived = gather_pieces(arrived)
 
@@ -506,8 +508,6 @@
                 pieces.append(douts[src][:, at : at + quarter])
             dout = jnp.concatenate([absolute(pieces, mine, t) for t in range(ways)], axis=1)
             dy_ref[part] = (g * dout.astype(f32)).astype(bf16)
-        u_ref.send()
-        dy_ref.send()
         u = u_ref[...]
         dy = dy_ref[...]
         z = mm(u, win_ref[0])
@@ -515,13 +515,11 @@
         t = jnp.tanh(c * (z + 0.044715 * z * z * z))
         act = (0.5 * z * (1.0 + t)).astype(bf16)
         act_ref[...] = act
-        act_ref.send()
         slope = 0.5 * (1.0 + t) + 0.5 * z * (1.0 - t * t) * (c * (1.0 + 3 * 0.044715 * z * z))
         dact = mm_nt(dy, wout_ref[0])
         dot = jnp.sum(dact * act.astype(f32), axis=-1, keepdims=True)
         dz = (dact * slope).astype(bf16)
         dz_ref[...] = dz
-        dz_ref.send()
         du = mm_nt(dz, win_ref[0]).astype(bf16)
         tail = two_lanes(dot, LANES)
         for rel, out in enumerate((kept_ref, sent_ref.at[0], passed_ref, sent_ref.at[1])):
@@ -548,7 +546,7 @@
     du_sum = du_kept + du_beside[0] + du_across
     du_rows = over_experts(du_sum)
 
-    def value_body(act_ref, wout_ref, kept_ref, passed_ref, sent_ref):
+    def value_body(me_ref, act_ref, wout_ref, kept_ref, passed_ref, sent_ref):
         y = mm(act_ref[...], wout_ref[0]).astype(bf16)
         for rel, out in enumerate((kept_ref, sent_ref.at[0], passed_ref, sent_ref.at[1])):
             out[...] = y[rel * rows : (rel + 1) * rows]
@@ -556,7 +554,7 @@
     y_parts = run(
         value_body,
         [((rows, width), bf16), ((rows, width), bf16), ((2, rows, width), bf16)],
-        (Far(after(act, du_half)), w_out),
+        (after(me, du_half), Pin(act), w_out),
         "value",
         us=0.8,
     )
@@ -565,14 +563,14 @@
     y_across = swap(after(y_passed + y_beside[1], du_sum), "tp", 2)
     y_sum = y_kept + y_beside[0] + y_across
 
-    def weights_body(u_ref, dy_ref, act_ref, dz_ref, gin_ref, gout_ref):
+    def weights_body(me_ref, u_ref, dy_ref, act_ref, dz_ref, gin_ref, gout_ref):
         gin_ref[0] = mm_tn(u_ref[...], dz_ref[...]).astype(bf16)
         gout_ref[0] = mm_tn(act_ref[...], dy_ref[...]).astype(bf16)
 
     grad_in, grad_out = run(
         weights_body,
         [((1, width, hidden_here), bf16), ((1, hidden_here, width), bf16)],
-        (Far(u_all), Far(dy_all), Far(act), Far(after(dz, du_sum))),
+        (after(me, du_sum), Pin(u_all), Pin(dy_all), Pin(act), Pin(dz)),
         "expert_weights",
         us=2.5,
     )
@@ -608,13 +606,17 @@
     do_rows, few_parts = run(
         back_body,
         [((rows, width), bf16), ((few_rows, width), f32, True)],
-        (du_rows, h_rows, aux, dout_rows, small_far),
+        (du_rows, Pin(h_rows), Pin(aux), Pin(dout_rows), Pin(small_far)),
         "residual_back",
         us=2.0,
     )
     do_pieces = gather_pieces(do_rows)
-
-    chunk = 2 * here // owners
+    *do_pieces, y_rows = lax.optimization_barrier((*do_pieces, y_rows))
+
+    a_rows = 4 * here * 2 // 3
+    chunk_a = a_rows // owners
+    chunk_b = (4 * here - a_rows) // owners
+    a_part, b_part = a_rows // first_a, (4 * here - a_rows) // first_b
 
     def attend_back_body(
         me_ref,
@@ -639,20 +641,13 @@
         few_ref,
         bucket_ref,
         own_ref,
-        akeep_ref,
-        asend_ref,
-        bkeep_ref,
-        bsend_ref,
         kept_ref,
         passed_ref,
         sent_ref,
-        a_ref,
-        b_ref,
-        dq_ref,
-        dk_ref,
-        dv_ref,
-        all_ref,
+        *others,
     ):
+        a_outs, b_outs = others[:first_a], others[first_a : first_a + first_b]
+        a_ref, b_ref, dq_ref, dk_ref, dv_ref, all_ref = others[first_a + first_b :]
         mine = me_ref[0] & (ways - 1)
         place = me_ref[0] >> shift
         stack = jnp.concatenate([d[...] for d in (d0, d1, d2, d3)], axis=0)
@@ -663,7 +658,6 @@
             own = jnp.where(mine == t, stack[:, t * quarter : (t + 1) * quarter], own)
         hot = (iota((ways * rows, length), 0) == drow_ref[...]).astype(bf16)
         own_ref[...] = mm_tn(own, hot).astype(bf16)
-        own_ref.send()
         wo = wo_ref[...]
         da = mm_nt(wo, do).astype(bf16)
         hot = (iota((bins, span), 0) == bucket_ref[...]).astype(f32)
@@ -692,19 +686,20 @@
         back = jnp.sum(back + gv * wv_ref[...].astype(f32), axis=0, keepdims=True)
         gain = small_ref[experts : experts + 1].astype(f32)
         gwo = mm(attn_ref[...], do)
-        for c in range(owners):
-            for total, ref in (((gq, gk), a_ref), ((gv, gwo), b_ref)):
-                low, high = c * chunk, (c + 1) * chunk
-                picked = total[0][low:high] if high <= here else total[1][low - here : high - here]
-                ref[c] = picked.astype(bf16)
-        tail = (owners // 2) * chunk
-        for order, ref, keep, send in (
-            (order_a, a_ref, akeep_ref, asend_ref),
-            (order_b, b_ref, bkeep_ref, bsend_ref),
+        parts = [t.astype(bf16) for t in (gq, gk, gv, gwo)]
+        for ref, chunk, start in ((a_ref, chunk_a, 0), (b_ref, chunk_b, a_rows)):
+            for c in range(owners):
+                low = start + c * chunk
+                which, low = low // here, low % here
+                ref[c] = parts[which][low : low + chunk]
+        for order, ref, outs, chunk in (
+            (order_a, a_ref, a_outs, chunk_a),
+            (order_b, b_ref, b_outs, chunk_b),
         ):
+            each = owners // len(outs)
             for at in range(owners):
-                out, line = (keep, at) if at < owners // 2 else (send, at - owners // 2)
-                out[line * chunk : (line + 1) * chunk] = ref[rel_of(at, order) ^ place]
+                line = at % each
+                outs[at // each][line * chunk : (line + 1) * chunk] = ref[rel_of(at, order) ^ place]
         few = few_ref[...]
         line = iota((few_rows, 1), 0)
         few = few + jnp.where(line == experts + 1, back / gain, 0.0)
@@ -718,8 +713,8 @@
         for h in range(heads):
             few = few + jnp.where(line == experts + 2 + h, wide[h : h + 1], 0.0)
         few = few.astype(bf16)
-        akeep_ref[tail : tail + few_rows] = few
-        asend_ref[tail : tail + few_rows] = few
+        for out in b_outs:
+            out[b_part : b_part + few_rows] = few
         dn1 = mm_tn(wq_ref[...], dq_ref[...])
         dn1 = dn1 + mm_tn(wk_ref[...], dk_ref[...])
         dn1 = dn1 + mm_tn(wv_ref[...], dv_ref[...])
@@ -734,44 +729,41 @@
             out[0:quarter] = all_ref[pl.ds(at, quarter), :]
             out[quarter : quarter + 16] = tail
 
-    side = (owners // 2) * chunk
-    dh_own, a_keep, a_send, b_keep, b_send, *dn1_parts = run(
+    dh_own, *others = run(
         attend_back_body,
         [
             ((quarter, length), bf16, True),
-            ((side + few_rows, width), bf16),
-            ((side + few_rows, width), bf16),
-            ((side, width), bf16),
-            ((side, width), bf16),
             ((quarter + 16, length), bf16),
             ((quarter + 16, length), bf16),
             ((2, quarter + 16, length), bf16),
+            *[((a_part, width), bf16)] * first_a,
+            *[((b_part + few_rows, width), bf16)] * first_b,
         ],
         (
             me,
             *do_pieces,
-            Far(dest_far),
-            Far(dest_col),
+            Pin(dest_far),
+            Pin(dest_col),
             Far(w_output),
-            Far(attn),
-            Far(q),
-            Far(k),
-            Far(v),
-            Far(probs),
-            Far(n1),
+            Pin(attn),
+            Pin(q),
+            Pin(k),
+            Pin(v),
+            Pin(probs),
+            Pin(n1),
             Far(wq_t),
             Far(wk_t),
             Far(wv_t),
-            Far(x_full),
-            Far(small_far),
-            Far(few_parts),
+            Pin(x_full),
+            Pin(small_far),
+            Pin(few_parts),
             Far(bucket_row),
         ),
         "attend_back",
         us=6.0,
         scratch=[
-            pltpu.VMEM((owners, chunk, width), bf16),
-            pltpu.VMEM((owners, chunk, width), bf16),
+            pltpu.VMEM((owners, chunk_a, width), bf16),
+            pltpu.VMEM((owners, chunk_b, width), bf16),
             pltpu.VMEM((here, length), bf16),
             pltpu.VMEM((here, length), bf16),
             pltpu.VMEM((here, length), bf16),
@@ -780,10 +772,11 @@
         limit=32,
     )
 
-    a_mine, a_other, few = chain_sum(a_keep, a_send, order_a, few_rows)
-    b_mine, b_other, none = chain_sum(b_keep, b_send, order_b, 0)
-
-    *dn1_parts, none = scatter_sum(*dn1_parts)
+    a_blocks, b_blocks, few = two_chains(
+        others[3 : 3 + first_a], others[3 + first_a :], order_a, order_b, few_rows
+    )
+
+    *dn1_parts, none = scatter_sum(*others[:3])
 
     def tokens_body(
         me_ref, kept_ref, beside_ref, across_ref, dh_ref, tok_ref, r1_ref, small_ref, out_ref
@@ -807,7 +800,7 @@
     (grad_tokens,) = run(
         tokens_body,
         [((quarter, length), bf16)],
-        (me, *dn1_parts, Far(dh_own), Far(tok_t), Far(r1), Far(small_far)),
+        (me, *dn1_parts, Pin(dh_own), Far(tok_t), Pin(r1), Pin(small_far)),
         "tokens_back",
         us=0.5,
     )
@@ -824,7 +817,7 @@
     lo = run(
         out_rows_body,
         [((quarter, rows), bf16)] * ways,
-        (me, Far(h_rows), Far(aux), y_rows),
+        (me, Pin(h_rows), Pin(aux), y_rows),
         "layer_rows",
         us=0.5,
         scratch=[pltpu.VMEM((width, rows), bf16)],
@@ -840,48 +833,31 @@
         out_ref[...] = total.astype(bf16)
 
     (layer_out,) = run(
-        out_body, [((quarter, length), bf16)], (Far(dest_far), *lo), "layer_out", us=0.5
+        out_body, [((quarter, length), bf16)], (Pin(dest_far), *lo), "layer_out", us=0.5
     )
 
     few = few.astype(f32)
     few = few + swap(few, "tp", 1)
     few_other = swap(few, "tp", 2)
 
-    def unpack_body(
-        me_ref,
-        am_ref,
-        ao_ref,
-        bm_ref,
-        bo_ref,
-        few_ref,
-        other_ref,
-        gq_ref,
-        gk_ref,
-        gv_ref,
-        go_ref,
-        router_ref,
-        g1_ref,
-        g2_ref,
-        table_ref,
-        a_ref,
-        b_ref,
-    ):
+    def unpack_body(me_ref, few_ref, other_ref, *others):
+        a_ins, b_ins = others[:first_a], others[first_a : first_a + first_b]
+        *results, a_ref, b_ref = others[first_a + first_b :]
+        gq_ref, gk_ref, gv_ref, go_ref, router_ref, g1_ref, g2_ref, table_ref = results
         mine = me_ref[0] & (ways - 1)
         place = me_ref[0] >> shift
-        for order, ref, first, second in (
-            (order_a, a_ref, am_ref, ao_ref),
-            (order_b, b_ref, bm_ref, bo_ref),
+        for order, ref, ins, chunk, start in (
+            (order_a, a_ref, a_ins, chunk_a, 0),
+            (order_b, b_ref, b_ins, chunk_b, a_rows),
         ):
+            each = owners // len(ins)
             for at in range(owners):
-                src, line = (first, at) if at < owners // 2 else (second, at - owners // 2)
-                ref[rel_of(at, order) ^ place] = src[line * chunk : (line + 1) * chunk]
-        for c in range(owners):
-            low, high = c * chunk, (c + 1) * chunk
-            for ref, outs in ((a_ref, (gq_ref, gk_ref)), (b_ref, (gv_ref, go_ref))):
-                if high <= here:
-                    outs[0][low:high] = ref[c]
-                else:
-                    outs[1][low - here : high - here] = ref[c]
+                line = at % each
+                ref[rel_of(at, order) ^ place] = ins[at // each][line * chunk : (line + 1) * chunk]
+            for c in range(owners):
+                low = start + c * chunk
+                which, low = low // here, low % here
+                (gq_ref, gk_ref, gv_ref, go_ref)[which][low : low + chunk] = ref[c]
         total = few_ref[...] + other_ref[...]
         own = total[:, 0:quarter]
         for t in range(1, ways):
@@ -907,12 +883,12 @@
             ((1, quarter), bf16),
             ((heads, bins), bf16),
         ],
-        (me, a_mine, a_other, b_mine, b_other, few, few_other),
+        (me, few, few_other, *a_blocks, *b_blocks),
         "unpack",
         us=1.0,
         scratch=[
-            pltpu.VMEM((owners, chunk, width), bf16),
-            pltpu.VMEM((owners, chunk, width), bf16),
+            pltpu.VMEM((owners, chunk_a, width), bf16),
+            pltpu.VMEM((owners, chunk_b, width), bf16),
         ],
     )
     return (

time: 204 us -> 191 us (0.936)
  local copies, waits for them, and re-layouts: 36.5 us -> 26.3 us
  Pallas kernels: 35.2 us -> 25.9 us
  starting transfers between devices: 53.3 us -> 60.2 us
    unnamed x154 -> x114, local copies, waits for them, and re-layouts: 35.1 us -> 24.9 us
    pallas_call x12, Pallas kernels: 35.2 us -> 25.9 us  [run(): pl.pallas_call(wrapped, out_shape=[pltpu.VMEM(o[0], o[1]) if len(o) == 3...]
    ppermute x40 -> x44, waiting for transfers between devices: 63.4 us -> 55.4 us  [swap(): return lax.ppermute(value, axis, [(i, i ^ mask) for i in range(size)])]
    ppermute x40 -> x44, starting transfers between devices: 31.4 us -> 38.3 us  [swap(): return lax.ppermute(value, axis, [(i, i ^ mask) for i in range(size)])]
    all_to_all x4, waiting for transfers between devices: 9 us -> 15.1 us  [over_experts(): lax.all_to_all(blocks, 'exp', split_axis=0, concat_axis=0, tiled=True)]
  transfers between devices with their start and end apart: 44 -> 48, of which waited for: 22 -> 23; matrix products, arithmetic and copies ran while one was open for 2% -> 3% of each run, Pallas kernels for 10% -> 5%
where the time goes in v3:
time: 191 us; the launch traced here: 190 us
  waiting for transfers between devices  70.6 us (37%)
  starting transfers between devices  60.2 us (32%)
  local copies, waits for them, and re-layouts  26.3 us (14%)
  Pallas kernels  25.9 us (14%)
  other arithmetic  5.4 us (3%)
    ppermute x44, waiting for transfers between devices, swap(): return lax.ppermute(value, axis, [(i, i ^ mask) for i in range(size)])  55.4 us
    ppermute x44, starting transfers between devices, swap(): return lax.ppermute(value, axis, [(i, i ^ mask) for i in range(size)])  38.3 us
    pallas_call x12, Pallas kernels, run(): pl.pallas_call(wrapped, out_shape=[pltpu.VMEM(o[0], o[1]) if len(o) == 3...  25.9 us
    unnamed x114, local copies, waits for them, and re-layouts  24.9 us
    all_to_all x4, starting transfers between devices, over_experts(): lax.all_to_all(blocks, 'exp', split_axis=0, concat_axis=0, tiled=True)  21.8 us
    all_to_all x4, waiting for transfers between devices, over_experts(): lax.all_to_all(blocks, 'exp', split_axis=0, concat_axis=0, tiled=True)  15.1 us
  transfers between devices with their start and end apart: 48, of which 23 were waited for; matrix products, arithmetic and copies ran while one was open for 3% of the time, Pallas kernels for 5%

profile of v3, /device:TPU:0, one launch (start us, length us, event | category | flops | bytes accessed | tf_op | source)
XLA Modules:
  0.0 189.6 jit_solution(3710789383938043815)
XLA Ops:
  0.6 3.0 %collective-permute-start.1 = (bf16[192,384]{1,0:T(8,128)(2,1)}, bf16[192,384]{1,0:T(8,128)(2,1)S(1)}, u32[]{:S(2)}, u32[]{:S(2)}) collective-permute-start(bf16[192,384]{1,0:T(8,128)(2,1)} %bitcast.74), channel_id=1, source_target_pairs={{0,2},{1,3},{2,0},{3,1},{4,6},{5,7},{6,4},{7,5},{8,10},{9,11},{10,... | collective-permute-start | bytes 442376 | tf_op jit(solution)/shard_map/ppermute | solution.py:95
  5.0 2.4 %slots.1 = (s32[1,384]{1,0:T(1,128)S(1)}, s32[1,384]{1,0:T(1,128)S(1)}, s32[384,1]{1,0:T(8,128)S(1)}, bf16[4,144,192]{2,1,0:T(8,128)(2,1)S(1)}, bf16[128,768]{1,0:T(8,128)(2,1)}) custom-call(s32[1]{0:T(128)} %bitcast.refs_0_, s32[1,384]{1,0:T(1,128)} %bitcast.81, bf16[192,384]{1,0:T(8,128)(2,1)} %bitcast.79, bf16[8,192]{1,0:T(8,128)(2,1)} %bitcast.80, ...), custom_call_target="tpu_custom_call" | custom-call | flops 770000000 | bytes 575236 | tf_op jit(solution)/shard_map/slots/pallas_call | solution.py:76
  8.0 1.7 collective-permute-start.5
  10.0 2.3 %collective-permute-done.5.refs_8_.refs_9_ = bf16[144,192]{1,0:T(8,128)(2,1)S(1)} collective-permute-done((bf16[144,192]{1,0:T(8,128)(2,1)S(1)}, bf16[144,192]{1,0:T(8,128)(2,1)S(1)}, u32[]{:S(2)}, u32[]{:S(2)}) %collective-permute-start.5) | collective-permute-done | bytes 55328 | tf_op jit(solution)/shard_map/ppermute | solution.py:95
  12.3 1.9 %collective-permute-done.4.refs_7_.refs_8_ = bf16[144,192]{1,0:T(8,128)(2,1)S(1)} collective-permute-done((bf16[144,192]{1,0:T(8,128)(2,1)S(1)}, bf16[144,192]{1,0:T(8,128)(2,1)S(1)}, u32[]{:S(2)}, u32[]{:S(2)}) %collective-permute-start.4) | collective-permute-done | bytes 55328 | tf_op jit(solution)/shard_map/ppermute | solution.py:95
  14.3 3.5 %attend.1 = (bf16[768,384]{1,0:T(8,128)(2,1)S(1)}, bf16[16,768]{1,0:T(8,128)(2,1)S(1)}, bf16[16,768]{1,0:T(8,128)(2,1)S(1)}, f32[1,384]{1,0:T(1,128)S(1)}, bf16[...) custom-call(s32[1]{0:T(128)} %bitcast.refs_0_, ...), custom_call_target="tpu_custom_call" | custom-call | flops 4400000000 | bytes 5684932 | tf_op jit(solution)/shard_map/attend/pallas_call | solution.py:76
  25.6 5.8 %all-to-all-start = ((bf16[8,16,768]{2,1,0:T(8,128)(2,1)}), bf16[8,16,768]{2,1,0:T(8,128)(2,1)S(1)}, u32[]{:S(2)}, u32[]{:S(2)}) async-start(bf16[8,16,768]{2,1,0:T(8,128)(2,1)} %bitcast.14), calls=%async_computation | async-start | bytes 393216 | tf_op jit(solution)/shard_map/all_to_all | solution.py:314
  31.5 8.6 %all-to-all-done = bf16[8,16,768]{2,1,0:T(8,128)(2,1)S(1)} async-done(((bf16[8,16,768]{2,1,0:T(8,128)(2,1)}), bf16[8,16,768]{2,1,0:T(8,128)(2,1)S(1)}, u32[]{:S(2)}, u32[]{:S(2)}) %all-to-all-start) | async-done | bytes 196640 | tf_op jit(solution)/shard_map/all_to_all | solution.py:314
  40.1 1.5 collective-permute-start.7
  41.5 4.2 %collective-permute-done.7.refs_3_ = bf16[128,768]{1,0:T(8,128)(2,1)S(1)} collective-permute-done((bf16[128,768]{1,0:T(8,128)(2,1)S(1)}, bf16[128,768]{1,0:T(8,128)(2,1)S(1)}, u32[]{:S(2)}, u32[]{:S(2)}) %collective-permute-start.7) | collective-permute-done | bytes 196640 | tf_op jit(solution)/shard_map/ppermute | solution.py:95
  51.0 1.5 route.1
  54.0 4.2 %all-to-all-start.1 = ((bf16[8,16,896]{2,1,0:T(8,128)(2,1)}), bf16[8,16,896]{2,1,0:T(8,128)(2,1)S(1)}, u32[]{:S(2)}, u32[]{:S(2)}) async-start(bf16[8,16,896]{2,1,0:T(8,128)(2,1)} %bitcast.16), calls=%async_computation.1 | async-start | bytes 458752 | tf_op jit(solution)/shard_map/all_to_all | solution.py:314
  58.2 1.5 collective-permute-start.9
  59.6 4.2 %collective-permute-done.9.refs_7_ = bf16[128,768]{1,0:T(8,128)(2,1)S(1)} collective-permute-done((bf16[128,768]{1,0:T(8,128)(2,1)S(1)}, bf16[128,768]{1,0:T(8,128)(2,1)S(1)}, u32[]{:S(2)}, u32[]{:S(2)}) %collective-permute-start.9) | collective-permute-done | bytes 196640 | tf_op jit(solution)/shard_map/ppermute | solution.py:95
  66.2 1.5 collective-permute-start.12
  67.6 6.0 %collective-permute-done.12.refs_3_ = bf16[128,896]{1,0:T(8,128)(2,1)S(1)} collective-permute-done((bf16[128,896]{1,0:T(8,128)(2,1)S(1)}, bf16[128,896]{1,0:T(8,128)(2,1)S(1)}, u32[]{:S(2)}, u32[]{:S(2)}) %collective-permute-start.12) | collective-permute-done | bytes 229408 | tf_op jit(solution)/shard_map/ppermute | solution.py:95
  73.6 1.5 collective-permute-done.13.refs_4_
  77.0 3.0 %expert.1 = (bf16[512,768]{1,0:T(8,128)(2,1)S(1)}, bf16[512,768]{1,0:T(8,128)(2,1)S(1)}, bf16[512,768]{1,0:T(8,128)(2,1)S(1)}, bf16[512,768]{1,0:T(8,128)(2,1)S(...) custom-call(s32[1]{0:T(128)} %bitcast.refs_0_, ...), custom_call_target="tpu_custom_call" | custom-call | flops 4400000000 | bytes 8126468 | tf_op jit(solution)/shard_map/expert/pallas_call | solution.py:76
  80.2 1.7 collective-permute-done.14
  81.9 1.5 collective-permute-start.15
  84.4 5.3 %collective-permute-done.15 = bf16[128,896]{1,0:T(8,128)(2,1)S(1)} collective-permute-done((bf16[128,896]{1,0:T(8,128)(2,1)S(1)}, bf16[128,896]{1,0:T(8,128)(2,1)S(1)}, u32[]{:S(2)}, u32[]{:S(2)}) %collective-permute-start.15) | collective-permute-done | bytes 229408 | tf_op jit(solution)/shard_map/ppermute | solution.py:95
  90.4 6.0 %all-to-all-start.2 = ((bf16[8,16,896]{2,1,0:T(8,128)(2,1)}), bf16[8,16,896]{2,1,0:T(8,128)(2,1)S(1)}, u32[]{:S(2)}, u32[]{:S(2)}) async-start(bf16[8,16,896]{2,1,0:T(8,128)(2,1)} %bitcast.20), calls=%async_computation.2 | async-start | bytes 458752 | tf_op jit(solution)/shard_map/all_to_all | solution.py:314
  99.8 2.4 %expert_weights.1 = (bf16[1,768,768]{2,1,0:T(8,128)(2,1)}, bf16[1,768,768]{2,1,0:T(8,128)(2,1)}) custom-call(s32[1]{0:T(128)} %bitcast.refs_0_, bf16[512,768]{1,0:T(8,128)(2,1)S(1)} %copy-done.35, bf16[512,768]{1,0:T(8,128)(2,1)S(1)} %copy-done.37, bf16[512,768]{1,0:T(8,128)(2,1)S(1)} %copy-done.21, bf16[512,768]{1,0:T(8,128)(2,1)S(1)} %copy-done.39), custom_call_target="tpu_custom_call" | custom-call | flops 2750000128 | bytes 5505028 | tf_op jit(solution)/shard_map/expert_weights/pallas_call | solution.py:76
  102.2 1.6 fusion.3
  103.8 1.5 collective-permute-start.20
  106.8 5.1 %collective-permute-done.20 = bf16[128,768]{1,0:T(8,128)(2,1)S(1)} collective-permute-done((bf16[128,768]{1,0:T(8,128)(2,1)}, bf16[128,768]{1,0:T(8,128)(2,1)S(1)}, u32[]{:S(2)}, u32[]{:S(2)}) %collective-permute-start.20) | collective-permute-done | bytes 196640 | tf_op jit(solution)/shard_map/ppermute | solution.py:95
  111.9 1.6 fusion.5
  113.5 5.8 %all-to-all-start.3 = ((bf16[8,16,768]{2,1,0:T(8,128)(2,1)}), bf16[8,16,768]{2,1,0:T(8,128)(2,1)S(1)}, u32[]{:S(2)}, u32[]{:S(2)}) async-start(bf16[8,16,768]{2,1,0:T(8,128)(2,1)} %bitcast.24), calls=%async_computation.3 | async-start | bytes 393216 | tf_op jit(solution)/shard_map/all_to_all | solution.py:314
  120.8 6.3 %all-to-all-done.3 = bf16[8,16,768]{2,1,0:T(8,128)(2,1)S(1)} async-done(((bf16[8,16,768]{2,1,0:T(8,128)(2,1)}), bf16[8,16,768]{2,1,0:T(8,128)(2,1)S(1)}, u32[]{:S(2)}, u32[]{:S(2)}) %all-to-all-start.3) | async-done | bytes 196640 | tf_op jit(solution)/shard_map/all_to_all | solution.py:314
  130.9 7.1 %attend_back.1 = (bf16[192,384]{1,0:T(8,128)(2,1)S(1)}, bf16[208,384]{1,0:T(8,128)(2,1)S(1)}, bf16[208,384]{1,0:T(8,128)(2,1)S(1)}, bf16[2,208,384]{2,1,0:T(8,12...) custom-call(s32[1]{0:T(128)} %bitcast.refs_0_, ...), custom_call_target="tpu_custom_call" | custom-call | flops 6600000000 | bytes 6764548 | tf_op jit(solution)/shard_map/attend_back/pallas_call | solution.py:76
  138.6 1.5 collective-permute-start.22
  140.1 1.4 collective-permute-start.27
  142.5 1.9 %collective-permute-start.29 = (bf16[80,768]{1,0:T(8,128)(2,1)S(1)}, bf16[80,768]{1,0:T(8,128)(2,1)S(1)}, u32[]{:S(2)}, u32[]{:S(2)}) collective-permute-start(bf16[80,768]{1,0:T(8,128)(2,1)S(1)} %get-tuple-element.172), channel_id=1, source_target_pairs={{0,24},{4,28},{8,16},{12,20},{16,8},{20,12},{24,0},{28,4},{1,25},{... | collective-permute-start | bytes 368648 | tf_op jit(solution)/shard_map/ppermute | solution.py:95
  144.5 3.5 %collective-permute-done.23.refs_4_ = bf16[192,128]{1,0:T(8,128)(2,1)S(1)} collective-permute-done((bf16[192,128]{1,0:T(8,128)(2,1)S(1)}, bf16[192,128]{1,0:T(8,128)(2,1)S(1)}, u32[]{:S(2)}, u32[]{:S(2)}) %collective-permute-start.23) | collective-permute-done | bytes 49184 | tf_op jit(solution)/shard_map/ppermute | solution.py:95
  149.0 4.4 %collective-permute-done.28 = bf16[80,768]{1,0:T(8,128)(2,1)S(1)} collective-permute-done((bf16[80,768]{1,0:T(8,128)(2,1)S(1)}, bf16[80,768]{1,0:T(8,128)(2,1)S(1)}, u32[]{:S(2)}, u32[]{:S(2)}) %collective-permute-start.28) | collective-permute-done | bytes 122912 | tf_op jit(solution)/shard_map/ppermute | solution.py:95
  154.8 2.0 %collective-permute-start.32 = (bf16[64,768]{1,0:T(8,128)(2,1)S(1)}, bf16[64,768]{1,0:T(8,128)(2,1)S(1)}, u32[]{:S(2)}, u32[]{:S(2)}) collective-permute-start(bf16[64,768]{1,0:T(8,128)(2,1)S(1)} %get-tuple-element.200), channel_id=1, source_target_pairs={{0,24},{4,28},{8,16},{12,20},{16,8},{20,12},{24,0},{28,4},{1,25},{... | collective-permute-start | bytes 294920 | tf_op jit(solution)/shard_map/ppermute | solution.py:95
  156.7 2.0 %collective-permute-start.31 = (bf16[64,768]{1,0:T(8,128)(2,1)S(1)}, bf16[64,768]{1,0:T(8,128)(2,1)S(1)}, u32[]{:S(2)}, u32[]{:S(2)}) collective-permute-start(bf16[64,768]{1,0:T(8,128)(2,1)S(1)} %get-tuple-element.201), channel_id=1, source_target_pairs={{0,16},{4,20},{8,24},{12,28},{16,0},{20,4},{24,8},{28,12},{1,17},{... | collective-permute-start | bytes 294920 | tf_op jit(solution)/shard_map/ppermute | solution.py:95
  159.9 2.4 %collective-permute-done.32 = bf16[64,768]{1,0:T(8,128)(2,1)S(1)} collective-permute-done((bf16[64,768]{1,0:T(8,128)(2,1)S(1)}, bf16[64,768]{1,0:T(8,128)(2,1)S(1)}, u32[]{:S(2)}, u32[]{:S(2)}) %collective-permute-start.32) | collective-permute-done | bytes 98336 | tf_op jit(solution)/shard_map/ppermute | solution.py:95
  162.3 3.6 %collective-permute-done.31 = bf16[64,768]{1,0:T(8,128)(2,1)S(1)} collective-permute-done((bf16[64,768]{1,0:T(8,128)(2,1)S(1)}, bf16[64,768]{1,0:T(8,128)(2,1)S(1)}, u32[]{:S(2)}, u32[]{:S(2)}) %collective-permute-start.31) | collective-permute-done | bytes 98336 | tf_op jit(solution)/shard_map/ppermute | solution.py:95
  166.0 1.6 collective-permute-start.38
  167.6 2.9 %collective-permute-start.36 = (bf16[64,768]{1,0:T(8,128)(2,1)S(1)}, bf16[64,768]{1,0:T(8,128)(2,1)S(1)}, u32[]{:S(2)}, u32[]{:S(2)}) collective-permute-start(bf16[64,768]{1,0:T(8,128)(2,1)S(1)} %add_convert_fusion.2), channel_id=1, source_target_pairs={{0,8},{4,12},{8,0},{12,4},{16,24},{20,28},{24,16},{28,20},{1,9},{5... | collective-permute-start | bytes 294920 | tf_op jit(solution)/shard_map/ppermute | solution.py:95
  170.5 1.4 collective-permute-start.39
  171.9 2.7 %collective-permute-done.39 = bf16[32,768]{1,0:T(8,128)(2,1)S(1)} collective-permute-done((bf16[32,768]{1,0:T(8,128)(2,1)S(1)}, bf16[32,768]{1,0:T(8,128)(2,1)S(1)}, u32[]{:S(2)}, u32[]{:S(2)}) %collective-permute-start.39) | collective-permute-done | bytes 49184 | tf_op jit(solution)/shard_map/ppermute | solution.py:95
  177.0 1.6 collective-permute-start.43
  178.7 2.8 %collective-permute-start.41 = (bf16[64,768]{1,0:T(8,128)(2,1)S(1)}, bf16[64,768]{1,0:T(8,128)(2,1)S(1)}, u32[]{:S(2)}, u32[]{:S(2)}) collective-permute-start(bf16[64,768]{1,0:T(8,128)(2,1)S(1)} %pad_maximum_fusion.1.refs_5_), channel_id=1, source_target_pairs={{0,8},{4,12},{8,0},{12,4},{16,24},{20,28},{24,16},{28,20},{1,9},{5... | collective-permute-start | bytes 294920 | tf_op jit(solution)/shard_map/ppermute | solution.py:95
  182.1 1.8 tokens_back.1
  184.7 2.5 %collective-permute-done.42.refs_7_ = bf16[64,768]{1,0:T(8,128)(2,1)S(1)} collective-permute-done((bf16[64,768]{1,0:T(8,128)(2,1)S(1)}, bf16[64,768]{1,0:T(8,128)(2,1)S(1)}, u32[]{:S(2)}, u32[]{:S(2)}) %collective-permute-start.42) | collective-permute-done | bytes 98336 | tf_op jit(solution)/shard_map/ppermute | solution.py:95
  187.2 1.3 unpack.1
  (200 shorter events, 42.7 us)
Async XLA Ops:
  0.6 7.1 %collective-permute-start.1 = (bf16[192,384]{1,0:T(8,128)(2,1)}, bf16[192,384]{1,0:T(8,128)(2,1)S(1)}, u32[]{:S(2)}, u32[]{:S(2)}) collective-permute-start(bf16[192,384]{1,0:T(8,128)(2,1)} %bitcast.74), channel_id=1, source_target_pairs={{0,2},{1,3},{2,0},{3,1},{4,6},{5,7},{6,4},{7,5},{8,10},{9,11},{10,... | collective-permute-start | bytes 442376 | tf_op jit(solution)/shard_map/ppermute | solution.py:95
  3.6 10.6 %collective-permute-start = (bf16[192,384]{1,0:T(8,128)(2,1)}, bf16[192,384]{1,0:T(8,128)(2,1)S(1)}, u32[]{:S(2)}, u32[]{:S(2)}) collective-permute-start(bf16[192,384]{1,0:T(8,128)(2,1)} %bitcast.75), channel_id=1, source_target_pairs={{0,1},{1,0},{2,3},{3,2},{4,5},{5,4},{6,7},{7,6},{8,9},{9,8},{10,11... | collective-permute-start | bytes 442376 | tf_op jit(solution)/shard_map/ppermute | solution.py:95
  7.7 6.5 %collective-permute-start.2 = (bf16[192,384]{1,0:T(8,128)(2,1)S(1)}, bf16[192,384]{1,0:T(8,128)(2,1)S(1)}, u32[]{:S(2)}, u32[]{:S(2)}) collective-permute-start(bf16[192,384]{1,0:T(8,128)(2,1)S(1)} %collective-permute-done.1.refs_3_), channel_id=1, source_target_pairs={{0,1},{1,0},{2,3},{3,2},{4,5},{5,4},{6,7},{7,6},{8,9},{9,8},{10,11... | collective-permute-start | bytes 442376 | tf_op jit(solution)/shard_map/ppermute | solution.py:95
  8.0 4.3 %collective-permute-start.5 = (bf16[144,192]{1,0:T(8,128)(2,1)S(1)}, bf16[144,192]{1,0:T(8,128)(2,1)S(1)}, u32[]{:S(2)}, u32[]{:S(2)}) collective-permute-start(bf16[144,192]{1,0:T(8,128)(2,1)S(1)} %get-tuple-element.203), channel_id=1, source_target_pairs={{0,3},{1,2},{2,1},{3,0},{4,7},{5,6},{6,5},{7,4},{8,11},{9,10},{10,... | collective-permute-start | bytes 165896 | tf_op jit(solution)/shard_map/ppermute | solution.py:95
  9.6 4.6 %collective-permute-start.4 = (bf16[144,192]{1,0:T(8,128)(2,1)S(1)}, bf16[144,192]{1,0:T(8,128)(2,1)S(1)}, u32[]{:S(2)}, u32[]{:S(2)}) collective-permute-start(bf16[144,192]{1,0:T(8,128)(2,1)S(1)} %get-tuple-element.204), channel_id=1, source_target_pairs={{0,2},{1,3},{2,0},{3,1},{4,6},{5,7},{6,4},{7,5},{8,10},{9,11},{10,... | collective-permute-start | bytes 165896 | tf_op jit(solution)/shard_map/ppermute | solution.py:95
  9.9 4.3 %collective-permute-start.3 = (bf16[144,192]{1,0:T(8,128)(2,1)S(1)}, bf16[144,192]{1,0:T(8,128)(2,1)S(1)}, u32[]{:S(2)}, u32[]{:S(2)}) collective-permute-start(bf16[144,192]{1,0:T(8,128)(2,1)S(1)} %get-tuple-element.205), channel_id=1, source_target_pairs={{0,1},{1,0},{2,3},{3,2},{4,5},{5,4},{6,7},{7,6},{8,9},{9,8},{10,11... | collective-permute-start | bytes 165896 | tf_op jit(solution)/shard_map/ppermute | solution.py:95
  25.6 5.8 %collective-permute-start.6 = (bf16[2,128,768]{2,1,0:T(8,128)(2,1)S(1)}, bf16[2,128,768]{2,1,0:T(8,128)(2,1)S(1)}, u32[]{:S(2)}, u32[]{:S(2)}) collective-permute-start(bf16[2,128,768]{2,1,0:T(8,128)(2,1)S(1)} %get-tuple-element.110), channel_id=1, source_target_pairs={{0,1},{1,0},{2,3},{3,2},{4,5},{5,4},{6,7},{7,6},{8,9},{9,8},{10,11... | collective-permute-start | bytes 1179656 | tf_op jit(solution)/shard_map/ppermute | solution.py:95
  25.6 14.5 %all-to-all-start = ((bf16[8,16,768]{2,1,0:T(8,128)(2,1)}), bf16[8,16,768]{2,1,0:T(8,128)(2,1)S(1)}, u32[]{:S(2)}, u32[]{:S(2)}) async-start(bf16[8,16,768]{2,1,0:T(8,128)(2,1)} %bitcast.14), calls=%async_computation | async-start | bytes 393216 | tf_op jit(solution)/shard_map/all_to_all | solution.py:314
  40.1 5.7 %collective-permute-start.7 = (bf16[128,768]{1,0:T(8,128)(2,1)S(1)}, bf16[128,768]{1,0:T(8,128)(2,1)S(1)}, u32[]{:S(2)}, u32[]{:S(2)}) collective-permute-start(bf16[128,768]{1,0:T(8,128)(2,1)S(1)} %fusion.6), channel_id=1, source_target_pairs={{0,2},{1,3},{2,0},{3,1},{4,6},{5,7},{6,4},{7,5},{8,10},{9,11},{10,... | collective-permute-start | bytes 589832 | tf_op jit(solution)/shard_map/ppermute | solution.py:95
  54.0 12.2 %all-to-all-start.1 = ((bf16[8,16,896]{2,1,0:T(8,128)(2,1)}), bf16[8,16,896]{2,1,0:T(8,128)(2,1)S(1)}, u32[]{:S(2)}, u32[]{:S(2)}) async-start(bf16[8,16,896]{2,1,0:T(8,128)(2,1)} %bitcast.16), calls=%async_computation.1 | async-start | bytes 458752 | tf_op jit(solution)/shard_map/all_to_all | solution.py:314
  58.2 5.7 %collective-permute-start.9 = (bf16[128,768]{1,0:T(8,128)(2,1)S(1)}, bf16[128,768]{1,0:T(8,128)(2,1)S(1)}, u32[]{:S(2)}, u32[]{:S(2)}) collective-permute-start(bf16[128,768]{1,0:T(8,128)(2,1)S(1)} %bitcast.64), channel_id=1, source_target_pairs={{0,2},{1,3},{2,0},{3,1},{4,6},{5,7},{6,4},{7,5},{8,10},{9,11},{10,... | collective-permute-start | bytes 589832 | tf_op jit(solution)/shard_map/ppermute | solution.py:95
  59.6 4.2 %collective-permute-start.8 = (bf16[128,768]{1,0:T(8,128)(2,1)S(1)}, bf16[128,768]{1,0:T(8,128)(2,1)S(1)}, u32[]{:S(2)}, u32[]{:S(2)}) collective-permute-start(bf16[128,768]{1,0:T(8,128)(2,1)S(1)} %bitcast.65), channel_id=1, source_target_pairs={{0,1},{1,0},{2,3},{3,2},{4,5},{5,4},{6,7},{7,6},{8,9},{9,8},{10,11... | collective-permute-start | bytes 589832 | tf_op jit(solution)/shard_map/ppermute | solution.py:95
  63.8 1.4 collective-permute-start.10
  66.2 7.4 %collective-permute-start.12 = (bf16[128,896]{1,0:T(8,128)(2,1)S(1)}, bf16[128,896]{1,0:T(8,128)(2,1)S(1)}, u32[]{:S(2)}, u32[]{:S(2)}) collective-permute-start(bf16[128,896]{1,0:T(8,128)(2,1)S(1)} %bitcast.60), channel_id=1, source_target_pairs={{0,2},{1,3},{2,0},{3,1},{4,6},{5,7},{6,4},{7,5},{8,10},{9,11},{10,... | collective-permute-start | bytes 688136 | tf_op jit(solution)/shard_map/ppermute | solution.py:95
  67.6 6.0 %collective-permute-start.11 = (bf16[128,896]{1,0:T(8,128)(2,1)S(1)}, bf16[128,896]{1,0:T(8,128)(2,1)S(1)}, u32[]{:S(2)}, u32[]{:S(2)}) collective-permute-start(bf16[128,896]{1,0:T(8,128)(2,1)S(1)} %bitcast.61), channel_id=1, source_target_pairs={{0,1},{1,0},{2,3},{3,2},{4,5},{5,4},{6,7},{7,6},{8,9},{9,8},{10,11... | collective-permute-start | bytes 688136 | tf_op jit(solution)/shard_map/ppermute | solution.py:95
  73.6 1.5 collective-permute-start.13
  80.0 1.9 collective-permute-start.14
  81.9 7.7 %collective-permute-start.15 = (bf16[128,896]{1,0:T(8,128)(2,1)S(1)}, bf16[128,896]{1,0:T(8,128)(2,1)S(1)}, u32[]{:S(2)}, u32[]{:S(2)}) collective-permute-start(bf16[128,896]{1,0:T(8,128)(2,1)S(1)} %fusion), channel_id=1, source_target_pairs={{0,2},{1,3},{2,0},{3,1},{4,6},{5,7},{6,4},{7,5},{8,10},{9,11},{10,... | collective-permute-start | bytes 688136 | tf_op jit(solution)/shard_map/ppermute | solution.py:95
  84.3 17.9 %collective-permute-start.19 = (bf16[2,128,768]{2,1,0:T(8,128)(2,1)S(1)}, bf16[2,128,768]{2,1,0:T(8,128)(2,1)}, u32[]{:S(2)}, u32[]{:S(2)}) collective-permute-start(bf16[2,128,768]{2,1,0:T(8,128)(2,1)S(1)} %get-tuple-element.142), channel_id=1, source_target_pairs={{0,1},{1,0},{2,3},{3,2},{4,5},{5,4},{6,7},{7,6},{8,9},{9,8},{10,11... | collective-permute-start | bytes 1179656 | tf_op jit(solution)/shard_map/ppermute | solution.py:95
  90.4 15.0 %all-to-all-start.2 = ((bf16[8,16,896]{2,1,0:T(8,128)(2,1)}), bf16[8,16,896]{2,1,0:T(8,128)(2,1)S(1)}, u32[]{:S(2)}, u32[]{:S(2)}) async-start(bf16[8,16,896]{2,1,0:T(8,128)(2,1)} %bitcast.20), calls=%async_computation.2 | async-start | bytes 458752 | tf_op jit(solution)/shard_map/all_to_all | solution.py:314
  103.8 8.0 %collective-permute-start.20 = (bf16[128,768]{1,0:T(8,128)(2,1)}, bf16[128,768]{1,0:T(8,128)(2,1)S(1)}, u32[]{:S(2)}, u32[]{:S(2)}) collective-permute-start(bf16[128,768]{1,0:T(8,128)(2,1)} %fusion.3), channel_id=1, source_target_pairs={{0,2},{1,3},{2,0},{3,1},{4,6},{5,7},{6,4},{7,5},{8,10},{9,11},{10,... | collective-permute-start | bytes 589832 | tf_op jit(solution)/shard_map/ppermute | solution.py:95
  106.2 13.2 %collective-permute-start.17 = (bf16[128,768]{1,0:T(8,128)(2,1)S(1)}, bf16[128,768]{1,0:T(8,128)(2,1)S(1)}, u32[]{:S(2)}, u32[]{:S(2)}) collective-permute-start(bf16[128,768]{1,0:T(8,128)(2,1)S(1)} %get-tuple-element.150.refs_1_), channel_id=1, source_target_pairs={{0,2},{1,3},{2,0},{3,1},{4,6},{5,7},{6,4},{7,5},{8,10},{9,11},{10,... | collective-permute-start | bytes 589832 | tf_op jit(solution)/shard_map/ppermute | solution.py:95
  113.5 13.6 %all-to-all-start.3 = ((bf16[8,16,768]{2,1,0:T(8,128)(2,1)}), bf16[8,16,768]{2,1,0:T(8,128)(2,1)S(1)}, u32[]{:S(2)}, u32[]{:S(2)}) async-start(bf16[8,16,768]{2,1,0:T(8,128)(2,1)} %bitcast.24), calls=%async_computation.3 | async-start | bytes 393216 | tf_op jit(solution)/shard_map/all_to_all | solution.py:314
  119.3 1.4 collective-permute-start.16
  119.3 7.8 %collective-permute-start.18 = (bf16[128,768]{1,0:T(8,128)(2,1)S(1)}, bf16[128,768]{1,0:T(8,128)(2,1)S(1)}, u32[]{:S(2)}, u32[]{:S(2)}) collective-permute-start(bf16[128,768]{1,0:T(8,128)(2,1)S(1)} %collective-permute-done.17.refs_3_), channel_id=1, source_target_pairs={{0,1},{1,0},{2,3},{3,2},{4,5},{5,4},{6,7},{7,6},{8,9},{9,8},{10,11... | collective-permute-start | bytes 589832 | tf_op jit(solution)/shard_map/ppermute | solution.py:95
  138.1 15.4 %collective-permute-start.26 = (bf16[256,768]{1,0:T(8,128)(2,1)S(1)}, bf16[256,768]{1,0:T(8,128)(2,1)S(1)}, u32[]{:S(2)}, u32[]{:S(2)}) collective-permute-start(bf16[256,768]{1,0:T(8,128)(2,1)S(1)} %get-tuple-element.169), channel_id=1, source_target_pairs={{0,4},{4,0},{8,12},{12,8},{16,20},{20,16},{24,28},{28,24},{1,5},{5... | collective-permute-start | bytes 1179656 | tf_op jit(solution)/shard_map/ppermute | solution.py:95
  138.5 4.1 %collective-permute-start.21 = (bf16[192,128]{1,0:T(8,128)(2,1)S(1)}, bf16[192,128]{1,0:T(8,128)(2,1)S(1)}, u32[]{:S(2)}, u32[]{:S(2)}) collective-permute-start(bf16[192,128]{1,0:T(8,128)(2,1)S(1)} %get-tuple-element.147), channel_id=1, source_target_pairs={{0,1},{1,0},{2,3},{3,2},{4,5},{5,4},{6,7},{7,6},{8,9},{9,8},{10,11... | collective-permute-start | bytes 147464 | tf_op jit(solution)/shard_map/ppermute | solution.py:95
  138.6 5.9 %collective-permute-start.22 = (bf16[192,128]{1,0:T(8,128)(2,1)S(1)}, bf16[192,128]{1,0:T(8,128)(2,1)S(1)}, u32[]{:S(2)}, u32[]{:S(2)}) collective-permute-start(bf16[192,128]{1,0:T(8,128)(2,1)S(1)} %get-tuple-element.148), channel_id=1, source_target_pairs={{0,2},{1,3},{2,0},{3,1},{4,6},{5,7},{6,4},{7,5},{8,10},{9,11},{10,... | collective-permute-start | bytes 147464 | tf_op jit(solution)/shard_map/ppermute | solution.py:95
  140.1 8.9 %collective-permute-start.27 = (bf16[80,768]{1,0:T(8,128)(2,1)S(1)}, bf16[80,768]{1,0:T(8,128)(2,1)S(1)}, u32[]{:S(2)}, u32[]{:S(2)}) collective-permute-start(bf16[80,768]{1,0:T(8,128)(2,1)S(1)} %get-tuple-element.170), channel_id=1, source_target_pairs={{0,8},{4,12},{8,0},{12,4},{16,24},{20,28},{24,16},{28,20},{1,9},{5... | collective-permute-start | bytes 368648 | tf_op jit(solution)/shard_map/ppermute | solution.py:95
  141.5 12.0 %collective-permute-start.28 = (bf16[80,768]{1,0:T(8,128)(2,1)S(1)}, bf16[80,768]{1,0:T(8,128)(2,1)S(1)}, u32[]{:S(2)}, u32[]{:S(2)}) collective-permute-start(bf16[80,768]{1,0:T(8,128)(2,1)S(1)} %get-tuple-element.171), channel_id=1, source_target_pairs={{0,16},{4,20},{8,24},{12,28},{16,0},{20,4},{24,8},{28,12},{1,17},{... | collective-permute-start | bytes 368648 | tf_op jit(solution)/shard_map/ppermute | solution.py:95
  142.5 10.9 %collective-permute-start.29 = (bf16[80,768]{1,0:T(8,128)(2,1)S(1)}, bf16[80,768]{1,0:T(8,128)(2,1)S(1)}, u32[]{:S(2)}, u32[]{:S(2)}) collective-permute-start(bf16[80,768]{1,0:T(8,128)(2,1)S(1)} %get-tuple-element.172), channel_id=1, source_target_pairs={{0,24},{4,28},{8,16},{12,20},{16,8},{20,12},{24,0},{28,4},{1,25},{... | collective-permute-start | bytes 368648 | tf_op jit(solution)/shard_map/ppermute | solution.py:95
  144.5 3.5 %collective-permute-start.23 = (bf16[192,128]{1,0:T(8,128)(2,1)S(1)}, bf16[192,128]{1,0:T(8,128)(2,1)S(1)}, u32[]{:S(2)}, u32[]{:S(2)}) collective-permute-start(bf16[192,128]{1,0:T(8,128)(2,1)S(1)} %get-tuple-element.149), channel_id=1, source_target_pairs={{0,3},{1,2},{2,1},{3,0},{4,7},{5,6},{6,5},{7,4},{8,11},{9,10},{10,... | collective-permute-start | bytes 147464 | tf_op jit(solution)/shard_map/ppermute | solution.py:95
  148.0 11.2 %collective-permute-start.24 = (bf16[2,208,384]{2,1,0:T(8,128)(2,1)S(1)}, bf16[2,208,384]{2,1,0:T(8,128)(2,1)S(1)}, u32[]{:S(2)}, u32[]{:S(2)}) collective-permute-start(bf16[2,208,384]{2,1,0:T(8,128)(2,1)S(1)} %get-tuple-element.164), channel_id=1, source_target_pairs={{0,1},{1,0},{2,3},{3,2},{4,5},{5,4},{6,7},{7,6},{8,9},{9,8},{10,11... | collective-permute-start | bytes 958472 | tf_op jit(solution)/shard_map/ppermute | solution.py:95
  153.5 6.3 %collective-permute-start.33 = (bf16[48,768]{1,0:T(8,128)(2,1)S(1)}, bf16[48,768]{1,0:T(8,128)(2,1)S(1)}, u32[]{:S(2)}, u32[]{:S(2)}) collective-permute-start(bf16[48,768]{1,0:T(8,128)(2,1)S(1)} %concatenate.16), channel_id=1, source_target_pairs={{0,4},{4,0},{8,12},{12,8},{16,20},{20,16},{24,28},{28,24},{1,5},{5... | collective-permute-start | bytes 221192 | tf_op jit(solution)/shard_map/ppermute | solution.py:95
  154.8 7.5 %collective-permute-start.32 = (bf16[64,768]{1,0:T(8,128)(2,1)S(1)}, bf16[64,768]{1,0:T(8,128)(2,1)S(1)}, u32[]{:S(2)}, u32[]{:S(2)}) collective-permute-start(bf16[64,768]{1,0:T(8,128)(2,1)S(1)} %get-tuple-element.200), channel_id=1, source_target_pairs={{0,24},{4,28},{8,16},{12,20},{16,8},{20,12},{24,0},{28,4},{1,25},{... | collective-permute-start | bytes 294920 | tf_op jit(solution)/shard_map/ppermute | solution.py:95
  156.7 9.2 %collective-permute-start.31 = (bf16[64,768]{1,0:T(8,128)(2,1)S(1)}, bf16[64,768]{1,0:T(8,128)(2,1)S(1)}, u32[]{:S(2)}, u32[]{:S(2)}) collective-permute-start(bf16[64,768]{1,0:T(8,128)(2,1)S(1)} %get-tuple-element.201), channel_id=1, source_target_pairs={{0,16},{4,20},{8,24},{12,28},{16,0},{20,4},{24,8},{28,12},{1,17},{... | collective-permute-start | bytes 294920 | tf_op jit(solution)/shard_map/ppermute | solution.py:95
  158.7 7.2 %collective-permute-start.30 = (bf16[64,768]{1,0:T(8,128)(2,1)S(1)}, bf16[64,768]{1,0:T(8,128)(2,1)S(1)}, u32[]{:S(2)}, u32[]{:S(2)}) collective-permute-start(bf16[64,768]{1,0:T(8,128)(2,1)S(1)} %get-tuple-element.202), channel_id=1, source_target_pairs={{0,8},{4,12},{8,0},{12,4},{16,24},{20,28},{24,16},{28,20},{1,9},{5... | collective-permute-start | bytes 294920 | tf_op jit(solution)/shard_map/ppermute | solution.py:95
  159.2 22.3 %collective-permute-start.25 = (bf16[208,384]{1,0:T(8,128)(2,1)S(1)}, bf16[208,384]{1,0:T(8,128)(2,1)S(1)}, u32[]{:S(2)}, u32[]{:S(2)}) collective-permute-start(bf16[208,384]{1,0:T(8,128)(2,1)S(1)} %fusion.7), channel_id=1, source_target_pairs={{0,2},{1,3},{2,0},{3,1},{4,6},{5,7},{6,4},{7,5},{8,10},{9,11},{10,... | collective-permute-start | bytes 479240 | tf_op jit(solution)/shard_map/ppermute | solution.py:95
  166.0 8.7 %collective-permute-start.38 = (bf16[64,768]{1,0:T(8,128)(2,1)S(1)}, bf16[64,768]{1,0:T(8,128)(2,1)S(1)}, u32[]{:S(2)}, u32[]{:S(2)}) collective-permute-start(bf16[64,768]{1,0:T(8,128)(2,1)S(1)} %add_convert_fusion.2), channel_id=1, source_target_pairs={{0,24},{4,28},{8,16},{12,20},{16,8},{20,12},{24,0},{28,4},{1,25},{... | collective-permute-start | bytes 294920 | tf_op jit(solution)/shard_map/ppermute | solution.py:95
  167.5 8.3 %collective-permute-start.37 = (bf16[64,768]{1,0:T(8,128)(2,1)S(1)}, bf16[64,768]{1,0:T(8,128)(2,1)S(1)}, u32[]{:S(2)}, u32[]{:S(2)}) collective-permute-start(bf16[64,768]{1,0:T(8,128)(2,1)S(1)} %add_convert_fusion.2), channel_id=1, source_target_pairs={{0,16},{4,20},{8,24},{12,28},{16,0},{20,4},{24,8},{28,12},{1,17},{... | collective-permute-start | bytes 294920 | tf_op jit(solution)/shard_map/ppermute | solution.py:95
  167.6 8.3 %collective-permute-start.36 = (bf16[64,768]{1,0:T(8,128)(2,1)S(1)}, bf16[64,768]{1,0:T(8,128)(2,1)S(1)}, u32[]{:S(2)}, u32[]{:S(2)}) collective-permute-start(bf16[64,768]{1,0:T(8,128)(2,1)S(1)} %add_convert_fusion.2), channel_id=1, source_target_pairs={{0,8},{4,12},{8,0},{12,4},{16,24},{20,28},{24,16},{28,20},{1,9},{5... | collective-permute-start | bytes 294920 | tf_op jit(solution)/shard_map/ppermute | solution.py:95
  170.5 4.2 %collective-permute-start.39 = (bf16[32,768]{1,0:T(8,128)(2,1)S(1)}, bf16[32,768]{1,0:T(8,128)(2,1)S(1)}, u32[]{:S(2)}, u32[]{:S(2)}) collective-permute-start(bf16[32,768]{1,0:T(8,128)(2,1)S(1)} %slice.87), channel_id=1, source_target_pairs={{0,4},{4,0},{8,12},{12,8},{16,20},{20,16},{24,28},{28,24},{1,5},{5... | collective-permute-start | bytes 147464 | tf_op jit(solution)/shard_map/ppermute | solution.py:95
  174.6 4.0 %collective-permute-start.34 = (f32[16,768]{1,0:T(8,128)S(1)}, f32[16,768]{1,0:T(8,128)S(1)}, u32[]{:S(2)}, u32[]{:S(2)}) collective-permute-start(f32[16,768]{1,0:T(8,128)S(1)} %slice_convert_fusion), channel_id=1, source_target_pairs={{0,1},{1,0},{2,3},{3,2},{4,5},{5,4},{6,7},{7,6},{8,9},{9,8},{10,11... | collective-permute-start | bytes 147464 | tf_op jit(solution)/shard_map/ppermute | solution.py:95
  175.9 11.3 %collective-permute-start.40 = (bf16[256,768]{1,0:T(8,128)(2,1)S(1)}, bf16[256,768]{1,0:T(8,128)(2,1)S(1)}, u32[]{:S(2)}, u32[]{:S(2)}) collective-permute-start(bf16[256,768]{1,0:T(8,128)(2,1)S(1)} %pad_maximum_fusion.refs_3_), channel_id=1, source_target_pairs={{0,4},{4,0},{8,12},{12,8},{16,20},{20,16},{24,28},{28,24},{1,5},{5... | collective-permute-start | bytes 1179656 | tf_op jit(solution)/shard_map/ppermute | solution.py:95
  177.0 7.6 %collective-permute-start.43 = (bf16[64,768]{1,0:T(8,128)(2,1)S(1)}, bf16[64,768]{1,0:T(8,128)(2,1)S(1)}, u32[]{:S(2)}, u32[]{:S(2)}) collective-permute-start(bf16[64,768]{1,0:T(8,128)(2,1)S(1)} %pad_maximum_fusion.1.refs_5_), channel_id=1, source_target_pairs={{0,24},{4,28},{8,16},{12,20},{16,8},{20,12},{24,0},{28,4},{1,25},{... | collective-permute-start | bytes 294920 | tf_op jit(solution)/shard_map/ppermute | solution.py:95
  178.7 8.6 %collective-permute-start.42 = (bf16[64,768]{1,0:T(8,128)(2,1)S(1)}, bf16[64,768]{1,0:T(8,128)(2,1)S(1)}, u32[]{:S(2)}, u32[]{:S(2)}) collective-permute-start(bf16[64,768]{1,0:T(8,128)(2,1)S(1)} %pad_maximum_fusion.1.refs_5_), channel_id=1, source_target_pairs={{0,16},{4,20},{8,24},{12,28},{16,0},{20,4},{24,8},{28,12},{1,17},{... | collective-permute-start | bytes 294920 | tf_op jit(solution)/shard_map/ppermute | solution.py:95
  178.7 8.6 %collective-permute-start.41 = (bf16[64,768]{1,0:T(8,128)(2,1)S(1)}, bf16[64,768]{1,0:T(8,128)(2,1)S(1)}, u32[]{:S(2)}, u32[]{:S(2)}) collective-permute-start(bf16[64,768]{1,0:T(8,128)(2,1)S(1)} %pad_maximum_fusion.1.refs_5_), channel_id=1, source_target_pairs={{0,8},{4,12},{8,0},{12,4},{16,24},{20,28},{24,16},{28,20},{1,9},{5... | collective-permute-start | bytes 294920 | tf_op jit(solution)/shard_map/ppermute | solution.py:95
  181.5 5.7 %collective-permute-start.35 = (f32[16,768]{1,0:T(8,128)S(1)}, f32[16,768]{1,0:T(8,128)S(1)}, u32[]{:S(2)}, u32[]{:S(2)}) collective-permute-start(f32[16,768]{1,0:T(8,128)S(1)} %fusion.8.refs_1_), channel_id=1, source_target_pairs={{0,2},{1,3},{2,0},{3,1},{4,6},{5,7},{6,4},{7,5},{8,10},{9,11},{10,... | collective-permute-start | bytes 147464 | tf_op jit(solution)/shard_map/ppermute | solution.py:95
  (57 other events, 302.0 us)

commit v4 on v3

--- a/solution.py
+++ b/solution.py
@@ -23,11 +23,6 @@
         self.value = pltpu.with_memory_space_constraint(value, pltpu.HBM)
 
 
-class Pin:
-    def __init__(self, value):
-        self.value = pltpu.with_memory_space_constraint(value, pltpu.VMEM)
-
-
 class Loaded:
     def __init__(self, copy, held):
         self.copy, self.held = copy, held
@@ -42,45 +37,73 @@
         return self.held[index]
 
 
+class Stored:
+    def __init__(self, copy, held):
+        self.copy, self.held, self.started = copy, held, False
+
+    def __setitem__(self, index, value):
+        self.held[index] = value
+
+    def __getitem__(self, index):
+        return self.held[index]
+
+    def send(self):
+        if not self.started:
+            self.started = True
+            self.copy.start()
+
+
 def run(body, outs, args, name, us=1.0, scratch=(), limit=16):
-    far = [isinstance(a, Far) for a in args]
-    args = [a.value if isinstance(a, (Far, Pin)) else a for a in args]
-    bufs = [pltpu.VMEM(a.shape, a.dtype) for a, f in zip(args, far) if f]
+    far_in = [isinstance(a, Far) for a in args]
+    args = [a.value if isinstance(a, Far) else a for a in args]
+    far_out = [len(o) == 3 for o in outs]
+    bufs = [pltpu.VMEM(a.shape, a.dtype) for a, far in zip(args, far_in) if far]
+    bufs += [pltpu.VMEM(o[0], o[1]) for o, far in zip(outs, far_out) if far]
     n_in, n_out, n_own = len(args), len(outs), len(scratch)
     hbm = pl.BlockSpec(memory_space=pltpu.HBM)
     specs = [
-        SMEM if a.shape == (1,) and a.dtype == jnp.int32 else hbm if f else VMEM
-        for a, f in zip(args, far)
+        SMEM if a.shape == (1,) and a.dtype == jnp.int32 else hbm if far else VMEM
+        for a, far in zip(args, far_in)
     ]
     moved = sum(a.size * a.dtype.itemsize for a in args)
     moved += sum(math.prod(o[0]) * jnp.dtype(o[1]).itemsize for o in outs)
 
     def wrapped(*refs):
+        ins, results = refs[:n_in], refs[n_in : n_in + n_out]
         own = refs[n_in + n_out : n_in + n_out + n_own]
         held = refs[n_in + n_out + n_own :]
         given, at = [], 0
-        for ref, f in zip(refs[:n_in], far):
-            if f:
+        for ref, far in zip((*ins, *results), (*far_in, *far_out)):
+            if not far:
+                given.append(ref)
+                continue
+            if len(given) < n_in:
                 copy = pltpu.make_async_copy(ref, held[at], held[-1].at[at])
                 copy.start()
                 given.append(Loaded(copy, held[at]))
-                at += 1
             else:
-                given.append(ref)
-        body(*given, *refs[n_in : n_in + n_out], *own)
+                copy = pltpu.make_async_copy(held[at], ref, held[-1].at[at])
+                given.append(Stored(copy, held[at]))
+            at += 1
+        body(*given, *own)
         for g in given:
-            if isinstance(g, Loaded):
+            if isinstance(g, Stored):
+                g.send()
+        for g in given:
+            if isinstance(g, Stored):
+                g.copy.wait()
+            elif isinstance(g, Loaded):
                 g.wait()
 
     sems = [pltpu.SemaphoreType.DMA((len(bufs),))] if bufs else []
     return pl.pallas_call(
         wrapped,
         out_shape=[
-            pltpu.VMEM(o[0], o[1]) if len(o) == 3 else jax.ShapeDtypeStruct(o[0], o[1])
+            pltpu.HBM(o[0], o[1]) if len(o) == 3 else jax.ShapeDtypeStruct(o[0], o[1])
             for o in outs
         ],
         in_specs=specs,
-        out_specs=[VMEM] * n_out,
+        out_specs=[hbm if far else VMEM for far in far_out],
         scratch_shapes=[*scratch, *bufs, *sems],
         compiler_params=pltpu.CompilerParams(vmem_limit_bytes=limit * 2**20),
         cost_estimate=pl.CostEstimate(
@@ -90,6 +113,31 @@
     )(*args)
 
 
+def fetch(token, values, name):
+    values = [pltpu.with_memory_space_constraint(v, pltpu.HBM) for v in values]
+    count = len(values)
+
+    def body(token_ref, *refs):
+        ins, outs, sems = refs[:count], refs[count : 2 * count], refs[-1]
+        copies = [
+            pltpu.make_async_copy(i, o, sems.at[n]) for n, (i, o) in enumerate(zip(ins, outs))
+        ]
+        for c in copies:
+            c.start()
+        for c in copies:
+            c.wait()
+
+    return pl.pallas_call(
+        body,
+        out_shape=[jax.ShapeDtypeStruct(v.shape, v.dtype) for v in values],
+        in_specs=[SMEM] + [pl.BlockSpec(memory_space=pltpu.HBM)] * count,
+        out_specs=[VMEM] * count,
+        scratch_shapes=[pltpu.SemaphoreType.DMA((count,))],
+        compiler_params=pltpu.CompilerParams(vmem_limit_bytes=16 * 2**20),
+        name=name,
+    )(token, *values)
+
+
 def swap(value, axis, mask):
     size = lax.axis_size(axis)
     return lax.ppermute(value, axis, [(i, i ^ mask) for i in range(size)])
@@ -176,11 +224,11 @@
     return total.astype(bf16)
 
 
-def two_chains(a_blocks, b_blocks, order_a, order_b, tail):
+def two_chains(a_blocks, b_blocks, order_a, order_b, tail, beside):
     for at, (digit_a, digit_b) in enumerate(zip(order_a, order_b)):
         b_came = trade(b_blocks, digit_b)
         a_came = trade(a_blocks, digit_a)
-        got = lax.optimization_barrier((*a_came, *b_came))
+        got = beside((*a_came, *b_came), b_blocks[0])
         a = sum_blocks(a_blocks[0], got[: len(a_came)])
         b = sum_blocks(b_blocks[0], got[len(a_came) :])
         few = b[b.shape[0] - tail :]
@@ -197,11 +245,11 @@
     for at, (digit_a, digit_b) in enumerate(zip(order_a[::-1], order_b[::-1])):
         a_came = trade([a] * digit_a[1], digit_a)
         b_came = trade([b] * digit_b[1], digit_b)
-        got = lax.optimization_barrier((*a_came, *b_came))
+        got = beside((*a_came, *b_came), few)
         a_blocks, b_blocks = [a, *got[: len(a_came)]], [b, *got[len(a_came) :]]
         if at + 1 < len(order_a):
             a, b = jnp.concatenate(a_blocks, axis=0), jnp.concatenate(b_blocks, axis=0)
-    return a_blocks, b_blocks, few
+    return a_blocks, b_blocks
 
 
 def local(
@@ -247,12 +295,10 @@
     tok_t = tokens.T
     wq_t, wk_t, wv_t = w_query.T, w_key.T, w_value.T
 
-    tok_pieces = gather_pieces(tok_t)
-
     def slot_body(
-        me_ref, route_ref, cot_ref, router_ref, g1_ref, g2_ref, *outs
+        me_ref, route_ref, cot_ref, *outs
     ):
-        drow_ref, drow_far, dcol_ref, cots_ref, d_ref = outs
+        drow_ref, cots_ref = outs
         mine = me_ref[0] & (ways - 1)
         row = route_ref[...]
         above = iota((length, length), 0)
@@ -267,54 +313,58 @@
             return (chunk ^ mine) * rows + expert * per + slot - chunk * per
 
         slot_row = jnp.sum(jnp.where(same & (above < along), 1, 0), axis=0, keepdims=True)
-        slot_col = jnp.sum(jnp.where(same & (along < above), 1, 0), axis=1, keepdims=True)
         dest_row = dest(slot_row, row)
         drow_ref[...] = dest_row
-        drow_far[...] = dest_row
-        dcol_ref[...] = dest(slot_col, col)
         cot = cot_ref[...]
-        line = iota((extra - experts, quarter), 0)
-        gains = jnp.where(
-            line == 0,
-            g1_ref[...].astype(f32),
-            jnp.where(line == 1, g2_ref[...].astype(f32), 0.0),
-        )
-        few = jnp.concatenate([router_ref[...].astype(f32), gains], axis=0).astype(bf16)
         for rel in range(ways):
             hot = (iota((rows, length), 0) + rel * rows == dest_row).astype(bf16)
             piece = mm_nt(hot, cot).astype(bf16)
-            cots_ref[rel, 0:rows] = piece
-            cots_ref[rel, rows : rows + extra] = few
-            d_ref[:, rel * quarter : (rel + 1) * quarter] = piece
-
-    dest_row, dest_far, dest_col, cots, d_send = run(
+            cots_ref[rel] = piece
+
+    dest_row, cots = run(
         slot_body,
         [
             ((1, length), jnp.int32),
-            ((1, length), jnp.int32, True),
-            ((length, 1), jnp.int32, True),
-            ((ways, rows + extra, quarter), bf16),
-            ((rows, width), bf16),
+            ((ways, rows, quarter), bf16),
         ],
         (
             me,
             Far(routes.T),
             Far(cotangent.T),
-            Far(w_router.T),
-            gain_attn[None],
-            gain_ffn[None],
         ),
         "slots",
         us=0.7,
     )
-    cot_pieces = [cots[0]] + [swap(cots[rel], "tp", rel) for rel in range(1, ways)]
+    def small_body(router_ref, g1_ref, g2_ref, small_ref):
+        line = iota((extra - experts, quarter), 0)
+        gains = jnp.where(
+            line == 0,
+            g1_ref[...].astype(f32)[None],
+            jnp.where(line == 1, g2_ref[...].astype(f32)[None], 0.0),
+        )
+        small_ref[...] = jnp.concatenate([router_ref[...].astype(f32), gains], 0).astype(bf16)
+
+    (small_own,) = run(
+        small_body,
+        [((extra, quarter), bf16)],
+        (Far(w_router.T), Far(gain_attn), Far(gain_ffn)),
+        "small",
+        us=0.2,
+    )
+    small_pieces = [small_own] + [swap(small_own, "tp", rel) for rel in range(1, ways)]
+    tok_across = swap(tok_t, "tp", 2)
+    tok_across, *small_pieces = lax.optimization_barrier((tok_across, *small_pieces))
+    tok_pieces = (tok_t, swap(tok_t, "tp", 1), tok_across, swap(tok_across, "tp", 1))
 
     def over_experts(value):
         blocks = value.reshape(experts, per, value.shape[1])
         moved = lax.all_to_all(blocks, "exp", split_axis=0, concat_axis=0, tiled=True)
         return moved.reshape(rows, value.shape[1])
 
-    bucket_row = jnp.pad(buckets, (0, span - buckets.shape[0]), constant_values=-1)[None]
+    def bucket_hot(ref, held, dtype):
+        held[...] = jnp.full((1, span), -1, jnp.int32)
+        held[:, 0 : buckets.shape[0]] = ref[...][None]
+        return (iota((bins, span), 0) == held[...]).astype(dtype)
 
     def spread_row(few, line, count):
         pick = (iota((few.shape[0], count), 0) == line).astype(bf16)
@@ -338,42 +388,54 @@
         bucket_ref,
         seg_ref,
         dest_ref,
-        x_ref,
         small_ref,
         small_far,
+        dest_far,
         r1_ref,
         n1_ref,
         q_ref,
         k_ref,
         v_ref,
-        p_ref,
+        p0_ref,
+        p1_ref,
+        p2_ref,
         attn_ref,
         kept_ref,
         passed_ref,
         sent_ref,
         xrow_ref,
+        x_ref,
+        bucket_held,
     ):
+        p_refs = (p0_ref, p1_ref, p2_ref)
         mine = me_ref[0] & (ways - 1)
         for rel, piece in enumerate((t0, t1, t2, t3)):
             at = pl.multiple_of((mine ^ rel) * quarter, quarter)
             x_ref[pl.ds(at, quarter), :] = piece[...]
-        pieces = [c[rows : rows + extra] for c in (c0, c1, c2, c3)]
+        pieces = [c[...] for c in (c0, c1, c2, c3)]
         small = jnp.concatenate([absolute(pieces, mine, t) for t in range(ways)], axis=1)
         small_ref[...] = small
         small_far[...] = small
+        small_far.send()
+        dest_far[...] = dest_ref[...]
+        dest_far.send()
         x_low = x_ref[...]
         x = x_low.astype(f32)
         r1 = lax.rsqrt(jnp.mean(x * x, axis=0, keepdims=True) + EPSILON)
         r1_ref[...] = r1
+        r1_ref.send()
         n1 = (x * r1 * spread_row(small, experts, length)).astype(bf16)
         n1_ref[...] = n1
+        n1_ref.send()
         q = mm(wq_ref[...], n1).astype(bf16)
         k = mm(wk_ref[...], n1).astype(bf16)
         v = mm(wv_ref[...], n1).astype(bf16)
         q_ref[...] = q
         k_ref[...] = k
         v_ref[...] = v
-        hot = (iota((bins, span), 0) == bucket_ref[...]).astype(bf16)
+        for ref in (q_ref, k_ref, v_ref):
+            ref.send()
+        hot = bucket_hot(bucket_ref, bucket_held, bf16)
         offsets = mm(table_ref[...], hot)
         above = iota((length, length), 0)
         along = iota((length, length), 1)
@@ -387,9 +449,11 @@
             s = jnp.where(same, mm_tn(k[part], q[part]) + bias, NEG_FILL)
             e = jnp.exp(s - jnp.max(s, axis=0, keepdims=True))
             p = (e / jnp.sum(e, axis=0, keepdims=True)).astype(bf16)
-            p_ref[h] = p
+            p_refs[h][...] = p
+            p_refs[h].send()
             attn_ref[part] = mm(v[part], p).astype(bf16)
         attn = attn_ref[...]
+        attn_ref.send()
         dest = dest_ref[...]
         wo = wo_ref[...]
         for rel, out in enumerate((kept_ref, sent_ref.at[0], passed_ref, sent_ref.at[1])):
@@ -398,18 +462,18 @@
             if rel == 0:
                 xrow_ref[...] = mm_nt(hot, x_low).astype(bf16)
 
-    x_full, small, small_far, r1, n1, q, k, v, probs, attn, *o_parts, x_rows = run(
+    small, small_far, dest_far, r1, n1, q, k, v, p0, p1, p2, attn, *o_parts, x_rows = run(
         attend_body,
         [
-            ((width, length), bf16, True),
             ((extra, width), bf16),
             ((extra, width), bf16, True),
+            ((1, length), jnp.int32, True),
             ((1, length), f32, True),
             ((width, length), bf16, True),
             ((here, length), bf16, True),
             ((here, length), bf16, True),
             ((here, length), bf16, True),
-            ((heads, length, length), bf16, True),
+            *[((length, length), bf16, True)] * heads,
             ((here, length), bf16, True),
             ((rows, width), bf16),
             ((rows, width), bf16),
@@ -419,47 +483,36 @@
         (
             me,
             *tok_pieces,
-            *cot_pieces,
+            *small_pieces,
             wq_t,
             wk_t,
             wv_t,
             w_output,
             bias_table.T,
-            bucket_row,
+            buckets,
             segments,
             dest_row,
         ),
         "attend",
-        us=4.0,
+        us=0.01,
+        scratch=[pltpu.VMEM((width, length), bf16), pltpu.VMEM((1, span), jnp.int32)],
         limit=24,
     )
     o_kept, o_passed, o_sent = o_parts
     o_beside = swap(o_sent, "tp", 1)
-
+    o_half = o_passed + o_beside[1]
+    o_across = swap(o_half, "tp", 2)
+
+    def join_body(me_ref, cots_ref, out_ref):
+        for rel in range(ways):
+            out_ref[:, rel * quarter : (rel + 1) * quarter] = cots_ref[rel]
+
+    (d_send,) = run(join_body, [((rows, width), bf16)], (after(me, o_half), cots), "join", us=0.3)
     d_arrived = over_experts(d_send)
-    o_half, d_arrived = lax.optimization_barrier((o_passed + o_beside[1], d_arrived))
-    o_across = swap(o_half, "tp", 2)
-
-    def route_body(
-        me_ref,
-        kept_ref,
-        beside_ref,
-        across_ref,
-        xrow_ref,
-        small_ref,
-        c0,
-        c1,
-        c2,
-        c3,
-        h_ref,
-        aux_ref,
-        dout_ref,
-        send_ref,
-    ):
-        mine = me_ref[0] & (ways - 1)
+
+    def routed(kept_ref, beside_ref, across_ref, xrow_ref, small_ref):
         o = kept_ref[...].astype(f32) + beside_ref[0].astype(f32) + across_ref[...].astype(f32)
         h = xrow_ref[...].astype(f32) + o
-        h_ref[...] = h
         r2 = lax.rsqrt(jnp.mean(h * h, axis=-1, keepdims=True) + EPSILON)
         gain = small_ref[experts + 1 : experts + 2].astype(f32)
         n2 = h * r2 * gain
@@ -469,30 +522,55 @@
         owner = iota((rows, experts), 0) - iota((rows, experts), 1) * per
         own = (owner >= 0) & (owner < per)
         g = jnp.sum(jnp.where(own, p, 0.0), axis=-1, keepdims=True)
-        pieces = [c[0:rows] for c in (c0, c1, c2, c3)]
+        return h, r2, n2, p, g
+
+    def route_body(kept_ref, beside_ref, across_ref, xrow_ref, small_ref, send_ref):
+        h, r2, n2, p, g = routed(kept_ref, beside_ref, across_ref, xrow_ref, small_ref)
+        send_ref[:, 0:width] = n2.astype(bf16)
+        send_ref[:, width : width + LANES] = two_lanes(g, LANES)
+
+    route_args = (o_kept, o_beside, o_across, x_rows, small)
+    (send,) = run(
+        route_body, [((rows, width + LANES), bf16)], route_args, "route", us=4
+    )
+
+    def state_body(
+        me_ref, kept_ref, beside_ref, across_ref, xrow_ref, small_ref, c0, c1, c2, c3, *outs
+    ):
+        h_ref, aux_ref, dout_ref = outs
+        mine = me_ref[0] & (ways - 1)
+        pieces = [c[...] for c in (c0, c1, c2, c3)]
         dout_ref[...] = jnp.concatenate([absolute(pieces, mine, t) for t in range(ways)], axis=1)
+        dout_ref.send()
+        h, r2, n2, p, g = routed(kept_ref, beside_ref, across_ref, xrow_ref, small_ref)
+        h_ref[...] = h
+        h_ref.send()
         aux_ref[...] = jnp.zeros((rows, LANES), f32)
         aux_ref[:, 0:experts] = p
         aux_ref[:, LANES - 2 : LANES - 1] = r2
         aux_ref[:, LANES - 1 : LANES] = g
-        send_ref[:, 0:width] = n2.astype(bf16)
-        send_ref[:, width : width + LANES] = two_lanes(g, LANES)
-
-    h_rows, aux, dout_rows, send = run(
-        route_body,
+
+    later = after(cots, send)
+    cot_pieces = [later[0]] + [swap(later[rel], "tp", rel) for rel in range(1, ways)]
+    h_rows, aux, dout_rows = run(
+        state_body,
         [
             ((rows, width), f32, True),
             ((rows, LANES), f32, True),
             ((rows, width), bf16, True),
-            ((rows, width + LANES), bf16),
         ],
-        (me, o_kept, o_beside, o_across, x_rows, small, *cot_pieces),
-        "route",
-        us=0.8,
-    )
-    d_pieces = gather_pieces(after(d_arrived, send))
-    arrived, *d_pieces = lax.optimization_barrier((over_experts(send), *d_pieces))
-    arrived = gather_pieces(arrived)
+        (after(me, send), *route_args, *cot_pieces),
+        "state",
+        us=0.01,
+    )
+    send, d_arrived = lax.optimization_barrier((send, d_arrived))
+    d_pieces = gather_pieces(d_arrived)
+    arrived, h_rows, aux, dout_rows, *d_pieces = lax.optimization_barrier(
+        (over_experts(send), h_rows, aux, dout_rows, *d_pieces)
+    )
+    weights = fetch(after(me, arrived), [w_in, w_out], "expert_arguments")
+    across, *weights = lax.optimization_barrier((swap(arrived, "tp", 2), *weights))
+    arrived = (arrived, swap(arrived, "tp", 1), across, swap(across, "tp", 1))
 
     def expert_body(me_ref, a0, a1, a2, a3, d0, d1, d2, d3, win_ref, wout_ref, *outs):
         u_ref, dy_ref, act_ref, dz_ref, kept_ref, passed_ref, sent_ref = outs
@@ -508,6 +586,8 @@
                 pieces.append(douts[src][:, at : at + quarter])
             dout = jnp.concatenate([absolute(pieces, mine, t) for t in range(ways)], axis=1)
             dy_ref[part] = (g * dout.astype(f32)).astype(bf16)
+        u_ref.send()
+        dy_ref.send()
         u = u_ref[...]
         dy = dy_ref[...]
         z = mm(u, win_ref[0])
@@ -515,11 +595,13 @@
         t = jnp.tanh(c * (z + 0.044715 * z * z * z))
         act = (0.5 * z * (1.0 + t)).astype(bf16)
         act_ref[...] = act
+        act_ref.send()
         slope = 0.5 * (1.0 + t) + 0.5 * z * (1.0 - t * t) * (c * (1.0 + 3 * 0.044715 * z * z))
         dact = mm_nt(dy, wout_ref[0])
         dot = jnp.sum(dact * act.astype(f32), axis=-1, keepdims=True)
         dz = (dact * slope).astype(bf16)
         dz_ref[...] = dz
+        dz_ref.send()
         du = mm_nt(dz, win_ref[0]).astype(bf16)
         tail = two_lanes(dot, LANES)
         for rel, out in enumerate((kept_ref, sent_ref.at[0], passed_ref, sent_ref.at[1])):
@@ -537,7 +619,7 @@
             ((rows, width + LANES), bf16),
             ((2, rows, width + LANES), bf16),
         ],
-        (me, *arrived, *d_pieces, w_in, w_out),
+        (me, *arrived, *d_pieces, *weights),
         "expert",
         us=4.0,
         limit=24,
@@ -554,7 +636,7 @@
     y_parts = run(
         value_body,
         [((rows, width), bf16), ((rows, width), bf16), ((2, rows, width), bf16)],
-        (after(me, du_half), Pin(act), w_out),
+        (after(me, du_half), Far(act), w_out),
         "value",
         us=0.8,
     )
@@ -563,21 +645,14 @@
     y_across = swap(after(y_passed + y_beside[1], du_sum), "tp", 2)
     y_sum = y_kept + y_beside[0] + y_across
 
-    def weights_body(me_ref, u_ref, dy_ref, act_ref, dz_ref, gin_ref, gout_ref):
-        gin_ref[0] = mm_tn(u_ref[...], dz_ref[...]).astype(bf16)
-        gout_ref[0] = mm_tn(act_ref[...], dy_ref[...]).astype(bf16)
-
-    grad_in, grad_out = run(
-        weights_body,
-        [((1, width, hidden_here), bf16), ((1, hidden_here, width), bf16)],
-        (after(me, du_sum), Pin(u_all), Pin(dy_all), Pin(act), Pin(dz)),
-        "expert_weights",
-        us=2.5,
-    )
     y_rows = over_experts(y_sum)
-    du_rows, grad_in, grad_out = lax.optimization_barrier((du_rows, grad_in, grad_out))
-
-    def back_body(du_ref, h_ref, aux_ref, dout_ref, small_ref, do_ref, parts_ref):
+    state = fetch(after(me, du_sum), [h_rows, aux, dout_rows, small_far, dest_far], "state_again")
+    du_rows, _, *state = lax.optimization_barrier((du_rows, y_sum, *state))
+
+    def back_body(
+        du_ref, h_ref, aux_ref, dout_ref, small_ref, dest_ref, do_ref, parts_ref, drow_ref
+    ):
+        drow_ref[...] = dest_ref[...]
         du = du_ref[:, 0:width].astype(f32)
         gg = du_ref[:, width : width + 1].astype(f32)
         gg = gg + du_ref[:, width + 1 : width + 2].astype(f32)
@@ -603,15 +678,19 @@
         )
         parts_ref[experts : experts + 1] = jnp.sum(dn2 * hr, axis=0, keepdims=True)
 
-    do_rows, few_parts = run(
+    do_rows, few_parts, dest_near = run(
         back_body,
-        [((rows, width), bf16), ((few_rows, width), f32, True)],
-        (du_rows, Pin(h_rows), Pin(aux), Pin(dout_rows), Pin(small_far)),
+        [((rows, width), bf16), ((few_rows, width), f32), ((1, length), jnp.int32)],
+        (du_rows, *state),
         "residual_back",
         us=2.0,
     )
-    do_pieces = gather_pieces(do_rows)
-    *do_pieces, y_rows = lax.optimization_barrier((*do_pieces, y_rows))
+    do_across = swap(do_rows, "tp", 2)
+    do_beside = swap(do_rows, "tp", 1)
+    wanted = [w_output, attn, q, k, v, p0, p1, p2, n1, wq_t, wk_t, wv_t, small_far]
+    fetched = fetch(after(me, do_rows), wanted, "attend_again")
+    do_across, *fetched = lax.optimization_barrier((do_across, *fetched))
+    do_pieces = (do_rows, do_beside, do_across, swap(do_across, "tp", 1))
 
     a_rows = 4 * here * 2 // 3
     chunk_a = a_rows // owners
@@ -625,18 +704,18 @@
         d2,
         d3,
         drow_ref,
-        dcol_ref,
         wo_ref,
         attn_ref,
         q_ref,
         k_ref,
         v_ref,
-        p_ref,
+        p0_ref,
+        p1_ref,
+        p2_ref,
         n1_ref,
         wq_ref,
         wk_ref,
         wv_ref,
-        x_ref,
         small_ref,
         few_ref,
         bucket_ref,
@@ -647,25 +726,28 @@
         *others,
     ):
         a_outs, b_outs = others[:first_a], others[first_a : first_a + first_b]
-        a_ref, b_ref, dq_ref, dk_ref, dv_ref, all_ref = others[first_a + first_b :]
+        a_ref, b_ref, dq_ref, dk_ref, dv_ref, all_ref, bucket_held = others[first_a + first_b :]
         mine = me_ref[0] & (ways - 1)
         place = me_ref[0] >> shift
         stack = jnp.concatenate([d[...] for d in (d0, d1, d2, d3)], axis=0)
-        hot_t = (iota((length, ways * rows), 1) == dcol_ref[...]).astype(bf16)
+        drow = drow_ref[...]
+        eye = iota((length, length), 0) == iota((length, length), 1)
+        dcol = jnp.sum(jnp.where(eye, drow, 0), axis=1, keepdims=True)
+        hot_t = (iota((length, ways * rows), 1) == dcol).astype(bf16)
         do = mm(hot_t, stack).astype(bf16)
         own = stack[:, 0:quarter]
         for t in range(1, ways):
             own = jnp.where(mine == t, stack[:, t * quarter : (t + 1) * quarter], own)
-        hot = (iota((ways * rows, length), 0) == drow_ref[...]).astype(bf16)
+        hot = (iota((ways * rows, length), 0) == drow).astype(bf16)
         own_ref[...] = mm_tn(own, hot).astype(bf16)
         wo = wo_ref[...]
         da = mm_nt(wo, do).astype(bf16)
-        hot = (iota((bins, span), 0) == bucket_ref[...]).astype(f32)
+        hot = bucket_hot(bucket_ref, bucket_held, f32)
         flip = (iota((length, length), 0) + iota((length, length), 1) == length - 1).astype(bf16)
         tables = []
         for h in range(heads):
             part = slice(h * HD, (h + 1) * HD)
-            p_low = p_ref[h]
+            p_low = (p0_ref, p1_ref, p2_ref)[h][...]
             p = p_low.astype(f32)
             dp = mm_tn(v_ref[part], da[part])
             dv_ref[part] = mm_nt(da[part], p_low).astype(bf16)
@@ -719,8 +801,7 @@
         dn1 = dn1 + mm_tn(wk_ref[...], dk_ref[...])
         dn1 = dn1 + mm_tn(wv_ref[...], dv_ref[...])
         all_ref[...] = dn1.astype(bf16)
-        gain = spread_row(small_ref[...], experts, length)
-        dot = jnp.sum(dn1 * gain * x_ref[...].astype(f32), axis=0, keepdims=True)
+        dot = jnp.sum(dn1 * n1.astype(f32), axis=0, keepdims=True)
         high, low = split_low(dot)
         line = iota((16, length), 0)
         tail = jnp.where(line == 0, high, jnp.where(line == 1, low, 0.0)).astype(bf16)
@@ -732,7 +813,7 @@
     dh_own, *others = run(
         attend_back_body,
         [
-            ((quarter, length), bf16, True),
+            ((quarter, length), bf16),
             ((quarter + 16, length), bf16),
             ((quarter + 16, length), bf16),
             ((2, quarter + 16, length), bf16),
@@ -742,25 +823,13 @@
         (
             me,
             *do_pieces,
-            Pin(dest_far),
-            Pin(dest_col),
-            Far(w_output),
-            Pin(attn),
-            Pin(q),
-            Pin(k),
-            Pin(v),
-            Pin(probs),
-            Pin(n1),
-            Far(wq_t),
-            Far(wk_t),
-            Far(wv_t),
-            Pin(x_full),
-            Pin(small_far),
-            Pin(few_parts),
-            Far(bucket_row),
+            dest_near,
+            *fetched,
+            few_parts,
+            buckets,
         ),
         "attend_back",
-        us=6.0,
+        us=0.01,
         scratch=[
             pltpu.VMEM((owners, chunk_a, width), bf16),
             pltpu.VMEM((owners, chunk_b, width), bf16),
@@ -768,15 +837,14 @@
             pltpu.VMEM((here, length), bf16),
             pltpu.VMEM((here, length), bf16),
             pltpu.VMEM((width, length), bf16),
+            pltpu.VMEM((1, span), jnp.int32),
         ],
         limit=32,
     )
 
-    a_blocks, b_blocks, few = two_chains(
-        others[3 : 3 + first_a], others[3 + first_a :], order_a, order_b, few_rows
-    )
-
-    *dn1_parts, none = scatter_sum(*others[:3])
+    y_rows, *others = lax.optimization_barrier((y_rows, *others))
+    dn1_kept, dn1_passed, dn1_sent = others[:3]
+    held = {}
 
     def tokens_body(
         me_ref, kept_ref, beside_ref, across_ref, dh_ref, tok_ref, r1_ref, small_ref, out_ref
@@ -794,16 +862,8 @@
         gain = spread_row(own, experts, length)
         x = tok_ref[...].astype(f32)
         out_ref[...] = (
-            dh_ref[...].astype(f32) + one * gain * dn1 - x * (one * one * one / width) * dot
+            dh_ref[...].astype(f32) + one * gain * dn1 - x * (one * one / width) * dot
         ).astype(bf16)
-
-    (grad_tokens,) = run(
-        tokens_body,
-        [((quarter, length), bf16)],
-        (me, *dn1_parts, Pin(dh_own), Far(tok_t), Pin(r1), Pin(small_far)),
-        "tokens_back",
-        us=0.5,
-    )
 
     def out_rows_body(me_ref, h_ref, aux_ref, y_ref, o0, o1, o2, o3, all_ref):
         mine = me_ref[0] & (ways - 1)
@@ -814,16 +874,6 @@
             at = pl.multiple_of((mine ^ rel) * quarter, quarter)
             piece[...] = all_ref[pl.ds(at, quarter), :]
 
-    lo = run(
-        out_rows_body,
-        [((quarter, rows), bf16)] * ways,
-        (me, Pin(h_rows), Pin(aux), y_rows),
-        "layer_rows",
-        us=0.5,
-        scratch=[pltpu.VMEM((width, rows), bf16)],
-    )
-    lo = [lo[0]] + [swap(lo[rel], "tp", rel) for rel in range(1, ways)]
-
     def out_body(dest_ref, l0, l1, l2, l3, out_ref):
         dest = dest_ref[...]
         total = jnp.zeros((quarter, length), f32)
@@ -832,13 +882,77 @@
             total = total + mm(piece[...], hot)
         out_ref[...] = total.astype(bf16)
 
-    (layer_out,) = run(
-        out_body, [((quarter, length), bf16)], (Pin(dest_far), *lo), "layer_out", us=0.5
-    )
-
-    few = few.astype(f32)
-    few = few + swap(few, "tp", 1)
-    few_other = swap(few, "tp", 2)
+    def weights_body(me_ref, u_ref, dy_ref, act_ref, dz_ref, gin_ref, gout_ref):
+        gin_ref[0] = mm_tn(u_ref[...], dz_ref[...]).astype(bf16)
+        gout_ref[0] = mm_tn(act_ref[...], dy_ref[...]).astype(bf16)
+
+    def beside(came, block):
+        phase = held.setdefault("phase", 0)
+        held["phase"] += 1
+        last = 2 * len(order_a) - 1
+        extras = {}
+        if phase == 0:
+            extras["dn1_beside"] = swap(dn1_sent, "tp", 1)
+            extras["grad_in"], extras["grad_out"] = run(
+                weights_body,
+                [((1, width, hidden_here), bf16), ((1, hidden_here, width), bf16)],
+                (after(me, dn1_sent), Far(u_all), Far(dy_all), Far(act), Far(dz)),
+                "expert_weights",
+                us=12,
+            )
+        if phase == 1:
+            half = dn1_passed + held["dn1_beside"][1]
+            extras["dn1_across"] = swap(half, "tp", 2)
+            lo = run(
+                out_rows_body,
+                [((quarter, rows), bf16)] * ways,
+                (me, Far(h_rows), Far(aux), y_rows),
+                "layer_rows",
+                us=12,
+                scratch=[pltpu.VMEM((width, rows), bf16)],
+            )
+            for rel in range(ways):
+                extras["lo%d" % rel] = lo[rel]
+        if phase == last - 1:
+            few = block.astype(f32)
+            extras["few"] = few + swap(few, "tp", 1)
+            for rel in range(1, ways):
+                extras["lo%d" % rel] = swap(held["lo%d" % rel], "tp", rel)
+            (extras["grad_tokens"],) = run(
+                tokens_body,
+                [((quarter, length), bf16)],
+                (
+                    me,
+                    dn1_kept,
+                    held["dn1_beside"],
+                    held["dn1_across"],
+                    dh_own,
+                    Far(tok_t),
+                    Far(r1),
+                    Far(small_far),
+                ),
+                "tokens_back",
+                us=12,
+            )
+        if phase == last:
+            extras["few_other"] = swap(held["few"], "tp", 2)
+            (extras["layer_out"],) = run(
+                out_body,
+                [((quarter, length), bf16)],
+                (Far(dest_far), *[held["lo%d" % rel] for rel in range(ways)]),
+                "layer_out",
+                us=12,
+            )
+        names = list(extras)
+        got = lax.optimization_barrier((*came, *[extras[n] for n in names]))
+        held.update(zip(names, got[len(came) :]))
+        return got[: len(came)]
+
+    a_blocks, b_blocks = two_chains(
+        others[3 : 3 + first_a], others[3 + first_a :], order_a, order_b, few_rows, beside
+    )
+    layer_out, grad_tokens = held["layer_out"], held["grad_tokens"]
+    grad_in, grad_out = held["grad_in"], held["grad_out"]
 
     def unpack_body(me_ref, few_ref, other_ref, *others):
         a_ins, b_ins = others[:first_a], others[first_a : first_a + first_b]
@@ -863,8 +977,8 @@
         for t in range(1, ways):
             own = jnp.where(mine == t, total[:, t * quarter : (t + 1) * quarter], own)
         router_ref[...] = own[0:experts].astype(bf16)
-        g2_ref[...] = own[experts : experts + 1].astype(bf16)
-        g1_ref[...] = own[experts + 1 : experts + 2].astype(bf16)
+        g2_ref[...] = own[experts].astype(bf16)
+        g1_ref[...] = own[experts + 1].astype(bf16)
         lines = total[experts + 2 : experts + 2 + heads]
         table = lines[:, 0:bins]
         for t in range(1, ways):
@@ -879,11 +993,11 @@
             ((here, width), bf16),
             ((here, width), bf16),
             ((experts, quarter), bf16),
-            ((1, quarter), bf16),
-            ((1, quarter), bf16),
+            ((quarter,), bf16),
+            ((quarter,), bf16),
             ((heads, bins), bf16),
         ],
-        (me, few, few_other, *a_blocks, *b_blocks),
+        (me, held["few"], held["few_other"], *a_blocks, *b_blocks),
         "unpack",
         us=1.0,
         scratch=[
@@ -902,8 +1016,8 @@
         g_router.T,
         grad_in,
         grad_out,
-        g_one[0],
-        g_two[0],
+        g_one,
+        g_two,
     )
 
 

time: 191 us -> 157 us (0.82)
  local copies, waits for them, and re-layouts: 26.3 us -> 0.11 us
  waiting for transfers between devices: 70.6 us -> 53.9 us
  Pallas kernels: 25.9 us -> 38.7 us
  other arithmetic: 5.4 us -> 1.82 us
    unnamed x114 -> x18, local copies, waits for them, and re-layouts: 24.9 us -> 0.05 us
    ppermute x44 -> x47, waiting for transfers between devices: 55.4 us -> 41.1 us  [swap(): return lax.ppermute(value, axis, [(i, i ^ mask) for i in range(size)])]
    pallas_call x12 -> x18, Pallas kernels: 25.9 us -> 38.7 us  [the longest x15 33.9 us: run(): pl.pallas_call(wrapped, out_shape=[pltpu.HBM(o[0], o[1]) if len(o) == 3 e...]
    ppermute x44 -> x47, starting transfers between devices: 38.3 us -> 41.4 us  [swap(): return lax.ppermute(value, axis, [(i, i ^ mask) for i in range(size)])]
    all_to_all x4, starting transfers between devices: 21.8 us -> 18.9 us  [over_experts(): lax.all_to_all(blocks, 'exp', split_axis=0, concat_axis=0, tiled=True)]
    all_to_all x4, waiting for transfers between devices: 15.1 us -> 12.8 us  [over_experts(): lax.all_to_all(blocks, 'exp', split_axis=0, concat_axis=0, tiled=True)]
  transfers between devices with their start and end apart: 48 -> 51, of which waited for: 23 -> 21; matrix products, arithmetic and copies ran while one was open for 3% -> 1% of each run, Pallas kernels for 5% -> 18%
where the time goes in v4:
time: 157 us; the launch traced here: 156 us
  starting transfers between devices  60.3 us (38%)
  waiting for transfers between devices  53.9 us (34%)
  Pallas kernels  38.7 us (25%)
  other arithmetic  1.82 us (1%)
    ppermute x47, starting transfers between devices, swap(): return lax.ppermute(value, axis, [(i, i ^ mask) for i in range(size)])  41.4 us
    ppermute x47, waiting for transfers between devices, swap(): return lax.ppermute(value, axis, [(i, i ^ mask) for i in range(size)])  41.1 us
    pallas_call x15, Pallas kernels, run(): pl.pallas_call(wrapped, out_shape=[pltpu.HBM(o[0], o[1]) if len(o) == 3 e...  33.9 us
    all_to_all x4, starting transfers between devices, over_experts(): lax.all_to_all(blocks, 'exp', split_axis=0, concat_axis=0, tiled=True)  18.9 us
    all_to_all x4, waiting for transfers between devices, over_experts(): lax.all_to_all(blocks, 'exp', split_axis=0, concat_axis=0, tiled=True)  12.8 us
    pallas_call x3, Pallas kernels, fetch(): pl.pallas_call(body, out_shape=[jax.ShapeDtypeStruct(v.shape, v.dtype) fo...  4.8 us
  transfers between devices with their start and end apart: 51, of which 21 were waited for; matrix products, arithmetic and copies ran while one was open for 1% of the time, Pallas kernels for 18%

profile of v4, /device:TPU:0, one launch (start us, length us, event | category | flops | bytes accessed | tf_op | source)
XLA Modules:
  0.0 156.1 jit_solution(5685389341885849400)
XLA Ops:
  0.6 3.0 %collective-permute-start.1 = (bf16[192,384]{1,0:T(8,128)(2,1)}, bf16[192,384]{1,0:T(8,128)(2,1)S(1)}, u32[]{:S(2)}, u32[]{:S(2)}) collective-permute-start(bf16[192,384]{1,0:T(8,128)(2,1)} %bitcast.72), channel_id=1, source_target_pairs={{0,2},{1,3},{2,0},{3,1},{4,6},{5,7},{6,4},{7,5},{8,10},{9,11},{10,... | collective-permute-start | bytes 442376 | tf_op jit(solution)/shard_map/ppermute | solution.py:143
  6.3 1.4 collective-permute-done.4.refs_8_
  8.3 1.4 slots.1
  9.8 4.8 %attend.1 = (bf16[16,768]{1,0:T(8,128)(2,1)S(1)}, bf16[16,768]{1,0:T(8,128)(2,1)}, s32[1,384]{1,0:T(1,128)}, f32[1,384]{1,0:T(1,128)}, bf16[768,384]{1,0:T(8,128...) custom-call(s32[1]{0:T(128)} %bitcast.refs_0_.token_ref, ...), custom_call_target="tpu_custom_call" | custom-call | flops 11000000 | bytes 4900032 | tf_op jit(solution)/shard_map/attend/pallas_call | solution.py:99
  15.1 1.3 collective-permute-done.6.refs_1_.refs_2_
  16.5 1.7 %collective-permute-start.7 = (bf16[128,768]{1,0:T(8,128)(2,1)S(1)}, bf16[128,768]{1,0:T(8,128)(2,1)S(1)}, u32[]{:S(2)}, u32[]{:S(2)}) collective-permute-start(bf16[128,768]{1,0:T(8,128)(2,1)S(1)} %fusion.6), channel_id=1, source_target_pairs={{0,2},{1,3},{2,0},{3,1},{4,6},{5,7},{6,4},{7,5},{8,10},{9,11},{10,... | collective-permute-start | bytes 589832 | tf_op jit(solution)/shard_map/ppermute | solution.py:143
  19.0 5.8 %all-to-all-start = ((bf16[8,16,768]{2,1,0:T(8,128)(2,1)}), bf16[8,16,768]{2,1,0:T(8,128)(2,1)S(1)}, u32[]{:S(2)}, u32[]{:S(2)}) async-start(bf16[8,16,768]{2,1,0:T(8,128)(2,1)} %bitcast.10), calls=%async_computation | async-start | bytes 393216 | tf_op jit(solution)/shard_map/all_to_all | solution.py:361
  24.8 1.5 route.1
  26.3 6.7 %all-to-all-done = bf16[8,16,768]{2,1,0:T(8,128)(2,1)S(1)} async-done(((bf16[8,16,768]{2,1,0:T(8,128)(2,1)}), bf16[8,16,768]{2,1,0:T(8,128)(2,1)S(1)}, u32[]{:S(2)}, u32[]{:S(2)}) %all-to-all-start) | async-done | bytes 196640 | tf_op jit(solution)/shard_map/all_to_all | solution.py:361
  33.5 3.4 %all-to-all-start.1 = ((bf16[8,16,896]{2,1,0:T(8,128)(2,1)}), bf16[8,16,896]{2,1,0:T(8,128)(2,1)S(1)}, u32[]{:S(2)}, u32[]{:S(2)}) async-start(bf16[8,16,896]{2,1,0:T(8,128)(2,1)} %bitcast.12), calls=%async_computation.1 | async-start | bytes 458752 | tf_op jit(solution)/shard_map/all_to_all | solution.py:361
  37.0 1.6 %collective-permute-done.12.refs_7_ = bf16[128,768]{1,0:T(8,128)(2,1)S(1)} collective-permute-done((bf16[128,768]{1,0:T(8,128)(2,1)S(1)}, bf16[128,768]{1,0:T(8,128)(2,1)S(1)}, u32[]{:S(2)}, u32[]{:S(2)}) %collective-permute-start.12) | collective-permute-done | bytes 196640 | tf_op jit(solution)/shard_map/ppermute | solution.py:143
  39.4 1.5 collective-permute-start.9
  40.9 1.6 %collective-permute-done.10.refs_9_ = bf16[128,192]{1,0:T(8,128)(2,1)S(1)} collective-permute-done((bf16[128,192]{1,0:T(8,128)(2,1)S(1)}, bf16[128,192]{1,0:T(8,128)(2,1)S(1)}, u32[]{:S(2)}, u32[]{:S(2)}) %collective-permute-start.10) | collective-permute-done | bytes 49184 | tf_op jit(solution)/shard_map/ppermute | solution.py:143
  42.5 2.1 %collective-permute-done.9.refs_8_ = bf16[128,192]{1,0:T(8,128)(2,1)S(1)} collective-permute-done((bf16[128,192]{1,0:T(8,128)(2,1)S(1)}, bf16[128,192]{1,0:T(8,128)(2,1)S(1)}, u32[]{:S(2)}, u32[]{:S(2)}) %collective-permute-start.9) | collective-permute-done | bytes 49184 | tf_op jit(solution)/shard_map/ppermute | solution.py:143
  44.6 1.7 %state.1 = (f32[128,768]{1,0:T(8,128)}, f32[128,128]{1,0:T(8,128)}, bf16[128,768]{1,0:T(8,128)(2,1)}) custom-call(s32[1]{0:T(128)} %bitcast.refs_0_.token_ref, bf16[128,768]{1,0:T(8,128)(2,1)S(1)} %get-tuple-element.184.refs_0_.refs_1_, bf16[2,128,768]{2,1,0:T(8,128)(2,1)S(1)} %collective-permute-done.6.refs_1_.refs_2_, ...), custom_call_target="tpu_custom_call" | custom-call | flops 11000000 | bytes 1859588 | tf_op jit(solution)/shard_map/state/pallas_call | solution.py:99
  47.0 1.6 %expert_arguments.1 = (bf16[1,768,768]{2,1,0:T(8,128)(2,1)S(1)}, bf16[1,768,768]{2,1,0:T(8,128)(2,1)S(1)}) custom-call(s32[1]{0:T(128)} %bitcast.refs_0_.token_ref, bf16[1,768,768]{2,1,0:T(8,128)(2,1)} %refs_0_.2, bf16[1,768,768]{2,1,0:T(8,128)(2,1)} %refs_2_.3), custom_call_target="tpu_custom_call" | custom-call | tf_op jit(solution)/shard_map/expert_arguments/pallas_call | solution.py:130
  48.6 4.7 %collective-permute-done.15.refs_3_ = bf16[128,896]{1,0:T(8,128)(2,1)S(1)} collective-permute-done((bf16[128,896]{1,0:T(8,128)(2,1)S(1)}, bf16[128,896]{1,0:T(8,128)(2,1)S(1)}, u32[]{:S(2)}, u32[]{:S(2)}) %collective-permute-start.15) | collective-permute-done | bytes 229408 | tf_op jit(solution)/shard_map/ppermute | solution.py:143
  53.4 1.5 collective-permute-done.16.refs_4_
  54.8 3.5 %expert.1 = (bf16[512,768]{1,0:T(8,128)(2,1)}, bf16[512,768]{1,0:T(8,128)(2,1)}, bf16[512,768]{1,0:T(8,128)(2,1)}, bf16[512,768]{1,0:T(8,128)(2,1)}, bf16[128,89...) custom-call(s32[1]{0:T(128)} %bitcast.refs_0_.token_ref, ...), custom_call_target="tpu_custom_call" | custom-call | flops 4400000000 | bytes 8126468 | tf_op jit(solution)/shard_map/expert/pallas_call | solution.py:99
  58.6 1.7 %collective-permute-done.17 = bf16[2,128,896]{2,1,0:T(8,128)(2,1)S(1)} collective-permute-done((bf16[2,128,896]{2,1,0:T(8,128)(2,1)S(1)}, bf16[2,128,896]{2,1,0:T(8,128)(2,1)S(1)}, u32[]{:S(2)}, u32[]{:S(2)}) %collective-permute-start.17) | collective-permute-done | bytes 458784 | tf_op jit(solution)/shard_map/ppermute | solution.py:143
  60.9 1.9 %value.1 = (bf16[128,768]{1,0:T(8,128)(2,1)S(1)}, bf16[128,768]{1,0:T(8,128)(2,1)S(1)}, bf16[2,128,768]{2,1,0:T(8,128)(2,1)S(1)}) custom-call(s32[1]{0:T(128)} %bitcast.refs_0_.token_ref, bf16[512,768]{1,0:T(8,128)(2,1)} %get-tuple-element.212.refs_1_.refs_3_, bf16[1,768,768]{2,1,0:T(8,128)(2,1)S(1)} %copy-done), custom_call_target="tpu_custom_call" | custom-call | flops 880000000 | bytes 2752516 | tf_op jit(solution)/shard_map/value/pallas_call | solution.py:99
  62.9 5.1 %collective-permute-done.19 = bf16[128,896]{1,0:T(8,128)(2,1)S(1)} collective-permute-done((bf16[128,896]{1,0:T(8,128)(2,1)S(1)}, bf16[128,896]{1,0:T(8,128)(2,1)S(1)}, u32[]{:S(2)}, u32[]{:S(2)}) %collective-permute-start.19) | collective-permute-done | bytes 229408 | tf_op jit(solution)/shard_map/ppermute | solution.py:143
  69.3 6.1 %all-to-all-start.3 = ((bf16[8,16,896]{2,1,0:T(8,128)(2,1)}), bf16[8,16,896]{2,1,0:T(8,128)(2,1)S(1)}, u32[]{:S(2)}, u32[]{:S(2)}) async-start(bf16[8,16,896]{2,1,0:T(8,128)(2,1)} %bitcast.24), calls=%async_computation.3 | async-start | bytes 458752 | tf_op jit(solution)/shard_map/all_to_all | solution.py:361
  77.3 6.2 %all-to-all-done.3 = bf16[8,16,896]{2,1,0:T(8,128)(2,1)S(1)} async-done(((bf16[8,16,896]{2,1,0:T(8,128)(2,1)}), bf16[8,16,896]{2,1,0:T(8,128)(2,1)S(1)}, u32[]{:S(2)}, u32[]{:S(2)}) %all-to-all-start.3) | async-done | bytes 229408 | tf_op jit(solution)/shard_map/all_to_all | solution.py:361
  84.8 3.6 %all-to-all-start.2 = ((bf16[8,16,768]{2,1,0:T(8,128)(2,1)}), bf16[8,16,768]{2,1,0:T(8,128)(2,1)S(1)}, u32[]{:S(2)}, u32[]{:S(2)}) async-start(bf16[8,16,768]{2,1,0:T(8,128)(2,1)} %bitcast.22), calls=%async_computation.2 | async-start | bytes 393216 | tf_op jit(solution)/shard_map/all_to_all | solution.py:361
  88.4 2.0 %attend_again.1 = (bf16[192,768]{1,0:T(8,128)(2,1)S(1)}, bf16[192,384]{1,0:T(8,128)(2,1)S(1)}, bf16[192,384]{1,0:T(8,128)(2,1)S(1)}, bf16[192,384]{1,0:T(8,128)(...) custom-call(s32[1]{0:T(128)} %bitcast.refs_0_.token_ref, ...), custom_call_target="tpu_custom_call" | custom-call | tf_op jit(solution)/shard_map/attend_again/pallas_call | solution.py:130
  92.1 5.4 %attend_back.1 = (bf16[192,384]{1,0:T(8,128)(2,1)S(1)}, bf16[208,384]{1,0:T(8,128)(2,1)S(1)}, bf16[208,384]{1,0:T(8,128)(2,1)S(1)}, bf16[2,208,384]{2,1,0:T(8,12...) custom-call(s32[1]{0:T(128)} %bitcast.refs_0_.token_ref, ...), custom_call_target="tpu_custom_call" | custom-call | flops 11000000 | bytes 6173184 | tf_op jit(solution)/shard_map/attend_back/pallas_call | solution.py:99
  98.0 1.7 %collective-permute-start.25 = (bf16[80,768]{1,0:T(8,128)(2,1)S(1)}, bf16[80,768]{1,0:T(8,128)(2,1)S(1)}, u32[]{:S(2)}, u32[]{:S(2)}) collective-permute-start(bf16[80,768]{1,0:T(8,128)(2,1)S(1)} %get-tuple-element.285), channel_id=1, source_target_pairs={{0,8},{4,12},{8,0},{12,4},{16,24},{20,28},{24,16},{28,20},{1,9},{5... | collective-permute-start | bytes 368648 | tf_op jit(solution)/shard_map/ppermute | solution.py:143
  99.7 2.4 %collective-permute-start.26 = (bf16[80,768]{1,0:T(8,128)(2,1)S(1)}, bf16[80,768]{1,0:T(8,128)(2,1)S(1)}, u32[]{:S(2)}, u32[]{:S(2)}) collective-permute-start(bf16[80,768]{1,0:T(8,128)(2,1)S(1)} %get-tuple-element.286), channel_id=1, source_target_pairs={{0,16},{4,20},{8,24},{12,28},{16,0},{20,4},{24,8},{28,12},{1,17},{... | collective-permute-start | bytes 368648 | tf_op jit(solution)/shard_map/ppermute | solution.py:143
  102.4 1.7 %collective-permute-start.24 = (bf16[256,768]{1,0:T(8,128)(2,1)S(1)}, bf16[256,768]{1,0:T(8,128)(2,1)S(1)}, u32[]{:S(2)}, u32[]{:S(2)}) collective-permute-start(bf16[256,768]{1,0:T(8,128)(2,1)S(1)} %get-tuple-element.284), channel_id=1, source_target_pairs={{0,4},{4,0},{8,12},{12,8},{16,20},{20,16},{24,28},{28,24},{1,5},{5... | collective-permute-start | bytes 1179656 | tf_op jit(solution)/shard_map/ppermute | solution.py:143
  104.1 4.9 %expert_weights.1 = (bf16[1,768,768]{2,1,0:T(8,128)(2,1)}, bf16[1,768,768]{2,1,0:T(8,128)(2,1)}) custom-call(s32[1]{0:T(128)} %bitcast.refs_0_.token_ref, bf16[512,768]{1,0:T(8,128)(2,1)} %get-tuple-element.290.refs_1_, bf16[512,768]{1,0:T(8,128)(2,1)} %get-tuple-element.291.refs_2_, bf16[512,768]{1,0:T(8,128)(2,1)} %get-tuple-element.212.refs_1_.refs_3_, ...), custom_call_target="tpu_custom_call" | custom-call | flops 13200000000 | bytes 5505028 | tf_op jit(solution)/shard_map/expert_weights/pallas_call | solution.py:99
  109.0 3.0 %collective-permute-done.26 = bf16[80,768]{1,0:T(8,128)(2,1)S(1)} collective-permute-done((bf16[80,768]{1,0:T(8,128)(2,1)S(1)}, bf16[80,768]{1,0:T(8,128)(2,1)S(1)}, u32[]{:S(2)}, u32[]{:S(2)}) %collective-permute-start.26) | collective-permute-done | bytes 122912 | tf_op jit(solution)/shard_map/ppermute | solution.py:143
  112.8 1.7 %collective-permute-start.32 = (bf16[48,768]{1,0:T(8,128)(2,1)S(1)}, bf16[48,768]{1,0:T(8,128)(2,1)S(1)}, u32[]{:S(2)}, u32[]{:S(2)}) collective-permute-start(bf16[48,768]{1,0:T(8,128)(2,1)S(1)} %concatenate.16), channel_id=1, source_target_pairs={{0,4},{4,0},{8,12},{12,8},{16,20},{20,16},{24,28},{28,24},{1,5},{5... | collective-permute-start | bytes 221192 | tf_op jit(solution)/shard_map/ppermute | solution.py:143
  114.5 1.6 %collective-permute-start.33 = (bf16[208,384]{1,0:T(8,128)(2,1)S(1)}, bf16[208,384]{1,0:T(8,128)(2,1)S(1)}, u32[]{:S(2)}, u32[]{:S(2)}) collective-permute-start(bf16[208,384]{1,0:T(8,128)(2,1)S(1)} %bitcast_add_fusion), channel_id=1, source_target_pairs={{0,2},{1,3},{2,0},{3,1},{4,6},{5,7},{6,4},{7,5},{8,10},{9,11},{10,... | collective-permute-start | bytes 479240 | tf_op jit(solution)/shard_map/ppermute | solution.py:143
  116.3 3.4 %collective-permute-start.31 = (bf16[64,768]{1,0:T(8,128)(2,1)S(1)}, bf16[64,768]{1,0:T(8,128)(2,1)S(1)}, u32[]{:S(2)}, u32[]{:S(2)}) collective-permute-start(bf16[64,768]{1,0:T(8,128)(2,1)S(1)} %get-tuple-element.344), channel_id=1, source_target_pairs={{0,24},{4,28},{8,16},{12,20},{16,8},{20,12},{24,0},{28,4},{1,25},{... | collective-permute-start | bytes 294920 | tf_op jit(solution)/shard_map/ppermute | solution.py:143
  120.8 1.4 layer_rows.1
  122.2 1.5 collective-permute-done.31
  123.7 3.1 %collective-permute-done.30 = bf16[64,768]{1,0:T(8,128)(2,1)S(1)} collective-permute-done((bf16[64,768]{1,0:T(8,128)(2,1)S(1)}, bf16[64,768]{1,0:T(8,128)(2,1)S(1)}, u32[]{:S(2)}, u32[]{:S(2)}) %collective-permute-start.30) | collective-permute-done | bytes 98336 | tf_op jit(solution)/shard_map/ppermute | solution.py:143
  127.0 2.1 %collective-permute-start.36 = (bf16[64,768]{1,0:T(8,128)(2,1)S(1)}, bf16[64,768]{1,0:T(8,128)(2,1)S(1)}, u32[]{:S(2)}, u32[]{:S(2)}) collective-permute-start(bf16[64,768]{1,0:T(8,128)(2,1)S(1)} %add_convert_fusion.2), channel_id=1, source_target_pairs={{0,24},{4,28},{8,16},{12,20},{16,8},{20,12},{24,0},{28,4},{1,25},{... | collective-permute-start | bytes 294920 | tf_op jit(solution)/shard_map/ppermute | solution.py:143
  129.9 2.0 %tokens_back.1 = bf16[192,384]{1,0:T(8,128)(2,1)} custom-call(s32[1]{0:T(128)} %bitcast.refs_0_.token_ref, bf16[208,384]{1,0:T(8,128)(2,1)S(1)} %get-tuple-element.314.refs_1_, bf16[2,208,384]{2,1,0:T(8,128)(2,1)S(1)} %collective-permute-done.28.refs_2_, bf16[208,384]{1,0:T(8,128)(2,1)S(1)} %collective-permute-done.33.refs_3_, ...), custom_call_target="tpu_custom_call" | custom-call | flops 13200000000 | bytes 1107460 | tf_op jit(solution)/shard_map/tokens_back/pallas_call | solution.py:99
  131.9 2.4 %collective-permute-start.34 = (bf16[64,768]{1,0:T(8,128)(2,1)S(1)}, bf16[64,768]{1,0:T(8,128)(2,1)S(1)}, u32[]{:S(2)}, u32[]{:S(2)}) collective-permute-start(bf16[64,768]{1,0:T(8,128)(2,1)S(1)} %add_convert_fusion.2), channel_id=1, source_target_pairs={{0,8},{4,12},{8,0},{12,4},{16,24},{20,28},{24,16},{28,20},{1,9},{5... | collective-permute-start | bytes 294920 | tf_op jit(solution)/shard_map/ppermute | solution.py:143
  135.7 3.1 %collective-permute-done.40.refs_3_ = bf16[192,128]{1,0:T(8,128)(2,1)S(1)} collective-permute-done((bf16[192,128]{1,0:T(8,128)(2,1)S(1)}, bf16[192,128]{1,0:T(8,128)(2,1)S(1)}, u32[]{:S(2)}, u32[]{:S(2)}) %collective-permute-start.40) | collective-permute-done | bytes 49184 | tf_op jit(solution)/shard_map/ppermute | solution.py:143
  139.1 2.0 %collective-permute-start.45 = (bf16[64,768]{1,0:T(8,128)(2,1)S(1)}, bf16[64,768]{1,0:T(8,128)(2,1)S(1)}, u32[]{:S(2)}, u32[]{:S(2)}) collective-permute-start(bf16[64,768]{1,0:T(8,128)(2,1)S(1)} %pad_maximum_fusion.1.refs_5_), channel_id=1, source_target_pairs={{0,24},{4,28},{8,16},{12,20},{16,8},{20,12},{24,0},{28,4},{1,25},{... | collective-permute-start | bytes 294920 | tf_op jit(solution)/shard_map/ppermute | solution.py:143
  141.7 1.9 %collective-permute-start.43 = (bf16[64,768]{1,0:T(8,128)(2,1)S(1)}, bf16[64,768]{1,0:T(8,128)(2,1)S(1)}, u32[]{:S(2)}, u32[]{:S(2)}) collective-permute-start(bf16[64,768]{1,0:T(8,128)(2,1)S(1)} %pad_maximum_fusion.1.refs_5_), channel_id=1, source_target_pairs={{0,8},{4,12},{8,0},{12,4},{16,24},{20,28},{24,16},{28,20},{1,9},{5... | collective-permute-start | bytes 294920 | tf_op jit(solution)/shard_map/ppermute | solution.py:143
  144.8 1.6 collective-permute-start.42
  146.3 1.7 %layer_out.1 = bf16[192,384]{1,0:T(8,128)(2,1)} custom-call(s32[1,384]{1,0:T(1,128)} %get-tuple-element.223.refs_4_.refs_0_, bf16[192,128]{1,0:T(8,128)(2,1)S(1)} %get-tuple-element.323.refs_1_, bf16[192,128]{1,0:T(8,128)(2,1)S(1)} %collective-permute-done.39.refs_2_, bf16[192,128]{1,0:T(8,128)(2,1)S(1)} %collective-permute-done.40.refs_3_, ...), custom_call_target="tpu_custom_call" | custom-call | flops 13200000000 | bytes 345600 | tf_op jit(solution)/shard_map/layer_out/pallas_call | solution.py:99
  148.0 3.0 %collective-permute-done.44.refs_7_ = bf16[64,768]{1,0:T(8,128)(2,1)S(1)} collective-permute-done((bf16[64,768]{1,0:T(8,128)(2,1)S(1)}, bf16[64,768]{1,0:T(8,128)(2,1)S(1)}, u32[]{:S(2)}, u32[]{:S(2)}) %collective-permute-start.44) | collective-permute-done | bytes 98336 | tf_op jit(solution)/shard_map/ppermute | solution.py:143
  151.0 3.8 %collective-permute-done.42.refs_4_ = bf16[256,768]{1,0:T(8,128)(2,1)S(1)} collective-permute-done((bf16[256,768]{1,0:T(8,128)(2,1)S(1)}, bf16[256,768]{1,0:T(8,128)(2,1)S(1)}, u32[]{:S(2)}, u32[]{:S(2)}) %collective-permute-start.42) | collective-permute-done | bytes 393248 | tf_op jit(solution)/shard_map/ppermute | solution.py:143
  (110 shorter events, 21.9 us)
Async XLA Ops:
  0.6 7.5 %collective-permute-start.1 = (bf16[192,384]{1,0:T(8,128)(2,1)}, bf16[192,384]{1,0:T(8,128)(2,1)S(1)}, u32[]{:S(2)}, u32[]{:S(2)}) collective-permute-start(bf16[192,384]{1,0:T(8,128)(2,1)} %bitcast.72), channel_id=1, source_target_pairs={{0,2},{1,3},{2,0},{3,1},{4,6},{5,7},{6,4},{7,5},{8,10},{9,11},{10,... | collective-permute-start | bytes 442376 | tf_op jit(solution)/shard_map/ppermute | solution.py:143
  4.4 3.3 %collective-permute-start.4 = (bf16[16,192]{1,0:T(8,128)(2,1)S(1)}, bf16[16,192]{1,0:T(8,128)(2,1)S(1)}, u32[]{:S(2)}, u32[]{:S(2)}) collective-permute-start(bf16[16,192]{1,0:T(8,128)(2,1)S(1)} %small.1.refs_5_), channel_id=1, source_target_pairs={{0,3},{1,2},{2,1},{3,0},{4,7},{5,6},{6,5},{7,4},{8,11},{9,10},{10,... | collective-permute-start | bytes 18440 | tf_op jit(solution)/shard_map/ppermute | solution.py:143
  4.5 3.7 %collective-permute-start.3 = (bf16[16,192]{1,0:T(8,128)(2,1)S(1)}, bf16[16,192]{1,0:T(8,128)(2,1)S(1)}, u32[]{:S(2)}, u32[]{:S(2)}) collective-permute-start(bf16[16,192]{1,0:T(8,128)(2,1)S(1)} %small.1.refs_5_), channel_id=1, source_target_pairs={{0,2},{1,3},{2,0},{3,1},{4,6},{5,7},{6,4},{7,5},{8,10},{9,11},{10,... | collective-permute-start | bytes 18440 | tf_op jit(solution)/shard_map/ppermute | solution.py:143
  5.6 2.5 %collective-permute-start.2 = (bf16[16,192]{1,0:T(8,128)(2,1)S(1)}, bf16[16,192]{1,0:T(8,128)(2,1)S(1)}, u32[]{:S(2)}, u32[]{:S(2)}) collective-permute-start(bf16[16,192]{1,0:T(8,128)(2,1)S(1)} %small.1.refs_5_), channel_id=1, source_target_pairs={{0,1},{1,0},{2,3},{3,2},{4,5},{5,4},{6,7},{7,6},{8,9},{9,8},{10,11... | collective-permute-start | bytes 18440 | tf_op jit(solution)/shard_map/ppermute | solution.py:143
  6.3 3.4 %collective-permute-start = (bf16[192,384]{1,0:T(8,128)(2,1)}, bf16[192,384]{1,0:T(8,128)(2,1)S(1)}, u32[]{:S(2)}, u32[]{:S(2)}) collective-permute-start(bf16[192,384]{1,0:T(8,128)(2,1)} %bitcast.73), channel_id=1, source_target_pairs={{0,1},{1,0},{2,3},{3,2},{4,5},{5,4},{6,7},{7,6},{8,9},{9,8},{10,11... | collective-permute-start | bytes 442376 | tf_op jit(solution)/shard_map/ppermute | solution.py:143
  14.6 1.9 %collective-permute-start.6 = (bf16[2,128,768]{2,1,0:T(8,128)(2,1)S(1)}, bf16[2,128,768]{2,1,0:T(8,128)(2,1)S(1)}, u32[]{:S(2)}, u32[]{:S(2)}) collective-permute-start(bf16[2,128,768]{2,1,0:T(8,128)(2,1)S(1)} %get-tuple-element.185), channel_id=1, source_target_pairs={{0,1},{1,0},{2,3},{3,2},{4,5},{5,4},{6,7},{7,6},{8,9},{9,8},{10,11... | collective-permute-start | bytes 1179656 | tf_op jit(solution)/shard_map/ppermute | solution.py:143
  16.5 8.3 %collective-permute-start.7 = (bf16[128,768]{1,0:T(8,128)(2,1)S(1)}, bf16[128,768]{1,0:T(8,128)(2,1)S(1)}, u32[]{:S(2)}, u32[]{:S(2)}) collective-permute-start(bf16[128,768]{1,0:T(8,128)(2,1)S(1)} %fusion.6), channel_id=1, source_target_pairs={{0,2},{1,3},{2,0},{3,1},{4,6},{5,7},{6,4},{7,5},{8,10},{9,11},{10,... | collective-permute-start | bytes 589832 | tf_op jit(solution)/shard_map/ppermute | solution.py:143
  19.0 14.0 %all-to-all-start = ((bf16[8,16,768]{2,1,0:T(8,128)(2,1)}), bf16[8,16,768]{2,1,0:T(8,128)(2,1)S(1)}, u32[]{:S(2)}, u32[]{:S(2)}) async-start(bf16[8,16,768]{2,1,0:T(8,128)(2,1)} %bitcast.10), calls=%async_computation | async-start | bytes 393216 | tf_op jit(solution)/shard_map/all_to_all | solution.py:361
  33.0 5.7 %collective-permute-start.12 = (bf16[128,768]{1,0:T(8,128)(2,1)S(1)}, bf16[128,768]{1,0:T(8,128)(2,1)S(1)}, u32[]{:S(2)}, u32[]{:S(2)}) collective-permute-start(bf16[128,768]{1,0:T(8,128)(2,1)S(1)} %bitcast.69), channel_id=1, source_target_pairs={{0,2},{1,3},{2,0},{3,1},{4,6},{5,7},{6,4},{7,5},{8,10},{9,11},{10,... | collective-permute-start | bytes 589832 | tf_op jit(solution)/shard_map/ppermute | solution.py:143
  33.5 12.8 %all-to-all-start.1 = ((bf16[8,16,896]{2,1,0:T(8,128)(2,1)}), bf16[8,16,896]{2,1,0:T(8,128)(2,1)S(1)}, u32[]{:S(2)}, u32[]{:S(2)}) async-start(bf16[8,16,896]{2,1,0:T(8,128)(2,1)} %bitcast.12), calls=%async_computation.1 | async-start | bytes 458752 | tf_op jit(solution)/shard_map/all_to_all | solution.py:361
  36.9 9.3 %collective-permute-start.11 = (bf16[128,768]{1,0:T(8,128)(2,1)S(1)}, bf16[128,768]{1,0:T(8,128)(2,1)S(1)}, u32[]{:S(2)}, u32[]{:S(2)}) collective-permute-start(bf16[128,768]{1,0:T(8,128)(2,1)S(1)} %bitcast.70), channel_id=1, source_target_pairs={{0,1},{1,0},{2,3},{3,2},{4,5},{5,4},{6,7},{7,6},{8,9},{9,8},{10,11... | collective-permute-start | bytes 589832 | tf_op jit(solution)/shard_map/ppermute | solution.py:143
  38.7 7.6 %collective-permute-start.13 = (bf16[128,768]{1,0:T(8,128)(2,1)S(1)}, bf16[128,768]{1,0:T(8,128)(2,1)S(1)}, u32[]{:S(2)}, u32[]{:S(2)}) collective-permute-start(bf16[128,768]{1,0:T(8,128)(2,1)S(1)} %collective-permute-done.12.refs_7_), channel_id=1, source_target_pairs={{0,1},{1,0},{2,3},{3,2},{4,5},{5,4},{6,7},{7,6},{8,9},{9,8},{10,11... | collective-permute-start | bytes 589832 | tf_op jit(solution)/shard_map/ppermute | solution.py:143
  38.7 3.8 %collective-permute-start.10 = (bf16[128,192]{1,0:T(8,128)(2,1)S(1)}, bf16[128,192]{1,0:T(8,128)(2,1)S(1)}, u32[]{:S(2)}, u32[]{:S(2)}) collective-permute-start(bf16[128,192]{1,0:T(8,128)(2,1)S(1)} %get-tuple-element.347), channel_id=1, source_target_pairs={{0,3},{1,2},{2,1},{3,0},{4,7},{5,6},{6,5},{7,4},{8,11},{9,10},{10,... | collective-permute-start | bytes 147464 | tf_op jit(solution)/shard_map/ppermute | solution.py:143
  39.4 5.1 %collective-permute-start.9 = (bf16[128,192]{1,0:T(8,128)(2,1)S(1)}, bf16[128,192]{1,0:T(8,128)(2,1)S(1)}, u32[]{:S(2)}, u32[]{:S(2)}) collective-permute-start(bf16[128,192]{1,0:T(8,128)(2,1)S(1)} %get-tuple-element.348), channel_id=1, source_target_pairs={{0,2},{1,3},{2,0},{3,1},{4,6},{5,7},{6,4},{7,5},{8,10},{9,11},{10,... | collective-permute-start | bytes 147464 | tf_op jit(solution)/shard_map/ppermute | solution.py:143
  40.9 3.7 %collective-permute-start.8 = (bf16[128,192]{1,0:T(8,128)(2,1)S(1)}, bf16[128,192]{1,0:T(8,128)(2,1)S(1)}, u32[]{:S(2)}, u32[]{:S(2)}) collective-permute-start(bf16[128,192]{1,0:T(8,128)(2,1)S(1)} %get-tuple-element.349), channel_id=1, source_target_pairs={{0,1},{1,0},{2,3},{3,2},{4,5},{5,4},{6,7},{7,6},{8,9},{9,8},{10,11... | collective-permute-start | bytes 147464 | tf_op jit(solution)/shard_map/ppermute | solution.py:143
  46.3 7.0 %collective-permute-start.15 = (bf16[128,896]{1,0:T(8,128)(2,1)S(1)}, bf16[128,896]{1,0:T(8,128)(2,1)S(1)}, u32[]{:S(2)}, u32[]{:S(2)}) collective-permute-start(bf16[128,896]{1,0:T(8,128)(2,1)S(1)} %bitcast.64), channel_id=1, source_target_pairs={{0,2},{1,3},{2,0},{3,1},{4,6},{5,7},{6,4},{7,5},{8,10},{9,11},{10,... | collective-permute-start | bytes 688136 | tf_op jit(solution)/shard_map/ppermute | solution.py:143
  47.0 6.4 %collective-permute-start.14 = (bf16[128,896]{1,0:T(8,128)(2,1)S(1)}, bf16[128,896]{1,0:T(8,128)(2,1)S(1)}, u32[]{:S(2)}, u32[]{:S(2)}) collective-permute-start(bf16[128,896]{1,0:T(8,128)(2,1)S(1)} %bitcast.65), channel_id=1, source_target_pairs={{0,1},{1,0},{2,3},{3,2},{4,5},{5,4},{6,7},{7,6},{8,9},{9,8},{10,11... | collective-permute-start | bytes 688136 | tf_op jit(solution)/shard_map/ppermute | solution.py:143
  58.4 1.9 %collective-permute-start.17 = (bf16[2,128,896]{2,1,0:T(8,128)(2,1)S(1)}, bf16[2,128,896]{2,1,0:T(8,128)(2,1)S(1)}, u32[]{:S(2)}, u32[]{:S(2)}) collective-permute-start(bf16[2,128,896]{2,1,0:T(8,128)(2,1)S(1)} %get-tuple-element.210), channel_id=1, source_target_pairs={{0,1},{1,0},{2,3},{3,2},{4,5},{5,4},{6,7},{7,6},{8,9},{9,8},{10,11... | collective-permute-start | bytes 1376264 | tf_op jit(solution)/shard_map/ppermute | solution.py:143
  60.3 7.7 %collective-permute-start.19 = (bf16[128,896]{1,0:T(8,128)(2,1)S(1)}, bf16[128,896]{1,0:T(8,128)(2,1)S(1)}, u32[]{:S(2)}, u32[]{:S(2)}) collective-permute-start(bf16[128,896]{1,0:T(8,128)(2,1)S(1)} %fusion.2), channel_id=1, source_target_pairs={{0,2},{1,3},{2,0},{3,1},{4,6},{5,7},{6,4},{7,5},{8,10},{9,11},{10,... | collective-permute-start | bytes 688136 | tf_op jit(solution)/shard_map/ppermute | solution.py:143
  62.8 6.0 %collective-permute-start.18 = (bf16[2,128,768]{2,1,0:T(8,128)(2,1)S(1)}, bf16[2,128,768]{2,1,0:T(8,128)(2,1)S(1)}, u32[]{:S(2)}, u32[]{:S(2)}) collective-permute-start(bf16[2,128,768]{2,1,0:T(8,128)(2,1)S(1)} %get-tuple-element.214), channel_id=1, source_target_pairs={{0,1},{1,0},{2,3},{3,2},{4,5},{5,4},{6,7},{7,6},{8,9},{9,8},{10,11... | collective-permute-start | bytes 1179656 | tf_op jit(solution)/shard_map/ppermute | solution.py:143
  68.8 7.8 %collective-permute-start.20 = (bf16[128,768]{1,0:T(8,128)(2,1)S(1)}, bf16[128,768]{1,0:T(8,128)(2,1)S(1)}, u32[]{:S(2)}, u32[]{:S(2)}) collective-permute-start(bf16[128,768]{1,0:T(8,128)(2,1)S(1)} %fusion.3), channel_id=1, source_target_pairs={{0,2},{1,3},{2,0},{3,1},{4,6},{5,7},{6,4},{7,5},{8,10},{9,11},{10,... | collective-permute-start | bytes 589832 | tf_op jit(solution)/shard_map/ppermute | solution.py:143
  69.3 14.1 %all-to-all-start.3 = ((bf16[8,16,896]{2,1,0:T(8,128)(2,1)}), bf16[8,16,896]{2,1,0:T(8,128)(2,1)S(1)}, u32[]{:S(2)}, u32[]{:S(2)}) async-start(bf16[8,16,896]{2,1,0:T(8,128)(2,1)} %bitcast.24), calls=%async_computation.3 | async-start | bytes 458752 | tf_op jit(solution)/shard_map/all_to_all | solution.py:361
  84.3 6.2 %collective-permute-start.22 = (bf16[128,768]{1,0:T(8,128)(2,1)S(1)}, bf16[128,768]{1,0:T(8,128)(2,1)S(1)}, u32[]{:S(2)}, u32[]{:S(2)}) collective-permute-start(bf16[128,768]{1,0:T(8,128)(2,1)S(1)} %get-tuple-element.235.refs_1_), channel_id=1, source_target_pairs={{0,2},{1,3},{2,0},{3,1},{4,6},{5,7},{6,4},{7,5},{8,10},{9,11},{10,... | collective-permute-start | bytes 589832 | tf_op jit(solution)/shard_map/ppermute | solution.py:143
  84.8 12.8 %all-to-all-start.2 = ((bf16[8,16,768]{2,1,0:T(8,128)(2,1)}), bf16[8,16,768]{2,1,0:T(8,128)(2,1)S(1)}, u32[]{:S(2)}, u32[]{:S(2)}) async-start(bf16[8,16,768]{2,1,0:T(8,128)(2,1)} %bitcast.22), calls=%async_computation.2 | async-start | bytes 393216 | tf_op jit(solution)/shard_map/all_to_all | solution.py:361
  88.4 2.7 %collective-permute-start.21 = (bf16[128,768]{1,0:T(8,128)(2,1)S(1)}, bf16[128,768]{1,0:T(8,128)(2,1)S(1)}, u32[]{:S(2)}, u32[]{:S(2)}) collective-permute-start(bf16[128,768]{1,0:T(8,128)(2,1)S(1)} %get-tuple-element.235.refs_1_), channel_id=1, source_target_pairs={{0,1},{1,0},{2,3},{3,2},{4,5},{5,4},{6,7},{7,6},{8,9},{9,8},{10,11... | collective-permute-start | bytes 589832 | tf_op jit(solution)/shard_map/ppermute | solution.py:143
  97.6 14.5 %collective-permute-start.28 = (bf16[2,208,384]{2,1,0:T(8,128)(2,1)S(1)}, bf16[2,208,384]{2,1,0:T(8,128)(2,1)S(1)}, u32[]{:S(2)}, u32[]{:S(2)}) collective-permute-start(bf16[2,208,384]{2,1,0:T(8,128)(2,1)S(1)} %get-tuple-element.288), channel_id=1, source_target_pairs={{0,1},{1,0},{2,3},{3,2},{4,5},{5,4},{6,7},{7,6},{8,9},{9,8},{10,11... | collective-permute-start | bytes 958472 | tf_op jit(solution)/shard_map/ppermute | solution.py:143
  98.0 11.0 %collective-permute-start.25 = (bf16[80,768]{1,0:T(8,128)(2,1)S(1)}, bf16[80,768]{1,0:T(8,128)(2,1)S(1)}, u32[]{:S(2)}, u32[]{:S(2)}) collective-permute-start(bf16[80,768]{1,0:T(8,128)(2,1)S(1)} %get-tuple-element.285), channel_id=1, source_target_pairs={{0,8},{4,12},{8,0},{12,4},{16,24},{20,28},{24,16},{28,20},{1,9},{5... | collective-permute-start | bytes 368648 | tf_op jit(solution)/shard_map/ppermute | solution.py:143
  99.7 12.4 %collective-permute-start.26 = (bf16[80,768]{1,0:T(8,128)(2,1)S(1)}, bf16[80,768]{1,0:T(8,128)(2,1)S(1)}, u32[]{:S(2)}, u32[]{:S(2)}) collective-permute-start(bf16[80,768]{1,0:T(8,128)(2,1)S(1)} %get-tuple-element.286), channel_id=1, source_target_pairs={{0,16},{4,20},{8,24},{12,28},{16,0},{20,4},{24,8},{28,12},{1,17},{... | collective-permute-start | bytes 368648 | tf_op jit(solution)/shard_map/ppermute | solution.py:143
  102.1 10.0 %collective-permute-start.27 = (bf16[80,768]{1,0:T(8,128)(2,1)S(1)}, bf16[80,768]{1,0:T(8,128)(2,1)S(1)}, u32[]{:S(2)}, u32[]{:S(2)}) collective-permute-start(bf16[80,768]{1,0:T(8,128)(2,1)S(1)} %get-tuple-element.287), channel_id=1, source_target_pairs={{0,24},{4,28},{8,16},{12,20},{16,8},{20,12},{24,0},{28,4},{1,25},{... | collective-permute-start | bytes 368648 | tf_op jit(solution)/shard_map/ppermute | solution.py:143
  102.4 10.3 %collective-permute-start.24 = (bf16[256,768]{1,0:T(8,128)(2,1)S(1)}, bf16[256,768]{1,0:T(8,128)(2,1)S(1)}, u32[]{:S(2)}, u32[]{:S(2)}) collective-permute-start(bf16[256,768]{1,0:T(8,128)(2,1)S(1)} %get-tuple-element.284), channel_id=1, source_target_pairs={{0,4},{4,0},{8,12},{12,8},{16,20},{20,16},{24,28},{28,24},{1,5},{5... | collective-permute-start | bytes 1179656 | tf_op jit(solution)/shard_map/ppermute | solution.py:143
  112.8 9.4 %collective-permute-start.32 = (bf16[48,768]{1,0:T(8,128)(2,1)S(1)}, bf16[48,768]{1,0:T(8,128)(2,1)S(1)}, u32[]{:S(2)}, u32[]{:S(2)}) collective-permute-start(bf16[48,768]{1,0:T(8,128)(2,1)S(1)} %concatenate.16), channel_id=1, source_target_pairs={{0,4},{4,0},{8,12},{12,8},{16,20},{20,16},{24,28},{28,24},{1,5},{5... | collective-permute-start | bytes 221192 | tf_op jit(solution)/shard_map/ppermute | solution.py:143
  114.5 12.3 %collective-permute-start.33 = (bf16[208,384]{1,0:T(8,128)(2,1)S(1)}, bf16[208,384]{1,0:T(8,128)(2,1)S(1)}, u32[]{:S(2)}, u32[]{:S(2)}) collective-permute-start(bf16[208,384]{1,0:T(8,128)(2,1)S(1)} %bitcast_add_fusion), channel_id=1, source_target_pairs={{0,2},{1,3},{2,0},{3,1},{4,6},{5,7},{6,4},{7,5},{8,10},{9,11},{10,... | collective-permute-start | bytes 479240 | tf_op jit(solution)/shard_map/ppermute | solution.py:143
  116.3 7.4 %collective-permute-start.31 = (bf16[64,768]{1,0:T(8,128)(2,1)S(1)}, bf16[64,768]{1,0:T(8,128)(2,1)S(1)}, u32[]{:S(2)}, u32[]{:S(2)}) collective-permute-start(bf16[64,768]{1,0:T(8,128)(2,1)S(1)} %get-tuple-element.344), channel_id=1, source_target_pairs={{0,24},{4,28},{8,16},{12,20},{16,8},{20,12},{24,0},{28,4},{1,25},{... | collective-permute-start | bytes 294920 | tf_op jit(solution)/shard_map/ppermute | solution.py:143
  119.7 7.2 %collective-permute-start.30 = (bf16[64,768]{1,0:T(8,128)(2,1)S(1)}, bf16[64,768]{1,0:T(8,128)(2,1)S(1)}, u32[]{:S(2)}, u32[]{:S(2)}) collective-permute-start(bf16[64,768]{1,0:T(8,128)(2,1)S(1)} %get-tuple-element.345), channel_id=1, source_target_pairs={{0,16},{4,20},{8,24},{12,28},{16,0},{20,4},{24,8},{28,12},{1,17},{... | collective-permute-start | bytes 294920 | tf_op jit(solution)/shard_map/ppermute | solution.py:143
  119.7 7.2 %collective-permute-start.29 = (bf16[64,768]{1,0:T(8,128)(2,1)S(1)}, bf16[64,768]{1,0:T(8,128)(2,1)S(1)}, u32[]{:S(2)}, u32[]{:S(2)}) collective-permute-start(bf16[64,768]{1,0:T(8,128)(2,1)S(1)} %get-tuple-element.346), channel_id=1, source_target_pairs={{0,8},{4,12},{8,0},{12,4},{16,24},{20,28},{24,16},{28,20},{1,9},{5... | collective-permute-start | bytes 294920 | tf_op jit(solution)/shard_map/ppermute | solution.py:143
  127.0 11.9 %collective-permute-start.36 = (bf16[64,768]{1,0:T(8,128)(2,1)S(1)}, bf16[64,768]{1,0:T(8,128)(2,1)S(1)}, u32[]{:S(2)}, u32[]{:S(2)}) collective-permute-start(bf16[64,768]{1,0:T(8,128)(2,1)S(1)} %add_convert_fusion.2), channel_id=1, source_target_pairs={{0,24},{4,28},{8,16},{12,20},{16,8},{20,12},{24,0},{28,4},{1,25},{... | collective-permute-start | bytes 294920 | tf_op jit(solution)/shard_map/ppermute | solution.py:143
  129.1 9.7 %collective-permute-start.35 = (bf16[64,768]{1,0:T(8,128)(2,1)S(1)}, bf16[64,768]{1,0:T(8,128)(2,1)S(1)}, u32[]{:S(2)}, u32[]{:S(2)}) collective-permute-start(bf16[64,768]{1,0:T(8,128)(2,1)S(1)} %add_convert_fusion.2), channel_id=1, source_target_pairs={{0,16},{4,20},{8,24},{12,28},{16,0},{20,4},{24,8},{28,12},{1,17},{... | collective-permute-start | bytes 294920 | tf_op jit(solution)/shard_map/ppermute | solution.py:143
  129.1 2.8 %collective-permute-start.38 = (f32[16,768]{1,0:T(8,128)S(1)}, f32[16,768]{1,0:T(8,128)S(1)}, u32[]{:S(2)}, u32[]{:S(2)}) collective-permute-start(f32[16,768]{1,0:T(8,128)S(1)} %slice_convert_fusion), channel_id=1, source_target_pairs={{0,1},{1,0},{2,3},{3,2},{4,5},{5,4},{6,7},{7,6},{8,9},{9,8},{10,11... | collective-permute-start | bytes 147464 | tf_op jit(solution)/shard_map/ppermute | solution.py:143
  129.1 5.2 %collective-permute-start.37 = (bf16[32,768]{1,0:T(8,128)(2,1)S(1)}, bf16[32,768]{1,0:T(8,128)(2,1)S(1)}, u32[]{:S(2)}, u32[]{:S(2)}) collective-permute-start(bf16[32,768]{1,0:T(8,128)(2,1)S(1)} %slice.85), channel_id=1, source_target_pairs={{0,4},{4,0},{8,12},{12,8},{16,20},{20,16},{24,28},{28,24},{1,5},{5... | collective-permute-start | bytes 147464 | tf_op jit(solution)/shard_map/ppermute | solution.py:143
  129.7 5.1 %collective-permute-start.39 = (bf16[192,128]{1,0:T(8,128)(2,1)S(1)}, bf16[192,128]{1,0:T(8,128)(2,1)S(1)}, u32[]{:S(2)}, u32[]{:S(2)}) collective-permute-start(bf16[192,128]{1,0:T(8,128)(2,1)S(1)} %get-tuple-element.311), channel_id=1, source_target_pairs={{0,1},{1,0},{2,3},{3,2},{4,5},{5,4},{6,7},{7,6},{8,9},{9,8},{10,11... | collective-permute-start | bytes 147464 | tf_op jit(solution)/shard_map/ppermute | solution.py:143
  131.9 7.1 %collective-permute-start.34 = (bf16[64,768]{1,0:T(8,128)(2,1)S(1)}, bf16[64,768]{1,0:T(8,128)(2,1)S(1)}, u32[]{:S(2)}, u32[]{:S(2)}) collective-permute-start(bf16[64,768]{1,0:T(8,128)(2,1)S(1)} %add_convert_fusion.2), channel_id=1, source_target_pairs={{0,8},{4,12},{8,0},{12,4},{16,24},{20,28},{24,16},{28,20},{1,9},{5... | collective-permute-start | bytes 294920 | tf_op jit(solution)/shard_map/ppermute | solution.py:143
  134.3 4.5 %collective-permute-start.40 = (bf16[192,128]{1,0:T(8,128)(2,1)S(1)}, bf16[192,128]{1,0:T(8,128)(2,1)S(1)}, u32[]{:S(2)}, u32[]{:S(2)}) collective-permute-start(bf16[192,128]{1,0:T(8,128)(2,1)S(1)} %get-tuple-element.312), channel_id=1, source_target_pairs={{0,2},{1,3},{2,0},{3,1},{4,6},{5,7},{6,4},{7,5},{8,10},{9,11},{10,... | collective-permute-start | bytes 147464 | tf_op jit(solution)/shard_map/ppermute | solution.py:143
  134.8 4.0 %collective-permute-start.41 = (bf16[192,128]{1,0:T(8,128)(2,1)S(1)}, bf16[192,128]{1,0:T(8,128)(2,1)S(1)}, u32[]{:S(2)}, u32[]{:S(2)}) collective-permute-start(bf16[192,128]{1,0:T(8,128)(2,1)S(1)} %get-tuple-element.313), channel_id=1, source_target_pairs={{0,3},{1,2},{2,1},{3,0},{4,7},{5,6},{6,5},{7,4},{8,11},{9,10},{10,... | collective-permute-start | bytes 147464 | tf_op jit(solution)/shard_map/ppermute | solution.py:143
  139.1 9.0 %collective-permute-start.45 = (bf16[64,768]{1,0:T(8,128)(2,1)S(1)}, bf16[64,768]{1,0:T(8,128)(2,1)S(1)}, u32[]{:S(2)}, u32[]{:S(2)}) collective-permute-start(bf16[64,768]{1,0:T(8,128)(2,1)S(1)} %pad_maximum_fusion.1.refs_5_), channel_id=1, source_target_pairs={{0,24},{4,28},{8,16},{12,20},{16,8},{20,12},{24,0},{28,4},{1,25},{... | collective-permute-start | bytes 294920 | tf_op jit(solution)/shard_map/ppermute | solution.py:143
  141.1 9.9 %collective-permute-start.44 = (bf16[64,768]{1,0:T(8,128)(2,1)S(1)}, bf16[64,768]{1,0:T(8,128)(2,1)S(1)}, u32[]{:S(2)}, u32[]{:S(2)}) collective-permute-start(bf16[64,768]{1,0:T(8,128)(2,1)S(1)} %pad_maximum_fusion.1.refs_5_), channel_id=1, source_target_pairs={{0,16},{4,20},{8,24},{12,28},{16,0},{20,4},{24,8},{28,12},{1,17},{... | collective-permute-start | bytes 294920 | tf_op jit(solution)/shard_map/ppermute | solution.py:143
  141.7 9.3 %collective-permute-start.43 = (bf16[64,768]{1,0:T(8,128)(2,1)S(1)}, bf16[64,768]{1,0:T(8,128)(2,1)S(1)}, u32[]{:S(2)}, u32[]{:S(2)}) collective-permute-start(bf16[64,768]{1,0:T(8,128)(2,1)S(1)} %pad_maximum_fusion.1.refs_5_), channel_id=1, source_target_pairs={{0,8},{4,12},{8,0},{12,4},{16,24},{20,28},{24,16},{28,20},{1,9},{5... | collective-permute-start | bytes 294920 | tf_op jit(solution)/shard_map/ppermute | solution.py:143
  143.5 4.5 %collective-permute-start.46 = (f32[16,768]{1,0:T(8,128)S(1)}, f32[16,768]{1,0:T(8,128)S(1)}, u32[]{:S(2)}, u32[]{:S(2)}) collective-permute-start(f32[16,768]{1,0:T(8,128)S(1)} %fusion.7.refs_1_), channel_id=1, source_target_pairs={{0,2},{1,3},{2,0},{3,1},{4,6},{5,7},{6,4},{7,5},{8,10},{9,11},{10,... | collective-permute-start | bytes 147464 | tf_op jit(solution)/shard_map/ppermute | solution.py:143
  144.8 10.0 %collective-permute-start.42 = (bf16[256,768]{1,0:T(8,128)(2,1)S(1)}, bf16[256,768]{1,0:T(8,128)(2,1)S(1)}, u32[]{:S(2)}, u32[]{:S(2)}) collective-permute-start(bf16[256,768]{1,0:T(8,128)(2,1)S(1)} %pad_maximum_fusion.refs_3_), channel_id=1, source_target_pairs={{0,4},{4,0},{8,12},{12,8},{16,20},{20,16},{24,28},{28,24},{1,5},{5... | collective-permute-start | bytes 1179656 | tf_op jit(solution)/shard_map/ppermute | solution.py:143
  (12 other events, 24.5 us)

commit v5 on v4

--- a/solution.py
+++ b/solution.py
@@ -228,7 +228,8 @@
     for at, (digit_a, digit_b) in enumerate(zip(order_a, order_b)):
         b_came = trade(b_blocks, digit_b)
         a_came = trade(a_blocks, digit_a)
-        got = beside((*a_came, *b_came), b_blocks[0])
+        got = beside((*b_came, *a_came), b_blocks[0])
+        got = (*got[len(b_came) :], *got[: len(b_came)])
         a = sum_blocks(a_blocks[0], got[: len(a_came)])
         b = sum_blocks(b_blocks[0], got[len(a_came) :])
         few = b[b.shape[0] - tail :]
@@ -242,14 +243,23 @@
                 jnp.concatenate([b[k * part : (k + 1) * part], few], axis=0) for k in range(radix)
             ]
     b = b[: b.shape[0] - tail]
+    last = len(order_a) - 1
+    early = []
     for at, (digit_a, digit_b) in enumerate(zip(order_a[::-1], order_b[::-1])):
-        a_came = trade([a] * digit_a[1], digit_a)
         b_came = trade([b] * digit_b[1], digit_b)
-        got = beside((*a_came, *b_came), few)
-        a_blocks, b_blocks = [a, *got[: len(a_came)]], [b, *got[len(a_came) :]]
-        if at + 1 < len(order_a):
-            a, b = jnp.concatenate(a_blocks, axis=0), jnp.concatenate(b_blocks, axis=0)
-    return a_blocks, b_blocks
+        a_came = trade([rest if at == last else a] * digit_a[1], digit_a)
+        ahead = trade([a] * order_a[0][1], order_a[0]) if at == last - 1 else []
+        got = beside((*ahead, *b_came, *a_came), few)
+        early += got[: len(ahead)]
+        b_blocks = [b, *got[len(ahead) : len(ahead) + len(b_came)]]
+        a_blocks = got[len(ahead) + len(b_came) :]
+        if at == last - 1:
+            own, rest = a, jnp.concatenate(a_blocks, axis=0)
+        elif at < last:
+            a = jnp.concatenate([a, *a_blocks], axis=0)
+        if at < last:
+            b = jnp.concatenate(b_blocks, axis=0)
+    return [own, rest, *early, *a_blocks], b_blocks
 
 
 def local(
@@ -284,6 +294,7 @@
         per += 1
     rows = experts * per
     span = 2 * length
+    tiles = length // LANES
     extra = -(-(experts + 2) // 16) * 16
     few_rows = -(-(experts + 2 + heads) // 16) * 16
     me = lax.axis_index(("exp", "tp")).astype(jnp.int32)[None]
@@ -444,11 +455,22 @@
         same = seg_col == seg_row
         for h in range(heads):
             part = slice(h * HD, (h + 1) * HD)
-            spread = jnp.broadcast_to(offsets[h : h + 1], (length, span))
-            bias = pltpu.roll(spread, length + 1, 1, stride=1, stride_axis=0)[:, :length]
+            diagonals = []
+            for d in range(2 * tiles - 1):
+                window = offsets[h : h + 1, d * LANES : (d + 2) * LANES]
+                spread = jnp.broadcast_to(window, (LANES, 2 * LANES))
+                turned = pltpu.roll(spread, LANES + 1, 1, stride=1, stride_axis=0)
+                diagonals.append(turned[:, :LANES])
+            bias = jnp.concatenate(
+                [
+                    jnp.concatenate([diagonals[bi - bj + tiles - 1] for bi in range(tiles)], axis=1)
+                    for bj in range(tiles)
+                ],
+                axis=0,
+            )
             s = jnp.where(same, mm_tn(k[part], q[part]) + bias, NEG_FILL)
             e = jnp.exp(s - jnp.max(s, axis=0, keepdims=True))
-            p = (e / jnp.sum(e, axis=0, keepdims=True)).astype(bf16)
+            p = (e * (1.0 / jnp.sum(e, axis=0, keepdims=True))).astype(bf16)
             p_refs[h][...] = p
             p_refs[h].send()
             attn_ref[part] = mm(v[part], p).astype(bf16)
@@ -569,34 +591,51 @@
         (over_experts(send), h_rows, aux, dout_rows, *d_pieces)
     )
     weights = fetch(after(me, arrived), [w_in, w_out], "expert_arguments")
-    across, *weights = lax.optimization_barrier((swap(arrived, "tp", 2), *weights))
+
+    def dout_body(me_ref, d0, d1, d2, d3, out_ref):
+        mine = me_ref[0] & (ways - 1)
+        came = (d0, d1, d2, d3)
+        for rel in range(ways):
+            pieces = []
+            for src in range(ways):
+                at = (rel ^ src) * quarter
+                pieces.append(came[src][:, at : at + quarter])
+            dout = jnp.concatenate([absolute(pieces, mine, t) for t in range(ways)], axis=1)
+            out_ref[rel * rows : (rel + 1) * rows] = dout
+
+    (douts,) = run(
+        dout_body,
+        [((ways * rows, width), bf16)],
+        (after(me, arrived), *d_pieces),
+        "douts",
+        us=0.01,
+    )
+    across, douts, *weights = lax.optimization_barrier(
+        (swap(arrived, "tp", 2), douts, *weights)
+    )
     arrived = (arrived, swap(arrived, "tp", 1), across, swap(across, "tp", 1))
 
-    def expert_body(me_ref, a0, a1, a2, a3, d0, d1, d2, d3, win_ref, wout_ref, *outs):
+    def expert_body(a0, a1, a2, a3, dout_ref, win_ref, wout_ref, *outs):
         u_ref, dy_ref, act_ref, dz_ref, kept_ref, passed_ref, sent_ref = outs
-        mine = me_ref[0] & (ways - 1)
-        douts = (d0, d1, d2, d3)
         for rel, a in enumerate((a0, a1, a2, a3)):
             part = slice(rel * rows, (rel + 1) * rows)
             u_ref[part] = a[:, 0:width]
             g = a[:, width : width + 1].astype(f32) + a[:, width + 1 : width + 2].astype(f32)
-            pieces = []
-            for src in range(ways):
-                at = (rel ^ src) * quarter
-                pieces.append(douts[src][:, at : at + quarter])
-            dout = jnp.concatenate([absolute(pieces, mine, t) for t in range(ways)], axis=1)
-            dy_ref[part] = (g * dout.astype(f32)).astype(bf16)
+            dy_ref[part] = (g * dout_ref[part].astype(f32)).astype(bf16)
         u_ref.send()
         dy_ref.send()
         u = u_ref[...]
         dy = dy_ref[...]
         z = mm(u, win_ref[0])
         c = math.sqrt(2.0 / math.pi)
-        t = jnp.tanh(c * (z + 0.044715 * z * z * z))
-        act = (0.5 * z * (1.0 + t)).astype(bf16)
+        z2 = z * z
+        t = jnp.tanh(z * (c + (0.044715 * c) * z2))
+        half = 0.5 + 0.5 * t
+        wide_act = z * half
+        act = wide_act.astype(bf16)
         act_ref[...] = act
         act_ref.send()
-        slope = 0.5 * (1.0 + t) + 0.5 * z * (1.0 - t * t) * (c * (1.0 + 3 * 0.044715 * z * z))
+        slope = half + wide_act * (1.0 - t) * (c + (3 * 0.044715 * c) * z2)
         dact = mm_nt(dy, wout_ref[0])
         dot = jnp.sum(dact * act.astype(f32), axis=-1, keepdims=True)
         dz = (dact * slope).astype(bf16)
@@ -619,7 +658,7 @@
             ((rows, width + LANES), bf16),
             ((2, rows, width + LANES), bf16),
         ],
-        (me, *arrived, *d_pieces, *weights),
+        (*arrived, douts, *weights),
         "expert",
         us=4.0,
         limit=24,
@@ -743,7 +782,7 @@
         wo = wo_ref[...]
         da = mm_nt(wo, do).astype(bf16)
         hot = bucket_hot(bucket_ref, bucket_held, f32)
-        flip = (iota((length, length), 0) + iota((length, length), 1) == length - 1).astype(bf16)
+        flip = (iota((LANES, LANES), 0) + iota((LANES, LANES), 1) == LANES - 1).astype(bf16)
         tables = []
         for h in range(heads):
             part = slice(h * HD, (h + 1) * HD)
@@ -755,10 +794,22 @@
             ds = (p * (dp - inner)).astype(bf16)
             dq_ref[part] = mm(k_ref[part], ds).astype(bf16)
             dk_ref[part] = mm_nt(q_ref[part], ds).astype(bf16)
-            flipped = mm(flip, ds)
-            flipped = jnp.concatenate([flipped, jnp.zeros_like(flipped)], axis=1)
-            offsets = pltpu.roll(flipped, 0, 1, stride=1, stride_axis=0)
-            offsets = jnp.sum(offsets, axis=0, keepdims=True)
+            rows_of = [mm(flip, ds[bj * LANES : (bj + 1) * LANES]) for bj in range(tiles)]
+            offsets = jnp.zeros((1, span), f32)
+            for d in range(2 * tiles - 1):
+                block = jnp.zeros((LANES, LANES), f32)
+                for bj in range(tiles):
+                    bi = bj + d - tiles + 1
+                    if 0 <= bi < tiles:
+                        block = block + rows_of[bj][:, bi * LANES : (bi + 1) * LANES]
+                block = jnp.concatenate([block, jnp.zeros_like(block)], axis=1)
+                block = pltpu.roll(block, 0, 1, stride=1, stride_axis=0)
+                block = [jnp.sum(block, axis=0, keepdims=True)]
+                if d:
+                    block = [jnp.zeros((1, d * LANES), f32), *block]
+                if d < 2 * tiles - 2:
+                    block = [*block, jnp.zeros((1, span - (d + 2) * LANES), f32)]
+                offsets = offsets + jnp.concatenate(block, axis=1)
             tables.append(mm_nt(offsets, hot, HIGHEST))
         n1 = n1_ref[...]
         gq = mm_nt(dq_ref[...], n1)
@@ -918,11 +969,20 @@
             extras["few"] = few + swap(few, "tp", 1)
             for rel in range(1, ways):
                 extras["lo%d" % rel] = swap(held["lo%d" % rel], "tp", rel)
+        if phase == last:
+            extras["few_other"] = swap(held["few"], "tp", 2)
+            (extras["layer_out"],) = run(
+                out_body,
+                [((quarter, length), bf16)],
+                (Far(dest_far), *[held["lo%d" % rel] for rel in range(ways)]),
+                "layer_out",
+                us=12,
+            )
             (extras["grad_tokens"],) = run(
                 tokens_body,
                 [((quarter, length), bf16)],
                 (
-                    me,
+                    after(me, held["few"]),
                     dn1_kept,
                     held["dn1_beside"],
                     held["dn1_across"],
@@ -934,19 +994,10 @@
                 "tokens_back",
                 us=12,
             )
-        if phase == last:
-            extras["few_other"] = swap(held["few"], "tp", 2)
-            (extras["layer_out"],) = run(
-                out_body,
-                [((quarter, length), bf16)],
-                (Far(dest_far), *[held["lo%d" % rel] for rel in range(ways)]),
-                "layer_out",
-                us=12,
-            )
         names = list(extras)
-        got = lax.optimization_barrier((*came, *[extras[n] for n in names]))
-        held.update(zip(names, got[len(came) :]))
-        return got[: len(came)]
+        got = lax.optimization_barrier((*[extras[n] for n in names], *came))
+        held.update(zip(names, got))
+        return got[len(names) :]
 
     a_blocks, b_blocks = two_chains(
         others[3 : 3 + first_a], others[3 + first_a :], order_a, order_b, few_rows, beside
@@ -955,8 +1006,8 @@
     grad_in, grad_out = held["grad_in"], held["grad_out"]
 
     def unpack_body(me_ref, few_ref, other_ref, *others):
-        a_ins, b_ins = others[:first_a], others[first_a : first_a + first_b]
-        *results, a_ref, b_ref = others[first_a + first_b :]
+        a_ins, b_ins = others[: len(a_blocks)], others[len(a_blocks) :][:first_b]
+        *results, a_ref, b_ref = others[len(a_blocks) + first_b :]
         gq_ref, gk_ref, gv_ref, go_ref, router_ref, g1_ref, g2_ref, table_ref = results
         mine = me_ref[0] & (ways - 1)
         place = me_ref[0] >> shift
@@ -964,10 +1015,12 @@
             (order_a, a_ref, a_ins, chunk_a, 0),
             (order_b, b_ref, b_ins, chunk_b, a_rows),
         ):
-            each = owners // len(ins)
-            for at in range(owners):
-                line = at % each
-                ref[rel_of(at, order) ^ place] = ins[at // each][line * chunk : (line + 1) * chunk]
+            at = 0
+            for piece in ins:
+                for line in range(piece.shape[0] // chunk):
+                    low = line * chunk
+                    ref[rel_of(at, order) ^ place] = piece[low : low + chunk]
+                    at += 1
             for c in range(owners):
                 low = start + c * chunk
                 which, low = low // here, low % here

time: 157 us -> 154 us (0.981)
  waiting for transfers between devices: 53.9 us -> 49.7 us
    ppermute x47 -> x48, waiting for transfers between devices: 41.1 us -> 36.9 us  [swap(): return lax.ppermute(value, axis, [(i, i ^ mask) for i in range(size)])]
    pallas_call x15 -> x16, Pallas kernels: 33.9 us -> 35.1 us  [run(): pl.pallas_call(wrapped, out_shape=[pltpu.HBM(o[0], o[1]) if len(o) == 3 e...]
    ppermute x47 -> x48, starting transfers between devices: 41.4 us -> 42 us  [swap(): return lax.ppermute(value, axis, [(i, i ^ mask) for i in range(size)])]
  transfers between devices with their start and end apart: 51 -> 52, of which waited for: 21 -> 22; matrix products, arithmetic and copies ran while one was open for 1% -> 1% of each run, Pallas kernels for 18% -> 19%
where the time goes in v5:
time: 154 us
  starting transfers between devices  60.9 us (40%)
  waiting for transfers between devices  49.7 us (32%)
  Pallas kernels  39.9 us (26%)
  other arithmetic  1.79 us (1%)
    ppermute x48, starting transfers between devices, swap(): return lax.ppermute(value, axis, [(i, i ^ mask) for i in range(size)])  42 us
    ppermute x48, waiting for transfers between devices, swap(): return lax.ppermute(value, axis, [(i, i ^ mask) for i in range(size)])  36.9 us
    pallas_call x16, Pallas kernels, run(): pl.pallas_call(wrapped, out_shape=[pltpu.HBM(o[0], o[1]) if len(o) == 3 e...  35.1 us
    all_to_all x4, starting transfers between devices, over_experts(): lax.all_to_all(blocks, 'exp', split_axis=0, concat_axis=0, tiled=True)  18.9 us
    all_to_all x4, waiting for transfers between devices, over_experts(): lax.all_to_all(blocks, 'exp', split_axis=0, concat_axis=0, tiled=True)  12.8 us
    pallas_call x3, Pallas kernels, fetch(): pl.pallas_call(body, out_shape=[jax.ShapeDtypeStruct(v.shape, v.dtype) fo...  4.8 us
  transfers between devices with their start and end apart: 52, of which 22 were waited for; matrix products, arithmetic and copies ran while one was open for 1% of the time, Pallas kernels for 19%

profile of v5, /device:TPU:0, one launch (start us, length us, event | category | flops | bytes accessed | tf_op | source)
XLA Modules:
  0.0 153.6 jit_solution(10437623608582338883)
XLA Ops:
  0.6 3.0 %collective-permute-start.1 = (bf16[192,384]{1,0:T(8,128)(2,1)}, bf16[192,384]{1,0:T(8,128)(2,1)S(1)}, u32[]{:S(2)}, u32[]{:S(2)}) collective-permute-start(bf16[192,384]{1,0:T(8,128)(2,1)} %bitcast.72), channel_id=1, source_target_pairs={{0,2},{1,3},{2,0},{3,1},{4,6},{5,7},{6,4},{7,5},{8,10},{9,11},{10,... | collective-permute-start | bytes 442376 | tf_op jit(solution)/shard_map/ppermute | solution.py:143
  6.3 1.4 collective-permute-done.4.refs_8_
  8.3 1.4 slots.1
  9.8 4.8 %attend.1 = (bf16[16,768]{1,0:T(8,128)(2,1)S(1)}, bf16[16,768]{1,0:T(8,128)(2,1)}, s32[1,384]{1,0:T(1,128)}, f32[1,384]{1,0:T(1,128)}, bf16[768,384]{1,0:T(8,128...) custom-call(s32[1]{0:T(128)} %bitcast.refs_0_.token_ref, ...), custom_call_target="tpu_custom_call" | custom-call | flops 11000000 | bytes 4900032 | tf_op jit(solution)/shard_map/attend/pallas_call | solution.py:99
  16.5 1.7 %collective-permute-start.7 = (bf16[128,768]{1,0:T(8,128)(2,1)S(1)}, bf16[128,768]{1,0:T(8,128)(2,1)S(1)}, u32[]{:S(2)}, u32[]{:S(2)}) collective-permute-start(bf16[128,768]{1,0:T(8,128)(2,1)S(1)} %fusion.6), channel_id=1, source_target_pairs={{0,2},{1,3},{2,0},{3,1},{4,6},{5,7},{6,4},{7,5},{8,10},{9,11},{10,... | collective-permute-start | bytes 589832 | tf_op jit(solution)/shard_map/ppermute | solution.py:143
  19.0 5.8 %all-to-all-start = ((bf16[8,16,768]{2,1,0:T(8,128)(2,1)}), bf16[8,16,768]{2,1,0:T(8,128)(2,1)S(1)}, u32[]{:S(2)}, u32[]{:S(2)}) async-start(bf16[8,16,768]{2,1,0:T(8,128)(2,1)} %bitcast.10), calls=%async_computation | async-start | bytes 393216 | tf_op jit(solution)/shard_map/all_to_all | solution.py:372
  24.8 1.5 %route.1 = bf16[128,896]{1,0:T(8,128)(2,1)} custom-call(bf16[128,768]{1,0:T(8,128)(2,1)S(1)} %get-tuple-element.187.refs_0_.refs_1_, bf16[2,128,768]{2,1,0:T(8,128)(2,1)S(1)} %collective-permute-done.6.refs_1_.refs_2_, bf16[128,768]{1,0:T(8,128)(2,1)S(1)} %collective-permute-done.7.refs_2_.refs_3_, bf16[128,768]{1,0:T(8,128)(2,1)S(1)} %get-tuple-element.190.refs_3_.refs_4_, ...), custom_call_target="tpu_custom_call" | custom-call | flops 4400000000 | bytes 1236992 | tf_op jit(solution)/shard_map/route/pallas_call | solution.py:99
  26.3 6.7 %all-to-all-done = bf16[8,16,768]{2,1,0:T(8,128)(2,1)S(1)} async-done(((bf16[8,16,768]{2,1,0:T(8,128)(2,1)}), bf16[8,16,768]{2,1,0:T(8,128)(2,1)S(1)}, u32[]{:S(2)}, u32[]{:S(2)}) %all-to-all-start) | async-done | bytes 196640 | tf_op jit(solution)/shard_map/all_to_all | solution.py:372
  33.5 3.4 %all-to-all-start.1 = ((bf16[8,16,896]{2,1,0:T(8,128)(2,1)}), bf16[8,16,896]{2,1,0:T(8,128)(2,1)S(1)}, u32[]{:S(2)}, u32[]{:S(2)}) async-start(bf16[8,16,896]{2,1,0:T(8,128)(2,1)} %bitcast.12), calls=%async_computation.1 | async-start | bytes 458752 | tf_op jit(solution)/shard_map/all_to_all | solution.py:372
  37.0 1.6 %collective-permute-done.12.refs_3_ = bf16[128,768]{1,0:T(8,128)(2,1)S(1)} collective-permute-done((bf16[128,768]{1,0:T(8,128)(2,1)S(1)}, bf16[128,768]{1,0:T(8,128)(2,1)S(1)}, u32[]{:S(2)}, u32[]{:S(2)}) %collective-permute-start.12) | collective-permute-done | bytes 196640 | tf_op jit(solution)/shard_map/ppermute | solution.py:143
  39.4 1.5 collective-permute-start.9
  40.9 1.6 %collective-permute-done.10.refs_9_ = bf16[128,192]{1,0:T(8,128)(2,1)S(1)} collective-permute-done((bf16[128,192]{1,0:T(8,128)(2,1)S(1)}, bf16[128,192]{1,0:T(8,128)(2,1)S(1)}, u32[]{:S(2)}, u32[]{:S(2)}) %collective-permute-start.10) | collective-permute-done | bytes 49184 | tf_op jit(solution)/shard_map/ppermute | solution.py:143
  42.5 2.1 %collective-permute-done.9.refs_8_ = bf16[128,192]{1,0:T(8,128)(2,1)S(1)} collective-permute-done((bf16[128,192]{1,0:T(8,128)(2,1)S(1)}, bf16[128,192]{1,0:T(8,128)(2,1)S(1)}, u32[]{:S(2)}, u32[]{:S(2)}) %collective-permute-start.9) | collective-permute-done | bytes 49184 | tf_op jit(solution)/shard_map/ppermute | solution.py:143
  44.6 1.7 %state.1 = (f32[128,768]{1,0:T(8,128)}, f32[128,128]{1,0:T(8,128)}, bf16[128,768]{1,0:T(8,128)(2,1)}) custom-call(s32[1]{0:T(128)} %bitcast.refs_0_.token_ref, bf16[128,768]{1,0:T(8,128)(2,1)S(1)} %get-tuple-element.187.refs_0_.refs_1_, bf16[2,128,768]{2,1,0:T(8,128)(2,1)S(1)} %collective-permute-done.6.refs_1_.refs_2_, ...), custom_call_target="tpu_custom_call" | custom-call | flops 11000000 | bytes 1859588 | tf_op jit(solution)/shard_map/state/pallas_call | solution.py:99
  47.0 1.6 %expert_arguments.1 = (bf16[1,768,768]{2,1,0:T(8,128)(2,1)S(1)}, bf16[1,768,768]{2,1,0:T(8,128)(2,1)S(1)}) custom-call(s32[1]{0:T(128)} %bitcast.refs_0_.token_ref, bf16[1,768,768]{2,1,0:T(8,128)(2,1)} %refs_0_.2, bf16[1,768,768]{2,1,0:T(8,128)(2,1)} %refs_2_.3), custom_call_target="tpu_custom_call" | custom-call | tf_op jit(solution)/shard_map/expert_arguments/pallas_call | solution.py:130
  48.6 1.6 %douts.1.refs_4_ = bf16[512,768]{1,0:T(8,128)(2,1)S(1)} custom-call(s32[1]{0:T(128)} %bitcast.refs_0_.token_ref, bf16[128,768]{1,0:T(8,128)(2,1)S(1)} %bitcast.66, bf16[128,768]{1,0:T(8,128)(2,1)S(1)} %collective-permute-done.11.refs_2_, bf16[128,768]{1,0:T(8,128)(2,1)S(1)} %collective-permute-done.12.refs_3_, ...), custom_call_target="tpu_custom_call" | custom-call | flops 11000000 | bytes 1572868 | tf_op jit(solution)/shard_map/douts/pallas_call | solution.py:99
  50.3 3.1 %collective-permute-done.15.refs_2_ = bf16[128,896]{1,0:T(8,128)(2,1)S(1)} collective-permute-done((bf16[128,896]{1,0:T(8,128)(2,1)S(1)}, bf16[128,896]{1,0:T(8,128)(2,1)S(1)}, u32[]{:S(2)}, u32[]{:S(2)}) %collective-permute-start.15) | collective-permute-done | bytes 229408 | tf_op jit(solution)/shard_map/ppermute | solution.py:143
  53.4 1.5 collective-permute-done.16.refs_3_
  54.8 3.4 %expert.1 = (bf16[512,768]{1,0:T(8,128)(2,1)}, bf16[512,768]{1,0:T(8,128)(2,1)}, bf16[512,768]{1,0:T(8,128)(2,1)}, bf16[512,768]{1,0:T(8,128)(2,1)}, bf16[128,89...) custom-call(bf16[128,896]{1,0:T(8,128)(2,1)S(1)} %bitcast.69, ...), custom_call_target="tpu_custom_call" | custom-call | flops 4400000000 | bytes 8126464 | tf_op jit(solution)/shard_map/expert/pallas_call | solution.py:99
  58.5 1.7 %collective-permute-done.17 = bf16[2,128,896]{2,1,0:T(8,128)(2,1)S(1)} collective-permute-done((bf16[2,128,896]{2,1,0:T(8,128)(2,1)S(1)}, bf16[2,128,896]{2,1,0:T(8,128)(2,1)S(1)}, u32[]{:S(2)}, u32[]{:S(2)}) %collective-permute-start.17) | collective-permute-done | bytes 458784 | tf_op jit(solution)/shard_map/ppermute | solution.py:143
  60.7 1.9 %value.1 = (bf16[128,768]{1,0:T(8,128)(2,1)S(1)}, bf16[128,768]{1,0:T(8,128)(2,1)S(1)}, bf16[2,128,768]{2,1,0:T(8,128)(2,1)S(1)}) custom-call(s32[1]{0:T(128)} %bitcast.refs_0_.token_ref, bf16[512,768]{1,0:T(8,128)(2,1)} %get-tuple-element.216.refs_1_.refs_3_, bf16[1,768,768]{2,1,0:T(8,128)(2,1)S(1)} %copy-done), custom_call_target="tpu_custom_call" | custom-call | flops 880000000 | bytes 2752516 | tf_op jit(solution)/shard_map/value/pallas_call | solution.py:99
  62.7 5.2 %collective-permute-done.19 = bf16[128,896]{1,0:T(8,128)(2,1)S(1)} collective-permute-done((bf16[128,896]{1,0:T(8,128)(2,1)S(1)}, bf16[128,896]{1,0:T(8,128)(2,1)S(1)}, u32[]{:S(2)}, u32[]{:S(2)}) %collective-permute-start.19) | collective-permute-done | bytes 229408 | tf_op jit(solution)/shard_map/ppermute | solution.py:143
  69.2 6.1 %all-to-all-start.3 = ((bf16[8,16,896]{2,1,0:T(8,128)(2,1)}), bf16[8,16,896]{2,1,0:T(8,128)(2,1)S(1)}, u32[]{:S(2)}, u32[]{:S(2)}) async-start(bf16[8,16,896]{2,1,0:T(8,128)(2,1)} %bitcast.24), calls=%async_computation.3 | async-start | bytes 458752 | tf_op jit(solution)/shard_map/all_to_all | solution.py:372
  77.2 6.2 %all-to-all-done.3 = bf16[8,16,896]{2,1,0:T(8,128)(2,1)S(1)} async-done(((bf16[8,16,896]{2,1,0:T(8,128)(2,1)}), bf16[8,16,896]{2,1,0:T(8,128)(2,1)S(1)}, u32[]{:S(2)}, u32[]{:S(2)}) %all-to-all-start.3) | async-done | bytes 229408 | tf_op jit(solution)/shard_map/all_to_all | solution.py:372
  84.6 3.6 %all-to-all-start.2 = ((bf16[8,16,768]{2,1,0:T(8,128)(2,1)}), bf16[8,16,768]{2,1,0:T(8,128)(2,1)S(1)}, u32[]{:S(2)}, u32[]{:S(2)}) async-start(bf16[8,16,768]{2,1,0:T(8,128)(2,1)} %bitcast.22), calls=%async_computation.2 | async-start | bytes 393216 | tf_op jit(solution)/shard_map/all_to_all | solution.py:372
  88.3 2.0 %attend_again.1 = (bf16[192,768]{1,0:T(8,128)(2,1)S(1)}, bf16[192,384]{1,0:T(8,128)(2,1)S(1)}, bf16[192,384]{1,0:T(8,128)(2,1)S(1)}, bf16[192,384]{1,0:T(8,128)(...) custom-call(s32[1]{0:T(128)} %bitcast.refs_0_.token_ref, ...), custom_call_target="tpu_custom_call" | custom-call | tf_op jit(solution)/shard_map/attend_again/pallas_call | solution.py:130
  92.0 5.1 %attend_back.1 = (bf16[192,384]{1,0:T(8,128)(2,1)S(1)}, bf16[208,384]{1,0:T(8,128)(2,1)S(1)}, bf16[208,384]{1,0:T(8,128)(2,1)S(1)}, bf16[2,208,384]{2,1,0:T(8,12...) custom-call(s32[1]{0:T(128)} %bitcast.refs_0_.token_ref, ...), custom_call_target="tpu_custom_call" | custom-call | flops 11000000 | bytes 6173184 | tf_op jit(solution)/shard_map/attend_back/pallas_call | solution.py:99
  97.5 1.7 %collective-permute-start.25 = (bf16[80,768]{1,0:T(8,128)(2,1)S(1)}, bf16[80,768]{1,0:T(8,128)(2,1)S(1)}, u32[]{:S(2)}, u32[]{:S(2)}) collective-permute-start(bf16[80,768]{1,0:T(8,128)(2,1)S(1)} %get-tuple-element.295), channel_id=1, source_target_pairs={{0,8},{4,12},{8,0},{12,4},{16,24},{20,28},{24,16},{28,20},{1,9},{5... | collective-permute-start | bytes 368648 | tf_op jit(solution)/shard_map/ppermute | solution.py:143
  99.2 2.4 %collective-permute-start.26 = (bf16[80,768]{1,0:T(8,128)(2,1)S(1)}, bf16[80,768]{1,0:T(8,128)(2,1)S(1)}, u32[]{:S(2)}, u32[]{:S(2)}) collective-permute-start(bf16[80,768]{1,0:T(8,128)(2,1)S(1)} %get-tuple-element.296), channel_id=1, source_target_pairs={{0,16},{4,20},{8,24},{12,28},{16,0},{20,4},{24,8},{28,12},{1,17},{... | collective-permute-start | bytes 368648 | tf_op jit(solution)/shard_map/ppermute | solution.py:143
  101.9 1.7 %collective-permute-start.28 = (bf16[256,768]{1,0:T(8,128)(2,1)S(1)}, bf16[256,768]{1,0:T(8,128)(2,1)S(1)}, u32[]{:S(2)}, u32[]{:S(2)}) collective-permute-start(bf16[256,768]{1,0:T(8,128)(2,1)S(1)} %get-tuple-element.298), channel_id=1, source_target_pairs={{0,4},{4,0},{8,12},{12,8},{16,20},{20,16},{24,28},{28,24},{1,5},{5... | collective-permute-start | bytes 1179656 | tf_op jit(solution)/shard_map/ppermute | solution.py:143
  103.6 4.9 %expert_weights.1 = (bf16[1,768,768]{2,1,0:T(8,128)(2,1)}, bf16[1,768,768]{2,1,0:T(8,128)(2,1)}) custom-call(s32[1]{0:T(128)} %bitcast.refs_0_.token_ref, bf16[512,768]{1,0:T(8,128)(2,1)} %get-tuple-element.290.refs_1_, bf16[512,768]{1,0:T(8,128)(2,1)} %get-tuple-element.291.refs_2_, bf16[512,768]{1,0:T(8,128)(2,1)} %get-tuple-element.216.refs_1_.refs_3_, ...), custom_call_target="tpu_custom_call" | custom-call | flops 13200000000 | bytes 5505028 | tf_op jit(solution)/shard_map/expert_weights/pallas_call | solution.py:99
  108.5 3.0 %collective-permute-done.26 = bf16[80,768]{1,0:T(8,128)(2,1)S(1)} collective-permute-done((bf16[80,768]{1,0:T(8,128)(2,1)S(1)}, bf16[80,768]{1,0:T(8,128)(2,1)S(1)}, u32[]{:S(2)}, u32[]{:S(2)}) %collective-permute-start.26) | collective-permute-done | bytes 122912 | tf_op jit(solution)/shard_map/ppermute | solution.py:143
  112.3 1.7 %collective-permute-start.30 = (bf16[48,768]{1,0:T(8,128)(2,1)S(1)}, bf16[48,768]{1,0:T(8,128)(2,1)S(1)}, u32[]{:S(2)}, u32[]{:S(2)}) collective-permute-start(bf16[48,768]{1,0:T(8,128)(2,1)S(1)} %concatenate.16), channel_id=1, source_target_pairs={{0,4},{4,0},{8,12},{12,8},{16,20},{20,16},{24,28},{28,24},{1,5},{5... | collective-permute-start | bytes 221192 | tf_op jit(solution)/shard_map/ppermute | solution.py:143
  114.1 1.6 %collective-permute-start.29 = (bf16[208,384]{1,0:T(8,128)(2,1)S(1)}, bf16[208,384]{1,0:T(8,128)(2,1)S(1)}, u32[]{:S(2)}, u32[]{:S(2)}) collective-permute-start(bf16[208,384]{1,0:T(8,128)(2,1)S(1)} %bitcast_add_fusion), channel_id=1, source_target_pairs={{0,2},{1,3},{2,0},{3,1},{4,6},{5,7},{6,4},{7,5},{8,10},{9,11},{10,... | collective-permute-start | bytes 479240 | tf_op jit(solution)/shard_map/ppermute | solution.py:143
  115.8 3.4 %collective-permute-start.33 = (bf16[64,768]{1,0:T(8,128)(2,1)S(1)}, bf16[64,768]{1,0:T(8,128)(2,1)S(1)}, u32[]{:S(2)}, u32[]{:S(2)}) collective-permute-start(bf16[64,768]{1,0:T(8,128)(2,1)S(1)} %get-tuple-element.350), channel_id=1, source_target_pairs={{0,24},{4,28},{8,16},{12,20},{16,8},{20,12},{24,0},{28,4},{1,25},{... | collective-permute-start | bytes 294920 | tf_op jit(solution)/shard_map/ppermute | solution.py:143
  120.3 1.4 layer_rows.1
  121.7 1.5 %collective-permute-done.33 = bf16[64,768]{1,0:T(8,128)(2,1)S(1)} collective-permute-done((bf16[64,768]{1,0:T(8,128)(2,1)S(1)}, bf16[64,768]{1,0:T(8,128)(2,1)S(1)}, u32[]{:S(2)}, u32[]{:S(2)}) %collective-permute-start.33) | collective-permute-done | bytes 98336 | tf_op jit(solution)/shard_map/ppermute | solution.py:143
  123.2 2.8 %collective-permute-done.32 = bf16[64,768]{1,0:T(8,128)(2,1)S(1)} collective-permute-done((bf16[64,768]{1,0:T(8,128)(2,1)S(1)}, bf16[64,768]{1,0:T(8,128)(2,1)S(1)}, u32[]{:S(2)}, u32[]{:S(2)}) %collective-permute-start.32) | collective-permute-done | bytes 98336 | tf_op jit(solution)/shard_map/ppermute | solution.py:143
  127.6 2.4 %collective-permute-start.42 = (bf16[64,768]{1,0:T(8,128)(2,1)S(1)}, bf16[64,768]{1,0:T(8,128)(2,1)S(1)}, u32[]{:S(2)}, u32[]{:S(2)}) collective-permute-start(bf16[64,768]{1,0:T(8,128)(2,1)S(1)} %add_convert_fusion.2.refs_3_), channel_id=1, source_target_pairs={{0,24},{4,28},{8,16},{12,20},{16,8},{20,12},{24,0},{28,4},{1,25},{... | collective-permute-start | bytes 294920 | tf_op jit(solution)/shard_map/ppermute | solution.py:143
  130.4 1.6 %collective-permute-start.40 = (bf16[64,768]{1,0:T(8,128)(2,1)S(1)}, bf16[64,768]{1,0:T(8,128)(2,1)S(1)}, u32[]{:S(2)}, u32[]{:S(2)}) collective-permute-start(bf16[64,768]{1,0:T(8,128)(2,1)S(1)} %add_convert_fusion.2.refs_3_), channel_id=1, source_target_pairs={{0,8},{4,12},{8,0},{12,4},{16,24},{20,28},{24,16},{28,20},{1,9},{5... | collective-permute-start | bytes 294920 | tf_op jit(solution)/shard_map/ppermute | solution.py:143
  132.0 1.5 collective-permute-start.38
  133.6 3.8 %collective-permute-done.37.refs_4_ = bf16[192,128]{1,0:T(8,128)(2,1)S(1)} collective-permute-done((bf16[192,128]{1,0:T(8,128)(2,1)S(1)}, bf16[192,128]{1,0:T(8,128)(2,1)S(1)}, u32[]{:S(2)}, u32[]{:S(2)}) %collective-permute-start.37) | collective-permute-done | bytes 49184 | tf_op jit(solution)/shard_map/ppermute | solution.py:143
  138.4 1.5 collective-permute-start.43
  139.9 2.4 %collective-permute-start.46 = (bf16[64,768]{1,0:T(8,128)(2,1)S(1)}, bf16[64,768]{1,0:T(8,128)(2,1)S(1)}, u32[]{:S(2)}, u32[]{:S(2)}) collective-permute-start(bf16[64,768]{1,0:T(8,128)(2,1)S(1)} %pad_maximum_fusion.refs_7_), channel_id=1, source_target_pairs={{0,24},{4,28},{8,16},{12,20},{16,8},{20,12},{24,0},{28,4},{1,25},{... | collective-permute-start | bytes 294920 | tf_op jit(solution)/shard_map/ppermute | solution.py:143
  142.4 2.0 %collective-permute-start.44 = (bf16[64,768]{1,0:T(8,128)(2,1)S(1)}, bf16[64,768]{1,0:T(8,128)(2,1)S(1)}, u32[]{:S(2)}, u32[]{:S(2)}) collective-permute-start(bf16[64,768]{1,0:T(8,128)(2,1)S(1)} %pad_maximum_fusion.refs_7_), channel_id=1, source_target_pairs={{0,8},{4,12},{8,0},{12,4},{16,24},{20,28},{24,16},{28,20},{1,9},{5... | collective-permute-start | bytes 294920 | tf_op jit(solution)/shard_map/ppermute | solution.py:143
  144.4 1.6 %collective-permute-start.47 = (bf16[192,768]{1,0:T(8,128)(2,1)S(1)}, bf16[192,768]{1,0:T(8,128)(2,1)S(1)}, u32[]{:S(2)}, u32[]{:S(2)}) collective-permute-start(bf16[192,768]{1,0:T(8,128)(2,1)S(1)} %constant_dynamic-update-slice_fusion.refs_4_), channel_id=1, source_target_pairs={{0,4},{4,0},{8,12},{12,8},{16,20},{20,16},{24,28},{28,24},{1,5},{5... | collective-permute-start | bytes 884744 | tf_op jit(solution)/shard_map/ppermute | solution.py:143
  146.0 1.7 %layer_out.1 = bf16[192,384]{1,0:T(8,128)(2,1)} custom-call(s32[1,384]{1,0:T(1,128)} %get-tuple-element.227.refs_4_.refs_0_, bf16[192,128]{1,0:T(8,128)(2,1)S(1)} %get-tuple-element.319.refs_1_, bf16[192,128]{1,0:T(8,128)(2,1)S(1)} %collective-permute-done.35.refs_2_, bf16[192,128]{1,0:T(8,128)(2,1)S(1)} %collective-permute-done.36.refs_3_, ...), custom_call_target="tpu_custom_call" | custom-call | flops 13200000000 | bytes 345600 | tf_op jit(solution)/shard_map/layer_out/pallas_call | solution.py:99
  147.6 2.0 %tokens_back.1 = bf16[192,384]{1,0:T(8,128)(2,1)} custom-call(s32[1]{0:T(128)} %bitcast.refs_0_.token_ref, bf16[208,384]{1,0:T(8,128)(2,1)S(1)} %get-tuple-element.324.refs_1_, bf16[2,208,384]{2,1,0:T(8,128)(2,1)S(1)} %collective-permute-done.24.refs_2_, bf16[208,384]{1,0:T(8,128)(2,1)S(1)} %collective-permute-done.29.refs_3_, ...), custom_call_target="tpu_custom_call" | custom-call | flops 13200000000 | bytes 1107460 | tf_op jit(solution)/shard_map/tokens_back/pallas_call | solution.py:99
  (115 shorter events, 24.5 us)
Async XLA Ops:
  0.6 7.5 %collective-permute-start.1 = (bf16[192,384]{1,0:T(8,128)(2,1)}, bf16[192,384]{1,0:T(8,128)(2,1)S(1)}, u32[]{:S(2)}, u32[]{:S(2)}) collective-permute-start(bf16[192,384]{1,0:T(8,128)(2,1)} %bitcast.72), channel_id=1, source_target_pairs={{0,2},{1,3},{2,0},{3,1},{4,6},{5,7},{6,4},{7,5},{8,10},{9,11},{10,... | collective-permute-start | bytes 442376 | tf_op jit(solution)/shard_map/ppermute | solution.py:143
  4.4 3.3 %collective-permute-start.4 = (bf16[16,192]{1,0:T(8,128)(2,1)S(1)}, bf16[16,192]{1,0:T(8,128)(2,1)S(1)}, u32[]{:S(2)}, u32[]{:S(2)}) collective-permute-start(bf16[16,192]{1,0:T(8,128)(2,1)S(1)} %small.1.refs_5_), channel_id=1, source_target_pairs={{0,3},{1,2},{2,1},{3,0},{4,7},{5,6},{6,5},{7,4},{8,11},{9,10},{10,... | collective-permute-start | bytes 18440 | tf_op jit(solution)/shard_map/ppermute | solution.py:143
  4.5 3.7 %collective-permute-start.3 = (bf16[16,192]{1,0:T(8,128)(2,1)S(1)}, bf16[16,192]{1,0:T(8,128)(2,1)S(1)}, u32[]{:S(2)}, u32[]{:S(2)}) collective-permute-start(bf16[16,192]{1,0:T(8,128)(2,1)S(1)} %small.1.refs_5_), channel_id=1, source_target_pairs={{0,2},{1,3},{2,0},{3,1},{4,6},{5,7},{6,4},{7,5},{8,10},{9,11},{10,... | collective-permute-start | bytes 18440 | tf_op jit(solution)/shard_map/ppermute | solution.py:143
  5.6 2.5 %collective-permute-start.2 = (bf16[16,192]{1,0:T(8,128)(2,1)S(1)}, bf16[16,192]{1,0:T(8,128)(2,1)S(1)}, u32[]{:S(2)}, u32[]{:S(2)}) collective-permute-start(bf16[16,192]{1,0:T(8,128)(2,1)S(1)} %small.1.refs_5_), channel_id=1, source_target_pairs={{0,1},{1,0},{2,3},{3,2},{4,5},{5,4},{6,7},{7,6},{8,9},{9,8},{10,11... | collective-permute-start | bytes 18440 | tf_op jit(solution)/shard_map/ppermute | solution.py:143
  6.3 3.4 %collective-permute-start = (bf16[192,384]{1,0:T(8,128)(2,1)}, bf16[192,384]{1,0:T(8,128)(2,1)S(1)}, u32[]{:S(2)}, u32[]{:S(2)}) collective-permute-start(bf16[192,384]{1,0:T(8,128)(2,1)} %bitcast.73), channel_id=1, source_target_pairs={{0,1},{1,0},{2,3},{3,2},{4,5},{5,4},{6,7},{7,6},{8,9},{9,8},{10,11... | collective-permute-start | bytes 442376 | tf_op jit(solution)/shard_map/ppermute | solution.py:143
  16.5 8.3 %collective-permute-start.7 = (bf16[128,768]{1,0:T(8,128)(2,1)S(1)}, bf16[128,768]{1,0:T(8,128)(2,1)S(1)}, u32[]{:S(2)}, u32[]{:S(2)}) collective-permute-start(bf16[128,768]{1,0:T(8,128)(2,1)S(1)} %fusion.6), channel_id=1, source_target_pairs={{0,2},{1,3},{2,0},{3,1},{4,6},{5,7},{6,4},{7,5},{8,10},{9,11},{10,... | collective-permute-start | bytes 589832 | tf_op jit(solution)/shard_map/ppermute | solution.py:143
  19.0 14.0 %all-to-all-start = ((bf16[8,16,768]{2,1,0:T(8,128)(2,1)}), bf16[8,16,768]{2,1,0:T(8,128)(2,1)S(1)}, u32[]{:S(2)}, u32[]{:S(2)}) async-start(bf16[8,16,768]{2,1,0:T(8,128)(2,1)} %bitcast.10), calls=%async_computation | async-start | bytes 393216 | tf_op jit(solution)/shard_map/all_to_all | solution.py:372
  33.0 5.7 %collective-permute-start.12 = (bf16[128,768]{1,0:T(8,128)(2,1)S(1)}, bf16[128,768]{1,0:T(8,128)(2,1)S(1)}, u32[]{:S(2)}, u32[]{:S(2)}) collective-permute-start(bf16[128,768]{1,0:T(8,128)(2,1)S(1)} %bitcast.64), channel_id=1, source_target_pairs={{0,2},{1,3},{2,0},{3,1},{4,6},{5,7},{6,4},{7,5},{8,10},{9,11},{10,... | collective-permute-start | bytes 589832 | tf_op jit(solution)/shard_map/ppermute | solution.py:143
  33.5 12.8 %all-to-all-start.1 = ((bf16[8,16,896]{2,1,0:T(8,128)(2,1)}), bf16[8,16,896]{2,1,0:T(8,128)(2,1)S(1)}, u32[]{:S(2)}, u32[]{:S(2)}) async-start(bf16[8,16,896]{2,1,0:T(8,128)(2,1)} %bitcast.12), calls=%async_computation.1 | async-start | bytes 458752 | tf_op jit(solution)/shard_map/all_to_all | solution.py:372
  36.9 9.3 %collective-permute-start.11 = (bf16[128,768]{1,0:T(8,128)(2,1)S(1)}, bf16[128,768]{1,0:T(8,128)(2,1)S(1)}, u32[]{:S(2)}, u32[]{:S(2)}) collective-permute-start(bf16[128,768]{1,0:T(8,128)(2,1)S(1)} %bitcast.65), channel_id=1, source_target_pairs={{0,1},{1,0},{2,3},{3,2},{4,5},{5,4},{6,7},{7,6},{8,9},{9,8},{10,11... | collective-permute-start | bytes 589832 | tf_op jit(solution)/shard_map/ppermute | solution.py:143
  38.7 7.6 %collective-permute-start.13 = (bf16[128,768]{1,0:T(8,128)(2,1)S(1)}, bf16[128,768]{1,0:T(8,128)(2,1)S(1)}, u32[]{:S(2)}, u32[]{:S(2)}) collective-permute-start(bf16[128,768]{1,0:T(8,128)(2,1)S(1)} %collective-permute-done.12.refs_3_), channel_id=1, source_target_pairs={{0,1},{1,0},{2,3},{3,2},{4,5},{5,4},{6,7},{7,6},{8,9},{9,8},{10,11... | collective-permute-start | bytes 589832 | tf_op jit(solution)/shard_map/ppermute | solution.py:143
  38.7 3.8 %collective-permute-start.10 = (bf16[128,192]{1,0:T(8,128)(2,1)S(1)}, bf16[128,192]{1,0:T(8,128)(2,1)S(1)}, u32[]{:S(2)}, u32[]{:S(2)}) collective-permute-start(bf16[128,192]{1,0:T(8,128)(2,1)S(1)} %get-tuple-element.353), channel_id=1, source_target_pairs={{0,3},{1,2},{2,1},{3,0},{4,7},{5,6},{6,5},{7,4},{8,11},{9,10},{10,... | collective-permute-start | bytes 147464 | tf_op jit(solution)/shard_map/ppermute | solution.py:143
  39.4 5.1 %collective-permute-start.9 = (bf16[128,192]{1,0:T(8,128)(2,1)S(1)}, bf16[128,192]{1,0:T(8,128)(2,1)S(1)}, u32[]{:S(2)}, u32[]{:S(2)}) collective-permute-start(bf16[128,192]{1,0:T(8,128)(2,1)S(1)} %get-tuple-element.354), channel_id=1, source_target_pairs={{0,2},{1,3},{2,0},{3,1},{4,6},{5,7},{6,4},{7,5},{8,10},{9,11},{10,... | collective-permute-start | bytes 147464 | tf_op jit(solution)/shard_map/ppermute | solution.py:143
  40.9 3.7 %collective-permute-start.8 = (bf16[128,192]{1,0:T(8,128)(2,1)S(1)}, bf16[128,192]{1,0:T(8,128)(2,1)S(1)}, u32[]{:S(2)}, u32[]{:S(2)}) collective-permute-start(bf16[128,192]{1,0:T(8,128)(2,1)S(1)} %get-tuple-element.355), channel_id=1, source_target_pairs={{0,1},{1,0},{2,3},{3,2},{4,5},{5,4},{6,7},{7,6},{8,9},{9,8},{10,11... | collective-permute-start | bytes 147464 | tf_op jit(solution)/shard_map/ppermute | solution.py:143
  46.3 7.0 %collective-permute-start.15 = (bf16[128,896]{1,0:T(8,128)(2,1)S(1)}, bf16[128,896]{1,0:T(8,128)(2,1)S(1)}, u32[]{:S(2)}, u32[]{:S(2)}) collective-permute-start(bf16[128,896]{1,0:T(8,128)(2,1)S(1)} %bitcast.67), channel_id=1, source_target_pairs={{0,2},{1,3},{2,0},{3,1},{4,6},{5,7},{6,4},{7,5},{8,10},{9,11},{10,... | collective-permute-start | bytes 688136 | tf_op jit(solution)/shard_map/ppermute | solution.py:143
  47.0 6.4 %collective-permute-start.14 = (bf16[128,896]{1,0:T(8,128)(2,1)S(1)}, bf16[128,896]{1,0:T(8,128)(2,1)S(1)}, u32[]{:S(2)}, u32[]{:S(2)}) collective-permute-start(bf16[128,896]{1,0:T(8,128)(2,1)S(1)} %bitcast.68), channel_id=1, source_target_pairs={{0,1},{1,0},{2,3},{3,2},{4,5},{5,4},{6,7},{7,6},{8,9},{9,8},{10,11... | collective-permute-start | bytes 688136 | tf_op jit(solution)/shard_map/ppermute | solution.py:143
  58.3 1.9 %collective-permute-start.17 = (bf16[2,128,896]{2,1,0:T(8,128)(2,1)S(1)}, bf16[2,128,896]{2,1,0:T(8,128)(2,1)S(1)}, u32[]{:S(2)}, u32[]{:S(2)}) collective-permute-start(bf16[2,128,896]{2,1,0:T(8,128)(2,1)S(1)} %get-tuple-element.214), channel_id=1, source_target_pairs={{0,1},{1,0},{2,3},{3,2},{4,5},{5,4},{6,7},{7,6},{8,9},{9,8},{10,11... | collective-permute-start | bytes 1376264 | tf_op jit(solution)/shard_map/ppermute | solution.py:143
  60.2 7.7 %collective-permute-start.19 = (bf16[128,896]{1,0:T(8,128)(2,1)S(1)}, bf16[128,896]{1,0:T(8,128)(2,1)S(1)}, u32[]{:S(2)}, u32[]{:S(2)}) collective-permute-start(bf16[128,896]{1,0:T(8,128)(2,1)S(1)} %fusion.2), channel_id=1, source_target_pairs={{0,2},{1,3},{2,0},{3,1},{4,6},{5,7},{6,4},{7,5},{8,10},{9,11},{10,... | collective-permute-start | bytes 688136 | tf_op jit(solution)/shard_map/ppermute | solution.py:143
  62.7 6.0 %collective-permute-start.18 = (bf16[2,128,768]{2,1,0:T(8,128)(2,1)S(1)}, bf16[2,128,768]{2,1,0:T(8,128)(2,1)S(1)}, u32[]{:S(2)}, u32[]{:S(2)}) collective-permute-start(bf16[2,128,768]{2,1,0:T(8,128)(2,1)S(1)} %get-tuple-element.218), channel_id=1, source_target_pairs={{0,1},{1,0},{2,3},{3,2},{4,5},{5,4},{6,7},{7,6},{8,9},{9,8},{10,11... | collective-permute-start | bytes 1179656 | tf_op jit(solution)/shard_map/ppermute | solution.py:143
  68.7 7.8 %collective-permute-start.20 = (bf16[128,768]{1,0:T(8,128)(2,1)S(1)}, bf16[128,768]{1,0:T(8,128)(2,1)S(1)}, u32[]{:S(2)}, u32[]{:S(2)}) collective-permute-start(bf16[128,768]{1,0:T(8,128)(2,1)S(1)} %fusion.3), channel_id=1, source_target_pairs={{0,2},{1,3},{2,0},{3,1},{4,6},{5,7},{6,4},{7,5},{8,10},{9,11},{10,... | collective-permute-start | bytes 589832 | tf_op jit(solution)/shard_map/ppermute | solution.py:143
  69.2 14.1 %all-to-all-start.3 = ((bf16[8,16,896]{2,1,0:T(8,128)(2,1)}), bf16[8,16,896]{2,1,0:T(8,128)(2,1)S(1)}, u32[]{:S(2)}, u32[]{:S(2)}) async-start(bf16[8,16,896]{2,1,0:T(8,128)(2,1)} %bitcast.24), calls=%async_computation.3 | async-start | bytes 458752 | tf_op jit(solution)/shard_map/all_to_all | solution.py:372
  84.1 6.2 %collective-permute-start.22 = (bf16[128,768]{1,0:T(8,128)(2,1)S(1)}, bf16[128,768]{1,0:T(8,128)(2,1)S(1)}, u32[]{:S(2)}, u32[]{:S(2)}) collective-permute-start(bf16[128,768]{1,0:T(8,128)(2,1)S(1)} %get-tuple-element.239.refs_1_), channel_id=1, source_target_pairs={{0,2},{1,3},{2,0},{3,1},{4,6},{5,7},{6,4},{7,5},{8,10},{9,11},{10,... | collective-permute-start | bytes 589832 | tf_op jit(solution)/shard_map/ppermute | solution.py:143
  84.6 12.4 %all-to-all-start.2 = ((bf16[8,16,768]{2,1,0:T(8,128)(2,1)}), bf16[8,16,768]{2,1,0:T(8,128)(2,1)S(1)}, u32[]{:S(2)}, u32[]{:S(2)}) async-start(bf16[8,16,768]{2,1,0:T(8,128)(2,1)} %bitcast.22), calls=%async_computation.2 | async-start | bytes 393216 | tf_op jit(solution)/shard_map/all_to_all | solution.py:372
  88.2 2.7 %collective-permute-start.21 = (bf16[128,768]{1,0:T(8,128)(2,1)S(1)}, bf16[128,768]{1,0:T(8,128)(2,1)S(1)}, u32[]{:S(2)}, u32[]{:S(2)}) collective-permute-start(bf16[128,768]{1,0:T(8,128)(2,1)S(1)} %get-tuple-element.239.refs_1_), channel_id=1, source_target_pairs={{0,1},{1,0},{2,3},{3,2},{4,5},{5,4},{6,7},{7,6},{8,9},{9,8},{10,11... | collective-permute-start | bytes 589832 | tf_op jit(solution)/shard_map/ppermute | solution.py:143
  97.1 14.5 %collective-permute-start.24 = (bf16[2,208,384]{2,1,0:T(8,128)(2,1)S(1)}, bf16[2,208,384]{2,1,0:T(8,128)(2,1)S(1)}, u32[]{:S(2)}, u32[]{:S(2)}) collective-permute-start(bf16[2,208,384]{2,1,0:T(8,128)(2,1)S(1)} %get-tuple-element.288), channel_id=1, source_target_pairs={{0,1},{1,0},{2,3},{3,2},{4,5},{5,4},{6,7},{7,6},{8,9},{9,8},{10,11... | collective-permute-start | bytes 958472 | tf_op jit(solution)/shard_map/ppermute | solution.py:143
  97.5 11.0 %collective-permute-start.25 = (bf16[80,768]{1,0:T(8,128)(2,1)S(1)}, bf16[80,768]{1,0:T(8,128)(2,1)S(1)}, u32[]{:S(2)}, u32[]{:S(2)}) collective-permute-start(bf16[80,768]{1,0:T(8,128)(2,1)S(1)} %get-tuple-element.295), channel_id=1, source_target_pairs={{0,8},{4,12},{8,0},{12,4},{16,24},{20,28},{24,16},{28,20},{1,9},{5... | collective-permute-start | bytes 368648 | tf_op jit(solution)/shard_map/ppermute | solution.py:143
  99.2 12.4 %collective-permute-start.26 = (bf16[80,768]{1,0:T(8,128)(2,1)S(1)}, bf16[80,768]{1,0:T(8,128)(2,1)S(1)}, u32[]{:S(2)}, u32[]{:S(2)}) collective-permute-start(bf16[80,768]{1,0:T(8,128)(2,1)S(1)} %get-tuple-element.296), channel_id=1, source_target_pairs={{0,16},{4,20},{8,24},{12,28},{16,0},{20,4},{24,8},{28,12},{1,17},{... | collective-permute-start | bytes 368648 | tf_op jit(solution)/shard_map/ppermute | solution.py:143
  101.6 10.0 %collective-permute-start.27 = (bf16[80,768]{1,0:T(8,128)(2,1)S(1)}, bf16[80,768]{1,0:T(8,128)(2,1)S(1)}, u32[]{:S(2)}, u32[]{:S(2)}) collective-permute-start(bf16[80,768]{1,0:T(8,128)(2,1)S(1)} %get-tuple-element.297), channel_id=1, source_target_pairs={{0,24},{4,28},{8,16},{12,20},{16,8},{20,12},{24,0},{28,4},{1,25},{... | collective-permute-start | bytes 368648 | tf_op jit(solution)/shard_map/ppermute | solution.py:143
  101.9 10.3 %collective-permute-start.28 = (bf16[256,768]{1,0:T(8,128)(2,1)S(1)}, bf16[256,768]{1,0:T(8,128)(2,1)S(1)}, u32[]{:S(2)}, u32[]{:S(2)}) collective-permute-start(bf16[256,768]{1,0:T(8,128)(2,1)S(1)} %get-tuple-element.298), channel_id=1, source_target_pairs={{0,4},{4,0},{8,12},{12,8},{16,20},{20,16},{24,28},{28,24},{1,5},{5... | collective-permute-start | bytes 1179656 | tf_op jit(solution)/shard_map/ppermute | solution.py:143
  112.3 9.4 %collective-permute-start.30 = (bf16[48,768]{1,0:T(8,128)(2,1)S(1)}, bf16[48,768]{1,0:T(8,128)(2,1)S(1)}, u32[]{:S(2)}, u32[]{:S(2)}) collective-permute-start(bf16[48,768]{1,0:T(8,128)(2,1)S(1)} %concatenate.16), channel_id=1, source_target_pairs={{0,4},{4,0},{8,12},{12,8},{16,20},{20,16},{24,28},{28,24},{1,5},{5... | collective-permute-start | bytes 221192 | tf_op jit(solution)/shard_map/ppermute | solution.py:143
  114.1 12.0 %collective-permute-start.29 = (bf16[208,384]{1,0:T(8,128)(2,1)S(1)}, bf16[208,384]{1,0:T(8,128)(2,1)S(1)}, u32[]{:S(2)}, u32[]{:S(2)}) collective-permute-start(bf16[208,384]{1,0:T(8,128)(2,1)S(1)} %bitcast_add_fusion), channel_id=1, source_target_pairs={{0,2},{1,3},{2,0},{3,1},{4,6},{5,7},{6,4},{7,5},{8,10},{9,11},{10,... | collective-permute-start | bytes 479240 | tf_op jit(solution)/shard_map/ppermute | solution.py:143
  115.8 7.4 %collective-permute-start.33 = (bf16[64,768]{1,0:T(8,128)(2,1)S(1)}, bf16[64,768]{1,0:T(8,128)(2,1)S(1)}, u32[]{:S(2)}, u32[]{:S(2)}) collective-permute-start(bf16[64,768]{1,0:T(8,128)(2,1)S(1)} %get-tuple-element.350), channel_id=1, source_target_pairs={{0,24},{4,28},{8,16},{12,20},{16,8},{20,12},{24,0},{28,4},{1,25},{... | collective-permute-start | bytes 294920 | tf_op jit(solution)/shard_map/ppermute | solution.py:143
  119.2 6.9 %collective-permute-start.32 = (bf16[64,768]{1,0:T(8,128)(2,1)S(1)}, bf16[64,768]{1,0:T(8,128)(2,1)S(1)}, u32[]{:S(2)}, u32[]{:S(2)}) collective-permute-start(bf16[64,768]{1,0:T(8,128)(2,1)S(1)} %get-tuple-element.351), channel_id=1, source_target_pairs={{0,16},{4,20},{8,24},{12,28},{16,0},{20,4},{24,8},{28,12},{1,17},{... | collective-permute-start | bytes 294920 | tf_op jit(solution)/shard_map/ppermute | solution.py:143
  119.2 6.9 %collective-permute-start.31 = (bf16[64,768]{1,0:T(8,128)(2,1)S(1)}, bf16[64,768]{1,0:T(8,128)(2,1)S(1)}, u32[]{:S(2)}, u32[]{:S(2)}) collective-permute-start(bf16[64,768]{1,0:T(8,128)(2,1)S(1)} %get-tuple-element.352), channel_id=1, source_target_pairs={{0,8},{4,12},{8,0},{12,4},{16,24},{20,28},{24,16},{28,20},{1,9},{5... | collective-permute-start | bytes 294920 | tf_op jit(solution)/shard_map/ppermute | solution.py:143
  126.1 3.8 %collective-permute-start.34 = (f32[16,768]{1,0:T(8,128)S(1)}, f32[16,768]{1,0:T(8,128)S(1)}, u32[]{:S(2)}, u32[]{:S(2)}) collective-permute-start(f32[16,768]{1,0:T(8,128)S(1)} %slice_convert_fusion), channel_id=1, source_target_pairs={{0,1},{1,0},{2,3},{3,2},{4,5},{5,4},{6,7},{7,6},{8,9},{9,8},{10,11... | collective-permute-start | bytes 147464 | tf_op jit(solution)/shard_map/ppermute | solution.py:143
  126.2 4.2 %collective-permute-start.39 = (bf16[32,768]{1,0:T(8,128)(2,1)S(1)}, bf16[32,768]{1,0:T(8,128)(2,1)S(1)}, u32[]{:S(2)}, u32[]{:S(2)}) collective-permute-start(bf16[32,768]{1,0:T(8,128)(2,1)S(1)} %slice.86), channel_id=1, source_target_pairs={{0,4},{4,0},{8,12},{12,8},{16,20},{20,16},{24,28},{28,24},{1,5},{5... | collective-permute-start | bytes 147464 | tf_op jit(solution)/shard_map/ppermute | solution.py:143
  126.8 5.2 %collective-permute-start.35 = (bf16[192,128]{1,0:T(8,128)(2,1)S(1)}, bf16[192,128]{1,0:T(8,128)(2,1)S(1)}, u32[]{:S(2)}, u32[]{:S(2)}) collective-permute-start(bf16[192,128]{1,0:T(8,128)(2,1)S(1)} %get-tuple-element.312), channel_id=1, source_target_pairs={{0,1},{1,0},{2,3},{3,2},{4,5},{5,4},{6,7},{7,6},{8,9},{9,8},{10,11... | collective-permute-start | bytes 147464 | tf_op jit(solution)/shard_map/ppermute | solution.py:143
  127.0 6.5 %collective-permute-start.36 = (bf16[192,128]{1,0:T(8,128)(2,1)S(1)}, bf16[192,128]{1,0:T(8,128)(2,1)S(1)}, u32[]{:S(2)}, u32[]{:S(2)}) collective-permute-start(bf16[192,128]{1,0:T(8,128)(2,1)S(1)} %get-tuple-element.313), channel_id=1, source_target_pairs={{0,2},{1,3},{2,0},{3,1},{4,6},{5,7},{6,4},{7,5},{8,10},{9,11},{10,... | collective-permute-start | bytes 147464 | tf_op jit(solution)/shard_map/ppermute | solution.py:143
  127.6 9.9 %collective-permute-start.42 = (bf16[64,768]{1,0:T(8,128)(2,1)S(1)}, bf16[64,768]{1,0:T(8,128)(2,1)S(1)}, u32[]{:S(2)}, u32[]{:S(2)}) collective-permute-start(bf16[64,768]{1,0:T(8,128)(2,1)S(1)} %add_convert_fusion.2.refs_3_), channel_id=1, source_target_pairs={{0,24},{4,28},{8,16},{12,20},{16,8},{20,12},{24,0},{28,4},{1,25},{... | collective-permute-start | bytes 294920 | tf_op jit(solution)/shard_map/ppermute | solution.py:143
  130.0 8.4 %collective-permute-start.41 = (bf16[64,768]{1,0:T(8,128)(2,1)S(1)}, bf16[64,768]{1,0:T(8,128)(2,1)S(1)}, u32[]{:S(2)}, u32[]{:S(2)}) collective-permute-start(bf16[64,768]{1,0:T(8,128)(2,1)S(1)} %add_convert_fusion.2.refs_3_), channel_id=1, source_target_pairs={{0,16},{4,20},{8,24},{12,28},{16,0},{20,4},{24,8},{28,12},{1,17},{... | collective-permute-start | bytes 294920 | tf_op jit(solution)/shard_map/ppermute | solution.py:143
  130.4 8.0 %collective-permute-start.40 = (bf16[64,768]{1,0:T(8,128)(2,1)S(1)}, bf16[64,768]{1,0:T(8,128)(2,1)S(1)}, u32[]{:S(2)}, u32[]{:S(2)}) collective-permute-start(bf16[64,768]{1,0:T(8,128)(2,1)S(1)} %add_convert_fusion.2.refs_3_), channel_id=1, source_target_pairs={{0,8},{4,12},{8,0},{12,4},{16,24},{20,28},{24,16},{28,20},{1,9},{5... | collective-permute-start | bytes 294920 | tf_op jit(solution)/shard_map/ppermute | solution.py:143
  132.0 6.4 %collective-permute-start.38 = (bf16[64,768]{1,0:T(8,128)(2,1)S(1)}, bf16[64,768]{1,0:T(8,128)(2,1)S(1)}, u32[]{:S(2)}, u32[]{:S(2)}) collective-permute-start(bf16[64,768]{1,0:T(8,128)(2,1)S(1)} %add_convert_fusion.2.refs_3_), channel_id=1, source_target_pairs={{0,4},{4,0},{8,12},{12,8},{16,20},{20,16},{24,28},{28,24},{1,5},{5... | collective-permute-start | bytes 294920 | tf_op jit(solution)/shard_map/ppermute | solution.py:143
  133.5 3.9 %collective-permute-start.37 = (bf16[192,128]{1,0:T(8,128)(2,1)S(1)}, bf16[192,128]{1,0:T(8,128)(2,1)S(1)}, u32[]{:S(2)}, u32[]{:S(2)}) collective-permute-start(bf16[192,128]{1,0:T(8,128)(2,1)S(1)} %get-tuple-element.314), channel_id=1, source_target_pairs={{0,3},{1,2},{2,1},{3,0},{4,7},{5,6},{6,5},{7,4},{8,11},{9,10},{10,... | collective-permute-start | bytes 147464 | tf_op jit(solution)/shard_map/ppermute | solution.py:143
  138.4 11.3 %collective-permute-start.43 = (f32[16,768]{1,0:T(8,128)S(1)}, f32[16,768]{1,0:T(8,128)S(1)}, u32[]{:S(2)}, u32[]{:S(2)}) collective-permute-start(f32[16,768]{1,0:T(8,128)S(1)} %fusion.7.refs_1_), channel_id=1, source_target_pairs={{0,2},{1,3},{2,0},{3,1},{4,6},{5,7},{6,4},{7,5},{8,10},{9,11},{10,... | collective-permute-start | bytes 147464 | tf_op jit(solution)/shard_map/ppermute | solution.py:143
  139.9 9.8 %collective-permute-start.46 = (bf16[64,768]{1,0:T(8,128)(2,1)S(1)}, bf16[64,768]{1,0:T(8,128)(2,1)S(1)}, u32[]{:S(2)}, u32[]{:S(2)}) collective-permute-start(bf16[64,768]{1,0:T(8,128)(2,1)S(1)} %pad_maximum_fusion.refs_7_), channel_id=1, source_target_pairs={{0,24},{4,28},{8,16},{12,20},{16,8},{20,12},{24,0},{28,4},{1,25},{... | collective-permute-start | bytes 294920 | tf_op jit(solution)/shard_map/ppermute | solution.py:143
  142.4 8.6 %collective-permute-start.45 = (bf16[64,768]{1,0:T(8,128)(2,1)S(1)}, bf16[64,768]{1,0:T(8,128)(2,1)S(1)}, u32[]{:S(2)}, u32[]{:S(2)}) collective-permute-start(bf16[64,768]{1,0:T(8,128)(2,1)S(1)} %pad_maximum_fusion.refs_7_), channel_id=1, source_target_pairs={{0,16},{4,20},{8,24},{12,28},{16,0},{20,4},{24,8},{28,12},{1,17},{... | collective-permute-start | bytes 294920 | tf_op jit(solution)/shard_map/ppermute | solution.py:143
  142.4 8.6 %collective-permute-start.44 = (bf16[64,768]{1,0:T(8,128)(2,1)S(1)}, bf16[64,768]{1,0:T(8,128)(2,1)S(1)}, u32[]{:S(2)}, u32[]{:S(2)}) collective-permute-start(bf16[64,768]{1,0:T(8,128)(2,1)S(1)} %pad_maximum_fusion.refs_7_), channel_id=1, source_target_pairs={{0,8},{4,12},{8,0},{12,4},{16,24},{20,28},{24,16},{28,20},{1,9},{5... | collective-permute-start | bytes 294920 | tf_op jit(solution)/shard_map/ppermute | solution.py:143
  144.4 7.9 %collective-permute-start.47 = (bf16[192,768]{1,0:T(8,128)(2,1)S(1)}, bf16[192,768]{1,0:T(8,128)(2,1)S(1)}, u32[]{:S(2)}, u32[]{:S(2)}) collective-permute-start(bf16[192,768]{1,0:T(8,128)(2,1)S(1)} %constant_dynamic-update-slice_fusion.refs_4_), channel_id=1, source_target_pairs={{0,4},{4,0},{8,12},{12,8},{16,20},{20,16},{24,28},{28,24},{1,5},{5... | collective-permute-start | bytes 884744 | tf_op jit(solution)/shard_map/ppermute | solution.py:143
  (13 other events, 26.3 us)

commit v6 on v5

--- a/solution.py
+++ b/solution.py
@@ -136,6 +136,30 @@
         compiler_params=pltpu.CompilerParams(vmem_limit_bytes=16 * 2**20),
         name=name,
     )(token, *values)
+
+
+def store(values, name):
+    count = len(values)
+
+    def body(*refs):
+        ins, outs, sems = refs[:count], refs[count : 2 * count], refs[-1]
+        copies = [
+            pltpu.make_async_copy(i, o, sems.at[n]) for n, (i, o) in enumerate(zip(ins, outs))
+        ]
+        for c in copies:
+            c.start()
+        for c in copies:
+            c.wait()
+
+    return pl.pallas_call(
+        body,
+        out_shape=[pltpu.HBM(v.shape, v.dtype) for v in values],
+        in_specs=[VMEM] * count,
+        out_specs=[pl.BlockSpec(memory_space=pltpu.HBM)] * count,
+        scratch_shapes=[pltpu.SemaphoreType.DMA((count,))],
+        compiler_params=pltpu.CompilerParams(vmem_limit_bytes=16 * 2**20),
+        name=name,
+    )(*values)
 
 
 def swap(value, axis, mask):
@@ -364,7 +388,9 @@
     )
     small_pieces = [small_own] + [swap(small_own, "tp", rel) for rel in range(1, ways)]
     tok_across = swap(tok_t, "tp", 2)
-    tok_across, *small_pieces = lax.optimization_barrier((tok_across, *small_pieces))
+    tok_across, dest_row, *small_pieces = lax.optimization_barrier(
+        (tok_across, dest_row, *small_pieces)
+    )
     tok_pieces = (tok_t, swap(tok_t, "tp", 1), tok_across, swap(tok_across, "tp", 1))
 
     def over_experts(value):
@@ -400,7 +426,6 @@
         seg_ref,
         dest_ref,
         small_ref,
-        small_far,
         dest_far,
         r1_ref,
         n1_ref,
@@ -426,26 +451,19 @@
         pieces = [c[...] for c in (c0, c1, c2, c3)]
         small = jnp.concatenate([absolute(pieces, mine, t) for t in range(ways)], axis=1)
         small_ref[...] = small
-        small_far[...] = small
-        small_far.send()
         dest_far[...] = dest_ref[...]
-        dest_far.send()
         x_low = x_ref[...]
         x = x_low.astype(f32)
         r1 = lax.rsqrt(jnp.mean(x * x, axis=0, keepdims=True) + EPSILON)
         r1_ref[...] = r1
-        r1_ref.send()
         n1 = (x * r1 * spread_row(small, experts, length)).astype(bf16)
         n1_ref[...] = n1
-        n1_ref.send()
         q = mm(wq_ref[...], n1).astype(bf16)
         k = mm(wk_ref[...], n1).astype(bf16)
         v = mm(wv_ref[...], n1).astype(bf16)
         q_ref[...] = q
         k_ref[...] = k
         v_ref[...] = v
-        for ref in (q_ref, k_ref, v_ref):
-            ref.send()
         hot = bucket_hot(bucket_ref, bucket_held, bf16)
         offsets = mm(table_ref[...], hot)
         above = iota((length, length), 0)
@@ -472,10 +490,8 @@
             e = jnp.exp(s - jnp.max(s, axis=0, keepdims=True))
             p = (e * (1.0 / jnp.sum(e, axis=0, keepdims=True))).astype(bf16)
             p_refs[h][...] = p
-            p_refs[h].send()
             attn_ref[part] = mm(v[part], p).astype(bf16)
         attn = attn_ref[...]
-        attn_ref.send()
         dest = dest_ref[...]
         wo = wo_ref[...]
         for rel, out in enumerate((kept_ref, sent_ref.at[0], passed_ref, sent_ref.at[1])):
@@ -484,19 +500,18 @@
             if rel == 0:
                 xrow_ref[...] = mm_nt(hot, x_low).astype(bf16)
 
-    small, small_far, dest_far, r1, n1, q, k, v, p0, p1, p2, attn, *o_parts, x_rows = run(
+    small, *long_lived, o_kept, o_passed, o_sent, x_rows = run(
         attend_body,
         [
             ((extra, width), bf16),
-            ((extra, width), bf16, True),
-            ((1, length), jnp.int32, True),
-            ((1, length), f32, True),
-            ((width, length), bf16, True),
-            ((here, length), bf16, True),
-            ((here, length), bf16, True),
-            ((here, length), bf16, True),
-            *[((length, length), bf16, True)] * heads,
-            ((here, length), bf16, True),
+            ((1, length), jnp.int32),
+            ((1, length), f32),
+            ((width, length), bf16),
+            ((here, length), bf16),
+            ((here, length), bf16),
+            ((here, length), bf16),
+            *[((length, length), bf16)] * heads,
+            ((here, length), bf16),
             ((rows, width), bf16),
             ((rows, width), bf16),
             ((2, rows, width), bf16),
@@ -520,9 +535,11 @@
         scratch=[pltpu.VMEM((width, length), bf16), pltpu.VMEM((1, span), jnp.int32)],
         limit=24,
     )
-    o_kept, o_passed, o_sent = o_parts
+    dest_far, r1, n1, q, k, v, p0, p1, p2, attn, small_far = store(
+        [*long_lived, small], "attend_store"
+    )
     o_beside = swap(o_sent, "tp", 1)
-    o_half = o_passed + o_beside[1]
+    o_half, n1 = lax.optimization_barrier((o_passed + o_beside[1], n1))
     o_across = swap(o_half, "tp", 2)
 
     def join_body(me_ref, cots_ref, out_ref):
@@ -537,8 +554,9 @@
         h = xrow_ref[...].astype(f32) + o
         r2 = lax.rsqrt(jnp.mean(h * h, axis=-1, keepdims=True) + EPSILON)
         gain = small_ref[experts + 1 : experts + 2].astype(f32)
-        n2 = h * r2 * gain
-        logits = mm_nt(n2, small_ref[0:experts].astype(f32), HIGHEST)
+        scaled = h * gain
+        n2 = scaled * r2
+        logits = r2 * mm_nt(scaled, small_ref[0:experts].astype(f32), HIGHEST)
         e = jnp.exp(logits - jnp.max(logits, axis=-1, keepdims=True))
         p = e / jnp.sum(e, axis=-1, keepdims=True)
         owner = iota((rows, experts), 0) - iota((rows, experts), 1) * per
@@ -592,7 +610,7 @@
     )
     weights = fetch(after(me, arrived), [w_in, w_out], "expert_arguments")
 
-    def dout_body(me_ref, d0, d1, d2, d3, out_ref):
+    def dout_body(me_ref, d0, d1, d2, d3, *outs):
         mine = me_ref[0] & (ways - 1)
         came = (d0, d1, d2, d3)
         for rel in range(ways):
@@ -601,29 +619,24 @@
                 at = (rel ^ src) * quarter
                 pieces.append(came[src][:, at : at + quarter])
             dout = jnp.concatenate([absolute(pieces, mine, t) for t in range(ways)], axis=1)
-            out_ref[rel * rows : (rel + 1) * rows] = dout
-
-    (douts,) = run(
+            outs[rel // 2][rel % 2 * rows : (rel % 2 + 1) * rows] = dout
+
+    near_douts, far_douts = run(
         dout_body,
-        [((ways * rows, width), bf16)],
+        [((2 * rows, width), bf16), ((2 * rows, width), bf16)],
         (after(me, arrived), *d_pieces),
         "douts",
         us=0.01,
     )
-    across, douts, *weights = lax.optimization_barrier(
-        (swap(arrived, "tp", 2), douts, *weights)
-    )
-    arrived = (arrived, swap(arrived, "tp", 1), across, swap(across, "tp", 1))
-
-    def expert_body(a0, a1, a2, a3, dout_ref, win_ref, wout_ref, *outs):
-        u_ref, dy_ref, act_ref, dz_ref, kept_ref, passed_ref, sent_ref = outs
-        for rel, a in enumerate((a0, a1, a2, a3)):
-            part = slice(rel * rows, (rel + 1) * rows)
+    across, beside = swap(arrived, "tp", 2), swap(arrived, "tp", 1)
+
+    def expert_body(a0, a1, dout_ref, win_ref, wout_ref, *outs):
+        u_ref, dy_ref, act_ref, dz_ref, kept_ref, sent_ref = outs
+        for at, a in enumerate((a0, a1)):
+            part = slice(at * rows, (at + 1) * rows)
             u_ref[part] = a[:, 0:width]
             g = a[:, width : width + 1].astype(f32) + a[:, width + 1 : width + 2].astype(f32)
             dy_ref[part] = (g * dout_ref[part].astype(f32)).astype(bf16)
-        u_ref.send()
-        dy_ref.send()
         u = u_ref[...]
         dy = dy_ref[...]
         z = mm(u, win_ref[0])
@@ -634,48 +647,59 @@
         wide_act = z * half
         act = wide_act.astype(bf16)
         act_ref[...] = act
-        act_ref.send()
         slope = half + wide_act * (1.0 - t) * (c + (3 * 0.044715 * c) * z2)
         dact = mm_nt(dy, wout_ref[0])
         dot = jnp.sum(dact * act.astype(f32), axis=-1, keepdims=True)
         dz = (dact * slope).astype(bf16)
         dz_ref[...] = dz
-        dz_ref.send()
         du = mm_nt(dz, win_ref[0]).astype(bf16)
         tail = two_lanes(dot, LANES)
-        for rel, out in enumerate((kept_ref, sent_ref.at[0], passed_ref, sent_ref.at[1])):
-            out[:, 0:width] = du[rel * rows : (rel + 1) * rows]
-            out[:, width : width + LANES] = tail[rel * rows : (rel + 1) * rows]
-
-    u_all, dy_all, act, dz, *du_parts = run(
-        expert_body,
-        [
-            ((ways * rows, width), bf16, True),
-            ((ways * rows, width), bf16, True),
-            ((ways * rows, hidden_here), bf16, True),
-            ((ways * rows, hidden_here), bf16, True),
-            ((rows, width + LANES), bf16),
-            ((rows, width + LANES), bf16),
-            ((2, rows, width + LANES), bf16),
-        ],
-        (*arrived, douts, *weights),
-        "expert",
-        us=4.0,
-        limit=24,
-    )
-    du_kept, du_beside, du_across, du_half = scatter_sum(*du_parts)
-    du_sum = du_kept + du_beside[0] + du_across
+        for at, out in enumerate((kept_ref, sent_ref)):
+            out[:, 0:width] = du[at * rows : (at + 1) * rows]
+            out[:, width : width + LANES] = tail[at * rows : (at + 1) * rows]
+
+    def expert(pieces, dout, name):
+        return run(
+            expert_body,
+            [
+                ((2 * rows, width), bf16),
+                ((2 * rows, width), bf16),
+                ((2 * rows, hidden_here), bf16),
+                ((2 * rows, hidden_here), bf16),
+                ((rows, width + LANES), bf16),
+                ((rows, width + LANES), bf16),
+            ],
+            (*pieces, dout, *weights),
+            name,
+            us=0.01,
+            limit=24,
+        )
+
+    *near, du_kept, du_sent = expert((arrived, beside), near_douts, "expert_near")
+    du_beside = swap(du_sent, "tp", 1)
+    across, du_kept, du_beside, *near = lax.optimization_barrier(
+        (across, du_kept, du_beside, *near)
+    )
+    *wide, du_passed, du_sent = expert(
+        (across, swap(across, "tp", 1)), far_douts, "expert_far"
+    )
+    du_half = du_passed + swap(du_sent, "tp", 1)
+    du_across = swap(du_half, "tp", 2)
+    stored = store([*near, *wide], "expert_store")
+    du_across, *stored = lax.optimization_barrier((du_across, *stored))
+    du_sum = du_kept + du_beside + du_across
     du_rows = over_experts(du_sum)
 
-    def value_body(me_ref, act_ref, wout_ref, kept_ref, passed_ref, sent_ref):
-        y = mm(act_ref[...], wout_ref[0]).astype(bf16)
+    def value_body(me_ref, near_ref, far_ref, wout_ref, kept_ref, passed_ref, sent_ref):
+        act = jnp.concatenate([near_ref[...], far_ref[...]], axis=0)
+        y = mm(act, wout_ref[0]).astype(bf16)
         for rel, out in enumerate((kept_ref, sent_ref.at[0], passed_ref, sent_ref.at[1])):
             out[...] = y[rel * rows : (rel + 1) * rows]
 
     y_parts = run(
         value_body,
         [((rows, width), bf16), ((rows, width), bf16), ((2, rows, width), bf16)],
-        (after(me, du_half), Far(act), w_out),
+        (after(me, du_half), near[2], wide[2], w_out),
         "value",
         us=0.8,
     )
@@ -933,9 +957,11 @@
             total = total + mm(piece[...], hot)
         out_ref[...] = total.astype(bf16)
 
-    def weights_body(me_ref, u_ref, dy_ref, act_ref, dz_ref, gin_ref, gout_ref):
-        gin_ref[0] = mm_tn(u_ref[...], dz_ref[...]).astype(bf16)
-        gout_ref[0] = mm_tn(act_ref[...], dy_ref[...]).astype(bf16)
+    def weights_body(me_ref, u0, dy0, act0, dz0, u1, dy1, act1, dz1, gin_ref, gout_ref):
+        gin = mm_tn(u0[...], dz0[...]) + mm_tn(u1[...], dz1[...])
+        gin_ref[0] = gin.astype(bf16)
+        gout = mm_tn(act0[...], dy0[...]) + mm_tn(act1[...], dy1[...])
+        gout_ref[0] = gout.astype(bf16)
 
     def beside(came, block):
         phase = held.setdefault("phase", 0)
@@ -947,7 +973,7 @@
             extras["grad_in"], extras["grad_out"] = run(
                 weights_body,
                 [((1, width, hidden_here), bf16), ((1, hidden_here, width), bf16)],
-                (after(me, dn1_sent), Far(u_all), Far(dy_all), Far(act), Far(dz)),
+                (after(me, dn1_sent), *[Far(v) for v in stored]),
                 "expert_weights",
                 us=12,
             )

time: 154 us -> 151 us (0.981)
  waiting for transfers between devices: 49.7 us -> 47.4 us
    pallas_call x16 -> x17, Pallas kernels: 35.1 us -> 31.8 us  [run(): pl.pallas_call(wrapped, out_shape=[pltpu.HBM(o[0], o[1]) if len(o) == 3 e...]
    pallas_call x0 -> x2, Pallas kernels: none -> 3.11 us  [store(): pl.pallas_call(body, out_shape=[pltpu.HBM(v.shape, v.dtype) for v in valu...]
    ppermute x48 -> x49, waiting for transfers between devices: 36.9 us -> 34.7 us  [swap(): return lax.ppermute(value, axis, [(i, i ^ mask) for i in range(size)])]
    ppermute x48 -> x49, starting transfers between devices: 42 us -> 41.9 us  [swap(): return lax.ppermute(value, axis, [(i, i ^ mask) for i in range(size)])]
  transfers between devices with their start and end apart: 52 -> 53, of which waited for: 22 -> 19; matrix products, arithmetic and copies ran while one was open for 1% -> 1% of each run, Pallas kernels for 19% -> 22%
where the time goes in v6:
time: 151 us; the launch traced here: 150 us
  starting transfers between devices  59.8 us (40%)
  waiting for transfers between devices  47.4 us (31%)
  Pallas kernels  39.7 us (26%)
  other arithmetic  1.82 us (1%)
    ppermute x49, starting transfers between devices, swap(): return lax.ppermute(value, axis, [(i, i ^ mask) for i in range(size)])  41.9 us
    ppermute x49, waiting for transfers between devices, swap(): return lax.ppermute(value, axis, [(i, i ^ mask) for i in range(size)])  34.7 us
    pallas_call x17, Pallas kernels, run(): pl.pallas_call(wrapped, out_shape=[pltpu.HBM(o[0], o[1]) if len(o) == 3 e...  31.8 us
    all_to_all x4, starting transfers between devices, over_experts(): lax.all_to_all(blocks, 'exp', split_axis=0, concat_axis=0, tiled=True)  18 us
    all_to_all x4, waiting for transfers between devices, over_experts(): lax.all_to_all(blocks, 'exp', split_axis=0, concat_axis=0, tiled=True)  12.8 us
    pallas_call x3, Pallas kernels, fetch(): pl.pallas_call(body, out_shape=[jax.ShapeDtypeStruct(v.shape, v.dtype) fo...  4.8 us
    pallas_call x2, Pallas kernels, store(): pl.pallas_call(body, out_shape=[pltpu.HBM(v.shape, v.dtype) for v in valu...  3.11 us
  transfers between devices with their start and end apart: 53, of which 19 were waited for; matrix products, arithmetic and copies ran while one was open for 1% of the time, Pallas kernels for 22%

profile of v6, /device:TPU:0, one launch (start us, length us, event | category | flops | bytes accessed | tf_op | source)
XLA Modules:
  0.0 150.1 jit_solution(9321891890499245054)
XLA Ops:
  0.6 3.0 %collective-permute-start.1 = (bf16[192,384]{1,0:T(8,128)(2,1)}, bf16[192,384]{1,0:T(8,128)(2,1)S(1)}, u32[]{:S(2)}, u32[]{:S(2)}) collective-permute-start(bf16[192,384]{1,0:T(8,128)(2,1)} %bitcast.62), channel_id=1, source_target_pairs={{0,2},{1,3},{2,0},{3,1},{4,6},{5,7},{6,4},{7,5},{8,10},{9,11},{10,... | collective-permute-start | bytes 442376 | tf_op jit(solution)/shard_map/ppermute | solution.py:167
  4.5 1.8 %collective-permute-start.4 = (bf16[16,192]{1,0:T(8,128)(2,1)S(1)}, bf16[16,192]{1,0:T(8,128)(2,1)S(1)}, u32[]{:S(2)}, u32[]{:S(2)}) collective-permute-start(bf16[16,192]{1,0:T(8,128)(2,1)S(1)} %small.1.refs_5_), channel_id=1, source_target_pairs={{0,3},{1,2},{2,1},{3,0},{4,7},{5,6},{6,5},{7,4},{8,11},{9,10},{10,... | collective-permute-start | bytes 18440 | tf_op jit(solution)/shard_map/ppermute | solution.py:167
  6.7 1.4 slots.1
  9.7 3.5 %attend.1 = (bf16[16,768]{1,0:T(8,128)(2,1)S(1)}, s32[1,384]{1,0:T(1,128)S(1)}, f32[1,384]{1,0:T(1,128)S(1)}, bf16[768,384]{1,0:T(8,128)(2,1)S(1)}, bf16[192,384...) custom-call(s32[1]{0:T(128)} %bitcast.refs_0_.token_ref, ...), custom_call_target="tpu_custom_call" | custom-call | flops 11000000 | bytes 4875456 | tf_op jit(solution)/shard_map/attend/pallas_call | solution.py:99
  13.4 1.4 attend_store.1
  15.0 1.5 %collective-permute-start.7 = (bf16[128,768]{1,0:T(8,128)(2,1)S(1)}, bf16[128,768]{1,0:T(8,128)(2,1)S(1)}, u32[]{:S(2)}, u32[]{:S(2)}) collective-permute-start(bf16[128,768]{1,0:T(8,128)(2,1)S(1)} %fusion.3), channel_id=1, source_target_pairs={{0,2},{1,3},{2,0},{3,1},{4,6},{5,7},{6,4},{7,5},{8,10},{9,11},{10,... | collective-permute-start | bytes 589832 | tf_op jit(solution)/shard_map/ppermute | solution.py:167
  17.3 5.8 %all-to-all-start = ((bf16[8,16,768]{2,1,0:T(8,128)(2,1)}), bf16[8,16,768]{2,1,0:T(8,128)(2,1)S(1)}, u32[]{:S(2)}, u32[]{:S(2)}) async-start(bf16[8,16,768]{2,1,0:T(8,128)(2,1)} %bitcast.10), calls=%async_computation | async-start | bytes 393216 | tf_op jit(solution)/shard_map/all_to_all | solution.py:398
  23.1 1.4 route.1
  24.6 6.6 %all-to-all-done = bf16[8,16,768]{2,1,0:T(8,128)(2,1)S(1)} async-done(((bf16[8,16,768]{2,1,0:T(8,128)(2,1)}), bf16[8,16,768]{2,1,0:T(8,128)(2,1)S(1)}, u32[]{:S(2)}, u32[]{:S(2)}) %all-to-all-start) | async-done | bytes 196640 | tf_op jit(solution)/shard_map/all_to_all | solution.py:398
  31.7 3.4 %all-to-all-start.1 = ((bf16[8,16,896]{2,1,0:T(8,128)(2,1)}), bf16[8,16,896]{2,1,0:T(8,128)(2,1)S(1)}, u32[]{:S(2)}, u32[]{:S(2)}) async-start(bf16[8,16,896]{2,1,0:T(8,128)(2,1)} %bitcast.12), calls=%async_computation.1 | async-start | bytes 458752 | tf_op jit(solution)/shard_map/all_to_all | solution.py:398
  35.2 1.6 %collective-permute-done.12.refs_3_ = bf16[128,768]{1,0:T(8,128)(2,1)S(1)} collective-permute-done((bf16[128,768]{1,0:T(8,128)(2,1)S(1)}, bf16[128,768]{1,0:T(8,128)(2,1)S(1)}, u32[]{:S(2)}, u32[]{:S(2)}) %collective-permute-start.12) | collective-permute-done | bytes 196640 | tf_op jit(solution)/shard_map/ppermute | solution.py:167
  37.6 1.4 collective-permute-start.9
  39.1 1.6 %collective-permute-done.10.refs_9_ = bf16[128,192]{1,0:T(8,128)(2,1)S(1)} collective-permute-done((bf16[128,192]{1,0:T(8,128)(2,1)S(1)}, bf16[128,192]{1,0:T(8,128)(2,1)S(1)}, u32[]{:S(2)}, u32[]{:S(2)}) %collective-permute-start.10) | collective-permute-done | bytes 49184 | tf_op jit(solution)/shard_map/ppermute | solution.py:167
  40.7 2.0 %collective-permute-done.9.refs_8_ = bf16[128,192]{1,0:T(8,128)(2,1)S(1)} collective-permute-done((bf16[128,192]{1,0:T(8,128)(2,1)S(1)}, bf16[128,192]{1,0:T(8,128)(2,1)S(1)}, u32[]{:S(2)}, u32[]{:S(2)}) %collective-permute-start.9) | collective-permute-done | bytes 49184 | tf_op jit(solution)/shard_map/ppermute | solution.py:167
  42.7 1.6 %state.1 = (f32[128,768]{1,0:T(8,128)}, f32[128,128]{1,0:T(8,128)}, bf16[128,768]{1,0:T(8,128)(2,1)}) custom-call(s32[1]{0:T(128)} %bitcast.refs_0_.token_ref, bf16[128,768]{1,0:T(8,128)(2,1)S(1)} %get-tuple-element.228.refs_0_.refs_1_, bf16[2,128,768]{2,1,0:T(8,128)(2,1)S(1)} %collective-permute-done.6.refs_1_.refs_2_, ...), custom_call_target="tpu_custom_call" | custom-call | flops 11000000 | bytes 1859588 | tf_op jit(solution)/shard_map/state/pallas_call | solution.py:99
  45.4 1.6 %expert_arguments.1 = (bf16[1,768,768]{2,1,0:T(8,128)(2,1)S(1)}, bf16[1,768,768]{2,1,0:T(8,128)(2,1)S(1)}) custom-call(s32[1]{0:T(128)} %bitcast.refs_0_.token_ref, bf16[1,768,768]{2,1,0:T(8,128)(2,1)} %refs_0_.2, bf16[1,768,768]{2,1,0:T(8,128)(2,1)} %refs_3_.1), custom_call_target="tpu_custom_call" | custom-call | tf_op jit(solution)/shard_map/expert_arguments/pallas_call | solution.py:130
  47.0 1.6 %douts.1 = (bf16[256,768]{1,0:T(8,128)(2,1)S(1)}, bf16[256,768]{1,0:T(8,128)(2,1)S(1)}) custom-call(s32[1]{0:T(128)} %bitcast.refs_0_.token_ref, bf16[128,768]{1,0:T(8,128)(2,1)S(1)} %bitcast.59, bf16[128,768]{1,0:T(8,128)(2,1)S(1)} %collective-permute-done.11.refs_2_, bf16[128,768]{1,0:T(8,128)(2,1)S(1)} %collective-permute-done.12.refs_3_, ...), custom_call_target="tpu_custom_call" | custom-call | flops 11000000 | bytes 1572868 | tf_op jit(solution)/shard_map/douts/pallas_call | solution.py:99
  48.7 1.4 expert_near.1
  50.3 2.2 %collective-permute-done.14.refs_0_ = bf16[128,896]{1,0:T(8,128)(2,1)S(1)} collective-permute-done((bf16[128,896]{1,0:T(8,128)(2,1)S(1)}, bf16[128,896]{1,0:T(8,128)(2,1)S(1)}, u32[]{:S(2)}, u32[]{:S(2)}) %collective-permute-start.14) | collective-permute-done | bytes 229408 | tf_op jit(solution)/shard_map/ppermute | solution.py:167
  52.5 1.5 collective-permute-done.17.refs_1_
  55.5 1.4 collective-permute-done.18
  58.7 1.7 %expert_store.1 = (bf16[256,768]{1,0:T(8,128)(2,1)}, bf16[256,768]{1,0:T(8,128)(2,1)}, bf16[256,768]{1,0:T(8,128)(2,1)}, bf16[256,768]{1,0:T(8,128)(2,1)}, bf16[...) custom-call(bf16[256,768]{1,0:T(8,128)(2,1)S(1)} %get-tuple-element.281.ref, ...), custom_call_target="tpu_custom_call" | custom-call | tf_op jit(solution)/shard_map/expert_store/pallas_call | solution.py:154
  60.4 4.2 %collective-permute-done.20 = bf16[128,896]{1,0:T(8,128)(2,1)S(1)} collective-permute-done((bf16[128,896]{1,0:T(8,128)(2,1)S(1)}, bf16[128,896]{1,0:T(8,128)(2,1)S(1)}, u32[]{:S(2)}, u32[]{:S(2)}) %collective-permute-start.20) | collective-permute-done | bytes 229408 | tf_op jit(solution)/shard_map/ppermute | solution.py:167
  66.3 5.4 %all-to-all-start.3 = ((bf16[8,16,896]{2,1,0:T(8,128)(2,1)}), bf16[8,16,896]{2,1,0:T(8,128)(2,1)S(1)}, u32[]{:S(2)}, u32[]{:S(2)}) async-start(bf16[8,16,896]{2,1,0:T(8,128)(2,1)} %bitcast.22), calls=%async_computation.3 | async-start | bytes 458752 | tf_op jit(solution)/shard_map/all_to_all | solution.py:398
  73.5 6.2 %all-to-all-done.3 = bf16[8,16,896]{2,1,0:T(8,128)(2,1)S(1)} async-done(((bf16[8,16,896]{2,1,0:T(8,128)(2,1)}), bf16[8,16,896]{2,1,0:T(8,128)(2,1)S(1)}, u32[]{:S(2)}, u32[]{:S(2)}) %all-to-all-start.3) | async-done | bytes 229408 | tf_op jit(solution)/shard_map/all_to_all | solution.py:398
  81.2 3.4 %all-to-all-start.2 = ((bf16[8,16,768]{2,1,0:T(8,128)(2,1)}), bf16[8,16,768]{2,1,0:T(8,128)(2,1)S(1)}, u32[]{:S(2)}, u32[]{:S(2)}) async-start(bf16[8,16,768]{2,1,0:T(8,128)(2,1)} %bitcast.20), calls=%async_computation.2 | async-start | bytes 393216 | tf_op jit(solution)/shard_map/all_to_all | solution.py:398
  84.6 2.0 %attend_again.1 = (bf16[192,768]{1,0:T(8,128)(2,1)S(1)}, bf16[192,384]{1,0:T(8,128)(2,1)S(1)}, bf16[192,384]{1,0:T(8,128)(2,1)S(1)}, bf16[192,384]{1,0:T(8,128)(...) custom-call(s32[1]{0:T(128)} %bitcast.refs_0_.token_ref, ...), custom_call_target="tpu_custom_call" | custom-call | tf_op jit(solution)/shard_map/attend_again/pallas_call | solution.py:130
  88.3 5.1 %attend_back.1 = (bf16[192,384]{1,0:T(8,128)(2,1)S(1)}, bf16[208,384]{1,0:T(8,128)(2,1)S(1)}, bf16[208,384]{1,0:T(8,128)(2,1)S(1)}, bf16[2,208,384]{2,1,0:T(8,12...) custom-call(s32[1]{0:T(128)} %bitcast.refs_0_.token_ref, ...), custom_call_target="tpu_custom_call" | custom-call | flops 11000000 | bytes 6173184 | tf_op jit(solution)/shard_map/attend_back/pallas_call | solution.py:99
  93.9 1.9 %collective-permute-start.29 = (bf16[256,768]{1,0:T(8,128)(2,1)S(1)}, bf16[256,768]{1,0:T(8,128)(2,1)S(1)}, u32[]{:S(2)}, u32[]{:S(2)}) collective-permute-start(bf16[256,768]{1,0:T(8,128)(2,1)S(1)} %get-tuple-element.378), channel_id=1, source_target_pairs={{0,4},{4,0},{8,12},{12,8},{16,20},{20,16},{24,28},{28,24},{1,5},{5... | collective-permute-start | bytes 1179656 | tf_op jit(solution)/shard_map/ppermute | solution.py:167
  95.7 1.5 collective-permute-start.26
  97.2 2.4 %collective-permute-start.27 = (bf16[80,768]{1,0:T(8,128)(2,1)S(1)}, bf16[80,768]{1,0:T(8,128)(2,1)S(1)}, u32[]{:S(2)}, u32[]{:S(2)}) collective-permute-start(bf16[80,768]{1,0:T(8,128)(2,1)S(1)} %get-tuple-element.376), channel_id=1, source_target_pairs={{0,16},{4,20},{8,24},{12,28},{16,0},{20,4},{24,8},{28,12},{1,17},{... | collective-permute-start | bytes 368648 | tf_op jit(solution)/shard_map/ppermute | solution.py:167
  100.1 5.0 %expert_weights.1 = (bf16[1,768,768]{2,1,0:T(8,128)(2,1)}, bf16[1,768,768]{2,1,0:T(8,128)(2,1)}) custom-call(s32[1]{0:T(128)} %bitcast.refs_0_.token_ref, bf16[256,768]{1,0:T(8,128)(2,1)} %get-tuple-element.365.refs_1_, bf16[256,768]{1,0:T(8,128)(2,1)} %get-tuple-element.366.refs_2_, bf16[256,768]{1,0:T(8,128)(2,1)} %get-tuple-element.367.refs_3_, ...), custom_call_target="tpu_custom_call" | custom-call | flops 13200000000 | bytes 5505028 | tf_op jit(solution)/shard_map/expert_weights/pallas_call | solution.py:99
  105.1 4.4 %collective-permute-done.27 = bf16[80,768]{1,0:T(8,128)(2,1)S(1)} collective-permute-done((bf16[80,768]{1,0:T(8,128)(2,1)S(1)}, bf16[80,768]{1,0:T(8,128)(2,1)S(1)}, u32[]{:S(2)}, u32[]{:S(2)}) %collective-permute-start.27) | collective-permute-done | bytes 122912 | tf_op jit(solution)/shard_map/ppermute | solution.py:167
  109.7 1.9 %collective-permute-start.32 = (bf16[64,768]{1,0:T(8,128)(2,1)S(1)}, bf16[64,768]{1,0:T(8,128)(2,1)S(1)}, u32[]{:S(2)}, u32[]{:S(2)}) collective-permute-start(bf16[64,768]{1,0:T(8,128)(2,1)S(1)} %get-tuple-element.432), channel_id=1, source_target_pairs={{0,8},{4,12},{8,0},{12,4},{16,24},{20,28},{24,16},{28,20},{1,9},{5... | collective-permute-start | bytes 294920 | tf_op jit(solution)/shard_map/ppermute | solution.py:167
  112.6 1.6 %collective-permute-start.34 = (bf16[64,768]{1,0:T(8,128)(2,1)S(1)}, bf16[64,768]{1,0:T(8,128)(2,1)S(1)}, u32[]{:S(2)}, u32[]{:S(2)}) collective-permute-start(bf16[64,768]{1,0:T(8,128)(2,1)S(1)} %get-tuple-element.430), channel_id=1, source_target_pairs={{0,24},{4,28},{8,16},{12,20},{16,8},{20,12},{24,0},{28,4},{1,25},{... | collective-permute-start | bytes 294920 | tf_op jit(solution)/shard_map/ppermute | solution.py:167
  114.9 1.5 collective-permute-start.30
  116.3 1.4 layer_rows.1
  118.6 2.2 %collective-permute-done.33 = bf16[64,768]{1,0:T(8,128)(2,1)S(1)} collective-permute-done((bf16[64,768]{1,0:T(8,128)(2,1)S(1)}, bf16[64,768]{1,0:T(8,128)(2,1)S(1)}, u32[]{:S(2)}, u32[]{:S(2)}) %collective-permute-start.33) | collective-permute-done | bytes 98336 | tf_op jit(solution)/shard_map/ppermute | solution.py:167
  122.0 1.4 collective-permute-start.37
  124.7 1.6 %collective-permute-start.41 = (bf16[64,768]{1,0:T(8,128)(2,1)S(1)}, bf16[64,768]{1,0:T(8,128)(2,1)S(1)}, u32[]{:S(2)}, u32[]{:S(2)}) collective-permute-start(bf16[64,768]{1,0:T(8,128)(2,1)S(1)} %add_convert_fusion.2.refs_3_), channel_id=1, source_target_pairs={{0,8},{4,12},{8,0},{12,4},{16,24},{20,28},{24,16},{28,20},{1,9},{5... | collective-permute-start | bytes 294920 | tf_op jit(solution)/shard_map/ppermute | solution.py:167
  127.7 1.4 collective-permute-start.43
  129.1 3.9 %collective-permute-done.38.refs_4_ = bf16[192,128]{1,0:T(8,128)(2,1)S(1)} collective-permute-done((bf16[192,128]{1,0:T(8,128)(2,1)S(1)}, bf16[192,128]{1,0:T(8,128)(2,1)S(1)}, u32[]{:S(2)}, u32[]{:S(2)}) %collective-permute-start.38) | collective-permute-done | bytes 49184 | tf_op jit(solution)/shard_map/ppermute | solution.py:167
  133.1 3.6 %collective-permute-done.42 = bf16[64,768]{1,0:T(8,128)(2,1)S(1)} collective-permute-done((bf16[64,768]{1,0:T(8,128)(2,1)S(1)}, bf16[64,768]{1,0:T(8,128)(2,1)S(1)}, u32[]{:S(2)}, u32[]{:S(2)}) %collective-permute-start.42) | collective-permute-done | bytes 98336 | tf_op jit(solution)/shard_map/ppermute | solution.py:167
  136.7 1.7 %collective-permute-start.45 = (bf16[64,768]{1,0:T(8,128)(2,1)S(1)}, bf16[64,768]{1,0:T(8,128)(2,1)S(1)}, u32[]{:S(2)}, u32[]{:S(2)}) collective-permute-start(bf16[64,768]{1,0:T(8,128)(2,1)S(1)} %pad_maximum_fusion.refs_7_), channel_id=1, source_target_pairs={{0,8},{4,12},{8,0},{12,4},{16,24},{20,28},{24,16},{28,20},{1,9},{5... | collective-permute-start | bytes 294920 | tf_op jit(solution)/shard_map/ppermute | solution.py:167
  139.3 1.8 %collective-permute-start.47 = (bf16[64,768]{1,0:T(8,128)(2,1)S(1)}, bf16[64,768]{1,0:T(8,128)(2,1)S(1)}, u32[]{:S(2)}, u32[]{:S(2)}) collective-permute-start(bf16[64,768]{1,0:T(8,128)(2,1)S(1)} %pad_maximum_fusion.refs_7_), channel_id=1, source_target_pairs={{0,24},{4,28},{8,16},{12,20},{16,8},{20,12},{24,0},{28,4},{1,25},{... | collective-permute-start | bytes 294920 | tf_op jit(solution)/shard_map/ppermute | solution.py:167
  142.4 1.7 %layer_out.1 = bf16[192,384]{1,0:T(8,128)(2,1)} custom-call(s32[1,384]{1,0:T(1,128)} %get-tuple-element.302.refs_4_.refs_0_, bf16[192,128]{1,0:T(8,128)(2,1)S(1)} %get-tuple-element.399.refs_1_, bf16[192,128]{1,0:T(8,128)(2,1)S(1)} %collective-permute-done.36.refs_2_, bf16[192,128]{1,0:T(8,128)(2,1)S(1)} %collective-permute-done.37.refs_3_, ...), custom_call_target="tpu_custom_call" | custom-call | flops 13200000000 | bytes 345600 | tf_op jit(solution)/shard_map/layer_out/pallas_call | solution.py:99
  144.1 2.0 %tokens_back.1 = bf16[192,384]{1,0:T(8,128)(2,1)} custom-call(s32[1]{0:T(128)} %bitcast.refs_0_.token_ref, bf16[208,384]{1,0:T(8,128)(2,1)S(1)} %get-tuple-element.404.refs_1_, bf16[2,208,384]{2,1,0:T(8,128)(2,1)S(1)} %collective-permute-done.25.refs_2_, bf16[208,384]{1,0:T(8,128)(2,1)S(1)} %collective-permute-done.30.refs_3_, ...), custom_call_target="tpu_custom_call" | custom-call | flops 13200000000 | bytes 1107460 | tf_op jit(solution)/shard_map/tokens_back/pallas_call | solution.py:99
  146.2 1.7 %collective-permute-done.46.refs_9_ = bf16[64,768]{1,0:T(8,128)(2,1)S(1)} collective-permute-done((bf16[64,768]{1,0:T(8,128)(2,1)S(1)}, bf16[64,768]{1,0:T(8,128)(2,1)S(1)}, u32[]{:S(2)}, u32[]{:S(2)}) %collective-permute-start.46) | collective-permute-done | bytes 98336 | tf_op jit(solution)/shard_map/ppermute | solution.py:167
  (120 shorter events, 28.5 us)
Async XLA Ops:
  0.6 7.5 %collective-permute-start.1 = (bf16[192,384]{1,0:T(8,128)(2,1)}, bf16[192,384]{1,0:T(8,128)(2,1)S(1)}, u32[]{:S(2)}, u32[]{:S(2)}) collective-permute-start(bf16[192,384]{1,0:T(8,128)(2,1)} %bitcast.62), channel_id=1, source_target_pairs={{0,2},{1,3},{2,0},{3,1},{4,6},{5,7},{6,4},{7,5},{8,10},{9,11},{10,... | collective-permute-start | bytes 442376 | tf_op jit(solution)/shard_map/ppermute | solution.py:167
  4.4 3.8 %collective-permute-start.2 = (bf16[16,192]{1,0:T(8,128)(2,1)S(1)}, bf16[16,192]{1,0:T(8,128)(2,1)S(1)}, u32[]{:S(2)}, u32[]{:S(2)}) collective-permute-start(bf16[16,192]{1,0:T(8,128)(2,1)S(1)} %small.1.refs_5_), channel_id=1, source_target_pairs={{0,1},{1,0},{2,3},{3,2},{4,5},{5,4},{6,7},{7,6},{8,9},{9,8},{10,11... | collective-permute-start | bytes 18440 | tf_op jit(solution)/shard_map/ppermute | solution.py:167
  4.5 3.7 %collective-permute-start.3 = (bf16[16,192]{1,0:T(8,128)(2,1)S(1)}, bf16[16,192]{1,0:T(8,128)(2,1)S(1)}, u32[]{:S(2)}, u32[]{:S(2)}) collective-permute-start(bf16[16,192]{1,0:T(8,128)(2,1)S(1)} %small.1.refs_5_), channel_id=1, source_target_pairs={{0,2},{1,3},{2,0},{3,1},{4,6},{5,7},{6,4},{7,5},{8,10},{9,11},{10,... | collective-permute-start | bytes 18440 | tf_op jit(solution)/shard_map/ppermute | solution.py:167
  4.5 3.6 %collective-permute-start.4 = (bf16[16,192]{1,0:T(8,128)(2,1)S(1)}, bf16[16,192]{1,0:T(8,128)(2,1)S(1)}, u32[]{:S(2)}, u32[]{:S(2)}) collective-permute-start(bf16[16,192]{1,0:T(8,128)(2,1)S(1)} %small.1.refs_5_), channel_id=1, source_target_pairs={{0,3},{1,2},{2,1},{3,0},{4,7},{5,6},{6,5},{7,4},{8,11},{9,10},{10,... | collective-permute-start | bytes 18440 | tf_op jit(solution)/shard_map/ppermute | solution.py:167
  6.3 2.1 %collective-permute-start = (bf16[192,384]{1,0:T(8,128)(2,1)}, bf16[192,384]{1,0:T(8,128)(2,1)S(1)}, u32[]{:S(2)}, u32[]{:S(2)}) collective-permute-start(bf16[192,384]{1,0:T(8,128)(2,1)} %bitcast.63), channel_id=1, source_target_pairs={{0,1},{1,0},{2,3},{3,2},{4,5},{5,4},{6,7},{7,6},{8,9},{9,8},{10,11... | collective-permute-start | bytes 442376 | tf_op jit(solution)/shard_map/ppermute | solution.py:167
  15.0 8.1 %collective-permute-start.7 = (bf16[128,768]{1,0:T(8,128)(2,1)S(1)}, bf16[128,768]{1,0:T(8,128)(2,1)S(1)}, u32[]{:S(2)}, u32[]{:S(2)}) collective-permute-start(bf16[128,768]{1,0:T(8,128)(2,1)S(1)} %fusion.3), channel_id=1, source_target_pairs={{0,2},{1,3},{2,0},{3,1},{4,6},{5,7},{6,4},{7,5},{8,10},{9,11},{10,... | collective-permute-start | bytes 589832 | tf_op jit(solution)/shard_map/ppermute | solution.py:167
  17.3 13.9 %all-to-all-start = ((bf16[8,16,768]{2,1,0:T(8,128)(2,1)}), bf16[8,16,768]{2,1,0:T(8,128)(2,1)S(1)}, u32[]{:S(2)}, u32[]{:S(2)}) async-start(bf16[8,16,768]{2,1,0:T(8,128)(2,1)} %bitcast.10), calls=%async_computation | async-start | bytes 393216 | tf_op jit(solution)/shard_map/all_to_all | solution.py:398
  31.2 5.7 %collective-permute-start.12 = (bf16[128,768]{1,0:T(8,128)(2,1)S(1)}, bf16[128,768]{1,0:T(8,128)(2,1)S(1)}, u32[]{:S(2)}, u32[]{:S(2)}) collective-permute-start(bf16[128,768]{1,0:T(8,128)(2,1)S(1)} %bitcast.57), channel_id=1, source_target_pairs={{0,2},{1,3},{2,0},{3,1},{4,6},{5,7},{6,4},{7,5},{8,10},{9,11},{10,... | collective-permute-start | bytes 589832 | tf_op jit(solution)/shard_map/ppermute | solution.py:167
  31.7 12.6 %all-to-all-start.1 = ((bf16[8,16,896]{2,1,0:T(8,128)(2,1)}), bf16[8,16,896]{2,1,0:T(8,128)(2,1)S(1)}, u32[]{:S(2)}, u32[]{:S(2)}) async-start(bf16[8,16,896]{2,1,0:T(8,128)(2,1)} %bitcast.12), calls=%async_computation.1 | async-start | bytes 458752 | tf_op jit(solution)/shard_map/all_to_all | solution.py:398
  35.2 9.2 %collective-permute-start.11 = (bf16[128,768]{1,0:T(8,128)(2,1)S(1)}, bf16[128,768]{1,0:T(8,128)(2,1)S(1)}, u32[]{:S(2)}, u32[]{:S(2)}) collective-permute-start(bf16[128,768]{1,0:T(8,128)(2,1)S(1)} %bitcast.58), channel_id=1, source_target_pairs={{0,1},{1,0},{2,3},{3,2},{4,5},{5,4},{6,7},{7,6},{8,9},{9,8},{10,11... | collective-permute-start | bytes 589832 | tf_op jit(solution)/shard_map/ppermute | solution.py:167
  36.8 7.5 %collective-permute-start.13 = (bf16[128,768]{1,0:T(8,128)(2,1)S(1)}, bf16[128,768]{1,0:T(8,128)(2,1)S(1)}, u32[]{:S(2)}, u32[]{:S(2)}) collective-permute-start(bf16[128,768]{1,0:T(8,128)(2,1)S(1)} %collective-permute-done.12.refs_3_), channel_id=1, source_target_pairs={{0,1},{1,0},{2,3},{3,2},{4,5},{5,4},{6,7},{7,6},{8,9},{9,8},{10,11... | collective-permute-start | bytes 589832 | tf_op jit(solution)/shard_map/ppermute | solution.py:167
  36.9 3.8 %collective-permute-start.10 = (bf16[128,192]{1,0:T(8,128)(2,1)S(1)}, bf16[128,192]{1,0:T(8,128)(2,1)S(1)}, u32[]{:S(2)}, u32[]{:S(2)}) collective-permute-start(bf16[128,192]{1,0:T(8,128)(2,1)S(1)} %get-tuple-element.433), channel_id=1, source_target_pairs={{0,3},{1,2},{2,1},{3,0},{4,7},{5,6},{6,5},{7,4},{8,11},{9,10},{10,... | collective-permute-start | bytes 147464 | tf_op jit(solution)/shard_map/ppermute | solution.py:167
  37.6 3.1 %collective-permute-start.8 = (bf16[128,192]{1,0:T(8,128)(2,1)S(1)}, bf16[128,192]{1,0:T(8,128)(2,1)S(1)}, u32[]{:S(2)}, u32[]{:S(2)}) collective-permute-start(bf16[128,192]{1,0:T(8,128)(2,1)S(1)} %get-tuple-element.435), channel_id=1, source_target_pairs={{0,1},{1,0},{2,3},{3,2},{4,5},{5,4},{6,7},{7,6},{8,9},{9,8},{10,11... | collective-permute-start | bytes 147464 | tf_op jit(solution)/shard_map/ppermute | solution.py:167
  37.6 5.1 %collective-permute-start.9 = (bf16[128,192]{1,0:T(8,128)(2,1)S(1)}, bf16[128,192]{1,0:T(8,128)(2,1)S(1)}, u32[]{:S(2)}, u32[]{:S(2)}) collective-permute-start(bf16[128,192]{1,0:T(8,128)(2,1)S(1)} %get-tuple-element.434), channel_id=1, source_target_pairs={{0,2},{1,3},{2,0},{3,1},{4,6},{5,7},{6,4},{7,5},{8,10},{9,11},{10,... | collective-permute-start | bytes 147464 | tf_op jit(solution)/shard_map/ppermute | solution.py:167
  44.4 4.3 %collective-permute-start.15 = (bf16[128,896]{1,0:T(8,128)(2,1)S(1)}, bf16[128,896]{1,0:T(8,128)(2,1)S(1)}, u32[]{:S(2)}, u32[]{:S(2)}) collective-permute-start(bf16[128,896]{1,0:T(8,128)(2,1)S(1)} %bitcast.54), channel_id=1, source_target_pairs={{0,1},{1,0},{2,3},{3,2},{4,5},{5,4},{6,7},{7,6},{8,9},{9,8},{10,11... | collective-permute-start | bytes 688136 | tf_op jit(solution)/shard_map/ppermute | solution.py:167
  44.5 8.0 %collective-permute-start.14 = (bf16[128,896]{1,0:T(8,128)(2,1)S(1)}, bf16[128,896]{1,0:T(8,128)(2,1)S(1)}, u32[]{:S(2)}, u32[]{:S(2)}) collective-permute-start(bf16[128,896]{1,0:T(8,128)(2,1)S(1)} %bitcast.55), channel_id=1, source_target_pairs={{0,2},{1,3},{2,0},{3,1},{4,6},{5,7},{6,4},{7,5},{8,10},{9,11},{10,... | collective-permute-start | bytes 688136 | tf_op jit(solution)/shard_map/ppermute | solution.py:167
  50.0 2.4 %collective-permute-start.16 = (bf16[128,896]{1,0:T(8,128)(2,1)S(1)}, bf16[128,896]{1,0:T(8,128)(2,1)S(1)}, u32[]{:S(2)}, u32[]{:S(2)}) collective-permute-start(bf16[128,896]{1,0:T(8,128)(2,1)S(1)} %get-tuple-element.264), channel_id=1, source_target_pairs={{0,1},{1,0},{2,3},{3,2},{4,5},{5,4},{6,7},{7,6},{8,9},{9,8},{10,11... | collective-permute-start | bytes 688136 | tf_op jit(solution)/shard_map/ppermute | solution.py:167
  56.9 7.7 %collective-permute-start.20 = (bf16[128,896]{1,0:T(8,128)(2,1)S(1)}, bf16[128,896]{1,0:T(8,128)(2,1)S(1)}, u32[]{:S(2)}, u32[]{:S(2)}) collective-permute-start(bf16[128,896]{1,0:T(8,128)(2,1)S(1)} %add.56), channel_id=1, source_target_pairs={{0,2},{1,3},{2,0},{3,1},{4,6},{5,7},{6,4},{7,5},{8,10},{9,11},{10,... | collective-permute-start | bytes 688136 | tf_op jit(solution)/shard_map/ppermute | solution.py:167
  58.6 6.7 %collective-permute-start.19 = (bf16[2,128,768]{2,1,0:T(8,128)(2,1)S(1)}, bf16[2,128,768]{2,1,0:T(8,128)(2,1)S(1)}, u32[]{:S(2)}, u32[]{:S(2)}) collective-permute-start(bf16[2,128,768]{2,1,0:T(8,128)(2,1)S(1)} %get-tuple-element.277), channel_id=1, source_target_pairs={{0,1},{1,0},{2,3},{3,2},{4,5},{5,4},{6,7},{7,6},{8,9},{9,8},{10,11... | collective-permute-start | bytes 1179656 | tf_op jit(solution)/shard_map/ppermute | solution.py:167
  65.4 7.4 %collective-permute-start.21 = (bf16[128,768]{1,0:T(8,128)(2,1)S(1)}, bf16[128,768]{1,0:T(8,128)(2,1)S(1)}, u32[]{:S(2)}, u32[]{:S(2)}) collective-permute-start(bf16[128,768]{1,0:T(8,128)(2,1)S(1)} %fusion), channel_id=1, source_target_pairs={{0,2},{1,3},{2,0},{3,1},{4,6},{5,7},{6,4},{7,5},{8,10},{9,11},{10,... | collective-permute-start | bytes 589832 | tf_op jit(solution)/shard_map/ppermute | solution.py:167
  66.3 13.4 %all-to-all-start.3 = ((bf16[8,16,896]{2,1,0:T(8,128)(2,1)}), bf16[8,16,896]{2,1,0:T(8,128)(2,1)S(1)}, u32[]{:S(2)}, u32[]{:S(2)}) async-start(bf16[8,16,896]{2,1,0:T(8,128)(2,1)} %bitcast.22), calls=%async_computation.3 | async-start | bytes 458752 | tf_op jit(solution)/shard_map/all_to_all | solution.py:398
  80.5 6.2 %collective-permute-start.23 = (bf16[128,768]{1,0:T(8,128)(2,1)S(1)}, bf16[128,768]{1,0:T(8,128)(2,1)S(1)}, u32[]{:S(2)}, u32[]{:S(2)}) collective-permute-start(bf16[128,768]{1,0:T(8,128)(2,1)S(1)} %get-tuple-element.314.refs_1_), channel_id=1, source_target_pairs={{0,2},{1,3},{2,0},{3,1},{4,6},{5,7},{6,4},{7,5},{8,10},{9,11},{10,... | collective-permute-start | bytes 589832 | tf_op jit(solution)/shard_map/ppermute | solution.py:167
  81.2 12.2 %all-to-all-start.2 = ((bf16[8,16,768]{2,1,0:T(8,128)(2,1)}), bf16[8,16,768]{2,1,0:T(8,128)(2,1)S(1)}, u32[]{:S(2)}, u32[]{:S(2)}) async-start(bf16[8,16,768]{2,1,0:T(8,128)(2,1)} %bitcast.20), calls=%async_computation.2 | async-start | bytes 393216 | tf_op jit(solution)/shard_map/all_to_all | solution.py:398
  84.6 2.7 %collective-permute-start.22 = (bf16[128,768]{1,0:T(8,128)(2,1)S(1)}, bf16[128,768]{1,0:T(8,128)(2,1)S(1)}, u32[]{:S(2)}, u32[]{:S(2)}) collective-permute-start(bf16[128,768]{1,0:T(8,128)(2,1)S(1)} %get-tuple-element.314.refs_1_), channel_id=1, source_target_pairs={{0,1},{1,0},{2,3},{3,2},{4,5},{5,4},{6,7},{7,6},{8,9},{9,8},{10,11... | collective-permute-start | bytes 589832 | tf_op jit(solution)/shard_map/ppermute | solution.py:167
  93.4 16.1 %collective-permute-start.25 = (bf16[2,208,384]{2,1,0:T(8,128)(2,1)S(1)}, bf16[2,208,384]{2,1,0:T(8,128)(2,1)S(1)}, u32[]{:S(2)}, u32[]{:S(2)}) collective-permute-start(bf16[2,208,384]{2,1,0:T(8,128)(2,1)S(1)} %get-tuple-element.363), channel_id=1, source_target_pairs={{0,1},{1,0},{2,3},{3,2},{4,5},{5,4},{6,7},{7,6},{8,9},{9,8},{10,11... | collective-permute-start | bytes 958472 | tf_op jit(solution)/shard_map/ppermute | solution.py:167
  93.9 15.7 %collective-permute-start.29 = (bf16[256,768]{1,0:T(8,128)(2,1)S(1)}, bf16[256,768]{1,0:T(8,128)(2,1)S(1)}, u32[]{:S(2)}, u32[]{:S(2)}) collective-permute-start(bf16[256,768]{1,0:T(8,128)(2,1)S(1)} %get-tuple-element.378), channel_id=1, source_target_pairs={{0,4},{4,0},{8,12},{12,8},{16,20},{20,16},{24,28},{28,24},{1,5},{5... | collective-permute-start | bytes 1179656 | tf_op jit(solution)/shard_map/ppermute | solution.py:167
  95.7 9.4 %collective-permute-start.26 = (bf16[80,768]{1,0:T(8,128)(2,1)S(1)}, bf16[80,768]{1,0:T(8,128)(2,1)S(1)}, u32[]{:S(2)}, u32[]{:S(2)}) collective-permute-start(bf16[80,768]{1,0:T(8,128)(2,1)S(1)} %get-tuple-element.375), channel_id=1, source_target_pairs={{0,8},{4,12},{8,0},{12,4},{16,24},{20,28},{24,16},{28,20},{1,9},{5... | collective-permute-start | bytes 368648 | tf_op jit(solution)/shard_map/ppermute | solution.py:167
  97.2 12.3 %collective-permute-start.27 = (bf16[80,768]{1,0:T(8,128)(2,1)S(1)}, bf16[80,768]{1,0:T(8,128)(2,1)S(1)}, u32[]{:S(2)}, u32[]{:S(2)}) collective-permute-start(bf16[80,768]{1,0:T(8,128)(2,1)S(1)} %get-tuple-element.376), channel_id=1, source_target_pairs={{0,16},{4,20},{8,24},{12,28},{16,0},{20,4},{24,8},{28,12},{1,17},{... | collective-permute-start | bytes 368648 | tf_op jit(solution)/shard_map/ppermute | solution.py:167
  99.6 9.9 %collective-permute-start.28 = (bf16[80,768]{1,0:T(8,128)(2,1)S(1)}, bf16[80,768]{1,0:T(8,128)(2,1)S(1)}, u32[]{:S(2)}, u32[]{:S(2)}) collective-permute-start(bf16[80,768]{1,0:T(8,128)(2,1)S(1)} %get-tuple-element.377), channel_id=1, source_target_pairs={{0,24},{4,28},{8,16},{12,20},{16,8},{20,12},{24,0},{28,4},{1,25},{... | collective-permute-start | bytes 368648 | tf_op jit(solution)/shard_map/ppermute | solution.py:167
  109.7 9.0 %collective-permute-start.32 = (bf16[64,768]{1,0:T(8,128)(2,1)S(1)}, bf16[64,768]{1,0:T(8,128)(2,1)S(1)}, u32[]{:S(2)}, u32[]{:S(2)}) collective-permute-start(bf16[64,768]{1,0:T(8,128)(2,1)S(1)} %get-tuple-element.432), channel_id=1, source_target_pairs={{0,8},{4,12},{8,0},{12,4},{16,24},{20,28},{24,16},{28,20},{1,9},{5... | collective-permute-start | bytes 294920 | tf_op jit(solution)/shard_map/ppermute | solution.py:167
  111.6 9.2 %collective-permute-start.33 = (bf16[64,768]{1,0:T(8,128)(2,1)S(1)}, bf16[64,768]{1,0:T(8,128)(2,1)S(1)}, u32[]{:S(2)}, u32[]{:S(2)}) collective-permute-start(bf16[64,768]{1,0:T(8,128)(2,1)S(1)} %get-tuple-element.431), channel_id=1, source_target_pairs={{0,16},{4,20},{8,24},{12,28},{16,0},{20,4},{24,8},{28,12},{1,17},{... | collective-permute-start | bytes 294920 | tf_op jit(solution)/shard_map/ppermute | solution.py:167
  112.6 8.2 %collective-permute-start.34 = (bf16[64,768]{1,0:T(8,128)(2,1)S(1)}, bf16[64,768]{1,0:T(8,128)(2,1)S(1)}, u32[]{:S(2)}, u32[]{:S(2)}) collective-permute-start(bf16[64,768]{1,0:T(8,128)(2,1)S(1)} %get-tuple-element.430), channel_id=1, source_target_pairs={{0,24},{4,28},{8,16},{12,20},{16,8},{20,12},{24,0},{28,4},{1,25},{... | collective-permute-start | bytes 294920 | tf_op jit(solution)/shard_map/ppermute | solution.py:167
  114.2 4.4 %collective-permute-start.31 = (bf16[48,768]{1,0:T(8,128)(2,1)S(1)}, bf16[48,768]{1,0:T(8,128)(2,1)S(1)}, u32[]{:S(2)}, u32[]{:S(2)}) collective-permute-start(bf16[48,768]{1,0:T(8,128)(2,1)S(1)} %concatenate.16), channel_id=1, source_target_pairs={{0,4},{4,0},{8,12},{12,8},{16,20},{20,16},{24,28},{28,24},{1,5},{5... | collective-permute-start | bytes 221192 | tf_op jit(solution)/shard_map/ppermute | solution.py:167
  114.9 5.9 %collective-permute-start.30 = (bf16[208,384]{1,0:T(8,128)(2,1)S(1)}, bf16[208,384]{1,0:T(8,128)(2,1)S(1)}, u32[]{:S(2)}, u32[]{:S(2)}) collective-permute-start(bf16[208,384]{1,0:T(8,128)(2,1)S(1)} %bitcast_add_fusion), channel_id=1, source_target_pairs={{0,2},{1,3},{2,0},{3,1},{4,6},{5,7},{6,4},{7,5},{8,10},{9,11},{10,... | collective-permute-start | bytes 479240 | tf_op jit(solution)/shard_map/ppermute | solution.py:167
  120.8 3.9 %collective-permute-start.35 = (f32[16,768]{1,0:T(8,128)S(1)}, f32[16,768]{1,0:T(8,128)S(1)}, u32[]{:S(2)}, u32[]{:S(2)}) collective-permute-start(f32[16,768]{1,0:T(8,128)S(1)} %slice_convert_fusion), channel_id=1, source_target_pairs={{0,1},{1,0},{2,3},{3,2},{4,5},{5,4},{6,7},{7,6},{8,9},{9,8},{10,11... | collective-permute-start | bytes 147464 | tf_op jit(solution)/shard_map/ppermute | solution.py:167
  120.9 5.4 %collective-permute-start.40 = (bf16[32,768]{1,0:T(8,128)(2,1)S(1)}, bf16[32,768]{1,0:T(8,128)(2,1)S(1)}, u32[]{:S(2)}, u32[]{:S(2)}) collective-permute-start(bf16[32,768]{1,0:T(8,128)(2,1)S(1)} %slice.76), channel_id=1, source_target_pairs={{0,4},{4,0},{8,12},{12,8},{16,20},{20,16},{24,28},{28,24},{1,5},{5... | collective-permute-start | bytes 147464 | tf_op jit(solution)/shard_map/ppermute | solution.py:167
  121.9 5.8 %collective-permute-start.36 = (bf16[192,128]{1,0:T(8,128)(2,1)S(1)}, bf16[192,128]{1,0:T(8,128)(2,1)S(1)}, u32[]{:S(2)}, u32[]{:S(2)}) collective-permute-start(bf16[192,128]{1,0:T(8,128)(2,1)S(1)} %get-tuple-element.392), channel_id=1, source_target_pairs={{0,1},{1,0},{2,3},{3,2},{4,5},{5,4},{6,7},{7,6},{8,9},{9,8},{10,11... | collective-permute-start | bytes 147464 | tf_op jit(solution)/shard_map/ppermute | solution.py:167
  122.0 7.1 %collective-permute-start.37 = (bf16[192,128]{1,0:T(8,128)(2,1)S(1)}, bf16[192,128]{1,0:T(8,128)(2,1)S(1)}, u32[]{:S(2)}, u32[]{:S(2)}) collective-permute-start(bf16[192,128]{1,0:T(8,128)(2,1)S(1)} %get-tuple-element.393), channel_id=1, source_target_pairs={{0,2},{1,3},{2,0},{3,1},{4,6},{5,7},{6,4},{7,5},{8,10},{9,11},{10,... | collective-permute-start | bytes 147464 | tf_op jit(solution)/shard_map/ppermute | solution.py:167
  123.5 9.6 %collective-permute-start.39 = (bf16[64,768]{1,0:T(8,128)(2,1)S(1)}, bf16[64,768]{1,0:T(8,128)(2,1)S(1)}, u32[]{:S(2)}, u32[]{:S(2)}) collective-permute-start(bf16[64,768]{1,0:T(8,128)(2,1)S(1)} %add_convert_fusion.2.refs_3_), channel_id=1, source_target_pairs={{0,4},{4,0},{8,12},{12,8},{16,20},{20,16},{24,28},{28,24},{1,5},{5... | collective-permute-start | bytes 294920 | tf_op jit(solution)/shard_map/ppermute | solution.py:167
  124.7 8.4 %collective-permute-start.41 = (bf16[64,768]{1,0:T(8,128)(2,1)S(1)}, bf16[64,768]{1,0:T(8,128)(2,1)S(1)}, u32[]{:S(2)}, u32[]{:S(2)}) collective-permute-start(bf16[64,768]{1,0:T(8,128)(2,1)S(1)} %add_convert_fusion.2.refs_3_), channel_id=1, source_target_pairs={{0,8},{4,12},{8,0},{12,4},{16,24},{20,28},{24,16},{28,20},{1,9},{5... | collective-permute-start | bytes 294920 | tf_op jit(solution)/shard_map/ppermute | solution.py:167
  126.3 10.4 %collective-permute-start.42 = (bf16[64,768]{1,0:T(8,128)(2,1)S(1)}, bf16[64,768]{1,0:T(8,128)(2,1)S(1)}, u32[]{:S(2)}, u32[]{:S(2)}) collective-permute-start(bf16[64,768]{1,0:T(8,128)(2,1)S(1)} %add_convert_fusion.2.refs_3_), channel_id=1, source_target_pairs={{0,16},{4,20},{8,24},{12,28},{16,0},{20,4},{24,8},{28,12},{1,17},{... | collective-permute-start | bytes 294920 | tf_op jit(solution)/shard_map/ppermute | solution.py:167
  127.7 9.0 %collective-permute-start.43 = (bf16[64,768]{1,0:T(8,128)(2,1)S(1)}, bf16[64,768]{1,0:T(8,128)(2,1)S(1)}, u32[]{:S(2)}, u32[]{:S(2)}) collective-permute-start(bf16[64,768]{1,0:T(8,128)(2,1)S(1)} %add_convert_fusion.2.refs_3_), channel_id=1, source_target_pairs={{0,24},{4,28},{8,16},{12,20},{16,8},{20,12},{24,0},{28,4},{1,25},{... | collective-permute-start | bytes 294920 | tf_op jit(solution)/shard_map/ppermute | solution.py:167
  129.1 4.0 %collective-permute-start.38 = (bf16[192,128]{1,0:T(8,128)(2,1)S(1)}, bf16[192,128]{1,0:T(8,128)(2,1)S(1)}, u32[]{:S(2)}, u32[]{:S(2)}) collective-permute-start(bf16[192,128]{1,0:T(8,128)(2,1)S(1)} %get-tuple-element.394), channel_id=1, source_target_pairs={{0,3},{1,2},{2,1},{3,0},{4,7},{5,6},{6,5},{7,4},{8,11},{9,10},{10,... | collective-permute-start | bytes 147464 | tf_op jit(solution)/shard_map/ppermute | solution.py:167
  136.7 9.5 %collective-permute-start.45 = (bf16[64,768]{1,0:T(8,128)(2,1)S(1)}, bf16[64,768]{1,0:T(8,128)(2,1)S(1)}, u32[]{:S(2)}, u32[]{:S(2)}) collective-permute-start(bf16[64,768]{1,0:T(8,128)(2,1)S(1)} %pad_maximum_fusion.refs_7_), channel_id=1, source_target_pairs={{0,8},{4,12},{8,0},{12,4},{16,24},{20,28},{24,16},{28,20},{1,9},{5... | collective-permute-start | bytes 294920 | tf_op jit(solution)/shard_map/ppermute | solution.py:167
  138.4 9.5 %collective-permute-start.46 = (bf16[64,768]{1,0:T(8,128)(2,1)S(1)}, bf16[64,768]{1,0:T(8,128)(2,1)S(1)}, u32[]{:S(2)}, u32[]{:S(2)}) collective-permute-start(bf16[64,768]{1,0:T(8,128)(2,1)S(1)} %pad_maximum_fusion.refs_7_), channel_id=1, source_target_pairs={{0,16},{4,20},{8,24},{12,28},{16,0},{20,4},{24,8},{28,12},{1,17},{... | collective-permute-start | bytes 294920 | tf_op jit(solution)/shard_map/ppermute | solution.py:167
  139.3 8.6 %collective-permute-start.47 = (bf16[64,768]{1,0:T(8,128)(2,1)S(1)}, bf16[64,768]{1,0:T(8,128)(2,1)S(1)}, u32[]{:S(2)}, u32[]{:S(2)}) collective-permute-start(bf16[64,768]{1,0:T(8,128)(2,1)S(1)} %pad_maximum_fusion.refs_7_), channel_id=1, source_target_pairs={{0,24},{4,28},{8,16},{12,20},{16,8},{20,12},{24,0},{28,4},{1,25},{... | collective-permute-start | bytes 294920 | tf_op jit(solution)/shard_map/ppermute | solution.py:167
  141.2 5.0 %collective-permute-start.44 = (f32[16,768]{1,0:T(8,128)S(1)}, f32[16,768]{1,0:T(8,128)S(1)}, u32[]{:S(2)}, u32[]{:S(2)}) collective-permute-start(f32[16,768]{1,0:T(8,128)S(1)} %fusion.4.refs_1_), channel_id=1, source_target_pairs={{0,2},{1,3},{2,0},{3,1},{4,6},{5,7},{6,4},{7,5},{8,10},{9,11},{10,... | collective-permute-start | bytes 147464 | tf_op jit(solution)/shard_map/ppermute | solution.py:167
  141.8 7.0 %collective-permute-start.48 = (bf16[192,768]{1,0:T(8,128)(2,1)S(1)}, bf16[192,768]{1,0:T(8,128)(2,1)S(1)}, u32[]{:S(2)}, u32[]{:S(2)}) collective-permute-start(bf16[192,768]{1,0:T(8,128)(2,1)S(1)} %constant_dynamic-update-slice_fusion.refs_4_), channel_id=1, source_target_pairs={{0,4},{4,0},{8,12},{12,8},{16,20},{20,16},{24,28},{28,24},{1,5},{5... | collective-permute-start | bytes 884744 | tf_op jit(solution)/shard_map/ppermute | solution.py:167
  (14 other events, 35.5 us)

commit v7 on v6

--- a/solution.py
+++ b/solution.py
@@ -546,7 +546,7 @@
         for rel in range(ways):
             out_ref[:, rel * quarter : (rel + 1) * quarter] = cots_ref[rel]
 
-    (d_send,) = run(join_body, [((rows, width), bf16)], (after(me, o_half), cots), "join", us=0.3)
+    (d_send,) = run(join_body, [((rows, width), bf16)], (after(me, o_sent), cots), "join", us=0.3)
     d_arrived = over_experts(d_send)
 
     def routed(kept_ref, beside_ref, across_ref, xrow_ref, small_ref):
@@ -601,7 +601,7 @@
         ],
         (after(me, send), *route_args, *cot_pieces),
         "state",
-        us=0.01,
+        us=1,
     )
     send, d_arrived = lax.optimization_barrier((send, d_arrived))
     d_pieces = gather_pieces(d_arrived)
@@ -701,7 +701,7 @@
         [((rows, width), bf16), ((rows, width), bf16), ((2, rows, width), bf16)],
         (after(me, du_half), near[2], wide[2], w_out),
         "value",
-        us=0.8,
+        us=0.01,
     )
     y_kept, y_passed, y_sent = y_parts
     y_beside = swap(y_sent, "tp", 1)
@@ -1018,7 +1018,7 @@
                     Far(small_far),
                 ),
                 "tokens_back",
-                us=12,
+                us=0.01,
             )
         names = list(extras)
         got = lax.optimization_barrier((*[extras[n] for n in names], *came))
@@ -1078,7 +1078,7 @@
         ],
         (me, held["few"], held["few_other"], *a_blocks, *b_blocks),
         "unpack",
-        us=1.0,
+        us=4,
         scratch=[
             pltpu.VMEM((owners, chunk_a, width), bf16),
             pltpu.VMEM((owners, chunk_b, width), bf16),

time: 151 us -> 150 us (level)
  no operation moved by 1% of the time
where the time goes in v7:
time: 150 us
  starting transfers between devices  59.8 us (40%)
  waiting for transfers between devices  47.1 us (31%)
  Pallas kernels  39.7 us (26%)
  other arithmetic  1.84 us (1%)
    ppermute x49, starting transfers between devices, swap(): return lax.ppermute(value, axis, [(i, i ^ mask) for i in range(size)])  41.8 us
    ppermute x49, waiting for transfers between devices, swap(): return lax.ppermute(value, axis, [(i, i ^ mask) for i in range(size)])  34.3 us
    pallas_call x17, Pallas kernels, run(): pl.pallas_call(wrapped, out_shape=[pltpu.HBM(o[0], o[1]) if len(o) == 3 e...  31.8 us
    all_to_all x4, starting transfers between devices, over_experts(): lax.all_to_all(blocks, 'exp', split_axis=0, concat_axis=0, tiled=True)  18 us
    all_to_all x4, waiting for transfers between devices, over_experts(): lax.all_to_all(blocks, 'exp', split_axis=0, concat_axis=0, tiled=True)  12.7 us
    pallas_call x3, Pallas kernels, fetch(): pl.pallas_call(body, out_shape=[jax.ShapeDtypeStruct(v.shape, v.dtype) fo...  4.8 us
    pallas_call x2, Pallas kernels, store(): pl.pallas_call(body, out_shape=[pltpu.HBM(v.shape, v.dtype) for v in valu...  3.11 us
  transfers between devices with their start and end apart: 53, of which 19 were waited for; matrix products, arithmetic and copies ran while one was open for 1% of the time, Pallas kernels for 22%

profile of v7, /device:TPU:0, one launch (start us, length us, event | category | flops | bytes accessed | tf_op | source)
XLA Modules:
  0.0 149.7 jit_solution(18261283182705181815)
XLA Ops:
  0.6 3.0 %collective-permute-start.1 = (bf16[192,384]{1,0:T(8,128)(2,1)}, bf16[192,384]{1,0:T(8,128)(2,1)S(1)}, u32[]{:S(2)}, u32[]{:S(2)}) collective-permute-start(bf16[192,384]{1,0:T(8,128)(2,1)} %bitcast.60), channel_id=1, source_target_pairs={{0,2},{1,3},{2,0},{3,1},{4,6},{5,7},{6,4},{7,5},{8,10},{9,11},{10,... | collective-permute-start | bytes 442376 | tf_op jit(solution)/shard_map/ppermute | solution.py:167
  4.5 1.8 %collective-permute-start.4 = (bf16[16,192]{1,0:T(8,128)(2,1)S(1)}, bf16[16,192]{1,0:T(8,128)(2,1)S(1)}, u32[]{:S(2)}, u32[]{:S(2)}) collective-permute-start(bf16[16,192]{1,0:T(8,128)(2,1)S(1)} %small.1.refs_5_), channel_id=1, source_target_pairs={{0,3},{1,2},{2,1},{3,0},{4,7},{5,6},{6,5},{7,4},{8,11},{9,10},{10,... | collective-permute-start | bytes 18440 | tf_op jit(solution)/shard_map/ppermute | solution.py:167
  6.7 1.4 slots.1
  9.7 3.5 %attend.1 = (bf16[16,768]{1,0:T(8,128)(2,1)S(1)}, s32[1,384]{1,0:T(1,128)S(1)}, f32[1,384]{1,0:T(1,128)S(1)}, bf16[768,384]{1,0:T(8,128)(2,1)S(1)}, bf16[192,384...) custom-call(s32[1]{0:T(128)} %bitcast.refs_0_.token_ref, ...), custom_call_target="tpu_custom_call" | custom-call | flops 11000000 | bytes 4875456 | tf_op jit(solution)/shard_map/attend/pallas_call | solution.py:99
  13.4 1.4 attend_store.1
  15.0 1.5 %collective-permute-start.7 = (bf16[128,768]{1,0:T(8,128)(2,1)S(1)}, bf16[128,768]{1,0:T(8,128)(2,1)S(1)}, u32[]{:S(2)}, u32[]{:S(2)}) collective-permute-start(bf16[128,768]{1,0:T(8,128)(2,1)S(1)} %fusion.3), channel_id=1, source_target_pairs={{0,2},{1,3},{2,0},{3,1},{4,6},{5,7},{6,4},{7,5},{8,10},{9,11},{10,... | collective-permute-start | bytes 589832 | tf_op jit(solution)/shard_map/ppermute | solution.py:167
  17.3 5.8 %all-to-all-start = ((bf16[8,16,768]{2,1,0:T(8,128)(2,1)}), bf16[8,16,768]{2,1,0:T(8,128)(2,1)S(1)}, u32[]{:S(2)}, u32[]{:S(2)}) async-start(bf16[8,16,768]{2,1,0:T(8,128)(2,1)} %bitcast.10), calls=%async_computation | async-start | bytes 393216 | tf_op jit(solution)/shard_map/all_to_all | solution.py:398
  23.1 1.5 route.1
  24.6 6.6 %all-to-all-done = bf16[8,16,768]{2,1,0:T(8,128)(2,1)S(1)} async-done(((bf16[8,16,768]{2,1,0:T(8,128)(2,1)}), bf16[8,16,768]{2,1,0:T(8,128)(2,1)S(1)}, u32[]{:S(2)}, u32[]{:S(2)}) %all-to-all-start) | async-done | bytes 196640 | tf_op jit(solution)/shard_map/all_to_all | solution.py:398
  31.7 3.4 %all-to-all-start.1 = ((bf16[8,16,896]{2,1,0:T(8,128)(2,1)}), bf16[8,16,896]{2,1,0:T(8,128)(2,1)S(1)}, u32[]{:S(2)}, u32[]{:S(2)}) async-start(bf16[8,16,896]{2,1,0:T(8,128)(2,1)} %bitcast.12), calls=%async_computation.1 | async-start | bytes 458752 | tf_op jit(solution)/shard_map/all_to_all | solution.py:398
  35.2 1.6 %collective-permute-done.12.refs_3_ = bf16[128,768]{1,0:T(8,128)(2,1)S(1)} collective-permute-done((bf16[128,768]{1,0:T(8,128)(2,1)S(1)}, bf16[128,768]{1,0:T(8,128)(2,1)S(1)}, u32[]{:S(2)}, u32[]{:S(2)}) %collective-permute-start.12) | collective-permute-done | bytes 196640 | tf_op jit(solution)/shard_map/ppermute | solution.py:167
  37.6 1.4 collective-permute-start.9
  39.1 1.6 %collective-permute-done.10.refs_9_ = bf16[128,192]{1,0:T(8,128)(2,1)S(1)} collective-permute-done((bf16[128,192]{1,0:T(8,128)(2,1)S(1)}, bf16[128,192]{1,0:T(8,128)(2,1)S(1)}, u32[]{:S(2)}, u32[]{:S(2)}) %collective-permute-start.10) | collective-permute-done | bytes 49184 | tf_op jit(solution)/shard_map/ppermute | solution.py:167
  40.7 2.0 %collective-permute-done.9.refs_8_ = bf16[128,192]{1,0:T(8,128)(2,1)S(1)} collective-permute-done((bf16[128,192]{1,0:T(8,128)(2,1)S(1)}, bf16[128,192]{1,0:T(8,128)(2,1)S(1)}, u32[]{:S(2)}, u32[]{:S(2)}) %collective-permute-start.9) | collective-permute-done | bytes 49184 | tf_op jit(solution)/shard_map/ppermute | solution.py:167
  42.7 1.6 %state.1 = (f32[128,768]{1,0:T(8,128)}, f32[128,128]{1,0:T(8,128)}, bf16[128,768]{1,0:T(8,128)(2,1)}) custom-call(s32[1]{0:T(128)} %bitcast.refs_0_.token_ref, bf16[128,768]{1,0:T(8,128)(2,1)S(1)} %get-tuple-element.228.refs_0_.refs_1_, bf16[2,128,768]{2,1,0:T(8,128)(2,1)S(1)} %collective-permute-done.6.refs_1_.refs_2_, ...), custom_call_target="tpu_custom_call" | custom-call | flops 1100000000 | bytes 1859588 | tf_op jit(solution)/shard_map/state/pallas_call | solution.py:99
  45.4 1.6 %expert_arguments.1 = (bf16[1,768,768]{2,1,0:T(8,128)(2,1)S(1)}, bf16[1,768,768]{2,1,0:T(8,128)(2,1)S(1)}) custom-call(s32[1]{0:T(128)} %bitcast.refs_0_.token_ref, bf16[1,768,768]{2,1,0:T(8,128)(2,1)} %refs_0_.2, bf16[1,768,768]{2,1,0:T(8,128)(2,1)} %refs_3_.1), custom_call_target="tpu_custom_call" | custom-call | tf_op jit(solution)/shard_map/expert_arguments/pallas_call | solution.py:130
  47.0 1.6 %douts.1 = (bf16[256,768]{1,0:T(8,128)(2,1)S(1)}, bf16[256,768]{1,0:T(8,128)(2,1)S(1)}) custom-call(s32[1]{0:T(128)} %bitcast.refs_0_.token_ref, bf16[128,768]{1,0:T(8,128)(2,1)S(1)} %bitcast.59, bf16[128,768]{1,0:T(8,128)(2,1)S(1)} %collective-permute-done.11.refs_2_, bf16[128,768]{1,0:T(8,128)(2,1)S(1)} %collective-permute-done.12.refs_3_, ...), custom_call_target="tpu_custom_call" | custom-call | flops 11000000 | bytes 1572868 | tf_op jit(solution)/shard_map/douts/pallas_call | solution.py:99
  48.7 1.3 expert_near.1
  50.3 2.2 %collective-permute-done.14.refs_0_ = bf16[128,896]{1,0:T(8,128)(2,1)S(1)} collective-permute-done((bf16[128,896]{1,0:T(8,128)(2,1)S(1)}, bf16[128,896]{1,0:T(8,128)(2,1)S(1)}, u32[]{:S(2)}, u32[]{:S(2)}) %collective-permute-start.14) | collective-permute-done | bytes 229408 | tf_op jit(solution)/shard_map/ppermute | solution.py:167
  52.5 1.5 collective-permute-done.17.refs_1_
  58.7 1.7 %expert_store.1 = (bf16[256,768]{1,0:T(8,128)(2,1)}, bf16[256,768]{1,0:T(8,128)(2,1)}, bf16[256,768]{1,0:T(8,128)(2,1)}, bf16[256,768]{1,0:T(8,128)(2,1)}, bf16[...) custom-call(bf16[256,768]{1,0:T(8,128)(2,1)S(1)} %get-tuple-element.281.ref, ...), custom_call_target="tpu_custom_call" | custom-call | tf_op jit(solution)/shard_map/expert_store/pallas_call | solution.py:154
  60.4 4.2 %collective-permute-done.20 = bf16[128,896]{1,0:T(8,128)(2,1)S(1)} collective-permute-done((bf16[128,896]{1,0:T(8,128)(2,1)S(1)}, bf16[128,896]{1,0:T(8,128)(2,1)S(1)}, u32[]{:S(2)}, u32[]{:S(2)}) %collective-permute-start.20) | collective-permute-done | bytes 229408 | tf_op jit(solution)/shard_map/ppermute | solution.py:167
  66.3 5.4 %all-to-all-start.3 = ((bf16[8,16,896]{2,1,0:T(8,128)(2,1)}), bf16[8,16,896]{2,1,0:T(8,128)(2,1)S(1)}, u32[]{:S(2)}, u32[]{:S(2)}) async-start(bf16[8,16,896]{2,1,0:T(8,128)(2,1)} %bitcast.22), calls=%async_computation.3 | async-start | bytes 458752 | tf_op jit(solution)/shard_map/all_to_all | solution.py:398
  73.5 6.2 %all-to-all-done.3 = bf16[8,16,896]{2,1,0:T(8,128)(2,1)S(1)} async-done(((bf16[8,16,896]{2,1,0:T(8,128)(2,1)}), bf16[8,16,896]{2,1,0:T(8,128)(2,1)S(1)}, u32[]{:S(2)}, u32[]{:S(2)}) %all-to-all-start.3) | async-done | bytes 229408 | tf_op jit(solution)/shard_map/all_to_all | solution.py:398
  81.2 3.4 %all-to-all-start.2 = ((bf16[8,16,768]{2,1,0:T(8,128)(2,1)}), bf16[8,16,768]{2,1,0:T(8,128)(2,1)S(1)}, u32[]{:S(2)}, u32[]{:S(2)}) async-start(bf16[8,16,768]{2,1,0:T(8,128)(2,1)} %bitcast.20), calls=%async_computation.2 | async-start | bytes 393216 | tf_op jit(solution)/shard_map/all_to_all | solution.py:398
  84.6 2.0 %attend_again.1 = (bf16[192,768]{1,0:T(8,128)(2,1)S(1)}, bf16[192,384]{1,0:T(8,128)(2,1)S(1)}, bf16[192,384]{1,0:T(8,128)(2,1)S(1)}, bf16[192,384]{1,0:T(8,128)(...) custom-call(s32[1]{0:T(128)} %bitcast.refs_0_.token_ref, ...), custom_call_target="tpu_custom_call" | custom-call | tf_op jit(solution)/shard_map/attend_again/pallas_call | solution.py:130
  88.3 5.1 %attend_back.1 = (bf16[192,384]{1,0:T(8,128)(2,1)S(1)}, bf16[208,384]{1,0:T(8,128)(2,1)S(1)}, bf16[208,384]{1,0:T(8,128)(2,1)S(1)}, bf16[2,208,384]{2,1,0:T(8,12...) custom-call(s32[1]{0:T(128)} %bitcast.refs_0_.token_ref, ...), custom_call_target="tpu_custom_call" | custom-call | flops 11000000 | bytes 6173184 | tf_op jit(solution)/shard_map/attend_back/pallas_call | solution.py:99
  93.9 1.8 %collective-permute-start.29 = (bf16[256,768]{1,0:T(8,128)(2,1)S(1)}, bf16[256,768]{1,0:T(8,128)(2,1)S(1)}, u32[]{:S(2)}, u32[]{:S(2)}) collective-permute-start(bf16[256,768]{1,0:T(8,128)(2,1)S(1)} %get-tuple-element.378), channel_id=1, source_target_pairs={{0,4},{4,0},{8,12},{12,8},{16,20},{20,16},{24,28},{28,24},{1,5},{5... | collective-permute-start | bytes 1179656 | tf_op jit(solution)/shard_map/ppermute | solution.py:167
  95.7 1.5 collective-permute-start.26
  97.2 2.4 %collective-permute-start.27 = (bf16[80,768]{1,0:T(8,128)(2,1)S(1)}, bf16[80,768]{1,0:T(8,128)(2,1)S(1)}, u32[]{:S(2)}, u32[]{:S(2)}) collective-permute-start(bf16[80,768]{1,0:T(8,128)(2,1)S(1)} %get-tuple-element.376), channel_id=1, source_target_pairs={{0,16},{4,20},{8,24},{12,28},{16,0},{20,4},{24,8},{28,12},{1,17},{... | collective-permute-start | bytes 368648 | tf_op jit(solution)/shard_map/ppermute | solution.py:167
  100.1 5.0 %expert_weights.1 = (bf16[1,768,768]{2,1,0:T(8,128)(2,1)}, bf16[1,768,768]{2,1,0:T(8,128)(2,1)}) custom-call(s32[1]{0:T(128)} %bitcast.refs_0_.token_ref, bf16[256,768]{1,0:T(8,128)(2,1)} %get-tuple-element.365.refs_1_, bf16[256,768]{1,0:T(8,128)(2,1)} %get-tuple-element.366.refs_2_, bf16[256,768]{1,0:T(8,128)(2,1)} %get-tuple-element.367.refs_3_, ...), custom_call_target="tpu_custom_call" | custom-call | flops 13200000000 | bytes 5505028 | tf_op jit(solution)/shard_map/expert_weights/pallas_call | solution.py:99
  105.1 4.4 %collective-permute-done.27 = bf16[80,768]{1,0:T(8,128)(2,1)S(1)} collective-permute-done((bf16[80,768]{1,0:T(8,128)(2,1)S(1)}, bf16[80,768]{1,0:T(8,128)(2,1)S(1)}, u32[]{:S(2)}, u32[]{:S(2)}) %collective-permute-start.27) | collective-permute-done | bytes 122912 | tf_op jit(solution)/shard_map/ppermute | solution.py:167
  109.7 1.9 %collective-permute-start.32 = (bf16[64,768]{1,0:T(8,128)(2,1)S(1)}, bf16[64,768]{1,0:T(8,128)(2,1)S(1)}, u32[]{:S(2)}, u32[]{:S(2)}) collective-permute-start(bf16[64,768]{1,0:T(8,128)(2,1)S(1)} %get-tuple-element.432), channel_id=1, source_target_pairs={{0,8},{4,12},{8,0},{12,4},{16,24},{20,28},{24,16},{28,20},{1,9},{5... | collective-permute-start | bytes 294920 | tf_op jit(solution)/shard_map/ppermute | solution.py:167
  112.6 1.6 %collective-permute-start.34 = (bf16[64,768]{1,0:T(8,128)(2,1)S(1)}, bf16[64,768]{1,0:T(8,128)(2,1)S(1)}, u32[]{:S(2)}, u32[]{:S(2)}) collective-permute-start(bf16[64,768]{1,0:T(8,128)(2,1)S(1)} %get-tuple-element.430), channel_id=1, source_target_pairs={{0,24},{4,28},{8,16},{12,20},{16,8},{20,12},{24,0},{28,4},{1,25},{... | collective-permute-start | bytes 294920 | tf_op jit(solution)/shard_map/ppermute | solution.py:167
  114.9 1.5 collective-permute-start.30
  116.3 1.4 layer_rows.1
  118.6 2.2 %collective-permute-done.33 = bf16[64,768]{1,0:T(8,128)(2,1)S(1)} collective-permute-done((bf16[64,768]{1,0:T(8,128)(2,1)S(1)}, bf16[64,768]{1,0:T(8,128)(2,1)S(1)}, u32[]{:S(2)}, u32[]{:S(2)}) %collective-permute-start.33) | collective-permute-done | bytes 98336 | tf_op jit(solution)/shard_map/ppermute | solution.py:167
  122.0 1.4 collective-permute-start.37
  124.7 1.6 %collective-permute-start.41 = (bf16[64,768]{1,0:T(8,128)(2,1)S(1)}, bf16[64,768]{1,0:T(8,128)(2,1)S(1)}, u32[]{:S(2)}, u32[]{:S(2)}) collective-permute-start(bf16[64,768]{1,0:T(8,128)(2,1)S(1)} %add_convert_fusion.2.refs_3_), channel_id=1, source_target_pairs={{0,8},{4,12},{8,0},{12,4},{16,24},{20,28},{24,16},{28,20},{1,9},{5... | collective-permute-start | bytes 294920 | tf_op jit(solution)/shard_map/ppermute | solution.py:167
  126.3 1.4 collective-permute-start.42
  127.7 1.4 collective-permute-start.43
  129.1 3.9 %collective-permute-done.38.refs_4_ = bf16[192,128]{1,0:T(8,128)(2,1)S(1)} collective-permute-done((bf16[192,128]{1,0:T(8,128)(2,1)S(1)}, bf16[192,128]{1,0:T(8,128)(2,1)S(1)}, u32[]{:S(2)}, u32[]{:S(2)}) %collective-permute-start.38) | collective-permute-done | bytes 49184 | tf_op jit(solution)/shard_map/ppermute | solution.py:167
  133.1 3.6 %collective-permute-done.42 = bf16[64,768]{1,0:T(8,128)(2,1)S(1)} collective-permute-done((bf16[64,768]{1,0:T(8,128)(2,1)S(1)}, bf16[64,768]{1,0:T(8,128)(2,1)S(1)}, u32[]{:S(2)}, u32[]{:S(2)}) %collective-permute-start.42) | collective-permute-done | bytes 98336 | tf_op jit(solution)/shard_map/ppermute | solution.py:167
  136.7 1.7 %collective-permute-start.45 = (bf16[64,768]{1,0:T(8,128)(2,1)S(1)}, bf16[64,768]{1,0:T(8,128)(2,1)S(1)}, u32[]{:S(2)}, u32[]{:S(2)}) collective-permute-start(bf16[64,768]{1,0:T(8,128)(2,1)S(1)} %pad_maximum_fusion.refs_7_), channel_id=1, source_target_pairs={{0,8},{4,12},{8,0},{12,4},{16,24},{20,28},{24,16},{28,20},{1,9},{5... | collective-permute-start | bytes 294920 | tf_op jit(solution)/shard_map/ppermute | solution.py:167
  139.3 1.8 %collective-permute-start.47 = (bf16[64,768]{1,0:T(8,128)(2,1)S(1)}, bf16[64,768]{1,0:T(8,128)(2,1)S(1)}, u32[]{:S(2)}, u32[]{:S(2)}) collective-permute-start(bf16[64,768]{1,0:T(8,128)(2,1)S(1)} %pad_maximum_fusion.refs_7_), channel_id=1, source_target_pairs={{0,24},{4,28},{8,16},{12,20},{16,8},{20,12},{24,0},{28,4},{1,25},{... | collective-permute-start | bytes 294920 | tf_op jit(solution)/shard_map/ppermute | solution.py:167
  142.5 1.7 %layer_out.1 = bf16[192,384]{1,0:T(8,128)(2,1)} custom-call(s32[1,384]{1,0:T(1,128)} %get-tuple-element.302.refs_4_.refs_0_, bf16[192,128]{1,0:T(8,128)(2,1)S(1)} %get-tuple-element.399.refs_1_, bf16[192,128]{1,0:T(8,128)(2,1)S(1)} %collective-permute-done.36.refs_2_, bf16[192,128]{1,0:T(8,128)(2,1)S(1)} %collective-permute-done.37.refs_3_, ...), custom_call_target="tpu_custom_call" | custom-call | flops 13200000000 | bytes 345600 | tf_op jit(solution)/shard_map/layer_out/pallas_call | solution.py:99
  144.1 2.0 %tokens_back.1 = bf16[192,384]{1,0:T(8,128)(2,1)} custom-call(s32[1]{0:T(128)} %bitcast.refs_0_.token_ref, bf16[208,384]{1,0:T(8,128)(2,1)S(1)} %get-tuple-element.404.refs_1_, bf16[2,208,384]{2,1,0:T(8,128)(2,1)S(1)} %collective-permute-done.25.refs_2_, bf16[208,384]{1,0:T(8,128)(2,1)S(1)} %collective-permute-done.30.refs_3_, ...), custom_call_target="tpu_custom_call" | custom-call | flops 11000000 | bytes 1107460 | tf_op jit(solution)/shard_map/tokens_back/pallas_call | solution.py:99
  146.2 1.7 %collective-permute-done.46.refs_9_ = bf16[64,768]{1,0:T(8,128)(2,1)S(1)} collective-permute-done((bf16[64,768]{1,0:T(8,128)(2,1)S(1)}, bf16[64,768]{1,0:T(8,128)(2,1)S(1)}, u32[]{:S(2)}, u32[]{:S(2)}) %collective-permute-start.46) | collective-permute-done | bytes 98336 | tf_op jit(solution)/shard_map/ppermute | solution.py:167
  (120 shorter events, 28.1 us)
Async XLA Ops:
  0.6 7.5 %collective-permute-start.1 = (bf16[192,384]{1,0:T(8,128)(2,1)}, bf16[192,384]{1,0:T(8,128)(2,1)S(1)}, u32[]{:S(2)}, u32[]{:S(2)}) collective-permute-start(bf16[192,384]{1,0:T(8,128)(2,1)} %bitcast.60), channel_id=1, source_target_pairs={{0,2},{1,3},{2,0},{3,1},{4,6},{5,7},{6,4},{7,5},{8,10},{9,11},{10,... | collective-permute-start | bytes 442376 | tf_op jit(solution)/shard_map/ppermute | solution.py:167
  4.4 3.8 %collective-permute-start.2 = (bf16[16,192]{1,0:T(8,128)(2,1)S(1)}, bf16[16,192]{1,0:T(8,128)(2,1)S(1)}, u32[]{:S(2)}, u32[]{:S(2)}) collective-permute-start(bf16[16,192]{1,0:T(8,128)(2,1)S(1)} %small.1.refs_5_), channel_id=1, source_target_pairs={{0,1},{1,0},{2,3},{3,2},{4,5},{5,4},{6,7},{7,6},{8,9},{9,8},{10,11... | collective-permute-start | bytes 18440 | tf_op jit(solution)/shard_map/ppermute | solution.py:167
  4.5 3.7 %collective-permute-start.3 = (bf16[16,192]{1,0:T(8,128)(2,1)S(1)}, bf16[16,192]{1,0:T(8,128)(2,1)S(1)}, u32[]{:S(2)}, u32[]{:S(2)}) collective-permute-start(bf16[16,192]{1,0:T(8,128)(2,1)S(1)} %small.1.refs_5_), channel_id=1, source_target_pairs={{0,2},{1,3},{2,0},{3,1},{4,6},{5,7},{6,4},{7,5},{8,10},{9,11},{10,... | collective-permute-start | bytes 18440 | tf_op jit(solution)/shard_map/ppermute | solution.py:167
  4.5 3.6 %collective-permute-start.4 = (bf16[16,192]{1,0:T(8,128)(2,1)S(1)}, bf16[16,192]{1,0:T(8,128)(2,1)S(1)}, u32[]{:S(2)}, u32[]{:S(2)}) collective-permute-start(bf16[16,192]{1,0:T(8,128)(2,1)S(1)} %small.1.refs_5_), channel_id=1, source_target_pairs={{0,3},{1,2},{2,1},{3,0},{4,7},{5,6},{6,5},{7,4},{8,11},{9,10},{10,... | collective-permute-start | bytes 18440 | tf_op jit(solution)/shard_map/ppermute | solution.py:167
  6.3 2.1 %collective-permute-start = (bf16[192,384]{1,0:T(8,128)(2,1)}, bf16[192,384]{1,0:T(8,128)(2,1)S(1)}, u32[]{:S(2)}, u32[]{:S(2)}) collective-permute-start(bf16[192,384]{1,0:T(8,128)(2,1)} %bitcast.61), channel_id=1, source_target_pairs={{0,1},{1,0},{2,3},{3,2},{4,5},{5,4},{6,7},{7,6},{8,9},{9,8},{10,11... | collective-permute-start | bytes 442376 | tf_op jit(solution)/shard_map/ppermute | solution.py:167
  15.0 8.1 %collective-permute-start.7 = (bf16[128,768]{1,0:T(8,128)(2,1)S(1)}, bf16[128,768]{1,0:T(8,128)(2,1)S(1)}, u32[]{:S(2)}, u32[]{:S(2)}) collective-permute-start(bf16[128,768]{1,0:T(8,128)(2,1)S(1)} %fusion.3), channel_id=1, source_target_pairs={{0,2},{1,3},{2,0},{3,1},{4,6},{5,7},{6,4},{7,5},{8,10},{9,11},{10,... | collective-permute-start | bytes 589832 | tf_op jit(solution)/shard_map/ppermute | solution.py:167
  17.3 13.9 %all-to-all-start = ((bf16[8,16,768]{2,1,0:T(8,128)(2,1)}), bf16[8,16,768]{2,1,0:T(8,128)(2,1)S(1)}, u32[]{:S(2)}, u32[]{:S(2)}) async-start(bf16[8,16,768]{2,1,0:T(8,128)(2,1)} %bitcast.10), calls=%async_computation | async-start | bytes 393216 | tf_op jit(solution)/shard_map/all_to_all | solution.py:398
  31.2 5.7 %collective-permute-start.12 = (bf16[128,768]{1,0:T(8,128)(2,1)S(1)}, bf16[128,768]{1,0:T(8,128)(2,1)S(1)}, u32[]{:S(2)}, u32[]{:S(2)}) collective-permute-start(bf16[128,768]{1,0:T(8,128)(2,1)S(1)} %bitcast.57), channel_id=1, source_target_pairs={{0,2},{1,3},{2,0},{3,1},{4,6},{5,7},{6,4},{7,5},{8,10},{9,11},{10,... | collective-permute-start | bytes 589832 | tf_op jit(solution)/shard_map/ppermute | solution.py:167
  31.7 12.6 %all-to-all-start.1 = ((bf16[8,16,896]{2,1,0:T(8,128)(2,1)}), bf16[8,16,896]{2,1,0:T(8,128)(2,1)S(1)}, u32[]{:S(2)}, u32[]{:S(2)}) async-start(bf16[8,16,896]{2,1,0:T(8,128)(2,1)} %bitcast.12), calls=%async_computation.1 | async-start | bytes 458752 | tf_op jit(solution)/shard_map/all_to_all | solution.py:398
  35.2 9.2 %collective-permute-start.11 = (bf16[128,768]{1,0:T(8,128)(2,1)S(1)}, bf16[128,768]{1,0:T(8,128)(2,1)S(1)}, u32[]{:S(2)}, u32[]{:S(2)}) collective-permute-start(bf16[128,768]{1,0:T(8,128)(2,1)S(1)} %bitcast.58), channel_id=1, source_target_pairs={{0,1},{1,0},{2,3},{3,2},{4,5},{5,4},{6,7},{7,6},{8,9},{9,8},{10,11... | collective-permute-start | bytes 589832 | tf_op jit(solution)/shard_map/ppermute | solution.py:167
  36.8 7.5 %collective-permute-start.13 = (bf16[128,768]{1,0:T(8,128)(2,1)S(1)}, bf16[128,768]{1,0:T(8,128)(2,1)S(1)}, u32[]{:S(2)}, u32[]{:S(2)}) collective-permute-start(bf16[128,768]{1,0:T(8,128)(2,1)S(1)} %collective-permute-done.12.refs_3_), channel_id=1, source_target_pairs={{0,1},{1,0},{2,3},{3,2},{4,5},{5,4},{6,7},{7,6},{8,9},{9,8},{10,11... | collective-permute-start | bytes 589832 | tf_op jit(solution)/shard_map/ppermute | solution.py:167
  36.9 3.8 %collective-permute-start.10 = (bf16[128,192]{1,0:T(8,128)(2,1)S(1)}, bf16[128,192]{1,0:T(8,128)(2,1)S(1)}, u32[]{:S(2)}, u32[]{:S(2)}) collective-permute-start(bf16[128,192]{1,0:T(8,128)(2,1)S(1)} %get-tuple-element.433), channel_id=1, source_target_pairs={{0,3},{1,2},{2,1},{3,0},{4,7},{5,6},{6,5},{7,4},{8,11},{9,10},{10,... | collective-permute-start | bytes 147464 | tf_op jit(solution)/shard_map/ppermute | solution.py:167
  37.6 3.1 %collective-permute-start.8 = (bf16[128,192]{1,0:T(8,128)(2,1)S(1)}, bf16[128,192]{1,0:T(8,128)(2,1)S(1)}, u32[]{:S(2)}, u32[]{:S(2)}) collective-permute-start(bf16[128,192]{1,0:T(8,128)(2,1)S(1)} %get-tuple-element.435), channel_id=1, source_target_pairs={{0,1},{1,0},{2,3},{3,2},{4,5},{5,4},{6,7},{7,6},{8,9},{9,8},{10,11... | collective-permute-start | bytes 147464 | tf_op jit(solution)/shard_map/ppermute | solution.py:167
  37.6 5.1 %collective-permute-start.9 = (bf16[128,192]{1,0:T(8,128)(2,1)S(1)}, bf16[128,192]{1,0:T(8,128)(2,1)S(1)}, u32[]{:S(2)}, u32[]{:S(2)}) collective-permute-start(bf16[128,192]{1,0:T(8,128)(2,1)S(1)} %get-tuple-element.434), channel_id=1, source_target_pairs={{0,2},{1,3},{2,0},{3,1},{4,6},{5,7},{6,4},{7,5},{8,10},{9,11},{10,... | collective-permute-start | bytes 147464 | tf_op jit(solution)/shard_map/ppermute | solution.py:167
  44.4 4.3 %collective-permute-start.15 = (bf16[128,896]{1,0:T(8,128)(2,1)S(1)}, bf16[128,896]{1,0:T(8,128)(2,1)S(1)}, u32[]{:S(2)}, u32[]{:S(2)}) collective-permute-start(bf16[128,896]{1,0:T(8,128)(2,1)S(1)} %bitcast.54), channel_id=1, source_target_pairs={{0,1},{1,0},{2,3},{3,2},{4,5},{5,4},{6,7},{7,6},{8,9},{9,8},{10,11... | collective-permute-start | bytes 688136 | tf_op jit(solution)/shard_map/ppermute | solution.py:167
  44.5 8.0 %collective-permute-start.14 = (bf16[128,896]{1,0:T(8,128)(2,1)S(1)}, bf16[128,896]{1,0:T(8,128)(2,1)S(1)}, u32[]{:S(2)}, u32[]{:S(2)}) collective-permute-start(bf16[128,896]{1,0:T(8,128)(2,1)S(1)} %bitcast.55), channel_id=1, source_target_pairs={{0,2},{1,3},{2,0},{3,1},{4,6},{5,7},{6,4},{7,5},{8,10},{9,11},{10,... | collective-permute-start | bytes 688136 | tf_op jit(solution)/shard_map/ppermute | solution.py:167
  50.0 2.5 %collective-permute-start.16 = (bf16[128,896]{1,0:T(8,128)(2,1)S(1)}, bf16[128,896]{1,0:T(8,128)(2,1)S(1)}, u32[]{:S(2)}, u32[]{:S(2)}) collective-permute-start(bf16[128,896]{1,0:T(8,128)(2,1)S(1)} %get-tuple-element.264), channel_id=1, source_target_pairs={{0,1},{1,0},{2,3},{3,2},{4,5},{5,4},{6,7},{7,6},{8,9},{9,8},{10,11... | collective-permute-start | bytes 688136 | tf_op jit(solution)/shard_map/ppermute | solution.py:167
  56.9 7.7 %collective-permute-start.20 = (bf16[128,896]{1,0:T(8,128)(2,1)S(1)}, bf16[128,896]{1,0:T(8,128)(2,1)S(1)}, u32[]{:S(2)}, u32[]{:S(2)}) collective-permute-start(bf16[128,896]{1,0:T(8,128)(2,1)S(1)} %add.56), channel_id=1, source_target_pairs={{0,2},{1,3},{2,0},{3,1},{4,6},{5,7},{6,4},{7,5},{8,10},{9,11},{10,... | collective-permute-start | bytes 688136 | tf_op jit(solution)/shard_map/ppermute | solution.py:167
  58.6 6.8 %collective-permute-start.19 = (bf16[2,128,768]{2,1,0:T(8,128)(2,1)S(1)}, bf16[2,128,768]{2,1,0:T(8,128)(2,1)S(1)}, u32[]{:S(2)}, u32[]{:S(2)}) collective-permute-start(bf16[2,128,768]{2,1,0:T(8,128)(2,1)S(1)} %get-tuple-element.277), channel_id=1, source_target_pairs={{0,1},{1,0},{2,3},{3,2},{4,5},{5,4},{6,7},{7,6},{8,9},{9,8},{10,11... | collective-permute-start | bytes 1179656 | tf_op jit(solution)/shard_map/ppermute | solution.py:167
  65.4 7.4 %collective-permute-start.21 = (bf16[128,768]{1,0:T(8,128)(2,1)S(1)}, bf16[128,768]{1,0:T(8,128)(2,1)S(1)}, u32[]{:S(2)}, u32[]{:S(2)}) collective-permute-start(bf16[128,768]{1,0:T(8,128)(2,1)S(1)} %fusion), channel_id=1, source_target_pairs={{0,2},{1,3},{2,0},{3,1},{4,6},{5,7},{6,4},{7,5},{8,10},{9,11},{10,... | collective-permute-start | bytes 589832 | tf_op jit(solution)/shard_map/ppermute | solution.py:167
  66.3 13.4 %all-to-all-start.3 = ((bf16[8,16,896]{2,1,0:T(8,128)(2,1)}), bf16[8,16,896]{2,1,0:T(8,128)(2,1)S(1)}, u32[]{:S(2)}, u32[]{:S(2)}) async-start(bf16[8,16,896]{2,1,0:T(8,128)(2,1)} %bitcast.22), calls=%async_computation.3 | async-start | bytes 458752 | tf_op jit(solution)/shard_map/all_to_all | solution.py:398
  80.5 6.2 %collective-permute-start.23 = (bf16[128,768]{1,0:T(8,128)(2,1)S(1)}, bf16[128,768]{1,0:T(8,128)(2,1)S(1)}, u32[]{:S(2)}, u32[]{:S(2)}) collective-permute-start(bf16[128,768]{1,0:T(8,128)(2,1)S(1)} %get-tuple-element.314.refs_1_), channel_id=1, source_target_pairs={{0,2},{1,3},{2,0},{3,1},{4,6},{5,7},{6,4},{7,5},{8,10},{9,11},{10,... | collective-permute-start | bytes 589832 | tf_op jit(solution)/shard_map/ppermute | solution.py:167
  81.2 12.3 %all-to-all-start.2 = ((bf16[8,16,768]{2,1,0:T(8,128)(2,1)}), bf16[8,16,768]{2,1,0:T(8,128)(2,1)S(1)}, u32[]{:S(2)}, u32[]{:S(2)}) async-start(bf16[8,16,768]{2,1,0:T(8,128)(2,1)} %bitcast.20), calls=%async_computation.2 | async-start | bytes 393216 | tf_op jit(solution)/shard_map/all_to_all | solution.py:398
  84.6 2.7 %collective-permute-start.22 = (bf16[128,768]{1,0:T(8,128)(2,1)S(1)}, bf16[128,768]{1,0:T(8,128)(2,1)S(1)}, u32[]{:S(2)}, u32[]{:S(2)}) collective-permute-start(bf16[128,768]{1,0:T(8,128)(2,1)S(1)} %get-tuple-element.314.refs_1_), channel_id=1, source_target_pairs={{0,1},{1,0},{2,3},{3,2},{4,5},{5,4},{6,7},{7,6},{8,9},{9,8},{10,11... | collective-permute-start | bytes 589832 | tf_op jit(solution)/shard_map/ppermute | solution.py:167
  93.4 16.1 %collective-permute-start.25 = (bf16[2,208,384]{2,1,0:T(8,128)(2,1)S(1)}, bf16[2,208,384]{2,1,0:T(8,128)(2,1)S(1)}, u32[]{:S(2)}, u32[]{:S(2)}) collective-permute-start(bf16[2,208,384]{2,1,0:T(8,128)(2,1)S(1)} %get-tuple-element.363), channel_id=1, source_target_pairs={{0,1},{1,0},{2,3},{3,2},{4,5},{5,4},{6,7},{7,6},{8,9},{9,8},{10,11... | collective-permute-start | bytes 958472 | tf_op jit(solution)/shard_map/ppermute | solution.py:167
  93.9 15.7 %collective-permute-start.29 = (bf16[256,768]{1,0:T(8,128)(2,1)S(1)}, bf16[256,768]{1,0:T(8,128)(2,1)S(1)}, u32[]{:S(2)}, u32[]{:S(2)}) collective-permute-start(bf16[256,768]{1,0:T(8,128)(2,1)S(1)} %get-tuple-element.378), channel_id=1, source_target_pairs={{0,4},{4,0},{8,12},{12,8},{16,20},{20,16},{24,28},{28,24},{1,5},{5... | collective-permute-start | bytes 1179656 | tf_op jit(solution)/shard_map/ppermute | solution.py:167
  95.7 9.4 %collective-permute-start.26 = (bf16[80,768]{1,0:T(8,128)(2,1)S(1)}, bf16[80,768]{1,0:T(8,128)(2,1)S(1)}, u32[]{:S(2)}, u32[]{:S(2)}) collective-permute-start(bf16[80,768]{1,0:T(8,128)(2,1)S(1)} %get-tuple-element.375), channel_id=1, source_target_pairs={{0,8},{4,12},{8,0},{12,4},{16,24},{20,28},{24,16},{28,20},{1,9},{5... | collective-permute-start | bytes 368648 | tf_op jit(solution)/shard_map/ppermute | solution.py:167
  97.2 12.3 %collective-permute-start.27 = (bf16[80,768]{1,0:T(8,128)(2,1)S(1)}, bf16[80,768]{1,0:T(8,128)(2,1)S(1)}, u32[]{:S(2)}, u32[]{:S(2)}) collective-permute-start(bf16[80,768]{1,0:T(8,128)(2,1)S(1)} %get-tuple-element.376), channel_id=1, source_target_pairs={{0,16},{4,20},{8,24},{12,28},{16,0},{20,4},{24,8},{28,12},{1,17},{... | collective-permute-start | bytes 368648 | tf_op jit(solution)/shard_map/ppermute | solution.py:167
  99.6 10.0 %collective-permute-start.28 = (bf16[80,768]{1,0:T(8,128)(2,1)S(1)}, bf16[80,768]{1,0:T(8,128)(2,1)S(1)}, u32[]{:S(2)}, u32[]{:S(2)}) collective-permute-start(bf16[80,768]{1,0:T(8,128)(2,1)S(1)} %get-tuple-element.377), channel_id=1, source_target_pairs={{0,24},{4,28},{8,16},{12,20},{16,8},{20,12},{24,0},{28,4},{1,25},{... | collective-permute-start | bytes 368648 | tf_op jit(solution)/shard_map/ppermute | solution.py:167
  109.7 9.0 %collective-permute-start.32 = (bf16[64,768]{1,0:T(8,128)(2,1)S(1)}, bf16[64,768]{1,0:T(8,128)(2,1)S(1)}, u32[]{:S(2)}, u32[]{:S(2)}) collective-permute-start(bf16[64,768]{1,0:T(8,128)(2,1)S(1)} %get-tuple-element.432), channel_id=1, source_target_pairs={{0,8},{4,12},{8,0},{12,4},{16,24},{20,28},{24,16},{28,20},{1,9},{5... | collective-permute-start | bytes 294920 | tf_op jit(solution)/shard_map/ppermute | solution.py:167
  111.6 9.2 %collective-permute-start.33 = (bf16[64,768]{1,0:T(8,128)(2,1)S(1)}, bf16[64,768]{1,0:T(8,128)(2,1)S(1)}, u32[]{:S(2)}, u32[]{:S(2)}) collective-permute-start(bf16[64,768]{1,0:T(8,128)(2,1)S(1)} %get-tuple-element.431), channel_id=1, source_target_pairs={{0,16},{4,20},{8,24},{12,28},{16,0},{20,4},{24,8},{28,12},{1,17},{... | collective-permute-start | bytes 294920 | tf_op jit(solution)/shard_map/ppermute | solution.py:167
  112.6 8.2 %collective-permute-start.34 = (bf16[64,768]{1,0:T(8,128)(2,1)S(1)}, bf16[64,768]{1,0:T(8,128)(2,1)S(1)}, u32[]{:S(2)}, u32[]{:S(2)}) collective-permute-start(bf16[64,768]{1,0:T(8,128)(2,1)S(1)} %get-tuple-element.430), channel_id=1, source_target_pairs={{0,24},{4,28},{8,16},{12,20},{16,8},{20,12},{24,0},{28,4},{1,25},{... | collective-permute-start | bytes 294920 | tf_op jit(solution)/shard_map/ppermute | solution.py:167
  114.2 4.4 %collective-permute-start.31 = (bf16[48,768]{1,0:T(8,128)(2,1)S(1)}, bf16[48,768]{1,0:T(8,128)(2,1)S(1)}, u32[]{:S(2)}, u32[]{:S(2)}) collective-permute-start(bf16[48,768]{1,0:T(8,128)(2,1)S(1)} %concatenate.16), channel_id=1, source_target_pairs={{0,4},{4,0},{8,12},{12,8},{16,20},{20,16},{24,28},{28,24},{1,5},{5... | collective-permute-start | bytes 221192 | tf_op jit(solution)/shard_map/ppermute | solution.py:167
  114.9 6.0 %collective-permute-start.30 = (bf16[208,384]{1,0:T(8,128)(2,1)S(1)}, bf16[208,384]{1,0:T(8,128)(2,1)S(1)}, u32[]{:S(2)}, u32[]{:S(2)}) collective-permute-start(bf16[208,384]{1,0:T(8,128)(2,1)S(1)} %bitcast_add_fusion), channel_id=1, source_target_pairs={{0,2},{1,3},{2,0},{3,1},{4,6},{5,7},{6,4},{7,5},{8,10},{9,11},{10,... | collective-permute-start | bytes 479240 | tf_op jit(solution)/shard_map/ppermute | solution.py:167
  120.9 3.8 %collective-permute-start.35 = (f32[16,768]{1,0:T(8,128)S(1)}, f32[16,768]{1,0:T(8,128)S(1)}, u32[]{:S(2)}, u32[]{:S(2)}) collective-permute-start(f32[16,768]{1,0:T(8,128)S(1)} %slice_convert_fusion), channel_id=1, source_target_pairs={{0,1},{1,0},{2,3},{3,2},{4,5},{5,4},{6,7},{7,6},{8,9},{9,8},{10,11... | collective-permute-start | bytes 147464 | tf_op jit(solution)/shard_map/ppermute | solution.py:167
  120.9 5.4 %collective-permute-start.40 = (bf16[32,768]{1,0:T(8,128)(2,1)S(1)}, bf16[32,768]{1,0:T(8,128)(2,1)S(1)}, u32[]{:S(2)}, u32[]{:S(2)}) collective-permute-start(bf16[32,768]{1,0:T(8,128)(2,1)S(1)} %slice.76), channel_id=1, source_target_pairs={{0,4},{4,0},{8,12},{12,8},{16,20},{20,16},{24,28},{28,24},{1,5},{5... | collective-permute-start | bytes 147464 | tf_op jit(solution)/shard_map/ppermute | solution.py:167
  121.9 5.8 %collective-permute-start.36 = (bf16[192,128]{1,0:T(8,128)(2,1)S(1)}, bf16[192,128]{1,0:T(8,128)(2,1)S(1)}, u32[]{:S(2)}, u32[]{:S(2)}) collective-permute-start(bf16[192,128]{1,0:T(8,128)(2,1)S(1)} %get-tuple-element.392), channel_id=1, source_target_pairs={{0,1},{1,0},{2,3},{3,2},{4,5},{5,4},{6,7},{7,6},{8,9},{9,8},{10,11... | collective-permute-start | bytes 147464 | tf_op jit(solution)/shard_map/ppermute | solution.py:167
  122.0 7.1 %collective-permute-start.37 = (bf16[192,128]{1,0:T(8,128)(2,1)S(1)}, bf16[192,128]{1,0:T(8,128)(2,1)S(1)}, u32[]{:S(2)}, u32[]{:S(2)}) collective-permute-start(bf16[192,128]{1,0:T(8,128)(2,1)S(1)} %get-tuple-element.393), channel_id=1, source_target_pairs={{0,2},{1,3},{2,0},{3,1},{4,6},{5,7},{6,4},{7,5},{8,10},{9,11},{10,... | collective-permute-start | bytes 147464 | tf_op jit(solution)/shard_map/ppermute | solution.py:167
  123.5 9.6 %collective-permute-start.39 = (bf16[64,768]{1,0:T(8,128)(2,1)S(1)}, bf16[64,768]{1,0:T(8,128)(2,1)S(1)}, u32[]{:S(2)}, u32[]{:S(2)}) collective-permute-start(bf16[64,768]{1,0:T(8,128)(2,1)S(1)} %add_convert_fusion.2.refs_3_), channel_id=1, source_target_pairs={{0,4},{4,0},{8,12},{12,8},{16,20},{20,16},{24,28},{28,24},{1,5},{5... | collective-permute-start | bytes 294920 | tf_op jit(solution)/shard_map/ppermute | solution.py:167
  124.7 8.4 %collective-permute-start.41 = (bf16[64,768]{1,0:T(8,128)(2,1)S(1)}, bf16[64,768]{1,0:T(8,128)(2,1)S(1)}, u32[]{:S(2)}, u32[]{:S(2)}) collective-permute-start(bf16[64,768]{1,0:T(8,128)(2,1)S(1)} %add_convert_fusion.2.refs_3_), channel_id=1, source_target_pairs={{0,8},{4,12},{8,0},{12,4},{16,24},{20,28},{24,16},{28,20},{1,9},{5... | collective-permute-start | bytes 294920 | tf_op jit(solution)/shard_map/ppermute | solution.py:167
  126.3 10.4 %collective-permute-start.42 = (bf16[64,768]{1,0:T(8,128)(2,1)S(1)}, bf16[64,768]{1,0:T(8,128)(2,1)S(1)}, u32[]{:S(2)}, u32[]{:S(2)}) collective-permute-start(bf16[64,768]{1,0:T(8,128)(2,1)S(1)} %add_convert_fusion.2.refs_3_), channel_id=1, source_target_pairs={{0,16},{4,20},{8,24},{12,28},{16,0},{20,4},{24,8},{28,12},{1,17},{... | collective-permute-start | bytes 294920 | tf_op jit(solution)/shard_map/ppermute | solution.py:167
  127.7 9.0 %collective-permute-start.43 = (bf16[64,768]{1,0:T(8,128)(2,1)S(1)}, bf16[64,768]{1,0:T(8,128)(2,1)S(1)}, u32[]{:S(2)}, u32[]{:S(2)}) collective-permute-start(bf16[64,768]{1,0:T(8,128)(2,1)S(1)} %add_convert_fusion.2.refs_3_), channel_id=1, source_target_pairs={{0,24},{4,28},{8,16},{12,20},{16,8},{20,12},{24,0},{28,4},{1,25},{... | collective-permute-start | bytes 294920 | tf_op jit(solution)/shard_map/ppermute | solution.py:167
  129.1 3.9 %collective-permute-start.38 = (bf16[192,128]{1,0:T(8,128)(2,1)S(1)}, bf16[192,128]{1,0:T(8,128)(2,1)S(1)}, u32[]{:S(2)}, u32[]{:S(2)}) collective-permute-start(bf16[192,128]{1,0:T(8,128)(2,1)S(1)} %get-tuple-element.394), channel_id=1, source_target_pairs={{0,3},{1,2},{2,1},{3,0},{4,7},{5,6},{6,5},{7,4},{8,11},{9,10},{10,... | collective-permute-start | bytes 147464 | tf_op jit(solution)/shard_map/ppermute | solution.py:167
  136.7 9.5 %collective-permute-start.45 = (bf16[64,768]{1,0:T(8,128)(2,1)S(1)}, bf16[64,768]{1,0:T(8,128)(2,1)S(1)}, u32[]{:S(2)}, u32[]{:S(2)}) collective-permute-start(bf16[64,768]{1,0:T(8,128)(2,1)S(1)} %pad_maximum_fusion.refs_7_), channel_id=1, source_target_pairs={{0,8},{4,12},{8,0},{12,4},{16,24},{20,28},{24,16},{28,20},{1,9},{5... | collective-permute-start | bytes 294920 | tf_op jit(solution)/shard_map/ppermute | solution.py:167
  138.4 9.5 %collective-permute-start.46 = (bf16[64,768]{1,0:T(8,128)(2,1)S(1)}, bf16[64,768]{1,0:T(8,128)(2,1)S(1)}, u32[]{:S(2)}, u32[]{:S(2)}) collective-permute-start(bf16[64,768]{1,0:T(8,128)(2,1)S(1)} %pad_maximum_fusion.refs_7_), channel_id=1, source_target_pairs={{0,16},{4,20},{8,24},{12,28},{16,0},{20,4},{24,8},{28,12},{1,17},{... | collective-permute-start | bytes 294920 | tf_op jit(solution)/shard_map/ppermute | solution.py:167
  139.3 8.6 %collective-permute-start.47 = (bf16[64,768]{1,0:T(8,128)(2,1)S(1)}, bf16[64,768]{1,0:T(8,128)(2,1)S(1)}, u32[]{:S(2)}, u32[]{:S(2)}) collective-permute-start(bf16[64,768]{1,0:T(8,128)(2,1)S(1)} %pad_maximum_fusion.refs_7_), channel_id=1, source_target_pairs={{0,24},{4,28},{8,16},{12,20},{16,8},{20,12},{24,0},{28,4},{1,25},{... | collective-permute-start | bytes 294920 | tf_op jit(solution)/shard_map/ppermute | solution.py:167
  141.2 7.2 %collective-permute-start.48 = (bf16[192,768]{1,0:T(8,128)(2,1)S(1)}, bf16[192,768]{1,0:T(8,128)(2,1)S(1)}, u32[]{:S(2)}, u32[]{:S(2)}) collective-permute-start(bf16[192,768]{1,0:T(8,128)(2,1)S(1)} %constant_dynamic-update-slice_fusion.refs_4_), channel_id=1, source_target_pairs={{0,4},{4,0},{8,12},{12,8},{16,20},{20,16},{24,28},{28,24},{1,5},{5... | collective-permute-start | bytes 884744 | tf_op jit(solution)/shard_map/ppermute | solution.py:167
  141.8 4.3 %collective-permute-start.44 = (f32[16,768]{1,0:T(8,128)S(1)}, f32[16,768]{1,0:T(8,128)S(1)}, u32[]{:S(2)}, u32[]{:S(2)}) collective-permute-start(f32[16,768]{1,0:T(8,128)S(1)} %fusion.4.refs_1_), channel_id=1, source_target_pairs={{0,2},{1,3},{2,0},{3,1},{4,6},{5,7},{6,4},{7,5},{8,10},{9,11},{10,... | collective-permute-start | bytes 147464 | tf_op jit(solution)/shard_map/ppermute | solution.py:167
  (14 other events, 35.5 us)
